TPU v7x, 32 devices: a whole 2x2x4 slice. The times are simulated.
32 devices in a mesh: rows: 8 (over z, x), width: 4 (over y, core).
Axes of the slice: x: 2, y: 2, z: 4, core: 2. Of those that a mesh axis runs over, the one named last changes fastest.
Arguments:
- x_in: bfloat16 [768, 4096], P('width', 'rows'), may hold values from -6 to 6
- history: bfloat16 [30, 768, 4096], P(None, 'width', 'rows'), may hold values from -6 to 6
- cotangent: bfloat16 [768, 4096], P('width', 'rows'), may hold values from -6 to 6
- counts: int32 [8], P('rows'), may hold values from 128 to 512, as said below
- positions: int32 [4096], P('rows'), may hold values from 0 to 1022, as said below
- mix_weights: float32 [30], replicated, may hold values from -0.3 to 0.3
- self_weight: float32 [1], replicated, may hold values from 0.7 to 1.3
- first_norm_gain: float32 [768], P('width'), may hold values from 0.5 to 1.5
- first_norm_bias: float32 [768], P('width'), may hold values from -3 to 3
- w_qkv: bfloat16 [3, 768, 768], P(None, 'width'), may hold values from -0.21875 to 0.21875
- w_out: bfloat16 [768, 768], P('width'), may hold values from -0.875 to 0.875
- second_norm_gain: float32 [768], P('width'), may hold values from 0.5 to 1.5
- second_norm_bias: float32 [768], P('width'), may hold values from -3 to 3
- w_up: bfloat16 [768, 3072], P(None, 'width'), may hold values from -0.21875 to 0.21875
- w_down: bfloat16 [3072, 768], P('width'), may hold values from -0.109375 to 0.109375
Outputs:
- mixed: bfloat16 [768, 4096], P('width', 'rows')
- d_input: float32 [768, 4096], P('width', 'rows')
- d_history: bfloat16 [30, 768, 4096], P(None, 'width', 'rows')
- d_mix: float32 [30], replicated
- d_self: float32 [1], replicated
- d_gain1: float32 [768], P('width')
- d_bias1: float32 [768], P('width')
- d_w_qkv: float32 [3, 768, 768], P(None, 'width')
- d_w_out: float32 [768, 768], P('width')
- d_gain2: float32 [768], P('width')
- d_bias2: float32 [768], P('width')
- d_w_up: float32 [768, 3072], P(None, 'width')
- d_w_down: float32 [3072, 768], P('width')
Inputs may be any that keep to these rules, and one draw needn't show every extreme that they name: `counts`: one sequence has 512 real tokens and another 512 // 4; real tokens come first in a sequence. `positions`: 0 at the first token of each sequence, strictly increasing within it by 1 to 3.
All inputs are finite; a program needn't handle non-finite values.
Results may differ from a plain program's by a relative error of at most 0.011.
Values may be sent and summed in bfloat16 or wider, within the bound.
No kernel may reach another device: no remote copies, remote signals or barrier semaphores. Data moves between devices by JAX's collectives and lax.ppermute only.
A program may use at most 128 MiB of HBM per device.

v0:
```python
import jax
import jax.numpy as jnp
from jax import lax
from jax.sharding import PartitionSpec as P

HEAD_DIM = 64


EPSILON = 1e-05


def angle_table(positions, head_width):
    freq_index = jnp.arange(head_width // 2, dtype=jnp.float32)
    inverse = 1.0 / 10000.0 ** (freq_index * 2.0 / head_width)
    return positions.astype(jnp.float32)[:, None] * inverse[None, :]


def rotate(values, cosine, sine_table):
    half_width = values.shape[-1] // 2
    front_part = values[..., :half_width]
    back_part = values[..., half_width:]
    return jnp.concatenate(
        [
            front_part * cosine - back_part * sine_table,
            back_part * cosine + front_part * sine_table,
        ],
        axis=-1,
    )


def rotate_back(grads_in, cosine, sine_table):
    half_width = grads_in.shape[-1] // 2
    front_part = grads_in[..., :half_width]
    back_part = grads_in[..., half_width:]
    return jnp.concatenate(
        [
            front_part * cosine + back_part * sine_table,
            back_part * cosine - front_part * sine_table,
        ],
        axis=-1,
    )


def layernorm_forward(values, embedding_width):
    mean_row = lax.psum(jnp.sum(values, axis=1), "width") / embedding_width
    centred = values - mean_row[:, None]
    variance = lax.psum(jnp.sum(centred * centred, axis=1), "width") / embedding_width
    inverse_deviation = lax.rsqrt(variance + EPSILON)
    return ((values - mean_row[:, None]) * inverse_deviation[:, None], inverse_deviation)


def layernorm_backward(
    normalized_gradient, standardized, inverse_deviation, layernorm_gain, embedding_width
):
    gain_gradient = jnp.sum(normalized_gradient * standardized, axis=0)
    d_bias = jnp.sum(normalized_gradient, axis=0)
    standardized_gradient = normalized_gradient * layernorm_gain
    per_row_totals = lax.psum(
        (
            jnp.sum(standardized_gradient, axis=1),
            jnp.sum(standardized_gradient * standardized, axis=1),
        ),
        "width",
    )
    d_values = inverse_deviation[:, None] * (
        standardized_gradient
        - per_row_totals[0][:, None] / embedding_width
        - standardized * per_row_totals[1][:, None] / embedding_width
    )
    return (d_values, gain_gradient, d_bias)


def gather_features(values):
    return lax.all_gather(values, "width", axis=1, tiled=True)


def gather_gradient(values):
    return lax.all_gather(values, "width", axis=1, tiled=True)


def reduce_branch(partial_terms):
    return lax.psum_scatter(partial_terms, "width", scatter_dimension=1, tiled=True)


def reduce_input(partial_terms):
    return lax.psum_scatter(partial_terms, "width", scatter_dimension=1, tiled=True)


def contract_rows(left_side, right_side):
    return lax.dot_general(
        left_side, right_side, (((0,), (0,)), ((), ())), preferred_element_type=jnp.float32
    )


def scores_of(queries, keys_rot, causal, score_scale):
    raw_scores = (
        jnp.einsum("qhd,khd->hqk", queries, keys_rot, preferred_element_type=jnp.float32)
        * score_scale
    )
    return jnp.where(causal[None], raw_scores, -1e30)


def local(
    x_in,
    history,
    cotangent,
    counts,
    positions,
    mix_weights,
    self_weight,
    first_norm_gain,
    first_norm_bias,
    w_qkv,
    w_out,
    second_norm_gain,
    second_norm_bias,
    w_up,
    w_down,
):
    slice_width, row_count = x_in.shape
    embedding_width = w_out.shape[1]
    local_heads = slice_width // HEAD_DIM
    score_scale = HEAD_DIM ** (-0.5)
    live_total = lax.psum(counts, "rows")
    loss_scale = jnp.float32(row_count * lax.axis_size("rows")) / live_total[0].astype(jnp.float32)
    input_rows = x_in.astype(jnp.float32).T
    first_standardized, first_inverse_deviation = layernorm_forward(input_rows, embedding_width)
    first_normalized = (first_standardized * first_norm_gain + first_norm_bias).astype(jnp.bfloat16)
    full_one = gather_features(first_normalized)
    project = jnp.einsum(
        "tm,bom->tbo", full_one, w_qkv, preferred_element_type=jnp.float32
    ).reshape(row_count, 3, local_heads, HEAD_DIM)
    angles = angle_table(positions, HEAD_DIM)
    cosine = jnp.cos(angles)[:, None, :]
    sine_table = jnp.sin(angles)[:, None, :]
    queries = rotate(project[:, 0], cosine, sine_table).astype(jnp.bfloat16)
    keys_rot = rotate(project[:, 1], cosine, sine_table).astype(jnp.bfloat16)
    values_in = project[:, 2].astype(jnp.bfloat16)
    causal = jnp.arange(row_count)[:, None] >= jnp.arange(row_count)[None, :]
    scores = scores_of(queries, keys_rot, causal, score_scale)
    row_top = jnp.max(scores, axis=-1, keepdims=True)
    exp_scores = jnp.exp(scores - row_top)
    exp_total = jnp.sum(exp_scores, axis=-1, keepdims=True)
    soft_weights = exp_scores / exp_total
    log_total = row_top + jnp.log(exp_total)
    heads_out = jnp.einsum(
        "hqk,khd->qhd",
        soft_weights.astype(jnp.bfloat16),
        values_in,
        preferred_element_type=jnp.float32,
    )
    mixed_heads = heads_out.reshape(row_count, slice_width).astype(jnp.bfloat16)
    attended = reduce_branch(jnp.dot(mixed_heads, w_out, preferred_element_type=jnp.float32))
    between_layers = input_rows + attended
    second_standardized, second_inverse_deviation = layernorm_forward(
        between_layers, embedding_width
    )
    second_normalized = (second_standardized * second_norm_gain + second_norm_bias).astype(
        jnp.bfloat16
    )
    full_two = gather_features(second_normalized)
    hidden = jnp.dot(full_two, w_up, preferred_element_type=jnp.float32)
    active = jax.nn.gelu(hidden).astype(jnp.bfloat16)
    output = between_layers + reduce_branch(
        jnp.dot(active, w_down, preferred_element_type=jnp.float32)
    )
    live_rows = jnp.arange(row_count) < counts[0]
    grad_wide = cotangent.astype(jnp.float32) * jnp.where(live_rows, loss_scale, 0.0)[None, :]
    grad_out = grad_wide.T
    output_wide = output.T

    def mix_layer(running, layer_pair):
        weight_one, past_layer = layer_pair
        layer_wide = past_layer.astype(jnp.float32)
        return (
            running + weight_one * layer_wide,
            (jnp.sum(grad_wide * layer_wide), (weight_one * grad_wide).astype(jnp.bfloat16)),
        )

    mixed_out, (mix_partial, d_history) = lax.scan(
        mix_layer, self_weight[0] * output_wide, (mix_weights, history)
    )
    self_partial = jnp.sum(grad_wide * output_wide)
    d_mix, d_self = lax.psum((mix_partial, self_partial[None]), ("rows", "width"))
    d_output = self_weight[0] * grad_out
    full_dout = gather_gradient(d_output.astype(jnp.bfloat16))
    d_active = jnp.dot(full_dout, w_down.T, preferred_element_type=jnp.float32)
    d_w_down = contract_rows(active, full_dout)
    unused, gelu_back = jax.vjp(jax.nn.gelu, hidden)
    d_hidden = gelu_back(d_active)[0].astype(jnp.bfloat16)
    d_w_up = contract_rows(full_two, d_hidden)
    second_normalized_gradient = reduce_input(
        jnp.dot(d_hidden, w_up.T, preferred_element_type=jnp.float32)
    )
    d_middle_norm, d_gain_two, d_bias_two = layernorm_backward(
        second_normalized_gradient,
        second_standardized,
        second_inverse_deviation,
        second_norm_gain,
        embedding_width,
    )
    d_middle = d_output + d_middle_norm
    full_dmid = gather_gradient(d_middle.astype(jnp.bfloat16))
    d_heads = (
        jnp.dot(full_dmid, w_out.T, preferred_element_type=jnp.float32)
        .astype(jnp.bfloat16)
        .reshape(row_count, local_heads, HEAD_DIM)
    )
    d_w_out = contract_rows(mixed_heads, full_dmid)
    scores = scores_of(queries, keys_rot, causal, score_scale)
    probs_back = jnp.exp(scores - log_total)
    d_probs = jnp.einsum("qhd,khd->hqk", d_heads, values_in, preferred_element_type=jnp.float32)
    inner_sum = jnp.sum(d_probs * probs_back, axis=-1, keepdims=True)
    d_scores = (probs_back * (d_probs - inner_sum)).astype(jnp.bfloat16)
    d_queries = (
        jnp.einsum("hqk,khd->qhd", d_scores, keys_rot, preferred_element_type=jnp.float32)
        * score_scale
    )
    d_keys = (
        jnp.einsum("hqk,qhd->khd", d_scores, queries, preferred_element_type=jnp.float32)
        * score_scale
    )
    d_values = jnp.einsum(
        "hqk,qhd->khd", probs_back.astype(jnp.bfloat16), d_heads, preferred_element_type=jnp.float32
    )
    d_project = jnp.stack(
        [
            rotate_back(d_queries, cosine, sine_table),
            rotate_back(d_keys, cosine, sine_table),
            d_values,
        ],
        axis=1,
    )
    d_project = d_project.reshape(row_count, 3, slice_width).astype(jnp.bfloat16)
    d_w_qkv = jnp.einsum("tbo,tm->bom", d_project, full_one, preferred_element_type=jnp.float32)
    first_normalized_gradient = reduce_input(
        jnp.einsum("tbo,bom->tm", d_project, w_qkv, preferred_element_type=jnp.float32)
    )
    d_input_norm, d_gain_one, d_bias_one = layernorm_backward(
        first_normalized_gradient,
        first_standardized,
        first_inverse_deviation,
        first_norm_gain,
        embedding_width,
    )
    d_input = d_middle + d_input_norm
    d_gain_one, d_bias_one, d_w_qkv, d_w_out, d_gain_two, d_bias_two, d_w_up, d_w_down = lax.psum(
        (d_gain_one, d_bias_one, d_w_qkv, d_w_out, d_gain_two, d_bias_two, d_w_up, d_w_down), "rows"
    )
    return (
        mixed_out.astype(jnp.bfloat16),
        d_input.T,
        d_history,
        d_mix,
        d_self,
        d_gain_one,
        d_bias_one,
        d_w_qkv,
        d_w_out,
        d_gain_two,
        d_bias_two,
        d_w_up,
        d_w_down,
    )


def solution(mesh):
    return jax.shard_map(
        local,
        mesh=mesh,
        in_specs=(
            P("width", "rows"),
            P(None, "width", "rows"),
            P("width", "rows"),
            P("rows"),
            P("rows"),
            P(),
            P(),
            P("width"),
            P("width"),
            P(None, "width", None),
            P("width", None),
            P("width"),
            P("width"),
            P(None, "width"),
            P("width", None),
        ),
        out_specs=(
            P("width", "rows"),
            P("width", "rows"),
            P(None, "width", "rows"),
            P(),
            P(),
            P("width"),
            P("width"),
            P(None, "width", None),
            P("width", None),
            P("width"),
            P("width"),
            P(None, "width"),
            P("width", None),
        ),
        check_vma=False,
    )
```

profile of v0, /device:TPU:0, one launch (start us, length us, event | category | flops | bytes accessed | tf_op | source)
XLA Modules:
  0.0 482.8 jit_solution(15353187331105697334)
XLA Ops:
  9.2 8.4 %psum.133 = f32[512]{0:T(512)S(1)} all-reduce(f32[512]{0:T(512)S(1)} %convert_reduce_fusion), channel_id=1, replica_groups=mesh['rows'=8,'width'=4] {'width'}, use_global_device_ids=true, to_apply=%region_1.0 | all-reduce | flops 512 | bytes 4096 | tf_op jit(solution)/shard_map/psum | solution.py:45
  18.6 5.8 %psum.134 = f32[512]{0:T(512)S(1)} all-reduce(f32[512]{0:T(512)S(1)} %fusion.44), channel_id=1, replica_groups=mesh['rows'=8,'width'=4] {'width'}, use_global_device_ids=true, to_apply=%region_3.0 | all-reduce | flops 512 | bytes 4096 | tf_op jit(solution)/shard_map/psum | solution.py:47
  25.4 8.1 %all_gather.12 = bf16[512,768]{0,1:T(8,128)(2,1)S(1)} all-gather(bf16[512,192]{0,1:T(8,128)(2,1)S(1)} %fusion.36), channel_id=1, replica_groups=mesh['rows'=8,'width'=4] {'width'}, dimensions={1}, use_global_device_ids=true | all-gather | bytes 983040 | tf_op jit(solution)/shard_map/all_gather | solution.py:74
  40.5 29.1 %reduce-scatter.5.cloned.1.call-done = f32[512,192]{0,1:T(8,128)} async-done(((f32[512,768]{0,1:T(8,128)}), f32[512,192]{0,1:T(8,128)}) %reduce-scatter.5.cloned.1.call-update) | async-done | bytes 393232 | tf_op jit(solution)/shard_map/reduce_scatter | solution.py:82
  70.6 5.8 %psum.135 = f32[512]{0:T(512)S(1)} all-reduce(f32[512]{0:T(512)S(1)} %get-tuple-element.91), channel_id=1, replica_groups=mesh['rows'=8,'width'=4] {'width'}, use_global_device_ids=true, to_apply=%region_8.9 | all-reduce | flops 512 | bytes 4096 | tf_op jit(solution)/shard_map/psum | solution.py:45
  76.5 5.7 %psum.136 = f32[512]{0:T(512)S(1)} all-reduce(f32[512]{0:T(512)S(1)} %multiply_reduce_fusion.3), channel_id=1, replica_groups=mesh['rows'=8,'width'=4] {'width'}, use_global_device_ids=true, to_apply=%region_10.11 | all-reduce | flops 512 | bytes 4096 | tf_op jit(solution)/shard_map/psum | solution.py:47
  82.3 8.9 %all_gather.13 = bf16[512,768]{0,1:T(8,128)(2,1)S(1)} all-gather(bf16[512,192]{0,1:T(8,128)(2,1)S(1)} %add_convert_fusion), channel_id=1, replica_groups=mesh['rows'=8,'width'=4] {'width'}, dimensions={1}, use_global_device_ids=true | all-gather | bytes 983040 | tf_op jit(solution)/shard_map/all_gather | solution.py:74
  97.5 12.2 %psum.137 = s32[1]{0:T(128)} all-reduce(s32[1]{0:T(128)} %param.20), channel_id=1, replica_groups=mesh['rows'=8,'width'=4] {'rows'}, use_global_device_ids=true, to_apply=%region_12.13 | all-reduce | flops 1 | bytes 8 | tf_op jit(solution)/shard_map/psum | solution.py:124
  111.7 14.6 %reduce-scatter.7.cloned.1.call-done = f32[512,192]{0,1:T(8,128)} async-done(((f32[512,768]{0,1:T(8,128)}), f32[512,192]{0,1:T(8,128)}) %reduce-scatter.7.cloned.1.call-update) | async-done | bytes 393232 | tf_op jit(solution)/shard_map/reduce_scatter | solution.py:82
  128.2 8.2 %all_gather.14 = bf16[512,768]{0,1:T(8,128)(2,1)S(1)} all-gather(bf16[512,192]{0,1:T(8,128)(2,1)S(1)} %get-tuple-element.107), channel_id=1, replica_groups=mesh['rows'=8,'width'=4] {'width'}, dimensions={1}, use_global_device_ids=true | all-gather | bytes 983040 | tf_op jit(solution)/shard_map/all_gather | solution.py:78
  140.9 28.6 %reduce-scatter.9.cloned.1.call-done = f32[512,192]{0,1:T(8,128)} async-done(((f32[512,768]{0,1:T(8,128)}), f32[512,192]{0,1:T(8,128)}) %reduce-scatter.9.cloned.1.call-update) | async-done | bytes 393232 | tf_op jit(solution)/shard_map/reduce_scatter | solution.py:86
  171.3 5.7 %all-reduce.4 = (f32[512]{0:T(512)S(1)}, f32[512]{0:T(512)S(1)}) all-reduce(f32[512]{0:T(512)S(1)} %get-tuple-element.56, f32[512]{0:T(512)S(1)} %get-tuple-element.60), channel_id=1, replica_groups=mesh['rows'=8,'width'=4] {'width'}, use_global_device_ids=true, to_apply=%region_20.21 | all-reduce | flops 1024 | bytes 8192 | tf_op jit(solution)/shard_map/psum | solution.py:58
  178.9 9.0 %all_gather.15 = bf16[512,768]{0,1:T(8,128)(2,1)S(1)} all-gather(bf16[512,192]{0,1:T(8,128)(2,1)S(1)} %fusion.56), channel_id=1, replica_groups=mesh['rows'=8,'width'=4] {'width'}, dimensions={1}, use_global_device_ids=true | all-gather | bytes 983040 | tf_op jit(solution)/shard_map/all_gather | solution.py:78
  197.7 3.7 fusion.66
  201.5 2.6 fusion.57
  208.0 151.9 %while.14 = (s32[]{:T(128)}, f32[192,512]{1,0:T(8,128)S(1)}, f32[30]{0:T(128)S(1)}, bf16[30,192,512]{2,1,0:T(8,128)(2,1)}, f32[30]{0:T(128)S(1)}, /*index=5*/bf1...) while((s32[]{:T(128)}, f32[192,512]{1,0:T(8,128)S(1)}, f32[30]{0:T(128)S(1)}, ...), condition=%wide.region_15.16_spmd, body=%wide.region_13.15_spmd.sunk | while | flops 688129 | bytes 1966725 | solution.py:180
  208.6 2.4 fusion.91
  213.6 2.4 fusion.91
  218.7 2.4 fusion.91
  223.8 2.4 fusion.91
  228.8 2.4 fusion.91
  233.9 2.4 fusion.91
  238.9 2.4 fusion.91
  244.0 2.4 fusion.91
  249.1 2.4 fusion.91
  254.1 2.4 fusion.91
  259.2 2.4 fusion.91
  264.2 2.4 fusion.91
  269.3 2.4 fusion.91
  274.4 2.4 fusion.91
  279.5 2.4 fusion.91
  289.6 2.4 fusion.91
  294.7 2.4 fusion.91
  299.7 2.4 fusion.91
  304.8 2.4 fusion.91
  309.9 2.4 fusion.91
  314.9 2.4 fusion.91
  330.1 2.4 fusion.91
  335.2 2.4 fusion.91
  340.2 2.4 fusion.91
  345.3 2.4 fusion.91
  350.3 2.4 fusion.91
  355.4 2.4 fusion.91
  359.9 40.7 %all-reduce = (f32[30]{0:T(128)}, f32[1]{0:T(128)}) all-reduce(f32[30]{0:T(128)S(1)} %get-tuple-element.54, f32[1]{0:T(128)} %bitcast.27), channel_id=1, replica_groups=mesh['rows'=8,'width'=4] {'rows','width'}, use_global_device_ids=true, to_apply=%region_27.28 | all-reduce | flops 31 | bytes 248 | tf_op jit(solution)/shard_map/psum | solution.py:184
  402.6 22.7 %all-reduce.1 = (f32[192]{0:T(256)}, f32[192]{0:T(256)}, f32[192]{0:T(256)}, f32[192]{0:T(256)}) all-reduce(f32[192]{0:T(256)S(1)} %get-tuple-element.57, f32[192]{0:T(256)S(1)} %get-tuple-element.62, f32[192]{0:T(256)S(1)} %copy-done.52, f32[192]{0:T(256)S(1)} %copy-done.53), channel_id=1, replica_groups=mesh['rows'=8,'width'=4] {'rows'}, use_global_device_ids=true, to_apply=%region_31.32 | all-reduce | flops 768 | bytes 6144 | tf_op jit(solution)/shard_map/psum | solution.py:247
  425.3 6.0 %all-reduce.3 = (f32[512]{0:T(512)S(1)}, f32[512]{0:T(512)S(1)}) all-reduce(f32[512]{0:T(512)S(1)} %get-tuple-element.58, f32[512]{0:T(512)S(1)} %get-tuple-element.59), channel_id=1, replica_groups=mesh['rows'=8,'width'=4] {'width'}, use_global_device_ids=true, to_apply=%region_26.27 | all-reduce | flops 1024 | bytes 8192 | tf_op jit(solution)/shard_map/psum | solution.py:58
  433.4 35.1 %all-reduce.7.cloned.1.call-done = (f32[3,192,768]{2,1,0:T(8,128)}, f32[192,768]{1,0:T(8,128)}, f32[768,768]{1,0:T(8,128)}, f32[768,768]{1,0:T(8,128)}) async-done(((f32[3,192,768]{2,1,0:T(8,128)}, f32[192,768]{1,0:T(8,128)}, f32[768,768]{1,0:T(8,128)}, f32[768,768]{1,0:T(8,128)}), (f32[3,192,768]{2,1,0:T(8,128)}, f32[192,768]{1,0:T(8,128)}, f32[768,768]{1,0:T(8,128)}, ...) | async-done | bytes 7077904 | tf_op jit(solution)/shard_map/psum | solution.py:247
  468.6 2.9 copy.58
  (275 shorter events, 138.5 us)
Async XLA Ops:
  7.2 88.1 %copy-start = (bf16[768,768]{1,0:T(8,128)(2,1)S(1)}, bf16[768,768]{1,0:T(8,128)(2,1)}, u32[]{:S(2)}) copy-start(bf16[768,768]{1,0:T(8,128)(2,1)} %param.31) | copy-start | bytes 3538948
  7.2 26.4 %copy-start.13 = (bf16[3,192,768]{2,1,0:T(8,128)(2,1)S(1)}, bf16[3,192,768]{2,1,0:T(8,128)(2,1)}, u32[]{:S(2)}) copy-start(bf16[3,192,768]{2,1,0:T(8,128)(2,1)} %param.26) | copy-start | bytes 2654212
  7.2 62.4 %reduce-scatter.5.cloned.1.call-start = ((), (), s32[]{:S(2)}) async-start(), calls=%async_computation.4 | async-start | bytes 1966080 | tf_op jit(solution)/shard_map/reduce_scatter | solution.py:82
  24.3 9.8 %copy-start.41 = (f32[512]{0:T(512)}, f32[512]{0:T(512)S(1)}, u32[]{:S(2)}) copy-start(f32[512]{0:T(512)S(1)} %add_rsqrt_fusion.1) | copy-start | bytes 6148
  34.2 2.5 copy-start.4
  34.9 1.3 copy-start.25
  34.9 1.3 copy-start.27
  34.9 1.3 copy-start.29
  34.9 1.3 copy-start.31
  36.2 1.7 copy-start.1
  38.5 1.9 copy-start.18
  38.8 30.7 %copy-start.3 = (bf16[192,512]{1,0:T(8,128)(2,1)S(1)}, bf16[192,512]{1,0:T(8,128)(2,1)}, u32[]{:S(2)}) copy-start(bf16[192,512]{1,0:T(8,128)(2,1)} %param.17) | copy-start | bytes 589828
  40.4 41.8 %copy-start.47 = (f32[192]{0:T(256)S(1)}, f32[192]{0:T(256)}, u32[]{:S(2)}) copy-start(f32[192]{0:T(256)} %param.28) | copy-start | bytes 2308
  40.4 41.8 %copy-start.54 = (f32[192]{0:T(256)S(1)}, f32[192]{0:T(256)}, u32[]{:S(2)}) copy-start(f32[192]{0:T(256)} %param.29) | copy-start | bytes 2308
  40.4 85.9 %reduce-scatter.7.cloned.1.call-start = ((), (), s32[]{:S(2)}) async-start(), calls=%async_computation.5 | async-start | bytes 1966080 | tf_op jit(solution)/shard_map/reduce_scatter | solution.py:82
  82.1 94.9 %copy-start.39 = (f32[512]{0:T(512)}, f32[512]{0:T(512)S(1)}, u32[]{:S(2)}) copy-start(f32[512]{0:T(512)S(1)} %add_rsqrt_fusion) | copy-start | bytes 6148
  94.1 1.1 copy-start.57
  97.4 28.9 %copy-start.11 = (bf16[192,512]{1,0:T(8,128)(2,1)S(1)}, bf16[192,512]{1,0:T(8,128)(2,1)}, u32[]{:S(2)}) copy-start(bf16[192,512]{1,0:T(8,128)(2,1)} %param.19) | copy-start | bytes 589828
  97.4 72.1 %reduce-scatter.9.cloned.1.call-start = ((), (), s32[]{:S(2)}) async-start(), calls=%async_computation.6 | async-start | bytes 1966080 | tf_op jit(solution)/shard_map/reduce_scatter | solution.py:86
  111.7 65.3 %copy-start.43 = (f32[512]{0:T(512)}, f32[512]{0:T(512)S(1)}, u32[]{:S(2)}) copy-start(f32[512]{0:T(512)S(1)} %fusion.50) | copy-start | bytes 6148
  126.3 10.1 %copy-start.58 = (f32[512,768]{1,0:T(8,128)S(1)}, f32[512,768]{1,0:T(8,128)}, u32[]{:S(2)}) copy-start(f32[512,768]{1,0:T(8,128)} %copy-done.57) | copy-start | bytes 4718596
  136.4 1.6 copy-start.15
  136.4 2.5 copy-start.55
  140.8 260.5 %reduce-scatter.11.cloned.1.call-start = ((), (), s32[]{:S(2)}) async-start(), calls=%async_computation.7 | async-start | bytes 1966080 | tf_op jit(solution)/shard_map/reduce_scatter | solution.py:86
  177.6 11.6 %copy-start.2 = (f32[3,512,512]{1,2,0:T(8,128)S(1)}, f32[3,512,512]{1,2,0:T(8,128)}, u32[]{:S(2)}) copy-start(f32[3,512,512]{1,2,0:T(8,128)} %copy-done.1) | copy-start | bytes 9437188
  189.8 4.7 copy-start.33
  194.3 1.3 copy-start.14
  197.6 271.0 %all-reduce.7.cloned.1.call-start = ((), (), s32[]{:S(2)}) async-start(), calls=%async_computation.8 | async-start | bytes 14155776 | tf_op jit(solution)/shard_map/psum | solution.py:247
  197.7 3.7 copy-start.16
  197.7 3.7 copy-start.59
  201.4 2.7 copy-start.19
  201.4 3.9 copy-start.7
  201.5 3.9 copy-start.34
  201.5 3.9 copy-start.36
  201.5 3.9 copy-start.38
  207.9 193.4 %copy-start.42 = (f32[512]{0:T(512)S(1)}, f32[512]{0:T(512)}, u32[]{:S(2)}) copy-start(f32[512]{0:T(512)} %copy-done.41) | copy-start | bytes 6148
  207.9 193.4 %copy-start.49 = (f32[192]{0:T(256)S(1)}, f32[192]{0:T(256)}, u32[]{:S(2)}) copy-start(f32[192]{0:T(256)} %param.24) | copy-start | bytes 2308
  207.9 194.7 %copy-start.52 = (f32[192]{0:T(256)S(1)}, f32[192]{0:T(256)}, u32[]{:S(2)}) copy-start(f32[192]{0:T(256)} %get-tuple-element.55) | copy-start | bytes 2308
  207.9 194.7 %copy-start.53 = (f32[192]{0:T(256)S(1)}, f32[192]{0:T(256)}, u32[]{:S(2)}) copy-start(f32[192]{0:T(256)} %get-tuple-element.61) | copy-start | bytes 2308
  207.9 223.4 %copy-start.5 = (f32[512,192]{0,1:T(8,128)S(1)}, f32[512,192]{0,1:T(8,128)}, u32[]{:S(2)}) copy-start(f32[512,192]{0,1:T(8,128)} %reduce-scatter.9.cloned.1.call-done) | copy-start | bytes 1179652
  207.9 223.4 %copy-start.40 = (f32[512]{0:T(512)S(1)}, f32[512]{0:T(512)}, u32[]{:S(2)}) copy-start(f32[512]{0:T(512)} %copy-done.39) | copy-start | bytes 6148
  207.9 223.4 %copy-start.44 = (f32[512]{0:T(512)S(1)}, f32[512]{0:T(512)}, u32[]{:S(2)}) copy-start(f32[512]{0:T(512)} %copy-done.43) | copy-start | bytes 6148
  207.9 223.4 %copy-start.46 = (f32[512]{0:T(512)S(1)}, f32[512]{0:T(512)}, u32[]{:S(2)}) copy-start(f32[512]{0:T(512)} %copy-done.45) | copy-start | bytes 6148
  207.9 223.4 %copy-start.48 = (f32[192]{0:T(256)S(1)}, f32[192]{0:T(256)}, u32[]{:S(2)}) copy-start(f32[192]{0:T(256)} %param.28) | copy-start | bytes 2308
  208.0 223.4 %copy-start.51 = (f32[512]{0:T(512)S(1)}, f32[512]{0:T(512)}, u32[]{:S(2)}) copy-start(f32[512]{0:T(512)} %copy-done.50) | copy-start | bytes 6148
  468.6 3.0 copy-start.24
  468.6 3.8 copy-start.10
  472.4 2.5 copy-start.9
  (17 other events, 13.5 us)
Sparse Core Ops, SparseCore 0:
  40.5 28.9 reduce-scatter.4
  97.6 28.6 reduce-scatter.6
  140.9 28.5 reduce-scatter.8
  197.8 28.1 reduce-scatter.10
  231.4 237.1 all-reduce.6
where the time goes:
time: 485 us; the launch traced here: 483 us
  blocking collectives  147 us (30%)
  other arithmetic  128 us (26%)
  waiting for transfers between devices  108 us (22%)
  local copies, waits for them, and re-layouts  56.4 us (12%)
  matrix products  27.3 us (6%)
  between operations  16.4 us (3%)
    reduce_sum x30, other arithmetic, mix_layer(): jnp.sum(grad_wide * layer_wide)  71.1 us
    reduce_scatter x2, waiting for transfers between devices, reduce_branch(): lax.psum_scatter(partial_terms, 'width', scatter_dimension=1, tiled=True)  43.7 us
    psum x1, blocking collectives, local(): lax.psum((mix_partial, self_partial[None]), ('rows', 'width'))  40.7 us
    dynamic_update_slice x30, other arithmetic, local(): lax.scan(mix_layer, self_weight[0] * output_wide, (mix_weights, history))  40.6 us
    psum x1, waiting for transfers between devices, local(): lax.psum((d_gain_one, d_bias_one, d_w_qkv, d_w_out, d_gain_two, d_bias_tw...  35.1 us
    reduce_scatter x2, waiting for transfers between devices, reduce_input(): lax.psum_scatter(partial_terms, 'width', scatter_dimension=1, tiled=True)  28.6 us
    dynamic_update_slice x30, local copies, waits for them, and re-layouts, local(): lax.scan(mix_layer, self_weight[0] * output_wide, (mix_weights, history))  22.7 us
    psum x1, blocking collectives, local(): lax.psum((d_gain_one, d_bias_one, d_w_qkv, d_w_out, d_gain_two, d_bias_tw...  22.7 us
  transfers between devices with their start and end apart: 5, of which 4 were waited for; matrix products, arithmetic and copies ran while one was open for 34% of the time, Pallas kernels for 0%

commit v1 on v0

v1 whole, which is shorter than its diff:
```python
import functools

import jax
import jax.numpy as jnp
from jax import lax
from jax.experimental import pallas as pl
from jax.experimental.pallas import tpu as pltpu
from jax.sharding import PartitionSpec as P

HEAD_DIM = 64
EPSILON = 1e-05
BF16 = jnp.bfloat16
F32 = jnp.float32
VMEM_LIMIT = 56 * 1024 * 1024


def radices(count):
    found = []
    for radix in (2, 4, 8, 8, 8):
        if count % radix == 0 and count > 1:
            found.append(radix)
            count //= radix
    if count > 1:
        found.append(count)
    return found


def chunks_of(count, rows):
    while rows % (16 * count):
        count //= 2
    return count


def xor_send(value, axis, size, offset):
    return lax.ppermute(value, axis, [(i, i ^ offset) for i in range(size)])


def tree_sum(parts):
    while len(parts) > 1:
        parts = [parts[i] + parts[i + 1] for i in range(0, len(parts), 2)]
    return parts[0]


def sum_small(value, axis, size):
    stride = 1
    for radix in radices(size):
        value = tree_sum([value] + [xor_send(value, axis, size, e * stride) for e in range(1, radix)])
        stride *= radix
    return value


def by_width(pieces, width_index):
    low, high = width_index % 2 == 1, width_index // 2 == 1
    first = jnp.where(low, jnp.concatenate([pieces[1], pieces[0]]), jnp.concatenate([pieces[0], pieces[1]]))
    second = jnp.where(low, jnp.concatenate([pieces[3], pieces[2]]), jnp.concatenate([pieces[2], pieces[3]]))
    return jnp.where(high, jnp.concatenate([second, first]), jnp.concatenate([first, second]))


def gather_width(shard, width_index, width):
    near = xor_send(shard, "width", width, 1)
    far = xor_send(shard, "width", width, 2)
    both = xor_send(far, "width", width, 1)
    return by_width([shard, near, far, both], width_index)


def swap_halves(value):
    half = value.shape[-1] // 2
    return jnp.concatenate([value[..., half:], value[..., :half]], axis=-1)


def weight_gradient_kernel(pairs, me_ref, *refs):
    operands, (send_ref, keep_ref), (scratch,) = refs[: 2 * pairs], refs[2 * pairs : -1], refs[-1:]
    half, rows = keep_ref.shape[0], keep_ref.shape[1]
    start = 0
    for i in range(pairs):
        left, right = operands[2 * i], operands[2 * i + 1]
        count = left.shape[0]
        scratch[start : start + count] = lax.dot_general(
            left[...], right[...], (((1,), (1,)), ((), ())), preferred_element_type=F32
        )
        start += count
    for place in range(half):
        for low, target in ((1, send_ref), (0, keep_ref)):
            chunk = (me_ref[0] % (2 * half)) ^ (2 * place + low)
            target[place] = scratch[pl.ds(pl.multiple_of(chunk * rows, rows), rows), :].astype(BF16)


def weight_gradient(me, row_devices, *operands):
    pairs = len(operands) // 2
    total = sum(operands[2 * i].shape[0] for i in range(pairs))
    columns = operands[1].shape[0]
    count = chunks_of(row_devices, total)
    out = jax.ShapeDtypeStruct((count // 2, total // count, columns), BF16)
    vmem = pl.BlockSpec(memory_space=pltpu.VMEM)
    return pl.pallas_call(
        functools.partial(weight_gradient_kernel, pairs),
        out_shape=(out, out),
        in_specs=[pl.BlockSpec(memory_space=pltpu.SMEM)] + [vmem] * (2 * pairs),
        out_specs=(vmem, vmem),
        scratch_shapes=[pltpu.VMEM((total, columns), F32)],
        compiler_params=pltpu.CompilerParams(vmem_limit_bytes=VMEM_LIMIT),
        cost_estimate=pl.CostEstimate(
            flops=2 * total * columns * operands[0].shape[1], bytes_accessed=4 * total * columns, transcendentals=0
        ),
    )(me, *operands)


def place_kernel(bounds, me_ref, *refs):
    pieces, outs = refs[: -len(bounds)], refs[-len(bounds) :]
    rows = pieces[0].shape[0]
    for e, piece in enumerate(pieces):
        chunk = (me_ref[0] % len(pieces)) ^ e
        for (start, stop), out in zip(bounds, outs):

            @pl.when((chunk * rows >= start) & (chunk * rows < stop))
            def _():
                at = pl.multiple_of(chunk * rows - start, rows)
                out[pl.ds(at, rows), :] = piece[...].astype(F32)


def place(me, pieces, sizes):
    columns = pieces[0].shape[1]
    bounds, start = [], 0
    for size in sizes:
        bounds.append((start, start + size))
        start += size
    vmem = pl.BlockSpec(memory_space=pltpu.VMEM)
    return pl.pallas_call(
        functools.partial(place_kernel, tuple(bounds)),
        out_shape=tuple(jax.ShapeDtypeStruct((size, columns), F32) for size in sizes),
        in_specs=[pl.BlockSpec(memory_space=pltpu.SMEM)] + [vmem] * len(pieces),
        out_specs=tuple(vmem for _ in sizes),
        compiler_params=pltpu.CompilerParams(vmem_limit_bytes=VMEM_LIMIT),
        cost_estimate=pl.CostEstimate(flops=0, bytes_accessed=6 * start * columns, transcendentals=0),
    )(me, *pieces)


def reduce_gradient(me, row_devices, sizes, send, keep):
    count = 2 * send.shape[0]
    stages = radices(count)
    recv = xor_send(send, "rows", row_devices, 1)
    value = (keep.astype(F32) + recv.astype(F32)).astype(BF16)
    stride = 2
    for radix in stages[1:]:
        value = value.reshape((-1, radix) + value.shape[1:])
        parts = [value[:, 0]] + [xor_send(value[:, e], "rows", row_devices, e * stride) for e in range(1, radix)]
        value = tree_sum([part.astype(F32) for part in parts]).astype(BF16)
        stride *= radix
    chunk = value.reshape(value.shape[-2:])
    for radix in radices(row_devices // count):
        parts = [chunk] + [xor_send(chunk, "rows", row_devices, e * stride) for e in range(1, radix)]
        chunk = tree_sum([part.astype(F32) for part in parts]).astype(BF16)
        stride *= radix
    pieces = [chunk]
    strides = [1]
    for radix in stages[:-1]:
        strides.append(strides[-1] * radix)
    for radix, stride in reversed(list(zip(stages, strides))):
        grown = [None] * (len(pieces) * radix)
        for i, piece in enumerate(pieces):
            grown[i * radix] = piece
            for e in range(1, radix):
                grown[i * radix + e] = xor_send(piece, "rows", row_devices, e * stride)
        pieces = grown
    return place(me, pieces, sizes)


def history_kernel(mix_ref, history_ref, grad_ref, running_ref, d_history_ref, d_mix_ref):
    grad = grad_ref[...]
    layers = history_ref.shape[0]
    running = jnp.zeros_like(grad)
    sums = []
    for j in range(layers):
        layer = history_ref[j].astype(F32)
        weight = mix_ref[j]
        running = running + weight * layer
        d_history_ref[j] = (weight * grad).astype(BF16)
        sums.append(jnp.sum(grad * layer, axis=0, keepdims=True))
    running_ref[...] = running
    d_mix_ref[0] = jnp.concatenate(sums, axis=0)


def mix_history(mix_weights, history, grad):
    layers, features, tokens = history.shape
    block = 32
    steps = features // block
    return pl.pallas_call(
        history_kernel,
        grid=(steps,),
        out_shape=(
            jax.ShapeDtypeStruct((features, tokens), F32),
            jax.ShapeDtypeStruct(history.shape, BF16),
            jax.ShapeDtypeStruct((steps, layers, tokens), F32),
        ),
        in_specs=[
            pl.BlockSpec(memory_space=pltpu.SMEM),
            pl.BlockSpec((layers, block, tokens), lambda i: (0, i, 0)),
            pl.BlockSpec((block, tokens), lambda i: (i, 0)),
        ],
        out_specs=(
            pl.BlockSpec((block, tokens), lambda i: (i, 0)),
            pl.BlockSpec((layers, block, tokens), lambda i: (0, i, 0)),
            pl.BlockSpec((1, layers, tokens), lambda i: (i, 0, 0)),
        ),
        compiler_params=pltpu.CompilerParams(vmem_limit_bytes=VMEM_LIMIT),
        cost_estimate=pl.CostEstimate(
            flops=6 * history.size, bytes_accessed=4 * history.size, transcendentals=0
        ),
    )(mix_weights, history, grad)


def dot(left, right, left_dim, right_dim):
    return lax.dot_general(left, right, (((left_dim,), (right_dim,)), ((), ())), preferred_element_type=F32)


def normalise(values):
    centred = values - jnp.mean(values, axis=0, keepdims=True)
    scale = lax.rsqrt(jnp.mean(centred * centred, axis=0, keepdims=True) + EPSILON)
    return centred * scale, scale


def rotate(values, cosine, sine):
    front, back = jnp.split(values, 2, axis=1)
    return jnp.concatenate([front * cosine - back * sine, back * cosine + front * sine], axis=1)


def gelu_and_slope(hidden):
    inner = 0.7978845608028654 * (hidden + 0.044715 * hidden * hidden * hidden)
    curve = jnp.tanh(inner)
    slope = 0.5 * (1.0 + curve) + 0.5 * hidden * (1.0 - curve * curve) * 0.7978845608028654 * (
        1.0 + 3 * 0.044715 * hidden * hidden
    )
    return 0.5 * hidden * (1.0 + curve), slope


def local(
    width,
    row_devices,
    x_in,
    history,
    cotangent,
    counts,
    positions,
    mix_weights,
    self_weight,
    first_norm_gain,
    first_norm_bias,
    w_qkv,
    w_out,
    second_norm_gain,
    second_norm_bias,
    w_up,
    w_down,
):
    part, tokens = x_in.shape
    model = w_out.shape[1]
    heads = part // HEAD_DIM
    half = tokens // 2
    at_width = lax.axis_index("width")
    odd = at_width % 2
    me = lax.axis_index("rows").astype(jnp.int32)[None]
    score_scale = HEAD_DIM ** (-0.5)

    def own_first(value):
        return jnp.where(odd == 1, swap_halves(value), value)

    def own_rows(value, index):
        return lax.dynamic_slice_in_dim(value, index * part, part, 0)

    def to_rows_of_width(partial):
        blocks = partial.reshape(width // 2, 2, part, tokens)
        send = swap_halves(lax.dynamic_index_in_dim(blocks, 1 - odd, 1, False).astype(BF16))
        keep = lax.dynamic_index_in_dim(blocks, odd, 1, False)
        chip = keep + xor_send(send, "width", width, 1).astype(F32)
        side = at_width // 2
        send = lax.dynamic_index_in_dim(chip, 1 - side, 0, False).astype(BF16)
        return lax.dynamic_index_in_dim(chip, side, 0, False) + xor_send(send, "width", width, 2).astype(F32)

    def sum_own_tokens(weight, weight_dim, right):
        send = dot(weight, right[:, half:], weight_dim, 0).astype(BF16)
        recv = xor_send(send, "width", width, 1)
        chip = dot(weight, right[:, :half], weight_dim, 0) + recv.astype(F32)
        return chip + xor_send(chip.astype(BF16), "width", width, 2).astype(F32)

    def all_tokens(own):
        return jnp.concatenate([own, xor_send(own, "width", width, 1)], axis=1)

    def own_features(own):
        other = xor_send(own_rows(own, at_width ^ 1), "width", width, 1)
        return jnp.concatenate([own_rows(own, at_width), other], axis=1)

    x_full = own_first(gather_width(x_in, at_width, width))
    cot_full = own_first(gather_width(cotangent, at_width, width))
    norms = jnp.stack([first_norm_gain, first_norm_bias, second_norm_gain, second_norm_bias])
    norms = by_width(
        [norms.T] + [xor_send(norms, "width", width, e).T for e in range(1, width)], at_width
    )
    gain_one, bias_one, gain_two, bias_two = (norms[:, i : i + 1] for i in range(4))

    live_total = sum_small(counts, "rows", row_devices)
    loss_scale = jnp.float32(tokens * row_devices) / live_total[0].astype(F32)
    live = jnp.where(jnp.arange(tokens) < counts[0], loss_scale, 0.0)[None, :]

    order = jnp.arange(tokens)
    order = jnp.where(odd == 1, (order + half) % tokens, order)
    inverse = 1.0 / 10000.0 ** (jnp.arange(HEAD_DIM // 2, dtype=F32) * 2.0 / HEAD_DIM)
    angles = own_first(positions[None, :]).astype(F32) * inverse[:, None]
    cosine, sine = jnp.cos(angles)[None], jnp.sin(angles)[None]

    xhat_one, scale_one = normalise(x_full.astype(F32))
    normed_one = (xhat_one * gain_one + bias_one).astype(BF16)
    project = lax.dot_general(w_qkv, normed_one, (((2,), (0,)), ((), ())), preferred_element_type=F32)
    project = project.reshape(3, heads, HEAD_DIM, tokens)
    queries = rotate(project[0], cosine, sine).astype(BF16)
    keys = rotate(project[1], cosine, sine).astype(BF16)
    values = project[2].astype(BF16)
    scores = jnp.einsum("hds,hdt->hst", keys, queries, preferred_element_type=F32) * score_scale
    scores = jnp.where((order[:, None] <= order[None, :])[None], scores, -1e30)
    exponents = jnp.exp(scores - jnp.max(scores, axis=1, keepdims=True))
    probs = exponents / jnp.sum(exponents, axis=1, keepdims=True)
    probs_low = probs.astype(BF16)
    heads_out = jnp.einsum("hds,hst->hdt", values, probs_low, preferred_element_type=F32)
    heads_out = heads_out.reshape(part, tokens).astype(BF16)
    middle = x_full[:, :half].astype(F32) + sum_own_tokens(w_out, 0, heads_out)

    xhat_two, scale_two = normalise(middle)
    normed_two = all_tokens((xhat_two * gain_two + bias_two).astype(BF16))
    grad_full = own_first(live) * cot_full.astype(F32)
    g_out = (self_weight[0] * grad_full).astype(BF16)
    d_active = dot(w_down, g_out, 1, 0)
    hidden = dot(w_up, normed_two, 0, 0)
    active, slope = gelu_and_slope(hidden)
    active = active.astype(BF16)
    d_w_down = reduce_gradient(
        me, row_devices, (w_down.shape[0],), *weight_gradient(me, row_devices, active, g_out)
    )[0]
    d_hidden = (slope * d_active).astype(BF16)
    d_normed_two = sum_own_tokens(w_up, 1, d_hidden)
    d_w_up = reduce_gradient(
        me, row_devices, (w_up.shape[0],), *weight_gradient(me, row_devices, normed_two, d_hidden)
    )[0]

    d_gain_two = jnp.sum(d_normed_two * xhat_two, axis=1)
    d_bias_two = jnp.sum(d_normed_two, axis=1)
    lifted = d_normed_two * gain_two
    d_middle = self_weight[0] * grad_full[:, :half] + scale_two * (
        lifted
        - jnp.mean(lifted, axis=0, keepdims=True)
        - xhat_two * jnp.mean(lifted * xhat_two, axis=0, keepdims=True)
    )
    g_mid = all_tokens(d_middle.astype(BF16))
    d_heads = dot(w_out, g_mid, 1, 0).astype(BF16).reshape(heads, HEAD_DIM, tokens)
    d_probs = jnp.einsum("hds,hdt->hst", values, d_heads, preferred_element_type=F32)
    inner = jnp.sum(d_probs * probs, axis=1, keepdims=True)
    d_scores = (probs * (d_probs - inner)).astype(BF16)
    d_queries = jnp.einsum("hds,hst->hdt", keys, d_scores, preferred_element_type=F32) * score_scale
    d_keys = jnp.einsum("hdt,hst->hds", queries, d_scores, preferred_element_type=F32) * score_scale
    d_values = jnp.einsum("hdt,hst->hds", d_heads, probs_low, preferred_element_type=F32)
    d_project = jnp.stack([rotate(d_queries, cosine, -sine), rotate(d_keys, cosine, -sine), d_values])
    d_project = d_project.reshape(3 * part, tokens).astype(BF16)
    d_w_qkv, d_w_out = reduce_gradient(
        me,
        row_devices,
        (3 * part, part),
        *weight_gradient(me, row_devices, d_project, normed_one, heads_out, g_mid),
    )

    d_normed_one = dot(w_qkv.reshape(3 * part, model), d_project, 0, 0)
    lifted = d_normed_one * gain_one
    sums = jnp.stack([jnp.sum(lifted, axis=0), jnp.sum(lifted * xhat_one, axis=0)])
    sums = sums + swap_halves(xor_send(sums, "width", width, 1))
    sums = (sums + xor_send(sums, "width", width, 2)) / model
    own_one = to_rows_of_width(d_normed_one)
    own_xhat = own_rows(xhat_one, at_width)
    d_gain_one = jnp.sum(own_one * own_xhat, axis=1)
    d_bias_one = jnp.sum(own_one, axis=1)
    d_input = own_features(d_middle) + scale_one * (
        own_one * first_norm_gain[:, None] - sums[0:1] - own_xhat * sums[1:2]
    )

    output = own_first(own_features(middle) + to_rows_of_width(dot(w_down, active, 0, 0)))
    grad = cotangent.astype(F32) * live
    running, d_history, d_mix = mix_history(mix_weights, history, grad)
    mixed = (self_weight[0] * output + running).astype(BF16)
    d_mix = jnp.concatenate([jnp.sum(d_mix, axis=(0, 2)), jnp.sum(grad * output)[None]])
    d_mix = tree_sum([d_mix] + [xor_send(d_mix, "width", width, e) for e in range(1, width)])

    both = jnp.stack([d_gain_two, d_bias_two])
    mine = lax.dynamic_slice_in_dim(both, at_width * part, part, 1)
    theirs = lax.dynamic_slice_in_dim(both, (at_width ^ 1) * part, part, 1)
    both = mine + xor_send(theirs, "width", width, 1)
    small = jnp.concatenate([d_mix, d_gain_one, d_bias_one, both[0], both[1]])
    small = sum_small(small, "rows", row_devices)
    layers = mix_weights.shape[0]
    ends = [small[layers + 1 + i * part : layers + 1 + (i + 1) * part] for i in range(4)]
    return (
        mixed,
        own_first(d_input),
        d_history,
        small[:layers],
        small[layers : layers + 1],
        ends[0],
        ends[1],
        d_w_qkv.reshape(w_qkv.shape),
        d_w_out,
        ends[2],
        ends[3],
        d_w_up,
        d_w_down,
    )


def solution(mesh):
    return jax.shard_map(
        functools.partial(local, mesh.shape["width"], mesh.shape["rows"]),
        mesh=mesh,
        in_specs=(
            P("width", "rows"),
            P(None, "width", "rows"),
            P("width", "rows"),
            P("rows"),
            P("rows"),
            P(),
            P(),
            P("width"),
            P("width"),
            P(None, "width", None),
            P("width", None),
            P("width"),
            P("width"),
            P(None, "width"),
            P("width", None),
        ),
        out_specs=(
            P("width", "rows"),
            P("width", "rows"),
            P(None, "width", "rows"),
            P(),
            P(),
            P("width"),
            P("width"),
            P(None, "width", None),
            P("width", None),
            P("width"),
            P("width"),
            P(None, "width"),
            P("width", None),
        ),
        check_vma=False,
    )
```

time: 485 us -> 263 us (0.54)
  blocking collectives: 147 us -> 0 us
  other arithmetic: 128 us -> 25.3 us
  starting transfers between devices: 0.21 us -> 74.9 us
  local copies, waits for them, and re-layouts: 56.4 us -> 14 us
  Pallas kernels: 0 us -> 27.7 us
  between operations: 16.4 us -> 5.54 us
  matrix products: 27.3 us -> 17.1 us
  waiting for transfers between devices: 108 us -> 98 us
    psum x9 -> x0, blocking collectives: 113 us -> none  [the longest x1 40.7 us: local(): lax.psum((mix_partial, self_partial[None]), ('rows', 'width'))]
    ppermute x0 -> x68, waiting for transfers between devices: none -> 98 us  [xor_send(): return lax.ppermute(value, axis, [(i, i ^ offset) for i in range(size)])]
    ppermute x0 -> x68, starting transfers between devices: none -> 74.9 us  [xor_send(): return lax.ppermute(value, axis, [(i, i ^ offset) for i in range(size)])]
    reduce_sum x38 -> x8, other arithmetic: 79.5 us -> 4.83 us  [the longest x1 1.65 us: local(): jnp.sum(d_mix, axis=(0, 2))]
    reduce_scatter x4 -> x0, waiting for transfers between devices: 72.3 us -> none  [the longest x2 43.7 us: reduce_branch(): lax.psum_scatter(partial_terms, 'width', scatter_dimension=1, tiled=True)]
    dynamic_update_slice x30 -> x0, other arithmetic: 40.6 us -> none  [local(): lax.scan(mix_layer, self_weight[0] * output_wide, (mix_weights, history))]
    psum x1 -> x0, waiting for transfers between devices: 35.1 us -> none  [local(): lax.psum((d_gain_one, d_bias_one, d_w_qkv, d_w_out, d_gain_two, d_bias_tw...]
    all_gather x4 -> x0, blocking collectives: 34.2 us -> none  [the longest x2 17.2 us: gather_gradient(): return lax.all_gather(values, 'width', axis=1, tiled=True)]
  transfers between devices with their start and end apart: 5 -> 68, of which waited for: 4 -> 28; matrix products, arithmetic and copies ran while one was open for 34% -> 19% of each run, Pallas kernels for 0% -> 9%
where the time goes in v1:
time: 263 us
  waiting for transfers between devices  98 us (37%)
  starting transfers between devices  74.9 us (28%)
  Pallas kernels  27.7 us (11%)
  other arithmetic  25.3 us (10%)
  matrix products  17.1 us (7%)
  local copies, waits for them, and re-layouts  14 us (5%)
  between operations  5.54 us (2%)
    ppermute x68, waiting for transfers between devices, xor_send(): return lax.ppermute(value, axis, [(i, i ^ offset) for i in range(size)])  98 us
    ppermute x68, starting transfers between devices, xor_send(): return lax.ppermute(value, axis, [(i, i ^ offset) for i in range(size)])  74.9 us
    pallas_call x3, Pallas kernels, weight_gradient(): pl.pallas_call(functools.partial(weight_gradient_kernel, pairs), out_shap...  10.3 us
    pallas_call x3, Pallas kernels, place(): pl.pallas_call(functools.partial(place_kernel, tuple(bounds)), out_shape=...  9.13 us
    dot_general x9, matrix products, dot(): lax.dot_general(left, right, (((left_dim,), (right_dim,)), ((), ())), pre...  8.95 us
    pallas_call x1, Pallas kernels, mix_history(): pl.pallas_call(history_kernel, grid=(steps,), out_shape=(jax.ShapeDtypeSt...  8.22 us
    unnamed x148, local copies, waits for them, and re-layouts  5.3 us
  transfers between devices with their start and end apart: 68, of which 28 were waited for; matrix products, arithmetic and copies ran while one was open for 19% of the time, Pallas kernels for 9%

profile of v1, /device:TPU:0, one launch (start us, length us, event | category | flops | bytes accessed | tf_op | source)
XLA Modules:
  0.0 262.5 jit_solution(11098698709674707606)
XLA Ops:
  2.0 2.6 collective-permute-start.4
  4.7 1.7 collective-permute-start.12
  12.5 2.9 %collective-permute-start.13 = (s32[1]{0:T(128)}, s32[1]{0:T(128)}, u32[]{:S(2)}, u32[]{:S(2)}) collective-permute-start(s32[1]{0:T(128)} %add.281), channel_id=1, source_target_pairs={{0,8},{4,12},{8,0},{12,4},{16,24},{20,28},{24,16},{28,20},{1,9},{5... | collective-permute-start | bytes 20 | tf_op jit(solution)/shard_map/ppermute | solution.py:35
  16.2 4.9 %collective-permute-start.15 = (s32[1]{0:T(128)}, s32[1]{0:T(128)}, u32[]{:S(2)}, u32[]{:S(2)}) collective-permute-start(s32[1]{0:T(128)} %add.281), channel_id=1, source_target_pairs={{0,24},{4,28},{8,16},{12,20},{16,8},{20,12},{24,0},{28,4},{1,25},{... | collective-permute-start | bytes 20 | tf_op jit(solution)/shard_map/ppermute | solution.py:35
  21.6 2.1 collective-permute-start.14
  23.7 2.6 collective-permute-done.14
  27.5 1.7 convert_multiply_fusion.1.grad_ref
  35.5 3.0 %fusion.82 = (f32[3,512]{1,0:T(4,128)S(1)}, f32[3,512,512]{2,1,0:T(8,128)}) fusion(pred[512,512]{1,0:T(8,128)(4,1)S(1)} %broadcast_compare_fusion, bf16[3,32,512]{2,1,0:T(8,128)(2,1)S(1)} %get-tuple-element.97, bf16[3,32,512]{2,1,0:T(8,128)(2,1)S(1)} %get-tuple-element.98, bf16[3,32,512]{2,1,0:T(8,128)(2,1)S(1)} %get-tuple-element.84, ...), kind=kOutput, calls=%fused_computation.215 | convolution fusion | flops 104595968 | bytes 3807232 | tf_op jit(solution)/shard_map/sub | solution.py:319
  38.5 2.3 convolution_convert_fusion.2
  42.2 8.2 %shard_map.246 = (f32[192,512]{1,0:T(8,128)}, bf16[30,192,512]{2,1,0:T(8,128)(2,1)}, f32[6,30,512]{2,1,0:T(8,128)}) custom-call(f32[30]{0:T(128)} %mix_ref.1, bf16[30,192,512]{2,1,0:T(8,128)(2,1)} %history_ref.1, f32[192,512]{1,0:T(8,128)} %convert_multiply_fusion.1.grad_ref), custom_call_target="tpu_custom_call" | custom-call | flops 17694720 | bytes 11796480 | tf_op jit(solution)/shard_map/pallas_call | solution.py:187
  50.4 1.7 reduce_sum.154
  57.1 8.2 %collective-permute-done.7 = bf16[768,256]{1,0:T(8,128)(2,1)S(1)} collective-permute-done((bf16[768,256]{1,0:T(8,128)(2,1)S(1)}, bf16[768,256]{1,0:T(8,128)(2,1)S(1)}, u32[]{:S(2)}, u32[]{:S(2)}) %collective-permute-start.7) | collective-permute-done | bytes 393248 | tf_op jit(solution)/shard_map/ppermute | solution.py:35
  74.2 2.0 convolution_bitcast_fusion
  76.2 3.0 %copy.38 = f32[768,512]{1,0:T(8,128)} copy(f32[768,512]{0,1:T(8,128)} %convolution_bitcast_fusion) | data formatting | bytes 3145728 | tf_op jit(solution)/shard_map/dot_general | solution.py:213
  81.8 3.3 %shard_map.249 = (bf16[4,96,768]{2,1,0:T(8,128)(2,1)}, bf16[4,96,768]{2,1,0:T(8,128)(2,1)}) custom-call(s32[1]{0:T(128)} %bitcast.56.me_ref, bf16[768,512]{1,0:T(8,128)(2,1)} %pad_maximum_fusion.refs_0_, bf16[768,512]{1,0:T(8,128)(2,1)} %copy-done.36), custom_call_target="tpu_custom_call" | custom-call | flops 603979776 | bytes 2359296 | tf_op jit(solution)/shard_map/pallas_call | solution.py:95
  85.7 3.3 %shard_map.251 = (bf16[4,96,768]{2,1,0:T(8,128)(2,1)}, bf16[4,96,768]{2,1,0:T(8,128)(2,1)}) custom-call(s32[1]{0:T(128)} %bitcast.56.me_ref, bf16[768,512]{1,0:T(8,128)(2,1)} %copy-done.73, bf16[768,512]{1,0:T(8,128)(2,1)} %copy-done.15), custom_call_target="tpu_custom_call" | custom-call | flops 603979776 | bytes 2359296 | tf_op jit(solution)/shard_map/pallas_call | solution.py:95
  93.3 8.2 %collective-permute-done.46 = bf16[4,96,768]{2,1,0:T(8,128)(2,1)S(1)} collective-permute-done((bf16[4,96,768]{2,1,0:T(8,128)(2,1)}, bf16[4,96,768]{2,1,0:T(8,128)(2,1)S(1)}, u32[]{:S(2)}, u32[]{:S(2)}) %collective-permute-start.46) | collective-permute-done | bytes 589856 | tf_op jit(solution)/shard_map/ppermute | solution.py:35
  102.9 10.5 %collective-permute-done.57 = bf16[4,96,768]{2,1,0:T(8,128)(2,1)S(1)} collective-permute-done((bf16[4,96,768]{2,1,0:T(8,128)(2,1)}, bf16[4,96,768]{2,1,0:T(8,128)(2,1)S(1)}, u32[]{:S(2)}, u32[]{:S(2)}) %collective-permute-start.57) | collective-permute-done | bytes 589856 | tf_op jit(solution)/shard_map/ppermute | solution.py:35
  113.4 3.5 %collective-permute-start.49 = (bf16[1,96,768]{2,1,0:T(8,128)(2,1)S(1)}, bf16[1,96,768]{2,1,0:T(8,128)(2,1)S(1)}, u32[]{:S(2)}, u32[]{:S(2)}) collective-permute-start(bf16[1,96,768]{2,1,0:T(8,128)(2,1)S(1)} %get-tuple-element.74), channel_id=1, source_target_pairs={{0,24},{4,28},{8,16},{12,20},{16,8},{20,12},{24,0},{28,4},{1,25},{... | collective-permute-start | bytes 442376 | tf_op jit(solution)/shard_map/ppermute | solution.py:35
  122.0 1.9 collective-permute-done.28
  126.5 3.5 %collective-permute-start.60 = (bf16[1,96,768]{2,1,0:T(8,128)(2,1)S(1)}, bf16[1,96,768]{2,1,0:T(8,128)(2,1)S(1)}, u32[]{:S(2)}, u32[]{:S(2)}) collective-permute-start(bf16[1,96,768]{2,1,0:T(8,128)(2,1)S(1)} %get-tuple-element.71), channel_id=1, source_target_pairs={{0,24},{4,28},{8,16},{12,20},{16,8},{20,12},{24,0},{28,4},{1,25},{... | collective-permute-start | bytes 442376 | tf_op jit(solution)/shard_map/ppermute | solution.py:35
  130.1 12.1 %collective-permute-done.48 = bf16[1,96,768]{2,1,0:T(8,128)(2,1)S(1)} collective-permute-done((bf16[1,96,768]{2,1,0:T(8,128)(2,1)S(1)}, bf16[1,96,768]{2,1,0:T(8,128)(2,1)S(1)}, u32[]{:S(2)}, u32[]{:S(2)}) %collective-permute-start.48) | collective-permute-done | bytes 147488 | tf_op jit(solution)/shard_map/ppermute | solution.py:35
  142.2 3.0 %collective-permute-start.55 = (bf16[96,768]{1,0:T(8,128)(2,1)S(1)}, bf16[96,768]{1,0:T(8,128)(2,1)S(1)}, u32[]{:S(2)}, u32[]{:S(2)}) collective-permute-start(bf16[96,768]{1,0:T(8,128)(2,1)S(1)} %fusion.42.refs_0_), channel_id=1, source_target_pairs={{0,24},{4,28},{8,16},{12,20},{16,8},{20,12},{24,0},{28,4},{1,25},{... | collective-permute-start | bytes 442376 | tf_op jit(solution)/shard_map/ppermute | solution.py:35
  146.7 2.6 collective-permute-done.59
  149.4 5.8 %collective-permute-start.66 = (bf16[96,768]{1,0:T(8,128)(2,1)S(1)}, bf16[96,768]{1,0:T(8,128)(2,1)S(1)}, u32[]{:S(2)}, u32[]{:S(2)}) collective-permute-start(bf16[96,768]{1,0:T(8,128)(2,1)S(1)} %fusion.43.refs_0_), channel_id=1, source_target_pairs={{0,24},{4,28},{8,16},{12,20},{16,8},{20,12},{24,0},{28,4},{1,25},{... | collective-permute-start | bytes 442376 | tf_op jit(solution)/shard_map/ppermute | solution.py:35
  158.0 6.3 %collective-permute-done.53.refs_4_ = bf16[96,768]{1,0:T(8,128)(2,1)S(1)} collective-permute-done((bf16[96,768]{1,0:T(8,128)(2,1)S(1)}, bf16[96,768]{1,0:T(8,128)(2,1)S(1)}, u32[]{:S(2)}, u32[]{:S(2)}) %collective-permute-start.53) | collective-permute-done | bytes 147488 | tf_op jit(solution)/shard_map/ppermute | solution.py:35
  166.5 3.5 %collective-permute-done.64.refs_4_ = bf16[96,768]{1,0:T(8,128)(2,1)S(1)} collective-permute-done((bf16[96,768]{1,0:T(8,128)(2,1)S(1)}, bf16[96,768]{1,0:T(8,128)(2,1)S(1)}, u32[]{:S(2)}, u32[]{:S(2)}) %collective-permute-start.64) | collective-permute-done | bytes 147488 | tf_op jit(solution)/shard_map/ppermute | solution.py:35
  174.2 2.5 collective-permute-done.65.refs_5_
  177.2 2.6 collective-permute-done.63.refs_3_
  180.5 3.0 %shard_map.252 = f32[768,768]{1,0:T(8,128)} custom-call(s32[1]{0:T(128)} %bitcast.56.me_ref, bf16[96,768]{1,0:T(8,128)(2,1)} %copy-done.23, bf16[96,768]{1,0:T(8,128)(2,1)} %copy-done.53, bf16[96,768]{1,0:T(8,128)(2,1)} %copy-done.52, bf16[96,768]{1,0:T(8,128)(2,1)} %copy-done.58, bf16[96,768]{1,0:T(8,128)(2,1)} %copy-done.51, bf16[96,768]{1,0:T(8,128)(2,1)} %copy-done.56, ...), custom_call_target="tpu_custom_call" | custom-call | bytes 3538944 | tf_op jit(solution)/shard_map/pallas_call | solution.py:128
  183.6 2.6 collective-permute-done.56.refs_7_
  186.2 3.2 %collective-permute-done.54.refs_5_ = bf16[96,768]{1,0:T(8,128)(2,1)S(1)} collective-permute-done((bf16[96,768]{1,0:T(8,128)(2,1)S(1)}, bf16[96,768]{1,0:T(8,128)(2,1)S(1)}, u32[]{:S(2)}, u32[]{:S(2)}) %collective-permute-start.54) | collective-permute-done | bytes 147488 | tf_op jit(solution)/shard_map/ppermute | solution.py:35
  189.4 2.2 collective-permute-done.52.refs_3_
  192.3 3.1 %shard_map.250 = f32[768,768]{1,0:T(8,128)} custom-call(s32[1]{0:T(128)} %bitcast.56.me_ref, bf16[96,768]{1,0:T(8,128)(2,1)} %copy-done.22, bf16[96,768]{1,0:T(8,128)(2,1)} %copy-done.55, bf16[96,768]{1,0:T(8,128)(2,1)} %copy-done.49, bf16[96,768]{1,0:T(8,128)(2,1)} %copy-done.60, bf16[96,768]{1,0:T(8,128)(2,1)} %copy-done.48, bf16[96,768]{1,0:T(8,128)(2,1)} %copy-done.59, ...), custom_call_target="tpu_custom_call" | custom-call | bytes 3538944 | tf_op jit(solution)/shard_map/pallas_call | solution.py:128
  202.4 3.7 %shard_map.247 = (bf16[4,96,768]{2,1,0:T(8,128)(2,1)}, bf16[4,96,768]{2,1,0:T(8,128)(2,1)}) custom-call(s32[1]{0:T(128)} %bitcast.56.me_ref, bf16[576,512]{1,0:T(8,128)(2,1)} %bitcast.181, bf16[768,512]{1,0:T(8,128)(2,1)} %copy-done.2, bf16[192,512]{1,0:T(8,128)(2,1)} %bitcast.192, bf16[768,512]{1,0:T(8,128)(2,1)} %pad_maximum_fusion.1.refs_3_), custom_call_target="tpu_custom_call" | custom-call | flops 603979776 | bytes 2359296 | tf_op jit(solution)/shard_map/pallas_call | solution.py:95
  210.4 2.1 collective-permute-done.26
  214.2 6.5 %collective-permute-done.35 = bf16[4,96,768]{2,1,0:T(8,128)(2,1)S(1)} collective-permute-done((bf16[4,96,768]{2,1,0:T(8,128)(2,1)}, bf16[4,96,768]{2,1,0:T(8,128)(2,1)S(1)}, u32[]{:S(2)}, u32[]{:S(2)}) %collective-permute-start.35) | collective-permute-done | bytes 589856 | tf_op jit(solution)/shard_map/ppermute | solution.py:35
  221.0 2.6 collective-permute-start.38
  226.5 2.0 collective-permute-done.31
  228.5 2.5 collective-permute-start.34
  231.0 1.8 collective-permute-start.32
  232.9 3.1 %collective-permute-done.37 = bf16[1,96,768]{2,1,0:T(8,128)(2,1)} collective-permute-done((bf16[1,96,768]{2,1,0:T(8,128)(2,1)S(1)}, bf16[1,96,768]{2,1,0:T(8,128)(2,1)}, u32[]{:S(2)}, u32[]{:S(2)}) %collective-permute-start.37) | collective-permute-done | bytes 147488 | tf_op jit(solution)/shard_map/ppermute | solution.py:35
  237.2 2.3 collective-permute-start.44
  239.4 2.2 collective-permute-start.40
  244.1 1.7 collective-permute-done.44.refs_6_
  247.2 3.3 %collective-permute-done.42.refs_4_ = bf16[96,768]{1,0:T(8,128)(2,1)S(1)} collective-permute-done((bf16[96,768]{1,0:T(8,128)(2,1)S(1)}, bf16[96,768]{1,0:T(8,128)(2,1)S(1)}, u32[]{:S(2)}, u32[]{:S(2)}) %collective-permute-start.42) | collective-permute-done | bytes 147488 | tf_op jit(solution)/shard_map/ppermute | solution.py:35
  253.2 4.0 %collective-permute-done.43.refs_5_ = bf16[96,768]{1,0:T(8,128)(2,1)S(1)} collective-permute-done((bf16[96,768]{1,0:T(8,128)(2,1)S(1)}, bf16[96,768]{1,0:T(8,128)(2,1)S(1)}, u32[]{:S(2)}, u32[]{:S(2)}) %collective-permute-start.43) | collective-permute-done | bytes 147488 | tf_op jit(solution)/shard_map/ppermute | solution.py:35
  259.5 3.0 %shard_map.248 = (f32[576,768]{1,0:T(8,128)}, f32[192,768]{1,0:T(8,128)}) custom-call(s32[1]{0:T(128)} %bitcast.56.me_ref, bf16[96,768]{1,0:T(8,128)(2,1)} %copy-done.21, bf16[96,768]{1,0:T(8,128)(2,1)} %copy-done.43, bf16[96,768]{1,0:T(8,128)(2,1)} %copy-done.42, bf16[96,768]{1,0:T(8,128)(2,1)} %copy-done.46, bf16[96,768]{1,0:T(8,128)(2,1)} %copy-done.41, ...), custom_call_target="tpu_custom_call" | custom-call | bytes 3538944 | tf_op jit(solution)/shard_map/pallas_call | solution.py:128
  (354 shorter events, 82.7 us)
Async XLA Ops:
  1.5 27.8 %collective-permute-start.5 = (f32[4,192]{1,0:T(4,128)S(1)}, f32[4,192]{1,0:T(4,128)S(1)}, u32[]{:S(2)}, u32[]{:S(2)}) collective-permute-start(f32[4,192]{1,0:T(4,128)S(1)} %get-tuple-element.107), channel_id=1, source_target_pairs={{0,1},{1,0},{2,3},{3,2},{4,5},{5,4},{6,7},{7,6},{8,9},{9,8},{10,11... | collective-permute-start | bytes 9224 | tf_op jit(solution)/shard_map/ppermute | solution.py:35
  2.0 27.9 %collective-permute-start.4 = (f32[4,192]{1,0:T(4,128)S(1)}, f32[4,192]{1,0:T(4,128)S(1)}, u32[]{:S(2)}, u32[]{:S(2)}) collective-permute-start(f32[4,192]{1,0:T(4,128)S(1)} %get-tuple-element.107), channel_id=1, source_target_pairs={{0,2},{1,3},{2,0},{3,1},{4,6},{5,7},{6,4},{7,5},{8,10},{9,11},{10,... | collective-permute-start | bytes 9224 | tf_op jit(solution)/shard_map/ppermute | solution.py:35
  4.6 25.5 %collective-permute-start.3 = (f32[4,192]{1,0:T(4,128)S(1)}, f32[4,192]{1,0:T(4,128)S(1)}, u32[]{:S(2)}, u32[]{:S(2)}) collective-permute-start(f32[4,192]{1,0:T(4,128)S(1)} %get-tuple-element.107), channel_id=1, source_target_pairs={{0,3},{1,2},{2,1},{3,0},{4,7},{5,6},{6,5},{7,4},{8,11},{9,10},{10,... | collective-permute-start | bytes 9224 | tf_op jit(solution)/shard_map/ppermute | solution.py:35
  6.4 23.9 %collective-permute-start = (bf16[192,512]{1,0:T(8,128)(2,1)}, bf16[192,512]{1,0:T(8,128)(2,1)S(1)}, u32[]{:S(2)}, u32[]{:S(2)}) collective-permute-start(bf16[192,512]{1,0:T(8,128)(2,1)} %param.15), channel_id=1, source_target_pairs={{0,2},{1,3},{2,0},{3,1},{4,6},{5,7},{6,4},{7,5},{8,10},{9,11},{10,... | collective-permute-start | bytes 589832 | tf_op jit(solution)/shard_map/ppermute | solution.py:35
  29.3 22.8 %collective-permute-start.16 = (bf16[192,512]{1,0:T(8,128)(2,1)}, bf16[192,512]{1,0:T(8,128)(2,1)}, u32[]{:S(2)}, u32[]{:S(2)}) collective-permute-start(bf16[192,512]{1,0:T(8,128)(2,1)} %param.17), channel_id=1, source_target_pairs={{0,2},{1,3},{2,0},{3,1},{4,6},{5,7},{6,4},{7,5},{8,10},{9,11},{10,... | collective-permute-start | bytes 589832 | tf_op jit(solution)/shard_map/ppermute | solution.py:35
  29.9 22.5 %collective-permute-start.18 = (bf16[192,512]{1,0:T(8,128)(2,1)}, bf16[192,512]{1,0:T(8,128)(2,1)}, u32[]{:S(2)}, u32[]{:S(2)}) collective-permute-start(bf16[192,512]{1,0:T(8,128)(2,1)} %param.17), channel_id=1, source_target_pairs={{0,1},{1,0},{2,3},{3,2},{4,5},{5,4},{6,7},{7,6},{8,9},{9,8},{10,11... | collective-permute-start | bytes 589832 | tf_op jit(solution)/shard_map/ppermute | solution.py:35
  42.0 11.6 %collective-permute-start.6 = (bf16[768,256]{1,0:T(8,128)(2,1)}, bf16[768,256]{1,0:T(8,128)(2,1)S(1)}, u32[]{:S(2)}, u32[]{:S(2)}) collective-permute-start(bf16[768,256]{1,0:T(8,128)(2,1)} %fusion.16), channel_id=1, source_target_pairs={{0,1},{1,0},{2,3},{3,2},{4,5},{5,4},{6,7},{7,6},{8,9},{9,8},{10,11... | collective-permute-start | bytes 1179656 | tf_op jit(solution)/shard_map/ppermute | solution.py:35
  54.0 11.3 %collective-permute-start.7 = (bf16[768,256]{1,0:T(8,128)(2,1)S(1)}, bf16[768,256]{1,0:T(8,128)(2,1)S(1)}, u32[]{:S(2)}, u32[]{:S(2)}) collective-permute-start(bf16[768,256]{1,0:T(8,128)(2,1)S(1)} %get-tuple-element.120), channel_id=1, source_target_pairs={{0,2},{1,3},{2,0},{3,1},{4,6},{5,7},{6,4},{7,5},{8,10},{9,11},{10,... | collective-permute-start | bytes 1179656 | tf_op jit(solution)/shard_map/ppermute | solution.py:35
  68.7 48.4 %collective-permute-start.8 = (f32[192,256]{1,0:T(8,128)}, f32[192,256]{1,0:T(8,128)}, u32[]{:S(2)}, u32[]{:S(2)}) collective-permute-start(f32[192,256]{1,0:T(8,128)} %get-tuple-element.67), channel_id=1, source_target_pairs={{0,1},{1,0},{2,3},{3,2},{4,5},{5,4},{6,7},{7,6},{8,9},{9,8},{10,11... | collective-permute-start | bytes 589832 | tf_op jit(solution)/shard_map/ppermute | solution.py:35
  74.0 16.5 %collective-permute-start.19 = (bf16[768,256]{1,0:T(8,128)(2,1)}, bf16[768,256]{1,0:T(8,128)(2,1)S(1)}, u32[]{:S(2)}, u32[]{:S(2)}) collective-permute-start(bf16[768,256]{1,0:T(8,128)(2,1)} %fusion.17), channel_id=1, source_target_pairs={{0,1},{1,0},{2,3},{3,2},{4,5},{5,4},{6,7},{7,6},{8,9},{9,8},{10,11... | collective-permute-start | bytes 1179656 | tf_op jit(solution)/shard_map/ppermute | solution.py:35
  80.5 12.1 %collective-permute-start.10 = (bf16[2,192,512]{2,1,0:T(8,128)(2,1)S(1)}, bf16[2,192,512]{2,1,0:T(8,128)(2,1)S(1)}, u32[]{:S(2)}, u32[]{:S(2)}) collective-permute-start(bf16[2,192,512]{2,1,0:T(8,128)(2,1)S(1)} %pad_maximum_fusion.2), channel_id=1, source_target_pairs={{0,1},{1,0},{2,3},{3,2},{4,5},{5,4},{6,7},{7,6},{8,9},{9,8},{10,11... | collective-permute-start | bytes 1179656 | tf_op jit(solution)/shard_map/ppermute | solution.py:35
  85.1 16.4 %collective-permute-start.46 = (bf16[4,96,768]{2,1,0:T(8,128)(2,1)}, bf16[4,96,768]{2,1,0:T(8,128)(2,1)S(1)}, u32[]{:S(2)}, u32[]{:S(2)}) collective-permute-start(bf16[4,96,768]{2,1,0:T(8,128)(2,1)} %get-tuple-element.32), channel_id=1, source_target_pairs={{0,4},{4,0},{8,12},{12,8},{16,20},{20,16},{24,28},{28,24},{1,5},{5... | collective-permute-start | bytes 1769480 | tf_op jit(solution)/shard_map/ppermute | solution.py:35
  89.0 24.4 %collective-permute-start.57 = (bf16[4,96,768]{2,1,0:T(8,128)(2,1)}, bf16[4,96,768]{2,1,0:T(8,128)(2,1)S(1)}, u32[]{:S(2)}, u32[]{:S(2)}) collective-permute-start(bf16[4,96,768]{2,1,0:T(8,128)(2,1)} %get-tuple-element.34), channel_id=1, source_target_pairs={{0,4},{4,0},{8,12},{12,8},{16,20},{20,16},{24,28},{28,24},{1,5},{5... | collective-permute-start | bytes 1769480 | tf_op jit(solution)/shard_map/ppermute | solution.py:35
  91.0 64.2 %collective-permute-start.20 = (bf16[768,256]{1,0:T(8,128)(2,1)S(1)}, bf16[768,256]{1,0:T(8,128)(2,1)S(1)}, u32[]{:S(2)}, u32[]{:S(2)}) collective-permute-start(bf16[768,256]{1,0:T(8,128)(2,1)S(1)} %get-tuple-element.124), channel_id=1, source_target_pairs={{0,2},{1,3},{2,0},{3,1},{4,6},{5,7},{6,4},{7,5},{8,10},{9,11},{10,... | collective-permute-start | bytes 1179656 | tf_op jit(solution)/shard_map/ppermute | solution.py:35
  92.8 24.3 %collective-permute-start.11 = (bf16[192,512]{1,0:T(8,128)(2,1)S(1)}, bf16[192,512]{1,0:T(8,128)(2,1)S(1)}, u32[]{:S(2)}, u32[]{:S(2)}) collective-permute-start(bf16[192,512]{1,0:T(8,128)(2,1)S(1)} %fusion.39), channel_id=1, source_target_pairs={{0,2},{1,3},{2,0},{3,1},{4,6},{5,7},{6,4},{7,5},{8,10},{9,11},{10,... | collective-permute-start | bytes 589832 | tf_op jit(solution)/shard_map/ppermute | solution.py:35
  101.7 24.8 %collective-permute-start.47 = (bf16[1,96,768]{2,1,0:T(8,128)(2,1)S(1)}, bf16[1,96,768]{2,1,0:T(8,128)(2,1)S(1)}, u32[]{:S(2)}, u32[]{:S(2)}) collective-permute-start(bf16[1,96,768]{2,1,0:T(8,128)(2,1)S(1)} %get-tuple-element.73), channel_id=1, source_target_pairs={{0,8},{4,12},{8,0},{12,4},{16,24},{20,28},{24,16},{28,20},{1,9},{5... | collective-permute-start | bytes 442376 | tf_op jit(solution)/shard_map/ppermute | solution.py:35
  113.4 16.6 %collective-permute-start.49 = (bf16[1,96,768]{2,1,0:T(8,128)(2,1)S(1)}, bf16[1,96,768]{2,1,0:T(8,128)(2,1)S(1)}, u32[]{:S(2)}, u32[]{:S(2)}) collective-permute-start(bf16[1,96,768]{2,1,0:T(8,128)(2,1)S(1)} %get-tuple-element.74), channel_id=1, source_target_pairs={{0,24},{4,28},{8,16},{12,20},{16,8},{20,12},{24,0},{28,4},{1,25},{... | collective-permute-start | bytes 442376 | tf_op jit(solution)/shard_map/ppermute | solution.py:35
  124.9 17.2 %collective-permute-start.48 = (bf16[1,96,768]{2,1,0:T(8,128)(2,1)S(1)}, bf16[1,96,768]{2,1,0:T(8,128)(2,1)S(1)}, u32[]{:S(2)}, u32[]{:S(2)}) collective-permute-start(bf16[1,96,768]{2,1,0:T(8,128)(2,1)S(1)} %get-tuple-element.75), channel_id=1, source_target_pairs={{0,16},{4,20},{8,24},{12,28},{16,0},{20,4},{24,8},{28,12},{1,17},{... | collective-permute-start | bytes 442376 | tf_op jit(solution)/shard_map/ppermute | solution.py:35
  125.0 20.2 %collective-permute-start.58 = (bf16[1,96,768]{2,1,0:T(8,128)(2,1)S(1)}, bf16[1,96,768]{2,1,0:T(8,128)(2,1)S(1)}, u32[]{:S(2)}, u32[]{:S(2)}) collective-permute-start(bf16[1,96,768]{2,1,0:T(8,128)(2,1)S(1)} %get-tuple-element.70), channel_id=1, source_target_pairs={{0,8},{4,12},{8,0},{12,4},{16,24},{20,28},{24,16},{28,20},{1,9},{5... | collective-permute-start | bytes 442376 | tf_op jit(solution)/shard_map/ppermute | solution.py:35
  126.5 18.7 %collective-permute-start.60 = (bf16[1,96,768]{2,1,0:T(8,128)(2,1)S(1)}, bf16[1,96,768]{2,1,0:T(8,128)(2,1)S(1)}, u32[]{:S(2)}, u32[]{:S(2)}) collective-permute-start(bf16[1,96,768]{2,1,0:T(8,128)(2,1)S(1)} %get-tuple-element.71), channel_id=1, source_target_pairs={{0,24},{4,28},{8,16},{12,20},{16,8},{20,12},{24,0},{28,4},{1,25},{... | collective-permute-start | bytes 442376 | tf_op jit(solution)/shard_map/ppermute | solution.py:35
  130.1 19.2 %collective-permute-start.59 = (bf16[1,96,768]{2,1,0:T(8,128)(2,1)S(1)}, bf16[1,96,768]{2,1,0:T(8,128)(2,1)S(1)}, u32[]{:S(2)}, u32[]{:S(2)}) collective-permute-start(bf16[1,96,768]{2,1,0:T(8,128)(2,1)S(1)} %get-tuple-element.72), channel_id=1, source_target_pairs={{0,16},{4,20},{8,24},{12,28},{16,0},{20,4},{24,8},{28,12},{1,17},{... | collective-permute-start | bytes 442376 | tf_op jit(solution)/shard_map/ppermute | solution.py:35
  142.2 14.8 %collective-permute-start.55 = (bf16[96,768]{1,0:T(8,128)(2,1)S(1)}, bf16[96,768]{1,0:T(8,128)(2,1)S(1)}, u32[]{:S(2)}, u32[]{:S(2)}) collective-permute-start(bf16[96,768]{1,0:T(8,128)(2,1)S(1)} %fusion.42.refs_0_), channel_id=1, source_target_pairs={{0,24},{4,28},{8,16},{12,20},{16,8},{20,12},{24,0},{28,4},{1,25},{... | collective-permute-start | bytes 442376 | tf_op jit(solution)/shard_map/ppermute | solution.py:35
  145.2 19.1 %collective-permute-start.53 = (bf16[96,768]{1,0:T(8,128)(2,1)S(1)}, bf16[96,768]{1,0:T(8,128)(2,1)S(1)}, u32[]{:S(2)}, u32[]{:S(2)}) collective-permute-start(bf16[96,768]{1,0:T(8,128)(2,1)S(1)} %fusion.42.refs_0_), channel_id=1, source_target_pairs={{0,16},{4,20},{8,24},{12,28},{16,0},{20,4},{24,8},{28,12},{1,17},{... | collective-permute-start | bytes 442376 | tf_op jit(solution)/shard_map/ppermute | solution.py:35
  145.2 19.7 %collective-permute-start.51 = (bf16[96,768]{1,0:T(8,128)(2,1)S(1)}, bf16[96,768]{1,0:T(8,128)(2,1)S(1)}, u32[]{:S(2)}, u32[]{:S(2)}) collective-permute-start(bf16[96,768]{1,0:T(8,128)(2,1)S(1)} %fusion.42.refs_0_), channel_id=1, source_target_pairs={{0,8},{4,12},{8,0},{12,4},{16,24},{20,28},{24,16},{28,20},{1,9},{5... | collective-permute-start | bytes 442376 | tf_op jit(solution)/shard_map/ppermute | solution.py:35
  149.4 15.5 %collective-permute-start.66 = (bf16[96,768]{1,0:T(8,128)(2,1)S(1)}, bf16[96,768]{1,0:T(8,128)(2,1)S(1)}, u32[]{:S(2)}, u32[]{:S(2)}) collective-permute-start(bf16[96,768]{1,0:T(8,128)(2,1)S(1)} %fusion.43.refs_0_), channel_id=1, source_target_pairs={{0,24},{4,28},{8,16},{12,20},{16,8},{20,12},{24,0},{28,4},{1,25},{... | collective-permute-start | bytes 442376 | tf_op jit(solution)/shard_map/ppermute | solution.py:35
  157.1 12.8 %collective-permute-start.64 = (bf16[96,768]{1,0:T(8,128)(2,1)S(1)}, bf16[96,768]{1,0:T(8,128)(2,1)S(1)}, u32[]{:S(2)}, u32[]{:S(2)}) collective-permute-start(bf16[96,768]{1,0:T(8,128)(2,1)S(1)} %fusion.43.refs_0_), channel_id=1, source_target_pairs={{0,16},{4,20},{8,24},{12,28},{16,0},{20,4},{24,8},{28,12},{1,17},{... | collective-permute-start | bytes 442376 | tf_op jit(solution)/shard_map/ppermute | solution.py:35
  157.1 13.4 %collective-permute-start.62 = (bf16[96,768]{1,0:T(8,128)(2,1)S(1)}, bf16[96,768]{1,0:T(8,128)(2,1)S(1)}, u32[]{:S(2)}, u32[]{:S(2)}) collective-permute-start(bf16[96,768]{1,0:T(8,128)(2,1)S(1)} %fusion.43.refs_0_), channel_id=1, source_target_pairs={{0,8},{4,12},{8,0},{12,4},{16,24},{20,28},{24,16},{28,20},{1,9},{5... | collective-permute-start | bytes 442376 | tf_op jit(solution)/shard_map/ppermute | solution.py:35
  164.3 7.7 %collective-permute-start.61 = (bf16[96,768]{1,0:T(8,128)(2,1)S(1)}, bf16[96,768]{1,0:T(8,128)(2,1)S(1)}, u32[]{:S(2)}, u32[]{:S(2)}) collective-permute-start(bf16[96,768]{1,0:T(8,128)(2,1)S(1)} %fusion.43.refs_0_), channel_id=1, source_target_pairs={{0,4},{4,0},{8,12},{12,8},{16,20},{20,16},{24,28},{28,24},{1,5},{5... | collective-permute-start | bytes 442376 | tf_op jit(solution)/shard_map/ppermute | solution.py:35
  164.9 30.5 %collective-permute-start.22 = (bf16[768,256]{1,0:T(8,128)(2,1)S(1)}, bf16[768,256]{1,0:T(8,128)(2,1)S(1)}, u32[]{:S(2)}, u32[]{:S(2)}) collective-permute-start(bf16[768,256]{1,0:T(8,128)(2,1)S(1)} %get-tuple-element.47), channel_id=1, source_target_pairs={{0,1},{1,0},{2,3},{3,2},{4,5},{5,4},{6,7},{7,6},{8,9},{9,8},{10,11... | collective-permute-start | bytes 1179656 | tf_op jit(solution)/shard_map/ppermute | solution.py:35
  164.9 8.4 %collective-permute-start.67 = (bf16[96,768]{1,0:T(8,128)(2,1)S(1)}, bf16[96,768]{1,0:T(8,128)(2,1)S(1)}, u32[]{:S(2)}, u32[]{:S(2)}) collective-permute-start(bf16[96,768]{1,0:T(8,128)(2,1)S(1)} %collective-permute-done.66.refs_6_), channel_id=1, source_target_pairs={{0,4},{4,0},{8,12},{12,8},{16,20},{20,16},{24,28},{28,24},{1,5},{5... | collective-permute-start | bytes 442376 | tf_op jit(solution)/shard_map/ppermute | solution.py:35
  170.5 9.4 %collective-permute-start.63 = (bf16[96,768]{1,0:T(8,128)(2,1)S(1)}, bf16[96,768]{1,0:T(8,128)(2,1)S(1)}, u32[]{:S(2)}, u32[]{:S(2)}) collective-permute-start(bf16[96,768]{1,0:T(8,128)(2,1)S(1)} %collective-permute-done.62.refs_2_), channel_id=1, source_target_pairs={{0,4},{4,0},{8,12},{12,8},{16,20},{20,16},{24,28},{28,24},{1,5},{5... | collective-permute-start | bytes 442376 | tf_op jit(solution)/shard_map/ppermute | solution.py:35
  172.1 11.5 %collective-permute-start.50 = (bf16[96,768]{1,0:T(8,128)(2,1)S(1)}, bf16[96,768]{1,0:T(8,128)(2,1)S(1)}, u32[]{:S(2)}, u32[]{:S(2)}) collective-permute-start(bf16[96,768]{1,0:T(8,128)(2,1)S(1)} %fusion.42.refs_0_), channel_id=1, source_target_pairs={{0,4},{4,0},{8,12},{12,8},{16,20},{20,16},{24,28},{28,24},{1,5},{5... | collective-permute-start | bytes 442376 | tf_op jit(solution)/shard_map/ppermute | solution.py:35
  173.3 12.9 %collective-permute-start.56 = (bf16[96,768]{1,0:T(8,128)(2,1)S(1)}, bf16[96,768]{1,0:T(8,128)(2,1)S(1)}, u32[]{:S(2)}, u32[]{:S(2)}) collective-permute-start(bf16[96,768]{1,0:T(8,128)(2,1)S(1)} %collective-permute-done.55.refs_6_), channel_id=1, source_target_pairs={{0,4},{4,0},{8,12},{12,8},{16,20},{20,16},{24,28},{28,24},{1,5},{5... | collective-permute-start | bytes 442376 | tf_op jit(solution)/shard_map/ppermute | solution.py:35
  176.7 12.6 %collective-permute-start.54 = (bf16[96,768]{1,0:T(8,128)(2,1)S(1)}, bf16[96,768]{1,0:T(8,128)(2,1)S(1)}, u32[]{:S(2)}, u32[]{:S(2)}) collective-permute-start(bf16[96,768]{1,0:T(8,128)(2,1)S(1)} %collective-permute-done.53.refs_4_), channel_id=1, source_target_pairs={{0,4},{4,0},{8,12},{12,8},{16,20},{20,16},{24,28},{28,24},{1,5},{5... | collective-permute-start | bytes 442376 | tf_op jit(solution)/shard_map/ppermute | solution.py:35
  179.9 11.7 %collective-permute-start.52 = (bf16[96,768]{1,0:T(8,128)(2,1)S(1)}, bf16[96,768]{1,0:T(8,128)(2,1)S(1)}, u32[]{:S(2)}, u32[]{:S(2)}) collective-permute-start(bf16[96,768]{1,0:T(8,128)(2,1)S(1)} %collective-permute-done.51.refs_2_), channel_id=1, source_target_pairs={{0,4},{4,0},{8,12},{12,8},{16,20},{20,16},{24,28},{28,24},{1,5},{5... | collective-permute-start | bytes 442376 | tf_op jit(solution)/shard_map/ppermute | solution.py:35
  183.6 40.9 %collective-permute-start.21 = (f32[192,256]{1,0:T(8,128)S(1)}, f32[192,256]{1,0:T(8,128)S(1)}, u32[]{:S(2)}, u32[]{:S(2)}) collective-permute-start(f32[192,256]{1,0:T(8,128)S(1)} %get-tuple-element.63), channel_id=1, source_target_pairs={{0,1},{1,0},{2,3},{3,2},{4,5},{5,4},{6,7},{7,6},{8,9},{9,8},{10,11... | collective-permute-start | bytes 589832 | tf_op jit(solution)/shard_map/ppermute | solution.py:35
  206.1 14.6 %collective-permute-start.35 = (bf16[4,96,768]{2,1,0:T(8,128)(2,1)}, bf16[4,96,768]{2,1,0:T(8,128)(2,1)S(1)}, u32[]{:S(2)}, u32[]{:S(2)}) collective-permute-start(bf16[4,96,768]{2,1,0:T(8,128)(2,1)} %get-tuple-element.28), channel_id=1, source_target_pairs={{0,4},{4,0},{8,12},{12,8},{16,20},{20,16},{24,28},{28,24},{1,5},{5... | collective-permute-start | bytes 1769480 | tf_op jit(solution)/shard_map/ppermute | solution.py:35
  212.7 11.7 %collective-permute-start.24 = (bf16[192,512]{1,0:T(8,128)(2,1)S(1)}, bf16[192,512]{1,0:T(8,128)(2,1)S(1)}, u32[]{:S(2)}, u32[]{:S(2)}) collective-permute-start(bf16[192,512]{1,0:T(8,128)(2,1)S(1)} %fusion.40), channel_id=1, source_target_pairs={{0,2},{1,3},{2,0},{3,1},{4,6},{5,7},{6,4},{7,5},{8,10},{9,11},{10,... | collective-permute-start | bytes 589832 | tf_op jit(solution)/shard_map/ppermute | solution.py:35
  220.9 10.2 %collective-permute-start.36 = (bf16[1,96,768]{2,1,0:T(8,128)(2,1)S(1)}, bf16[1,96,768]{2,1,0:T(8,128)(2,1)}, u32[]{:S(2)}, u32[]{:S(2)}) collective-permute-start(bf16[1,96,768]{2,1,0:T(8,128)(2,1)S(1)} %get-tuple-element.76), channel_id=1, source_target_pairs={{0,8},{4,12},{8,0},{12,4},{16,24},{20,28},{24,16},{28,20},{1,9},{5... | collective-permute-start | bytes 442376 | tf_op jit(solution)/shard_map/ppermute | solution.py:35
  221.0 11.9 %collective-permute-start.38 = (bf16[1,96,768]{2,1,0:T(8,128)(2,1)S(1)}, bf16[1,96,768]{2,1,0:T(8,128)(2,1)}, u32[]{:S(2)}, u32[]{:S(2)}) collective-permute-start(bf16[1,96,768]{2,1,0:T(8,128)(2,1)S(1)} %get-tuple-element.77), channel_id=1, source_target_pairs={{0,24},{4,28},{8,16},{12,20},{16,8},{20,12},{24,0},{28,4},{1,25},{... | collective-permute-start | bytes 442376 | tf_op jit(solution)/shard_map/ppermute | solution.py:35
  223.6 12.4 %collective-permute-start.37 = (bf16[1,96,768]{2,1,0:T(8,128)(2,1)S(1)}, bf16[1,96,768]{2,1,0:T(8,128)(2,1)}, u32[]{:S(2)}, u32[]{:S(2)}) collective-permute-start(bf16[1,96,768]{2,1,0:T(8,128)(2,1)S(1)} %get-tuple-element.78), channel_id=1, source_target_pairs={{0,16},{4,20},{8,24},{12,28},{16,0},{20,4},{24,8},{28,12},{1,17},{... | collective-permute-start | bytes 442376 | tf_op jit(solution)/shard_map/ppermute | solution.py:35
  228.5 11.0 %collective-permute-start.34 = (f32[799]{0:T(1024)S(1)}, f32[799]{0:T(1024)S(1)}, u32[]{:S(2)}, u32[]{:S(2)}) collective-permute-start(f32[799]{0:T(1024)S(1)} %add.302), channel_id=1, source_target_pairs={{0,24},{4,28},{8,16},{12,20},{16,8},{20,12},{24,0},{28,4},{1,25},{... | collective-permute-start | bytes 9596 | tf_op jit(solution)/shard_map/ppermute | solution.py:35
  231.0 10.6 %collective-permute-start.33 = (f32[799]{0:T(1024)S(1)}, f32[799]{0:T(1024)S(1)}, u32[]{:S(2)}, u32[]{:S(2)}) collective-permute-start(f32[799]{0:T(1024)S(1)} %add.302), channel_id=1, source_target_pairs={{0,16},{4,20},{8,24},{12,28},{16,0},{20,4},{24,8},{28,12},{1,17},{... | collective-permute-start | bytes 9596 | tf_op jit(solution)/shard_map/ppermute | solution.py:35
  231.0 10.6 %collective-permute-start.32 = (f32[799]{0:T(1024)S(1)}, f32[799]{0:T(1024)S(1)}, u32[]{:S(2)}, u32[]{:S(2)}) collective-permute-start(f32[799]{0:T(1024)S(1)} %add.302), channel_id=1, source_target_pairs={{0,8},{4,12},{8,0},{12,4},{16,24},{20,28},{24,16},{28,20},{1,9},{5... | collective-permute-start | bytes 9596 | tf_op jit(solution)/shard_map/ppermute | solution.py:35
  237.2 8.6 %collective-permute-start.44 = (bf16[96,768]{1,0:T(8,128)(2,1)S(1)}, bf16[96,768]{1,0:T(8,128)(2,1)S(1)}, u32[]{:S(2)}, u32[]{:S(2)}) collective-permute-start(bf16[96,768]{1,0:T(8,128)(2,1)S(1)} %fusion.41.refs_0_), channel_id=1, source_target_pairs={{0,24},{4,28},{8,16},{12,20},{16,8},{20,12},{24,0},{28,4},{1,25},{... | collective-permute-start | bytes 442376 | tf_op jit(solution)/shard_map/ppermute | solution.py:35
  239.4 11.1 %collective-permute-start.42 = (bf16[96,768]{1,0:T(8,128)(2,1)S(1)}, bf16[96,768]{1,0:T(8,128)(2,1)S(1)}, u32[]{:S(2)}, u32[]{:S(2)}) collective-permute-start(bf16[96,768]{1,0:T(8,128)(2,1)S(1)} %fusion.41.refs_0_), channel_id=1, source_target_pairs={{0,16},{4,20},{8,24},{12,28},{16,0},{20,4},{24,8},{28,12},{1,17},{... | collective-permute-start | bytes 442376 | tf_op jit(solution)/shard_map/ppermute | solution.py:35
  239.4 12.7 %collective-permute-start.40 = (bf16[96,768]{1,0:T(8,128)(2,1)S(1)}, bf16[96,768]{1,0:T(8,128)(2,1)S(1)}, u32[]{:S(2)}, u32[]{:S(2)}) collective-permute-start(bf16[96,768]{1,0:T(8,128)(2,1)S(1)} %fusion.41.refs_0_), channel_id=1, source_target_pairs={{0,8},{4,12},{8,0},{12,4},{16,24},{20,28},{24,16},{28,20},{1,9},{5... | collective-permute-start | bytes 442376 | tf_op jit(solution)/shard_map/ppermute | solution.py:35
  242.7 10.5 %collective-permute-start.39 = (bf16[96,768]{1,0:T(8,128)(2,1)S(1)}, bf16[96,768]{1,0:T(8,128)(2,1)S(1)}, u32[]{:S(2)}, u32[]{:S(2)}) collective-permute-start(bf16[96,768]{1,0:T(8,128)(2,1)S(1)} %fusion.41.refs_0_), channel_id=1, source_target_pairs={{0,4},{4,0},{8,12},{12,8},{16,20},{20,16},{24,28},{28,24},{1,5},{5... | collective-permute-start | bytes 442376 | tf_op jit(solution)/shard_map/ppermute | solution.py:35
  (94 other events, 686.1 us)

commit v2 on v0

v2 whole, which is shorter than its diff:
```python
import functools

import jax
import jax.numpy as jnp
from jax import lax
from jax.experimental import pallas as pl
from jax.experimental.pallas import tpu as pltpu
from jax.sharding import PartitionSpec as P

HEAD_DIM = 64
EPSILON = 1e-05
BF16 = jnp.bfloat16
F32 = jnp.float32
STEP = 16


def shape(*dims, kind=F32):
    return jax.ShapeDtypeStruct(dims, kind)


def kernel(body, outs, scalars, arrays, scratch=(), flops=0, limit=12):
    return pl.pallas_call(
        body,
        out_shape=outs,
        in_specs=[pl.BlockSpec(memory_space=pltpu.SMEM)] * len(scalars)
        + [pl.BlockSpec(memory_space=pltpu.VMEM)] * len(arrays),
        out_specs=jax.tree.map(lambda _: pl.BlockSpec(memory_space=pltpu.VMEM), outs),
        scratch_shapes=list(scratch),
        compiler_params=pltpu.CompilerParams(vmem_limit_bytes=limit * 1024 * 1024),
        cost_estimate=pl.CostEstimate(flops=1024, bytes_accessed=1024, transcendentals=0),
    )(*scalars, *arrays)


def after(value, *others):
    return lax.optimization_barrier((value, others))[0]


def dot(left, right, left_dim, right_dim):
    return lax.dot_general(left, right, (((left_dim,), (right_dim,)), ((), ())), preferred_element_type=F32)


def rows_at(i):
    return pl.ds(pl.multiple_of(i * STEP, STEP), STEP)


def each_rows(count, body, start=None, first=0):
    return lax.fori_loop(first // STEP, count // STEP, body, start, unroll=4)


def column_sum(value):
    return jnp.sum(value, axis=0, keepdims=True)


def xor_send(value, axis, size, offset):
    return lax.ppermute(value, axis, [(i, i ^ offset) for i in range(size)])


def tree_sum(parts):
    while len(parts) > 1:
        parts = [parts[i] + parts[i + 1] for i in range(0, len(parts), 2)]
    return parts[0]


def sum_small(value, axis, size):
    stride = 1
    while stride < size:
        value = value + xor_send(value, axis, size, stride)
        stride *= 2
    return value


def gather_width(shard, width, order):
    far = xor_send(shard, "width", width, 2)
    near = xor_send(shard, "width", width, 1)
    both = xor_send(after(far, *order) if order else far, "width", width, 1)
    return [shard, near, far, both]


def chunks_of(count, rows):
    while rows % (16 * count):
        count //= 2
    return count


def digits_of(count, kind):
    if kind == "halving":
        strides = []
        stride = 1
        while stride < count:
            strides.append((stride, 2))
            stride *= 2
        return strides
    if kind == "crossed":
        strides = digits_of(count, "halving")
        return [strides[1], strides[0]] + strides[2:]
    if kind == "near":
        return [(1, 2), (2, count // 2)]
    return [(2, count // 2), (1, 2)]


def offsets_of(digits):
    found = [0]
    for stride, radix in digits:
        found = [low + e * stride for low in found for e in range(radix)]
    return found


class Stream:
    def __init__(self, row_devices, first, rows, kind):
        self.first, self.rows = first, rows
        self.count = chunks_of(row_devices, rows)
        self.row_devices = row_devices
        self.digits = digits_of(self.count, kind)
        self.chunk = rows // self.count

    def parts(self):
        stride, radix = self.digits[0]
        rest = offsets_of(self.digits[1:])
        return [[e * stride + low for low in rest] for e in range(radix)]

    def send(self, value, offset):
        return xor_send(value, "rows", self.row_devices, offset)


def weight_gradient_kernel(streams, pairs, me_ref, *refs):
    operands, outs, scratch = refs[: 2 * pairs], list(refs[2 * pairs : -1]), refs[-1]
    start = 0
    for i in range(pairs):
        left, right = operands[2 * i], operands[2 * i + 1]
        count = left.shape[0]
        scratch[start : start + count] = dot(left[...], right[...], 1, 1).astype(BF16)
        start += count
    for stream in streams:
        for offsets in stream.parts():
            out = outs.pop(0)
            for place, offset in enumerate(offsets):
                chunk = (me_ref[0] % stream.count) ^ offset
                at = pl.multiple_of(stream.first + chunk * stream.chunk, 16)
                out[place * stream.chunk : (place + 1) * stream.chunk] = scratch[pl.ds(at, stream.chunk), :]


def weight_gradient(me, streams, *operands):
    pairs = len(operands) // 2
    total = sum(operands[2 * i].shape[0] for i in range(pairs))
    columns, tokens = operands[1].shape
    outs = tuple(
        shape(len(offsets) * stream.chunk, columns, kind=BF16) for stream in streams for offsets in stream.parts()
    )
    found = list(
        kernel(
            functools.partial(weight_gradient_kernel, streams, pairs),
            outs,
            [me],
            operands,
            [pltpu.VMEM((total, columns), BF16)],
            2 * total * columns * tokens,
        )
    )
    return [[found.pop(0) for _ in stream.parts()] for stream in streams]


def start_stage(stream, parts, stage):
    stride, radix = stream.digits[stage]
    return [stream.send(parts[e], e * stride) for e in range(1, radix)]


def add_stage(stream, parts, received, stage):
    value = tree_sum([part.astype(F32) for part in [parts[0]] + received]).astype(BF16)
    if stage + 1 == len(stream.digits):
        return [value]
    radix = stream.digits[stage + 1][1]
    size = value.shape[0] // radix
    return [value[e * size : (e + 1) * size] for e in range(radix)]


def sum_rest(stream, value):
    stride = stream.count
    while stride < stream.row_devices:
        value = (value.astype(F32) + stream.send(value, stride).astype(F32)).astype(BF16)
        stride *= 2
    return value


def gather_stage(stream, value, stage):
    stride, radix = stream.digits[stage]
    return [value] + [stream.send(value, e * stride) for e in range(1, radix)]


def place_kernel(streams, bounds, me_ref, *refs):
    pieces, outs = list(refs[: -len(bounds)]), refs[-len(bounds) :]
    for stream in streams:
        for offsets in stream.parts():
            piece = pieces.pop(0)
            for place, offset in enumerate(offsets):
                chunk = (me_ref[0] % stream.count) ^ offset
                row = stream.first + chunk * stream.chunk
                for (first, last), out in zip(bounds, outs):

                    def store(out=out, first=first, piece=piece, place=place, row=row, size=stream.chunk):
                        at = pl.multiple_of(row - first, 16)
                        out[pl.ds(at, size), :] = piece[place * size : (place + 1) * size].astype(F32)

                    if len(bounds) == 1:
                        store()
                    else:
                        pl.when((row >= first) & (row < last))(store)


def place(me, streams, pieces, sizes):
    columns = pieces[0].shape[1]
    bounds, start = [], 0
    for size in sizes:
        bounds.append((start, start + size))
        start += size
    outs = tuple(shape(size, columns) for size in sizes)
    return kernel(functools.partial(place_kernel, streams, bounds), outs, [me], pieces, flops=start * columns)


def history_kernel(mix_ref, history_ref, cot_ref, live_ref, running_ref, d_history_ref, d_mix_ref):
    layers = history_ref.shape[0]
    features, tokens = cot_ref.shape

    @pl.when(pl.program_id(0) == 0)
    def _():
        d_mix_ref[...] = jnp.zeros_like(d_mix_ref)

    for i in range(features // STEP):
        rows = slice(i * STEP, (i + 1) * STEP)
        grad = cot_ref[rows].astype(F32) * live_ref[...]
        running = jnp.zeros_like(grad)
        for j in range(layers):
            layer = history_ref[j, rows].astype(F32)
            weight = mix_ref[j]
            running = running + weight * layer
            d_history_ref[j, rows] = (weight * grad).astype(BF16)
            terms = grad * layer
            terms = terms[: STEP // 2] + terms[STEP // 2 :]
            d_mix_ref[j] += sum(terms[:, k : k + 128] for k in range(0, tokens, 128))
        running_ref[rows] = running


def mix_history(mix_weights, history, cotangent, live):
    layers, features, tokens = history.shape
    block = 32
    return pl.pallas_call(
        history_kernel,
        grid=(features // block,),
        out_shape=(
            shape(features, tokens),
            shape(*history.shape, kind=BF16),
            shape(layers, STEP // 2, 128),
        ),
        in_specs=[
            pl.BlockSpec(memory_space=pltpu.SMEM),
            pl.BlockSpec((layers, block, tokens), lambda i: (0, i, 0)),
            pl.BlockSpec((block, tokens), lambda i: (i, 0)),
            pl.BlockSpec((1, tokens), lambda i: (0, 0)),
        ],
        out_specs=(
            pl.BlockSpec((block, tokens), lambda i: (i, 0)),
            pl.BlockSpec((layers, block, tokens), lambda i: (0, i, 0)),
            pl.BlockSpec((layers, STEP // 2, 128), lambda i: (0, 0, 0)),
        ),
        compiler_params=pltpu.CompilerParams(vmem_limit_bytes=12 * 1024 * 1024),
        cost_estimate=pl.CostEstimate(flops=1024, bytes_accessed=1024, transcendentals=0),
    )(mix_weights, history, cotangent, live)


def spread_of(load, count, width):
    zero = jnp.zeros((STEP, width), F32)
    mean = column_sum(each_rows(count, lambda i, acc: acc + load(i), zero)) / count

    def squares(i, acc):
        centred = load(i) - mean
        return acc + centred * centred

    return mean, lax.rsqrt(column_sum(each_rows(count, squares, zero)) / count + EPSILON)


def attention_kernel(
    at_ref, x0, x1, x2, x3, norms, cosine, sine, w_qkv, w_out,
    send, keep, x_half, x_all, normed, stats, qkv, heads_out, probs, project, scores,
):
    at = at_ref[0]
    part, tokens = x0.shape
    model = w_out.shape[1]
    half = tokens // 2
    for e, piece in enumerate((x0, x1, x2, x3)):
        x_all[pl.ds(pl.multiple_of((at ^ e) * part, 64), part), :] = piece[...]
    mean, scale = spread_of(lambda i: x_all[rows_at(i), :].astype(F32), model, tokens)
    stats[0:1] = mean
    stats[1:2] = scale

    def normalise(i, _):
        rows = rows_at(i)
        xhat = (x_all[rows, :].astype(F32) - mean) * scale
        normed[rows, :] = (xhat * norms[rows, 0:1] + norms[rows, 1:2]).astype(BF16)

    each_rows(model, normalise)
    project[...] = dot(w_qkv[...], normed[...], 1, 0)
    width = HEAD_DIM // 2
    for block, factor in ((0, HEAD_DIM ** (-0.5)), (1, 1.0)):
        for start in range(block * part, (block + 1) * part, HEAD_DIM):
            front, back = project[start : start + width], project[start + width : start + HEAD_DIM]
            cos, sin = cosine[...] * factor, sine[...] * factor
            qkv[start : start + width] = (front * cos - back * sin).astype(BF16)
            qkv[start + width : start + HEAD_DIM] = (back * cos + front * sin).astype(BF16)
    qkv[2 * part :] = project[2 * part :].astype(BF16)
    for h in range(part // HEAD_DIM):
        head = slice(h * HEAD_DIM, (h + 1) * HEAD_DIM)
        for t in range(2):
            now = slice(t * half, (t + 1) * half)
            count = (t + 1) * half
            query = qkv[head, now]
            key = qkv[part + h * HEAD_DIM : part + (h + 1) * HEAD_DIM, :count]
            value = qkv[2 * part + h * HEAD_DIM : 2 * part + (h + 1) * HEAD_DIM, :count]
            scores[:count] = dot(key, query, 0, 0)

            def masked_top(i, acc):
                rows = rows_at(i)
                behind = lax.broadcasted_iota(jnp.int32, (STEP, half), 0) + (i * STEP - t * half)
                found = jnp.where(behind <= lax.broadcasted_iota(jnp.int32, (STEP, half), 1), scores[rows, :], -1e30)
                scores[rows, :] = found
                return jnp.maximum(acc, found)

            top = each_rows(
                t * half, lambda i, acc: jnp.maximum(acc, scores[rows_at(i), :]), jnp.full((STEP, half), -1e30, F32)
            )
            top = jnp.max(each_rows(count, masked_top, top, first=t * half), axis=0, keepdims=True)

            def raise_rows(i, acc):
                rows = rows_at(i)
                found = jnp.exp(scores[rows, :] - top)
                scores[rows, :] = found
                return acc + found

            total = 1.0 / column_sum(each_rows(count, raise_rows, jnp.zeros((STEP, half), F32)))

            def settle(i, _):
                rows = rows_at(i)
                probs[h, rows, now] = (scores[rows, :] * total).astype(BF16)

            each_rows(count, settle)
            heads_out[head, now] = dot(value, probs[h, :count, now], 1, 0).astype(BF16)
    own = pl.multiple_of((at % 2) * half, half)
    other = pl.multiple_of((1 - at % 2) * half, half)
    send[...] = dot(w_out[...], heads_out[:, pl.ds(other, half)], 0, 0).astype(BF16)
    keep[...] = dot(w_out[...], heads_out[:, pl.ds(own, half)], 0, 0)
    x_half[...] = x_all[:, pl.ds(own, half)]


def output_gradient_kernel(at_ref, self_ref, c0, c1, c2, c3, live, w_down, g_out, d_active, cot_half, cot_all):
    at = at_ref[0]
    part, tokens = c0.shape
    half = tokens // 2
    for e, piece in enumerate((c0, c1, c2, c3)):
        cot_all[pl.ds(pl.multiple_of((at ^ e) * part, 64), part), :] = piece[...]
    for place, side in enumerate((at % 2, 1 - at % 2)):
        now = pl.ds(pl.multiple_of(side * half, half), half)
        factor = live[:, now]

        def scale(i, _, now=now, factor=factor, place=place):
            rows = rows_at(i)
            grad = cot_all[rows, now].astype(F32) * factor
            g_out[rows, place * half : (place + 1) * half] = (self_ref[0] * grad).astype(BF16)
            if place == 0:
                cot_half[rows, :] = cot_all[rows, now]

        each_rows(cot_all.shape[0], scale)
    d_active[...] = dot(w_down[...], g_out[...], 1, 0)


def middle_kernel(x_half, chip, received, norms, middle, stats, normed):
    model, half = chip.shape

    def add(i, _):
        rows = rows_at(i)
        middle[rows, :] = x_half[rows, :].astype(F32) + chip[rows, :] + received[rows, :].astype(F32)

    each_rows(model, add)
    mean, scale = spread_of(lambda i: middle[rows_at(i), :], model, half)
    stats[0:1] = mean
    stats[1:2] = scale

    def normalise(i, _):
        rows = rows_at(i)
        xhat = (middle[rows, :] - mean) * scale
        normed[rows, :] = (xhat * norms[rows, 2:3] + norms[rows, 3:4]).astype(BF16)

    each_rows(model, normalise)


def feed_forward_kernel(own, other, w_up, d_active, normed, active, d_hidden, send, keep, hidden):
    half = own.shape[1]
    normed[:, :half] = own[...]
    normed[:, half:] = other[...]
    hidden[...] = dot(w_up[...], normed[...], 0, 0)

    def bend(i, _):
        rows = rows_at(i)
        u = hidden[rows, :]
        squared = u * u
        curve = jnp.tanh(0.7978845608028654 * u * (1.0 + 0.044715 * squared))
        lifted = 0.5 * (1.0 + curve)
        active[rows, :] = (u * lifted).astype(BF16)
        slope = lifted + u * (0.5 * (1.0 - curve * curve)) * (
            0.7978845608028654 + (3 * 0.044715 * 0.7978845608028654) * squared
        )
        d_hidden[rows, :] = (slope * d_active[rows, :]).astype(BF16)

    each_rows(hidden.shape[0], bend)
    send[...] = dot(w_up[...], d_hidden[:, half:], 1, 0).astype(BF16)
    keep[...] = dot(w_up[...], d_hidden[:, :half], 1, 0)


def store_blocks(at, total, part, send, keep):
    for place in range(2):
        for low, out in ((1, send), (0, keep)):
            rows = pl.ds(pl.multiple_of((at ^ (2 * place + low)) * part, 64), part)
            out[place * part : (place + 1) * part] = total[rows, :].astype(out.dtype)


def output_kernel(at_ref, active, w_down, middle, send, keep, total):
    at = at_ref[0]
    model, half = middle.shape
    part = send.shape[0] // 2
    own = pl.ds(pl.multiple_of((at % 2) * half, half), half)
    other = pl.ds(pl.multiple_of((1 - at % 2) * half, half), half)
    total[:, own] = dot(w_down[...], active[:, :half], 0, 0) + 0.5 * middle[...]
    total[:, other] = dot(w_down[...], active[:, half:], 0, 0)
    store_blocks(at, total, part, send, keep)


def middle_gradient_kernel(
    at_ref, self_ref, chip, received, middle, stats, cot_half, live, norms, d_middle, g_mid, d_gain, d_bias, d_normed
):
    model, half = chip.shape
    mean, scale = stats[0:1], stats[1:2]
    zero = jnp.zeros((STEP, half), F32)

    def sums(i, acc):
        rows = rows_at(i)
        grad = chip[rows, :] + received[rows, :].astype(F32)
        d_normed[rows, :] = grad
        xhat = (middle[rows, :] - mean) * scale
        both = grad * xhat
        d_gain[rows, :] = jnp.sum(both, axis=1, keepdims=True)
        d_bias[rows, :] = jnp.sum(grad, axis=1, keepdims=True)
        gain = norms[rows, 2:3]
        return acc[0] + grad * gain, acc[1] + both * gain

    first, second = (column_sum(v) / model for v in each_rows(model, sums, (zero, zero)))
    own = pl.ds(pl.multiple_of((at_ref[0] % 2) * half, half), half)
    factor = self_ref[0] * live[:, own]

    def finish(i, _):
        rows = rows_at(i)
        xhat = (middle[rows, :] - mean) * scale
        found = cot_half[rows, :].astype(F32) * factor + scale * (
            d_normed[rows, :] * norms[rows, 2:3] - first - xhat * second
        )
        d_middle[rows, :] = found
        g_mid[rows, :] = found.astype(BF16)

    each_rows(model, finish)


def attention_gradient_kernel(
    at_ref, own, other, w_out, qkv, probs, cosine, sine,
    d_project, g_mid, d_heads, d_scores, products, d_queries, d_keys, d_values,
):
    at = at_ref[0]
    half = own.shape[1]
    part = w_out.shape[0]
    g_mid[:, pl.ds(pl.multiple_of((at % 2) * half, half), half)] = own[...]
    g_mid[:, pl.ds(pl.multiple_of((1 - at % 2) * half, half), half)] = other[...]
    d_heads[...] = dot(w_out[...], g_mid[...], 1, 0).astype(BF16)
    width = HEAD_DIM // 2
    for h in range(part // HEAD_DIM):
        head = slice(h * HEAD_DIM, (h + 1) * HEAD_DIM)
        query = qkv[head]
        key = qkv[part + h * HEAD_DIM : part + (h + 1) * HEAD_DIM]
        value = qkv[2 * part + h * HEAD_DIM : 2 * part + (h + 1) * HEAD_DIM]
        for t in range(2):
            now = slice(t * half, (t + 1) * half)
            count = (t + 1) * half
            products[:count] = dot(value[:, :count], d_heads[head, now], 0, 0)

            def weigh(i, acc):
                rows = rows_at(i)
                return acc + products[rows, :] * probs[h, rows, now].astype(F32)

            inner = column_sum(each_rows(count, weigh, jnp.zeros((STEP, half), F32)))

            def settle(i, _):
                rows = rows_at(i)
                d_scores[rows, :] = (probs[h, rows, now].astype(F32) * (products[rows, :] - inner)).astype(BF16)

            each_rows(count, settle)
            d_queries[:, now] = dot(key[:, :count], d_scores[:count], 1, 0) * HEAD_DIM ** (-0.5)
            d_key = dot(query[:, now], d_scores[:count], 1, 1)
            d_value = dot(d_heads[head, now], probs[h, :count, now], 1, 1)
            if t == 0:
                d_keys[:, :half] = d_key
                d_values[:, :half] = d_value
            else:
                d_keys[:, :half] += d_key[:, :half]
                d_values[:, :half] += d_value[:, :half]
                d_keys[:, half:] = d_key[:, half:]
                d_values[:, half:] = d_value[:, half:]
        for block, found in ((0, d_queries), (1, d_keys)):
            start = block * part + h * HEAD_DIM
            front, back = found[:width], found[width:]
            d_project[start : start + width] = (front * cosine[...] + back * sine[...]).astype(BF16)
            d_project[start + width : start + HEAD_DIM] = (back * cosine[...] - front * sine[...]).astype(BF16)
        d_project[2 * part + h * HEAD_DIM : 2 * part + (h + 1) * HEAD_DIM] = d_values[...].astype(BF16)


def input_gradient_kernel(
    at_ref, d_project, w_qkv, x_all, stats, d_middle, norms, send, keep, sums, d_gain, d_bias, total
):
    at = at_ref[0]
    model, half = d_middle.shape
    tokens = x_all.shape[1]
    part = send.shape[0] // 2
    total[...] = dot(w_qkv[...], d_project[...], 0, 0)
    mean, scale = stats[0:1], stats[1:2]
    zero = jnp.zeros((STEP, tokens), F32)
    own = pl.ds(pl.multiple_of((at % 2) * half, half), half)

    def body(i, acc):
        rows = rows_at(i)
        grad = total[rows, :]
        xhat = (x_all[rows, :].astype(F32) - mean) * scale
        both = grad * xhat
        d_gain[rows, :] = jnp.sum(both, axis=1, keepdims=True)
        d_bias[rows, :] = jnp.sum(grad, axis=1, keepdims=True)
        gain = norms[rows, 0:1]
        lifted = grad * gain
        total[rows, :] = lifted * scale
        total[rows, own] += 0.5 * d_middle[rows, :]
        return acc[0] + lifted, acc[1] + both * gain

    first, second = each_rows(model, body, (zero, zero))
    sums[0:1] = column_sum(first) / model
    sums[1:2] = column_sum(second) / model
    store_blocks(at, total, part, send, keep)


def local(
    width,
    row_devices,
    x_in,
    history,
    cotangent,
    counts,
    positions,
    mix_weights,
    self_weight,
    first_norm_gain,
    first_norm_bias,
    w_qkv,
    w_out,
    second_norm_gain,
    second_norm_bias,
    w_up,
    w_down,
):
    part, tokens = x_in.shape
    model = w_out.shape[1]
    hidden_units = w_up.shape[1]
    half = tokens // 2
    layers = mix_weights.shape[0]
    at_width = lax.axis_index("width")
    at = at_width.astype(jnp.int32)[None]
    me = lax.axis_index("rows").astype(jnp.int32)[None]
    to_width = lambda value, offset: xor_send(value, "width", width, offset)
    w_qkv = w_qkv.reshape(3 * part, model)

    x_pieces = gather_width(x_in, width, ())
    norms = jnp.stack([first_norm_gain, first_norm_bias, second_norm_gain, second_norm_bias])
    norms = after(norms, x_in)
    near = to_width(norms, 1)
    pair = jnp.where(at_width % 2 == 1, jnp.concatenate([near, norms], 1), jnp.concatenate([norms, near], 1))
    far = to_width(pair, 2)
    norms = jnp.where(at_width // 2 == 1, jnp.concatenate([far, pair], 1), jnp.concatenate([pair, far], 1)).T
    inverse = 1.0 / 10000.0 ** (jnp.arange(HEAD_DIM // 2, dtype=F32) * 2.0 / HEAD_DIM)
    angles = positions[None, :].astype(F32) * inverse[:, None]
    cosine, sine = jnp.cos(angles), jnp.sin(angles)
    live_total = counts
    for stride, radix in reversed(digits_of(row_devices, "near")):
        live_total = live_total + sum(
            xor_send(live_total, "rows", row_devices, e * stride) for e in range(1, radix)
        )
    loss_scale = jnp.float32(tokens * row_devices) / live_total[0].astype(F32)
    live = jnp.where(jnp.arange(tokens) < counts[0], loss_scale, 0.0)[None, :]

    send, keep, x_half, x_all, normed_one, stats_one, qkv, heads_out, probs = kernel(
        attention_kernel,
        (
            shape(model, half, kind=BF16),
            shape(model, half),
            shape(model, half, kind=BF16),
            shape(model, tokens, kind=BF16),
            shape(model, tokens, kind=BF16),
            shape(2, tokens),
            shape(3 * part, tokens, kind=BF16),
            shape(part, tokens, kind=BF16),
            shape(part // HEAD_DIM, tokens, tokens, kind=BF16),
        ),
        [at],
        [*x_pieces, after(norms, live), cosine, sine, w_qkv, w_out],
        [pltpu.VMEM((3 * part, tokens), F32), pltpu.VMEM((tokens, half), F32)],
        4 * 10**9,
    )
    chip = keep + to_width(send, 1).astype(F32)
    received = to_width(chip.astype(BF16), 2)
    cot_pieces = gather_width(after(cotangent, *x_pieces), width, (send,))

    g_out, d_active, cot_half = kernel(
        output_gradient_kernel,
        (shape(model, tokens, kind=BF16), shape(hidden_units, tokens), shape(model, half, kind=BF16)),
        [at, self_weight],
        [*cot_pieces, after(live, chip), w_down],
        [pltpu.VMEM((model, tokens), BF16)],
        10**9,
    )
    running, d_history, d_mix = mix_history(mix_weights, history, cotangent, after(live, d_active))

    middle, stats_two, normed_own = kernel(
        middle_kernel,
        (shape(model, half), shape(2, half), shape(model, half, kind=BF16)),
        [],
        [x_half, chip, after(received, running), norms],
        flops=10**8,
    )
    normed_two, active, d_hidden, send, keep = kernel(
        feed_forward_kernel,
        (
            shape(model, tokens, kind=BF16),
            shape(hidden_units, tokens, kind=BF16),
            shape(hidden_units, tokens, kind=BF16),
            shape(model, half, kind=BF16),
            shape(model, half),
        ),
        [],
        [normed_own, to_width(normed_own, 1), w_up, d_active],
        [pltpu.VMEM((hidden_units, tokens), F32)],
        2 * 10**9,
    )

    down = Stream(row_devices, 0, hidden_units, "halving")
    up = Stream(row_devices, 0, model, "crossed")
    down_parts = weight_gradient(me, [down], active, after(g_out, send))[0]
    down_got = start_stage(down, down_parts, 0)
    chip = keep + after(to_width(send, 1), *down_parts).astype(F32)
    received = to_width(chip.astype(BF16), 2)
    up_parts = weight_gradient(me, [up], normed_two, after(d_hidden, chip))[0]
    up_got = start_stage(up, up_parts, 0)

    blocks = (shape(2 * part, tokens, kind=BF16), shape(2 * part, tokens))
    out_send, out_keep = kernel(
        output_kernel,
        blocks,
        [at],
        [active, w_down, after(middle, *up_parts)],
        [pltpu.VMEM((model, tokens), F32)],
        10**9,
    )
    out_chip = out_keep + to_width(out_send, 1).astype(F32)
    output = out_chip[:part] + to_width(out_chip[part:].astype(BF16), 2).astype(F32)

    d_middle, g_own, d_gain_two, d_bias_two = kernel(
        middle_gradient_kernel,
        (shape(model, half), shape(model, half, kind=BF16), shape(model, 1), shape(model, 1)),
        [at, self_weight],
        [chip, after(received, out_chip), middle, stats_two, cot_half, live, norms],
        [pltpu.VMEM((model, half), F32)],
        10**8,
    )
    g_other = to_width(g_own, 1)
    down_parts = add_stage(down, down_parts, [after(v, g_own) for v in down_got], 0)
    down_got = start_stage(down, down_parts, 1)
    up_parts = add_stage(up, up_parts, [after(v, g_own) for v in up_got], 0)
    up_got = start_stage(up, up_parts, 1)
    d_project, g_mid = kernel(
        attention_gradient_kernel,
        (shape(3 * part, tokens, kind=BF16), shape(model, tokens, kind=BF16)),
        [at],
        [g_own, after(g_other, *down_parts, *up_parts), w_out, qkv, probs, cosine, sine],
        [
            pltpu.VMEM((part, tokens), BF16),
            pltpu.VMEM((tokens, half), BF16),
            pltpu.VMEM((tokens, half), F32),
            pltpu.VMEM((HEAD_DIM, tokens), F32),
            pltpu.VMEM((HEAD_DIM, tokens), F32),
            pltpu.VMEM((HEAD_DIM, tokens), F32),
        ],
        4 * 10**9,
    )
    tail_rows = 4 * part
    tail = [
        Stream(row_devices, 0, tail_rows * 2 // 3, "near"),
        Stream(row_devices, tail_rows * 2 // 3, tail_rows // 3, "far"),
    ]
    tail_parts = weight_gradient(me, tail, d_project, normed_one, heads_out, g_mid)
    tail_got = [start_stage(s, p, 0) for s, p in zip(tail, tail_parts)]

    in_send, in_keep, sums, d_gain_one, d_bias_one = kernel(
        input_gradient_kernel,
        blocks + (shape(2, tokens), shape(model, 1), shape(model, 1)),
        [at],
        [after(d_project, *tail_parts[0]), w_qkv, x_all, stats_one, d_middle, norms],
        [pltpu.VMEM((model, tokens), F32)],
        10**9,
    )
    in_near = to_width(in_send, 1)

    down_parts = add_stage(down, down_parts, [after(v, in_send) for v in down_got], 1)
    down_got = start_stage(down, down_parts, 2)
    up_parts = add_stage(up, up_parts, [after(v, in_send) for v in up_got], 1)
    up_got = start_stage(up, up_parts, 2)

    cot_wide = cotangent.astype(F32) * live
    mixed = (self_weight[0] * output + running).astype(BF16)
    d_mix = jnp.concatenate([jnp.sum(d_mix, axis=(1, 2)), jnp.sum(cot_wide * output)[None]])
    flat = jnp.concatenate(
        [d_gain_one[:, 0], d_bias_one[:, 0], 0.5 * d_gain_two[:, 0], 0.5 * d_bias_two[:, 0], sums[0], sums[1], d_mix]
    )
    flat = sum_small(flat, "width", width)
    in_chip = in_keep + in_near.astype(F32)
    in_total = in_chip[:part] + to_width(in_chip[part:].astype(BF16), 2).astype(F32)
    scale_one = stats_one[1:2]
    own_xhat = (x_in.astype(F32) - stats_one[0:1]) * scale_one
    d_input = in_total - scale_one * (
        flat[4 * model : 4 * model + tokens] + own_xhat * flat[4 * model + tokens : 4 * model + 2 * tokens]
    )
    ends = [lax.dynamic_slice_in_dim(flat, i * model + at_width * part, part) for i in range(4)]
    small = sum_small(jnp.concatenate([flat[4 * model + 2 * tokens :]] + ends), "rows", row_devices)
    ends = [small[layers + 1 + i * part : layers + 1 + (i + 1) * part] for i in range(4)]

    tail_parts = [add_stage(s, p, g, 0) for s, p, g in zip(tail, tail_parts, tail_got)]
    tail_got = [start_stage(s, p, 1) for s, p in zip(tail, tail_parts)]
    down_value = sum_rest(down, add_stage(down, down_parts, [after(v, *tail_parts[0]) for v in down_got], 2)[0])
    up_value = sum_rest(up, add_stage(up, up_parts, [after(v, *tail_parts[0]) for v in up_got], 2)[0])
    for stage in range(len(down.digits) - 1, 0, -1):
        down_value = jnp.concatenate(gather_stage(down, down_value, stage))
        up_value = jnp.concatenate(gather_stage(up, up_value, stage))
        if stage == len(down.digits) - 1:
            tail_values = [
                sum_rest(s, add_stage(s, p, [after(v, down_value) for v in g], 1)[0])
                for s, p, g in zip(tail, tail_parts, tail_got)
            ]
            tail_values = [jnp.concatenate(gather_stage(s, v, 1)) for s, v in zip(tail, tail_values)]
    down_pieces = gather_stage(down, down_value, 0)
    up_pieces = gather_stage(up, up_value, 0)
    tail_pieces = [piece for s, v in zip(tail, tail_values) for piece in gather_stage(s, v, 0)]
    d_w_down = place(me, [down], down_pieces, (hidden_units,))[0]
    d_w_up = place(me, [up], up_pieces, (model,))[0]
    d_w_qkv, d_w_out = place(me, tail, tail_pieces, (3 * part, part))
    return (
        mixed,
        d_input,
        d_history,
        small[:layers],
        small[layers : layers + 1],
        ends[0],
        ends[1],
        d_w_qkv.reshape(3, part, model),
        d_w_out,
        ends[2],
        ends[3],
        d_w_up,
        d_w_down,
    )


def solution(mesh):
    return jax.shard_map(
        functools.partial(local, mesh.shape["width"], mesh.shape["rows"]),
        mesh=mesh,
        in_specs=(
            P("width", "rows"),
            P(None, "width", "rows"),
            P("width", "rows"),
            P("rows"),
            P("rows"),
            P(),
            P(),
            P("width"),
            P("width"),
            P(None, "width", None),
            P("width", None),
            P("width"),
            P("width"),
            P(None, "width"),
            P("width", None),
        ),
        out_specs=(
            P("width", "rows"),
            P("width", "rows"),
            P(None, "width", "rows"),
            P(),
            P(),
            P("width"),
            P("width"),
            P(None, "width", None),
            P("width", None),
            P("width"),
            P("width"),
            P(None, "width"),
            P("width", None),
        ),
        check_vma=False,
    )
```

time: 485 us -> 213 us (0.44)
  blocking collectives: 147 us -> 0 us
  other arithmetic: 128 us -> 15 us
  starting transfers between devices: 0.21 us -> 53.7 us
  Pallas kernels: 0 us -> 39.6 us
  local copies, waits for them, and re-layouts: 56.4 us -> 18.6 us
  waiting for transfers between devices: 108 us -> 80.6 us
  matrix products: 27.3 us -> 0 us
  between operations: 16.4 us -> 5.26 us
    psum x9 -> x0, blocking collectives: 113 us -> none  [the longest x1 40.7 us: local(): lax.psum((mix_partial, self_partial[None]), ('rows', 'width'))]
    ppermute x0 -> x55, waiting for transfers between devices: none -> 80.6 us  [xor_send(): return lax.ppermute(value, axis, [(i, i ^ offset) for i in range(size)])]
    reduce_sum x38 -> x2, other arithmetic: 79.5 us -> 2.62 us  [the longest x1 1.41 us: local(): jnp.sum(cot_wide * output)[None]]
    reduce_scatter x4 -> x0, waiting for transfers between devices: 72.3 us -> none  [the longest x2 43.7 us: reduce_branch(): lax.psum_scatter(partial_terms, 'width', scatter_dimension=1, tiled=True)]
    ppermute x0 -> x55, starting transfers between devices: none -> 53.7 us  [xor_send(): return lax.ppermute(value, axis, [(i, i ^ offset) for i in range(size)])]
    dynamic_update_slice x30 -> x0, other arithmetic: 40.6 us -> none  [local(): lax.scan(mix_layer, self_weight[0] * output_wide, (mix_weights, history))]
    pallas_call x0 -> x15, Pallas kernels: none -> 39.6 us  [the longest x14 34.2 us: kernel(): pl.pallas_call(body, out_shape=outs, in_specs=[pl.BlockSpec(memory_space=...]
    psum x1 -> x0, waiting for transfers between devices: 35.1 us -> none  [local(): lax.psum((d_gain_one, d_bias_one, d_w_qkv, d_w_out, d_gain_two, d_bias_tw...]
  transfers between devices with their start and end apart: 5 -> 55, of which waited for: 4 -> 22; matrix products, arithmetic and copies ran while one was open for 34% -> 8% of each run, Pallas kernels for 0% -> 7%
where the time goes in v2:
time: 213 us
  waiting for transfers between devices  80.6 us (38%)
  starting transfers between devices  53.7 us (25%)
  Pallas kernels  39.6 us (19%)
  local copies, waits for them, and re-layouts  18.6 us (9%)
  other arithmetic  15 us (7%)
  between operations  5.26 us (2%)
    ppermute x55, waiting for transfers between devices, xor_send(): return lax.ppermute(value, axis, [(i, i ^ offset) for i in range(size)])  80.6 us
    ppermute x55, starting transfers between devices, xor_send(): return lax.ppermute(value, axis, [(i, i ^ offset) for i in range(size)])  53.7 us
    pallas_call x14, Pallas kernels, kernel(): pl.pallas_call(body, out_shape=outs, in_specs=[pl.BlockSpec(memory_space=...  34.2 us
    unnamed x108, local copies, waits for them, and re-layouts  12.4 us
    pallas_call x1, Pallas kernels, mix_history(): pl.pallas_call(history_kernel, grid=(features // block,), out_shape=(shap...  5.37 us
  transfers between devices with their start and end apart: 55, of which 22 were waited for; matrix products, arithmetic and copies ran while one was open for 8% of the time, Pallas kernels for 7%

profile of v2, /device:TPU:0, one launch (start us, length us, event | category | flops | bytes accessed | tf_op | source)
XLA Modules:
  0.0 212.7 jit_solution(6635727562409697802)
XLA Ops:
  0.7 4.1 %collective-permute-start.6 = (s32[1]{0:T(128)}, s32[1]{0:T(128)}, u32[]{:S(2)}, u32[]{:S(2)}) collective-permute-start(s32[1]{0:T(128)} %param.18), channel_id=1, source_target_pairs={{0,16},{4,20},{8,24},{12,28},{16,0},{20,4},{24,8},{28,12},{1,17},{... | collective-permute-start | bytes 20 | tf_op jit(solution)/shard_map/ppermute | solution.py:55
  4.8 1.6 collective-permute-start.5
  6.4 1.7 collective-permute-start.1
  13.0 2.9 %collective-permute-start.8 = (s32[1]{0:T(128)}, s32[1]{0:T(128)}, u32[]{:S(2)}, u32[]{:S(2)}) collective-permute-start(s32[1]{0:T(128)} %add.124), channel_id=1, source_target_pairs={{0,4},{4,0},{8,12},{12,8},{16,20},{20,16},{24,28},{28,24},{1,5},{5... | collective-permute-start | bytes 20 | tf_op jit(solution)/shard_map/ppermute | solution.py:55
  18.3 2.6 %collective-permute-done.4 = f32[4,384]{1,0:T(4,128)S(1)} collective-permute-done((f32[4,384]{1,0:T(4,128)S(1)}, f32[4,384]{1,0:T(4,128)S(1)}, u32[]{:S(2)}, u32[]{:S(2)}) %collective-permute-start.4) | collective-permute-done | bytes 6176 | tf_op jit(solution)/shard_map/ppermute | solution.py:55
  24.3 8.0 %shard_map.246 = (bf16[768,256]{1,0:T(8,128)(2,1)S(1)}, f32[768,256]{1,0:T(8,128)S(1)}, bf16[768,256]{1,0:T(8,128)(2,1)S(1)}, bf16[768,512]{1,0:T(8,128)(2,1)S(1...) custom-call(s32[1]{0:T(128)} %bitcast.1.at_ref, ...), custom_call_target="tpu_custom_call" | custom-call | flops 1024 | bytes 1024 | tf_op jit(solution)/shard_map/pallas_call | solution.py:22
  37.7 5.0 %collective-permute-done.12.c2 = bf16[192,512]{1,0:T(8,128)(2,1)S(1)} collective-permute-done((bf16[192,512]{1,0:T(8,128)(2,1)S(1)}, bf16[192,512]{1,0:T(8,128)(2,1)S(1)}, u32[]{:S(2)}, u32[]{:S(2)}) %collective-permute-start.12) | collective-permute-done | bytes 196640 | tf_op jit(solution)/shard_map/ppermute | solution.py:55
  45.4 5.4 %shard_map.248 = (f32[192,512]{1,0:T(8,128)S(1)}, bf16[30,192,512]{2,1,0:T(8,128)(2,1)}, f32[30,8,128]{2,1,0:T(8,128)S(1)}) custom-call(f32[30]{0:T(128)S(1)} %copy-done.46, bf16[30,192,512]{2,1,0:T(8,128)(2,1)S(1)} %copy-done, bf16[192,512]{1,0:T(8,128)(2,1)S(1)} %copy-done.7, f32[1,512]{1,0:T(1,128)S(1)} %compare_select_fusion.live.live_ref), custom_call_target="tpu_custom_call" | custom-call | flops 1024 | bytes 1024 | tf_op jit(solution)/shard_map/pallas_call | solution.py:245
  50.8 1.6 shard_map.249
  53.4 1.6 collective-permute-done.14.other
  55.0 3.4 %shard_map.250 = (bf16[768,512]{1,0:T(8,128)(2,1)S(1)}, bf16[768,512]{1,0:T(8,128)(2,1)S(1)}, bf16[768,512]{1,0:T(8,128)(2,1)S(1)}, bf16[768,256]{1,0:T(8,128)(2,1)}, f32[768,256]{1,0:T(8,128)S(1)}) custom-call(bf16[768,256]{1,0:T(8,128)(2,1)S(1)} %get-tuple-element.97.own, bf16[768,256]{1,0:T(8,128)(2,1)S(1)} %collective-permute-done.14.other, ...), custom_call_target="tpu_custom_call" | custom-call | flops 1024 | bytes 1024 | tf_op jit(solution)/shard_map/pallas_call | solution.py:22
  62.3 1.7 shard_map.251
  64.9 2.3 %fusion.2 = (bf16[768,256]{1,0:T(8,128)(2,1)}, f32[768,256]{1,0:T(8,128)}) fusion(f32[768,256]{1,0:T(8,128)S(1)} %copy-done.24, bf16[768,256]{1,0:T(8,128)(2,1)} %collective-permute-done.15), kind=kLoop, calls=%fused_computation.40 | loop fusion | flops 589824 | bytes 2359296 | tf_op jit(solution)/shard_map/convert_element_type | solution.py:657
  68.3 1.6 shard_map.253
  71.2 1.5 collective-permute-start.20
  75.1 1.4 convert_add_fusion.1
  76.6 1.6 collective-permute-start.17
  78.1 6.7 %collective-permute-done.18.received = bf16[768,256]{1,0:T(8,128)(2,1)S(1)} collective-permute-done((bf16[768,256]{1,0:T(8,128)(2,1)}, bf16[768,256]{1,0:T(8,128)(2,1)S(1)}, u32[]{:S(2)}, u32[]{:S(2)}) %collective-permute-start.18) | collective-permute-done | bytes 393248 | tf_op jit(solution)/shard_map/ppermute | solution.py:55
  84.9 2.8 %shard_map.254 = (f32[768,256]{1,0:T(8,128)S(1)}, bf16[768,256]{1,0:T(8,128)(2,1)S(1)}, f32[768,1]{1,0:T(8,128)S(1)}, f32[768,1]{1,0:T(8,128)S(1)}) custom-call(s32[1]{0:T(128)} %bitcast.1.at_ref, f32[1]{0:T(128)} %copy.35.self_ref, f32[768,256]{1,0:T(8,128)S(1)} %copy-done.6, bf16[768,256]{1,0:T(8,128)(2,1)S(1)} %collective-permute-done.18.received, ...), custom_call_target="tpu_custom_call" | custom-call | flops 1024 | bytes 1024 | tf_op jit(solution)/shard_map/pallas_call | solution.py:22
  91.2 1.4 multiply_reduce_fusion
  92.7 3.8 %shard_map.255 = (bf16[576,512]{1,0:T(8,128)(2,1)S(1)}, bf16[768,512]{1,0:T(8,128)(2,1)S(1)}) custom-call(s32[1]{0:T(128)} %bitcast.1.at_ref, bf16[768,256]{1,0:T(8,128)(2,1)S(1)} %get-tuple-element.118.own, bf16[768,256]{1,0:T(8,128)(2,1)S(1)} %collective-permute-done.19.other, bf16[192,768]{1,0:T(8,128)(2,1)S(1)} %copy-done.12, ...), custom_call_target="tpu_custom_call" | custom-call | flops 1024 | bytes 1024 | tf_op jit(solution)/shard_map/pallas_call | solution.py:22
  98.3 3.4 %shard_map.257 = (bf16[384,512]{1,0:T(8,128)(2,1)S(1)}, f32[384,512]{1,0:T(8,128)S(1)}, f32[2,512]{1,0:T(2,128)S(1)}, f32[768,1]{1,0:T(8,128)S(1)}, f32[768,1]{1,0:T(8,128)S(1)}) custom-call(s32[1]{0:T(128)} %bitcast.1.at_ref, bf16[576,512]{1,0:T(8,128)(2,1)S(1)} %get-tuple-element.130.refs_0_.d_project, bf16[576,768]{1,0:T(8,128)(2,1)S(1)} %bitcast.22, ...), custom_call_target="tpu_custom_call" | custom-call | flops 1024 | bytes 1024 | tf_op jit(solution)/shard_map/pallas_call | solution.py:22
  107.9 2.5 %collective-permute-done.25 = f32[4127]{0:T(1024)S(1)} collective-permute-done((f32[4127]{0:T(1024)S(1)}, f32[4127]{0:T(1024)S(1)}, u32[]{:S(2)}, u32[]{:S(2)}) %collective-permute-start.25) | collective-permute-done | bytes 16540 | tf_op jit(solution)/shard_map/ppermute | solution.py:55
  111.2 1.5 collective-permute-start.48
  113.9 3.8 %collective-permute-done.31 = bf16[192,768]{1,0:T(8,128)(2,1)S(1)} collective-permute-done((bf16[192,768]{1,0:T(8,128)(2,1)}, bf16[192,768]{1,0:T(8,128)(2,1)S(1)}, u32[]{:S(2)}, u32[]{:S(2)}) %collective-permute-start.31) | collective-permute-done | bytes 294944 | tf_op jit(solution)/shard_map/ppermute | solution.py:55
  119.1 2.3 %collective-permute-done.27 = f32[799]{0:T(1024)S(1)} collective-permute-done((f32[799]{0:T(1024)S(1)}, f32[799]{0:T(1024)S(1)}, u32[]{:S(2)}, u32[]{:S(2)}) %collective-permute-start.27) | collective-permute-done | bytes 3228 | tf_op jit(solution)/shard_map/ppermute | solution.py:55
  121.5 2.0 collective-permute-start.28
  123.5 2.5 %collective-permute-done.28 = f32[799]{0:T(1024)S(1)} collective-permute-done((f32[799]{0:T(1024)S(1)}, f32[799]{0:T(1024)S(1)}, u32[]{:S(2)}, u32[]{:S(2)}) %collective-permute-start.28) | collective-permute-done | bytes 3228 | tf_op jit(solution)/shard_map/ppermute | solution.py:55
  126.0 2.0 collective-permute-start.41
  129.3 2.0 collective-permute-start.32
  131.3 7.6 %collective-permute-done.41 = bf16[64,768]{1,0:T(8,128)(2,1)S(1)} collective-permute-done((bf16[64,768]{1,0:T(8,128)(2,1)S(1)}, bf16[64,768]{1,0:T(8,128)(2,1)S(1)}, u32[]{:S(2)}, u32[]{:S(2)}) %collective-permute-start.41) | collective-permute-done | bytes 98336 | tf_op jit(solution)/shard_map/ppermute | solution.py:55
  139.6 3.1 %collective-permute-start.49 = (bf16[96,768]{1,0:T(8,128)(2,1)S(1)}, bf16[96,768]{1,0:T(8,128)(2,1)S(1)}, u32[]{:S(2)}, u32[]{:S(2)}) collective-permute-start(bf16[96,768]{1,0:T(8,128)(2,1)S(1)} %slice.146), channel_id=1, source_target_pairs={{0,16},{4,20},{8,24},{12,28},{16,0},{20,4},{24,8},{28,12},{1,17},{... | collective-permute-start | bytes 442376 | tf_op jit(solution)/shard_map/ppermute | solution.py:55
  143.9 2.0 collective-permute-start.35
  146.0 1.4 collective-permute-start.30
  147.4 5.9 %collective-permute-done.49 = bf16[96,768]{1,0:T(8,128)(2,1)S(1)} collective-permute-done((bf16[96,768]{1,0:T(8,128)(2,1)S(1)}, bf16[96,768]{1,0:T(8,128)(2,1)S(1)}, u32[]{:S(2)}, u32[]{:S(2)}) %collective-permute-start.49) | collective-permute-done | bytes 147488 | tf_op jit(solution)/shard_map/ppermute | solution.py:55
  153.4 10.3 %collective-permute-done.33 = bf16[96,768]{1,0:T(8,128)(2,1)S(1)} collective-permute-done((bf16[96,768]{1,0:T(8,128)(2,1)S(1)}, bf16[96,768]{1,0:T(8,128)(2,1)S(1)}, u32[]{:S(2)}, u32[]{:S(2)}) %collective-permute-start.33) | collective-permute-done | bytes 147488 | tf_op jit(solution)/shard_map/ppermute | solution.py:55
  163.7 1.6 collective-permute-start.23
  165.4 3.3 %collective-permute-start.53 = (bf16[192,768]{1,0:T(8,128)(2,1)S(1)}, bf16[192,768]{1,0:T(8,128)(2,1)S(1)}, u32[]{:S(2)}, u32[]{:S(2)}) collective-permute-start(bf16[192,768]{1,0:T(8,128)(2,1)S(1)} %pad_maximum_fusion.3), channel_id=1, source_target_pairs={{0,8},{4,12},{8,0},{12,4},{16,24},{20,28},{24,16},{28,20},{1,9},{5... | collective-permute-start | bytes 884744 | tf_op jit(solution)/shard_map/ppermute | solution.py:55
  169.3 5.5 %collective-permute-done.50 = bf16[96,768]{1,0:T(8,128)(2,1)S(1)} collective-permute-done((bf16[96,768]{1,0:T(8,128)(2,1)S(1)}, bf16[96,768]{1,0:T(8,128)(2,1)S(1)}, u32[]{:S(2)}, u32[]{:S(2)}) %collective-permute-start.50) | collective-permute-done | bytes 147488 | tf_op jit(solution)/shard_map/ppermute | solution.py:55
  175.0 2.4 %collective-permute-start.38 = (bf16[64,768]{1,0:T(8,128)(2,1)S(1)}, bf16[64,768]{1,0:T(8,128)(2,1)S(1)}, u32[]{:S(2)}, u32[]{:S(2)}) collective-permute-start(bf16[64,768]{1,0:T(8,128)(2,1)S(1)} %add_convert_fusion.9), channel_id=1, source_target_pairs={{0,24},{4,28},{8,16},{12,20},{16,8},{20,12},{24,0},{28,4},{1,25},{... | collective-permute-start | bytes 294920 | tf_op jit(solution)/shard_map/ppermute | solution.py:55
  177.4 6.3 %collective-permute-done.51 = bf16[192,768]{1,0:T(8,128)(2,1)S(1)} collective-permute-done((bf16[192,768]{1,0:T(8,128)(2,1)S(1)}, bf16[192,768]{1,0:T(8,128)(2,1)S(1)}, u32[]{:S(2)}, u32[]{:S(2)}) %collective-permute-start.51) | collective-permute-done | bytes 294944 | tf_op jit(solution)/shard_map/ppermute | solution.py:55
  187.1 3.7 %collective-permute-done.36 = bf16[64,768]{1,0:T(8,128)(2,1)S(1)} collective-permute-done((bf16[64,768]{1,0:T(8,128)(2,1)S(1)}, bf16[64,768]{1,0:T(8,128)(2,1)S(1)}, u32[]{:S(2)}, u32[]{:S(2)}) %collective-permute-start.36) | collective-permute-done | bytes 98336 | tf_op jit(solution)/shard_map/ppermute | solution.py:55
  193.6 2.2 %collective-permute-start.45 = (bf16[64,768]{1,0:T(8,128)(2,1)S(1)}, bf16[64,768]{1,0:T(8,128)(2,1)S(1)}, u32[]{:S(2)}, u32[]{:S(2)}) collective-permute-start(bf16[64,768]{1,0:T(8,128)(2,1)S(1)} %pad_maximum_fusion.5.refs_2_), channel_id=1, source_target_pairs={{0,8},{4,12},{8,0},{12,4},{16,24},{20,28},{24,16},{28,20},{1,9},{5... | collective-permute-start | bytes 294920 | tf_op jit(solution)/shard_map/ppermute | solution.py:55
  196.7 6.6 %collective-permute-done.46.refs_4_ = bf16[64,768]{1,0:T(8,128)(2,1)S(1)} collective-permute-done((bf16[64,768]{1,0:T(8,128)(2,1)S(1)}, bf16[64,768]{1,0:T(8,128)(2,1)S(1)}, u32[]{:S(2)}, u32[]{:S(2)}) %collective-permute-start.46) | collective-permute-done | bytes 98336 | tf_op jit(solution)/shard_map/ppermute | solution.py:55
  203.3 4.0 %collective-permute-done.45.refs_3_ = bf16[64,768]{1,0:T(8,128)(2,1)S(1)} collective-permute-done((bf16[64,768]{1,0:T(8,128)(2,1)S(1)}, bf16[64,768]{1,0:T(8,128)(2,1)S(1)}, u32[]{:S(2)}, u32[]{:S(2)}) %collective-permute-start.45) | collective-permute-done | bytes 98336 | tf_op jit(solution)/shard_map/ppermute | solution.py:55
  207.7 1.8 shard_map.258
  209.6 1.6 shard_map.259
  211.1 1.6 shard_map.260
  (245 shorter events, 51.9 us)
Async XLA Ops:
  0.7 10.0 %collective-permute-start.6 = (s32[1]{0:T(128)}, s32[1]{0:T(128)}, u32[]{:S(2)}, u32[]{:S(2)}) collective-permute-start(s32[1]{0:T(128)} %param.18), channel_id=1, source_target_pairs={{0,16},{4,20},{8,24},{12,28},{16,0},{20,4},{24,8},{28,12},{1,17},{... | collective-permute-start | bytes 20 | tf_op jit(solution)/shard_map/ppermute | solution.py:55
  4.8 6.4 %collective-permute-start.5 = (s32[1]{0:T(128)}, s32[1]{0:T(128)}, u32[]{:S(2)}, u32[]{:S(2)}) collective-permute-start(s32[1]{0:T(128)} %param.18), channel_id=1, source_target_pairs={{0,8},{4,12},{8,0},{12,4},{16,24},{20,28},{24,16},{28,20},{1,9},{5... | collective-permute-start | bytes 20 | tf_op jit(solution)/shard_map/ppermute | solution.py:55
  6.4 6.1 %collective-permute-start.7 = (s32[1]{0:T(128)}, s32[1]{0:T(128)}, u32[]{:S(2)}, u32[]{:S(2)}) collective-permute-start(s32[1]{0:T(128)} %param.18), channel_id=1, source_target_pairs={{0,24},{4,28},{8,16},{12,20},{16,8},{20,12},{24,0},{28,4},{1,25},{... | collective-permute-start | bytes 20 | tf_op jit(solution)/shard_map/ppermute | solution.py:55
  6.4 16.5 %collective-permute-start.1 = (bf16[192,512]{1,0:T(8,128)(2,1)}, bf16[192,512]{1,0:T(8,128)(2,1)S(1)}, u32[]{:S(2)}, u32[]{:S(2)}) collective-permute-start(bf16[192,512]{1,0:T(8,128)(2,1)} %x0.1), channel_id=1, source_target_pairs={{0,2},{1,3},{2,0},{3,1},{4,6},{5,7},{6,4},{7,5},{8,10},{9,11},{10,... | collective-permute-start | bytes 589832 | tf_op jit(solution)/shard_map/ppermute | solution.py:55
  8.8 8.4 %collective-permute-start.3 = (f32[4,192]{1,0:T(4,128)S(1)}, f32[4,192]{1,0:T(4,128)S(1)}, u32[]{:S(2)}, u32[]{:S(2)}) collective-permute-start(f32[4,192]{1,0:T(4,128)S(1)} %pad_maximum_fusion.8), channel_id=1, source_target_pairs={{0,1},{1,0},{2,3},{3,2},{4,5},{5,4},{6,7},{7,6},{8,9},{9,8},{10,11... | collective-permute-start | bytes 9224 | tf_op jit(solution)/shard_map/ppermute | solution.py:55
  10.6 13.4 %collective-permute-start = (bf16[192,512]{1,0:T(8,128)(2,1)}, bf16[192,512]{1,0:T(8,128)(2,1)}, u32[]{:S(2)}, u32[]{:S(2)}) collective-permute-start(bf16[192,512]{1,0:T(8,128)(2,1)} %x0.1), channel_id=1, source_target_pairs={{0,1},{1,0},{2,3},{3,2},{4,5},{5,4},{6,7},{7,6},{8,9},{9,8},{10,11... | collective-permute-start | bytes 589832 | tf_op jit(solution)/shard_map/ppermute | solution.py:55
  35.0 7.7 %collective-permute-start.12 = (bf16[192,512]{1,0:T(8,128)(2,1)S(1)}, bf16[192,512]{1,0:T(8,128)(2,1)S(1)}, u32[]{:S(2)}, u32[]{:S(2)}) collective-permute-start(bf16[192,512]{1,0:T(8,128)(2,1)S(1)} %copy-done.7), channel_id=1, source_target_pairs={{0,2},{1,3},{2,0},{3,1},{4,6},{5,7},{6,4},{7,5},{8,10},{9,11},{10,... | collective-permute-start | bytes 589832 | tf_op jit(solution)/shard_map/ppermute | solution.py:55
  36.6 14.2 %collective-permute-start.10 = (bf16[768,256]{1,0:T(8,128)(2,1)S(1)}, bf16[768,256]{1,0:T(8,128)(2,1)S(1)}, u32[]{:S(2)}, u32[]{:S(2)}) collective-permute-start(bf16[768,256]{1,0:T(8,128)(2,1)S(1)} %get-tuple-element.159), channel_id=1, source_target_pairs={{0,2},{1,3},{2,0},{3,1},{4,6},{5,7},{6,4},{7,5},{8,10},{9,11},{10,... | collective-permute-start | bytes 1179656 | tf_op jit(solution)/shard_map/ppermute | solution.py:55
  37.7 5.7 %collective-permute-start.11 = (bf16[192,512]{1,0:T(8,128)(2,1)S(1)}, bf16[192,512]{1,0:T(8,128)(2,1)S(1)}, u32[]{:S(2)}, u32[]{:S(2)}) collective-permute-start(bf16[192,512]{1,0:T(8,128)(2,1)S(1)} %copy-done.7), channel_id=1, source_target_pairs={{0,1},{1,0},{2,3},{3,2},{4,5},{5,4},{6,7},{7,6},{8,9},{9,8},{10,11... | collective-permute-start | bytes 589832 | tf_op jit(solution)/shard_map/ppermute | solution.py:55
  61.0 3.8 %collective-permute-start.15 = (bf16[768,256]{1,0:T(8,128)(2,1)}, bf16[768,256]{1,0:T(8,128)(2,1)}, u32[]{:S(2)}, u32[]{:S(2)}) collective-permute-start(bf16[768,256]{1,0:T(8,128)(2,1)} %get-tuple-element.103), channel_id=1, source_target_pairs={{0,1},{1,0},{2,3},{3,2},{4,5},{5,4},{6,7},{7,6},{8,9},{9,8},{10,11... | collective-permute-start | bytes 1179656 | tf_op jit(solution)/shard_map/ppermute | solution.py:55
  70.8 4.3 %collective-permute-start.16 = (bf16[384,512]{1,0:T(8,128)(2,1)}, bf16[384,512]{1,0:T(8,128)(2,1)S(1)}, u32[]{:S(2)}, u32[]{:S(2)}) collective-permute-start(bf16[384,512]{1,0:T(8,128)(2,1)} %get-tuple-element.114), channel_id=1, source_target_pairs={{0,1},{1,0},{2,3},{3,2},{4,5},{5,4},{6,7},{7,6},{8,9},{9,8},{10,11... | collective-permute-start | bytes 1179656 | tf_op jit(solution)/shard_map/ppermute | solution.py:55
  71.2 16.6 %collective-permute-start.20 = (bf16[384,768]{1,0:T(8,128)(2,1)}, bf16[384,768]{1,0:T(8,128)(2,1)}, u32[]{:S(2)}, u32[]{:S(2)}) collective-permute-start(bf16[384,768]{1,0:T(8,128)(2,1)} %get-tuple-element.107), channel_id=1, source_target_pairs={{0,4},{4,0},{8,12},{12,8},{16,20},{20,16},{24,28},{28,24},{1,5},{5... | collective-permute-start | bytes 1769480 | tf_op jit(solution)/shard_map/ppermute | solution.py:55
  72.7 12.2 %collective-permute-start.18 = (bf16[768,256]{1,0:T(8,128)(2,1)}, bf16[768,256]{1,0:T(8,128)(2,1)S(1)}, u32[]{:S(2)}, u32[]{:S(2)}) collective-permute-start(bf16[768,256]{1,0:T(8,128)(2,1)} %get-tuple-element.157), channel_id=1, source_target_pairs={{0,2},{1,3},{2,0},{3,1},{4,6},{5,7},{6,4},{7,5},{8,10},{9,11},{10,... | collective-permute-start | bytes 1179656 | tf_op jit(solution)/shard_map/ppermute | solution.py:55
  74.9 15.4 %collective-permute-start.21 = (bf16[384,768]{1,0:T(8,128)(2,1)}, bf16[384,768]{1,0:T(8,128)(2,1)S(1)}, u32[]{:S(2)}, u32[]{:S(2)}) collective-permute-start(bf16[384,768]{1,0:T(8,128)(2,1)} %copy-done.47), channel_id=1, source_target_pairs={{0,8},{4,12},{8,0},{12,4},{16,24},{20,28},{24,16},{28,20},{1,9},{5... | collective-permute-start | bytes 1769480 | tf_op jit(solution)/shard_map/ppermute | solution.py:55
  76.6 14.7 %collective-permute-start.17 = (bf16[192,512]{1,0:T(8,128)(2,1)S(1)}, bf16[192,512]{1,0:T(8,128)(2,1)S(1)}, u32[]{:S(2)}, u32[]{:S(2)}) collective-permute-start(bf16[192,512]{1,0:T(8,128)(2,1)S(1)} %slice.164), channel_id=1, source_target_pairs={{0,2},{1,3},{2,0},{3,1},{4,6},{5,7},{6,4},{7,5},{8,10},{9,11},{10,... | collective-permute-start | bytes 589832 | tf_op jit(solution)/shard_map/ppermute | solution.py:55
  87.7 5.0 %collective-permute-start.19 = (bf16[768,256]{1,0:T(8,128)(2,1)S(1)}, bf16[768,256]{1,0:T(8,128)(2,1)S(1)}, u32[]{:S(2)}, u32[]{:S(2)}) collective-permute-start(bf16[768,256]{1,0:T(8,128)(2,1)S(1)} %get-tuple-element.118.own), channel_id=1, source_target_pairs={{0,1},{1,0},{2,3},{3,2},{4,5},{5,4},{6,7},{7,6},{8,9},{9,8},{10,11... | collective-permute-start | bytes 1179656 | tf_op jit(solution)/shard_map/ppermute | solution.py:55
  106.7 3.8 %collective-permute-start.25 = (f32[4127]{0:T(1024)S(1)}, f32[4127]{0:T(1024)S(1)}, u32[]{:S(2)}, u32[]{:S(2)}) collective-permute-start(f32[4127]{0:T(1024)S(1)} %add.135), channel_id=1, source_target_pairs={{0,2},{1,3},{2,0},{3,1},{4,6},{5,7},{6,4},{7,5},{8,10},{9,11},{10,... | collective-permute-start | bytes 49532 | tf_op jit(solution)/shard_map/ppermute | solution.py:55
  107.7 10.1 %collective-permute-start.31 = (bf16[192,768]{1,0:T(8,128)(2,1)}, bf16[192,768]{1,0:T(8,128)(2,1)S(1)}, u32[]{:S(2)}, u32[]{:S(2)}) collective-permute-start(bf16[192,768]{1,0:T(8,128)(2,1)} %slice.129), channel_id=1, source_target_pairs={{0,8},{4,12},{8,0},{12,4},{16,24},{20,28},{24,16},{28,20},{1,9},{5... | collective-permute-start | bytes 884744 | tf_op jit(solution)/shard_map/ppermute | solution.py:55
  110.6 7.1 %collective-permute-start.26 = (f32[799]{0:T(1024)S(1)}, f32[799]{0:T(1024)S(1)}, u32[]{:S(2)}, u32[]{:S(2)}) collective-permute-start(f32[799]{0:T(1024)S(1)} %concatenate.43), channel_id=1, source_target_pairs={{0,4},{4,0},{8,12},{12,8},{16,20},{20,16},{24,28},{28,24},{1,5},{5... | collective-permute-start | bytes 9596 | tf_op jit(solution)/shard_map/ppermute | solution.py:55
  111.2 16.7 %collective-permute-start.48 = (bf16[192,768]{1,0:T(8,128)(2,1)}, bf16[192,768]{1,0:T(8,128)(2,1)S(1)}, u32[]{:S(2)}, u32[]{:S(2)}) collective-permute-start(bf16[192,768]{1,0:T(8,128)(2,1)} %slice.131), channel_id=1, source_target_pairs={{0,4},{4,0},{8,12},{12,8},{16,20},{20,16},{24,28},{28,24},{1,5},{5... | collective-permute-start | bytes 884744 | tf_op jit(solution)/shard_map/ppermute | solution.py:55
  112.7 30.1 %collective-permute-start.29 = (bf16[256,768]{1,0:T(8,128)(2,1)}, bf16[256,768]{1,0:T(8,128)(2,1)S(1)}, u32[]{:S(2)}, u32[]{:S(2)}) collective-permute-start(bf16[256,768]{1,0:T(8,128)(2,1)} %copy-done.48), channel_id=1, source_target_pairs={{0,4},{4,0},{8,12},{12,8},{16,20},{20,16},{24,28},{28,24},{1,5},{5... | collective-permute-start | bytes 1179656 | tf_op jit(solution)/shard_map/ppermute | solution.py:55
  113.3 16.1 %collective-permute-start.40 = (bf16[64,768]{1,0:T(8,128)(2,1)}, bf16[64,768]{1,0:T(8,128)(2,1)S(1)}, u32[]{:S(2)}, u32[]{:S(2)}) collective-permute-start(bf16[64,768]{1,0:T(8,128)(2,1)} %copy-done.50), channel_id=1, source_target_pairs={{0,8},{4,12},{8,0},{12,4},{16,24},{20,28},{24,16},{28,20},{1,9},{5... | collective-permute-start | bytes 294920 | tf_op jit(solution)/shard_map/ppermute | solution.py:55
  117.8 25.0 %collective-permute-start.22 = (bf16[384,512]{1,0:T(8,128)(2,1)}, bf16[384,512]{1,0:T(8,128)(2,1)S(1)}, u32[]{:S(2)}, u32[]{:S(2)}) collective-permute-start(bf16[384,512]{1,0:T(8,128)(2,1)} %copy-done.49), channel_id=1, source_target_pairs={{0,1},{1,0},{2,3},{3,2},{4,5},{5,4},{6,7},{7,6},{8,9},{9,8},{10,11... | collective-permute-start | bytes 1179656 | tf_op jit(solution)/shard_map/ppermute | solution.py:55
  117.8 3.7 %collective-permute-start.27 = (f32[799]{0:T(1024)S(1)}, f32[799]{0:T(1024)S(1)}, u32[]{:S(2)}, u32[]{:S(2)}) collective-permute-start(f32[799]{0:T(1024)S(1)} %add.143), channel_id=1, source_target_pairs={{0,8},{4,12},{8,0},{12,4},{16,24},{20,28},{24,16},{28,20},{1,9},{5... | collective-permute-start | bytes 9596 | tf_op jit(solution)/shard_map/ppermute | solution.py:55
  121.5 4.5 %collective-permute-start.28 = (f32[799]{0:T(1024)S(1)}, f32[799]{0:T(1024)S(1)}, u32[]{:S(2)}, u32[]{:S(2)}) collective-permute-start(f32[799]{0:T(1024)S(1)} %add.144), channel_id=1, source_target_pairs={{0,16},{4,20},{8,24},{12,28},{16,0},{20,4},{24,8},{28,12},{1,17},{... | collective-permute-start | bytes 9596 | tf_op jit(solution)/shard_map/ppermute | solution.py:55
  126.0 12.9 %collective-permute-start.41 = (bf16[64,768]{1,0:T(8,128)(2,1)S(1)}, bf16[64,768]{1,0:T(8,128)(2,1)S(1)}, u32[]{:S(2)}, u32[]{:S(2)}) collective-permute-start(bf16[64,768]{1,0:T(8,128)(2,1)S(1)} %get-tuple-element.150), channel_id=1, source_target_pairs={{0,16},{4,20},{8,24},{12,28},{16,0},{20,4},{24,8},{28,12},{1,17},{... | collective-permute-start | bytes 294920 | tf_op jit(solution)/shard_map/ppermute | solution.py:55
  128.0 10.9 %collective-permute-start.42 = (bf16[64,768]{1,0:T(8,128)(2,1)S(1)}, bf16[64,768]{1,0:T(8,128)(2,1)S(1)}, u32[]{:S(2)}, u32[]{:S(2)}) collective-permute-start(bf16[64,768]{1,0:T(8,128)(2,1)S(1)} %get-tuple-element.151), channel_id=1, source_target_pairs={{0,24},{4,28},{8,16},{12,20},{16,8},{20,12},{24,0},{28,4},{1,25},{... | collective-permute-start | bytes 294920 | tf_op jit(solution)/shard_map/ppermute | solution.py:55
  129.3 16.6 %collective-permute-start.32 = (bf16[96,768]{1,0:T(8,128)(2,1)S(1)}, bf16[96,768]{1,0:T(8,128)(2,1)S(1)}, u32[]{:S(2)}, u32[]{:S(2)}) collective-permute-start(bf16[96,768]{1,0:T(8,128)(2,1)S(1)} %slice.140), channel_id=1, source_target_pairs={{0,16},{4,20},{8,24},{12,28},{16,0},{20,4},{24,8},{28,12},{1,17},{... | collective-permute-start | bytes 442376 | tf_op jit(solution)/shard_map/ppermute | solution.py:55
  139.0 26.3 %collective-permute-start.43 = (bf16[32,768]{1,0:T(8,128)(2,1)S(1)}, bf16[32,768]{1,0:T(8,128)(2,1)S(1)}, u32[]{:S(2)}, u32[]{:S(2)}) collective-permute-start(bf16[32,768]{1,0:T(8,128)(2,1)S(1)} %slice.144), channel_id=1, source_target_pairs={{0,4},{4,0},{8,12},{12,8},{16,20},{20,16},{24,28},{28,24},{1,5},{5... | collective-permute-start | bytes 147464 | tf_op jit(solution)/shard_map/ppermute | solution.py:55
  139.6 13.8 %collective-permute-start.49 = (bf16[96,768]{1,0:T(8,128)(2,1)S(1)}, bf16[96,768]{1,0:T(8,128)(2,1)S(1)}, u32[]{:S(2)}, u32[]{:S(2)}) collective-permute-start(bf16[96,768]{1,0:T(8,128)(2,1)S(1)} %slice.146), channel_id=1, source_target_pairs={{0,16},{4,20},{8,24},{12,28},{16,0},{20,4},{24,8},{28,12},{1,17},{... | collective-permute-start | bytes 442376 | tf_op jit(solution)/shard_map/ppermute | solution.py:55
  143.8 24.9 %collective-permute-start.34 = (bf16[64,768]{1,0:T(8,128)(2,1)S(1)}, bf16[64,768]{1,0:T(8,128)(2,1)S(1)}, u32[]{:S(2)}, u32[]{:S(2)}) collective-permute-start(bf16[64,768]{1,0:T(8,128)(2,1)S(1)} %get-tuple-element.163), channel_id=1, source_target_pairs={{0,16},{4,20},{8,24},{12,28},{16,0},{20,4},{24,8},{28,12},{1,17},{... | collective-permute-start | bytes 294920 | tf_op jit(solution)/shard_map/ppermute | solution.py:55
  143.9 21.4 %collective-permute-start.35 = (bf16[64,768]{1,0:T(8,128)(2,1)S(1)}, bf16[64,768]{1,0:T(8,128)(2,1)S(1)}, u32[]{:S(2)}, u32[]{:S(2)}) collective-permute-start(bf16[64,768]{1,0:T(8,128)(2,1)S(1)} %get-tuple-element.164), channel_id=1, source_target_pairs={{0,24},{4,28},{8,16},{12,20},{16,8},{20,12},{24,0},{28,4},{1,25},{... | collective-permute-start | bytes 294920 | tf_op jit(solution)/shard_map/ppermute | solution.py:55
  146.0 22.7 %collective-permute-start.30 = (bf16[64,768]{1,0:T(8,128)(2,1)S(1)}, bf16[64,768]{1,0:T(8,128)(2,1)S(1)}, u32[]{:S(2)}, u32[]{:S(2)}) collective-permute-start(bf16[64,768]{1,0:T(8,128)(2,1)S(1)} %get-tuple-element.165), channel_id=1, source_target_pairs={{0,8},{4,12},{8,0},{12,4},{16,24},{20,28},{24,16},{28,20},{1,9},{5... | collective-permute-start | bytes 294920 | tf_op jit(solution)/shard_map/ppermute | solution.py:55
  153.4 10.3 %collective-permute-start.33 = (bf16[96,768]{1,0:T(8,128)(2,1)S(1)}, bf16[96,768]{1,0:T(8,128)(2,1)S(1)}, u32[]{:S(2)}, u32[]{:S(2)}) collective-permute-start(bf16[96,768]{1,0:T(8,128)(2,1)S(1)} %add_convert_fusion.7), channel_id=1, source_target_pairs={{0,16},{4,20},{8,24},{12,28},{16,0},{20,4},{24,8},{28,12},{1,17},{... | collective-permute-start | bytes 442376 | tf_op jit(solution)/shard_map/ppermute | solution.py:55
  163.7 29.9 %collective-permute-start.23 = (bf16[192,512]{1,0:T(8,128)(2,1)S(1)}, bf16[192,512]{1,0:T(8,128)(2,1)S(1)}, u32[]{:S(2)}, u32[]{:S(2)}) collective-permute-start(bf16[192,512]{1,0:T(8,128)(2,1)S(1)} %slice.163), channel_id=1, source_target_pairs={{0,2},{1,3},{2,0},{3,1},{4,6},{5,7},{6,4},{7,5},{8,10},{9,11},{10,... | collective-permute-start | bytes 589832 | tf_op jit(solution)/shard_map/ppermute | solution.py:55
  165.3 9.6 %collective-permute-start.50 = (bf16[96,768]{1,0:T(8,128)(2,1)S(1)}, bf16[96,768]{1,0:T(8,128)(2,1)S(1)}, u32[]{:S(2)}, u32[]{:S(2)}) collective-permute-start(bf16[96,768]{1,0:T(8,128)(2,1)S(1)} %add_convert_fusion.6), channel_id=1, source_target_pairs={{0,16},{4,20},{8,24},{12,28},{16,0},{20,4},{24,8},{28,12},{1,17},{... | collective-permute-start | bytes 442376 | tf_op jit(solution)/shard_map/ppermute | solution.py:55
  165.4 18.4 %collective-permute-start.53 = (bf16[192,768]{1,0:T(8,128)(2,1)S(1)}, bf16[192,768]{1,0:T(8,128)(2,1)S(1)}, u32[]{:S(2)}, u32[]{:S(2)}) collective-permute-start(bf16[192,768]{1,0:T(8,128)(2,1)S(1)} %pad_maximum_fusion.3), channel_id=1, source_target_pairs={{0,8},{4,12},{8,0},{12,4},{16,24},{20,28},{24,16},{28,20},{1,9},{5... | collective-permute-start | bytes 884744 | tf_op jit(solution)/shard_map/ppermute | solution.py:55
  168.7 8.7 %collective-permute-start.44 = (bf16[32,768]{1,0:T(8,128)(2,1)S(1)}, bf16[32,768]{1,0:T(8,128)(2,1)S(1)}, u32[]{:S(2)}, u32[]{:S(2)}) collective-permute-start(bf16[32,768]{1,0:T(8,128)(2,1)S(1)} %add_convert_fusion.10), channel_id=1, source_target_pairs={{0,4},{4,0},{8,12},{12,8},{16,20},{20,16},{24,28},{28,24},{1,5},{5... | collective-permute-start | bytes 147464 | tf_op jit(solution)/shard_map/ppermute | solution.py:55
  174.9 8.8 %collective-permute-start.51 = (bf16[192,768]{1,0:T(8,128)(2,1)S(1)}, bf16[192,768]{1,0:T(8,128)(2,1)S(1)}, u32[]{:S(2)}, u32[]{:S(2)}) collective-permute-start(bf16[192,768]{1,0:T(8,128)(2,1)S(1)} %pad_maximum_fusion.4), channel_id=1, source_target_pairs={{0,4},{4,0},{8,12},{12,8},{16,20},{20,16},{24,28},{28,24},{1,5},{5... | collective-permute-start | bytes 884744 | tf_op jit(solution)/shard_map/ppermute | solution.py:55
  175.0 10.2 %collective-permute-start.38 = (bf16[64,768]{1,0:T(8,128)(2,1)S(1)}, bf16[64,768]{1,0:T(8,128)(2,1)S(1)}, u32[]{:S(2)}, u32[]{:S(2)}) collective-permute-start(bf16[64,768]{1,0:T(8,128)(2,1)S(1)} %add_convert_fusion.9), channel_id=1, source_target_pairs={{0,24},{4,28},{8,16},{12,20},{16,8},{20,12},{24,0},{28,4},{1,25},{... | collective-permute-start | bytes 294920 | tf_op jit(solution)/shard_map/ppermute | solution.py:55
  177.4 8.6 %collective-permute-start.37 = (bf16[64,768]{1,0:T(8,128)(2,1)S(1)}, bf16[64,768]{1,0:T(8,128)(2,1)S(1)}, u32[]{:S(2)}, u32[]{:S(2)}) collective-permute-start(bf16[64,768]{1,0:T(8,128)(2,1)S(1)} %add_convert_fusion.9), channel_id=1, source_target_pairs={{0,16},{4,20},{8,24},{12,28},{16,0},{20,4},{24,8},{28,12},{1,17},{... | collective-permute-start | bytes 294920 | tf_op jit(solution)/shard_map/ppermute | solution.py:55
  183.7 7.1 %collective-permute-start.36 = (bf16[64,768]{1,0:T(8,128)(2,1)S(1)}, bf16[64,768]{1,0:T(8,128)(2,1)S(1)}, u32[]{:S(2)}, u32[]{:S(2)}) collective-permute-start(bf16[64,768]{1,0:T(8,128)(2,1)S(1)} %add_convert_fusion.9), channel_id=1, source_target_pairs={{0,8},{4,12},{8,0},{12,4},{16,24},{20,28},{24,16},{28,20},{1,9},{5... | collective-permute-start | bytes 294920 | tf_op jit(solution)/shard_map/ppermute | solution.py:55
  183.8 9.8 %collective-permute-start.47 = (bf16[64,768]{1,0:T(8,128)(2,1)S(1)}, bf16[64,768]{1,0:T(8,128)(2,1)S(1)}, u32[]{:S(2)}, u32[]{:S(2)}) collective-permute-start(bf16[64,768]{1,0:T(8,128)(2,1)S(1)} %pad_maximum_fusion.5.refs_2_), channel_id=1, source_target_pairs={{0,24},{4,28},{8,16},{12,20},{16,8},{20,12},{24,0},{28,4},{1,25},{... | collective-permute-start | bytes 294920 | tf_op jit(solution)/shard_map/ppermute | solution.py:55
  185.2 26.0 %collective-permute-start.54 = (bf16[384,768]{1,0:T(8,128)(2,1)S(1)}, bf16[384,768]{1,0:T(8,128)(2,1)S(1)}, u32[]{:S(2)}, u32[]{:S(2)}) collective-permute-start(bf16[384,768]{1,0:T(8,128)(2,1)S(1)} %pad_maximum_fusion.1.refs_0_), channel_id=1, source_target_pairs={{0,4},{4,0},{8,12},{12,8},{16,20},{20,16},{24,28},{28,24},{1,5},{5... | collective-permute-start | bytes 1769480 | tf_op jit(solution)/shard_map/ppermute | solution.py:55
  186.0 23.5 %collective-permute-start.52 = (bf16[384,768]{1,0:T(8,128)(2,1)S(1)}, bf16[384,768]{1,0:T(8,128)(2,1)S(1)}, u32[]{:S(2)}, u32[]{:S(2)}) collective-permute-start(bf16[384,768]{1,0:T(8,128)(2,1)S(1)} %pad_maximum_fusion.refs_0_), channel_id=1, source_target_pairs={{0,8},{4,12},{8,0},{12,4},{16,24},{20,28},{24,16},{28,20},{1,9},{5... | collective-permute-start | bytes 1769480 | tf_op jit(solution)/shard_map/ppermute | solution.py:55
  190.8 16.9 %collective-permute-start.39 = (bf16[256,768]{1,0:T(8,128)(2,1)S(1)}, bf16[256,768]{1,0:T(8,128)(2,1)S(1)}, u32[]{:S(2)}, u32[]{:S(2)}) collective-permute-start(bf16[256,768]{1,0:T(8,128)(2,1)S(1)} %pad_maximum_fusion.2.refs_0_), channel_id=1, source_target_pairs={{0,4},{4,0},{8,12},{12,8},{16,20},{20,16},{24,28},{28,24},{1,5},{5... | collective-permute-start | bytes 1179656 | tf_op jit(solution)/shard_map/ppermute | solution.py:55
  193.6 9.7 %collective-permute-start.46 = (bf16[64,768]{1,0:T(8,128)(2,1)S(1)}, bf16[64,768]{1,0:T(8,128)(2,1)S(1)}, u32[]{:S(2)}, u32[]{:S(2)}) collective-permute-start(bf16[64,768]{1,0:T(8,128)(2,1)S(1)} %pad_maximum_fusion.5.refs_2_), channel_id=1, source_target_pairs={{0,16},{4,20},{8,24},{12,28},{16,0},{20,4},{24,8},{28,12},{1,17},{... | collective-permute-start | bytes 294920 | tf_op jit(solution)/shard_map/ppermute | solution.py:55
  193.6 13.7 %collective-permute-start.45 = (bf16[64,768]{1,0:T(8,128)(2,1)S(1)}, bf16[64,768]{1,0:T(8,128)(2,1)S(1)}, u32[]{:S(2)}, u32[]{:S(2)}) collective-permute-start(bf16[64,768]{1,0:T(8,128)(2,1)S(1)} %pad_maximum_fusion.5.refs_2_), channel_id=1, source_target_pairs={{0,8},{4,12},{8,0},{12,4},{16,24},{20,28},{24,16},{28,20},{1,9},{5... | collective-permute-start | bytes 294920 | tf_op jit(solution)/shard_map/ppermute | solution.py:55
  (61 other events, 322.5 us)

commit v3 on v2

--- a/solution.py
+++ b/solution.py
@@ -55,25 +55,67 @@
     return lax.ppermute(value, axis, [(i, i ^ offset) for i in range(size)])
 
 
-def tree_sum(parts):
-    while len(parts) > 1:
-        parts = [parts[i] + parts[i + 1] for i in range(0, len(parts), 2)]
-    return parts[0]
+def add_kernel(count, cuts, *refs):
+    parts, outs = refs[:count], refs[count:]
+
+    def one(rows):
+        found = parts[0][rows, :].astype(F32)
+        for part in parts[1:]:
+            found = found + part[rows, :].astype(F32)
+        return found
+
+    for (first, last), out in zip(cuts, outs):
+        if (last - first) % STEP:
+            out[...] = one(slice(first, last)).astype(out.dtype)
+        else:
+
+            def body(i, _, first=first, out=out):
+                out[rows_at(i), :] = one(pl.ds(pl.multiple_of(first + i * STEP, STEP), STEP)).astype(out.dtype)
+
+            each_rows(last - first, body)
+
+
+def add(parts, *cuts):
+    columns = parts[0].shape[1]
+    outs = tuple(shape(last - first, columns, kind=kind) for first, last, kind in cuts)
+    return list(kernel(functools.partial(add_kernel, len(parts), [cut[:2] for cut in cuts]), outs, [], parts))
 
 
 def sum_small(value, axis, size):
     stride = 1
     while stride < size:
-        value = value + xor_send(value, axis, size, stride)
+        value = add([value, xor_send(value, axis, size, stride)], (0, value.shape[0], F32))[0]
         stride *= 2
     return value
 
 
-def gather_width(shard, width, order):
-    far = xor_send(shard, "width", width, 2)
-    near = xor_send(shard, "width", width, 1)
-    both = xor_send(after(far, *order) if order else far, "width", width, 1)
-    return [shard, near, far, both]
+def join_kernel(*refs):
+    out, start = refs[-1], 0
+    for piece in refs[:-1]:
+        out[start : start + piece.shape[0]] = piece[...]
+        start += piece.shape[0]
+
+
+def join(pieces):
+    rows = sum(piece.shape[0] for piece in pieces)
+    return kernel(join_kernel, shape(rows, pieces[0].shape[1], kind=pieces[0].dtype), [], pieces)
+
+
+def count_kernel(*refs):
+    refs[-1][0] = sum((ref[0] for ref in refs[1:-1]), refs[0][0])
+
+
+def sum_counts(counts, row_devices):
+    for stride, radix in reversed(digits_of(row_devices, "near")):
+        parts = [counts] + [xor_send(counts, "rows", row_devices, e * stride) for e in range(1, radix)]
+        counts = pl.pallas_call(
+            count_kernel,
+            out_shape=jax.ShapeDtypeStruct((1,), jnp.int32),
+            in_specs=[pl.BlockSpec(memory_space=pltpu.SMEM)] * len(parts),
+            out_specs=pl.BlockSpec(memory_space=pltpu.SMEM),
+            compiler_params=pltpu.CompilerParams(vmem_limit_bytes=1024 * 1024),
+        )(*parts)
+    return counts
 
 
 def chunks_of(count, rows):
@@ -165,18 +207,16 @@
 
 
 def add_stage(stream, parts, received, stage):
-    value = tree_sum([part.astype(F32) for part in [parts[0]] + received]).astype(BF16)
-    if stage + 1 == len(stream.digits):
-        return [value]
-    radix = stream.digits[stage + 1][1]
-    size = value.shape[0] // radix
-    return [value[e * size : (e + 1) * size] for e in range(radix)]
+    rows = parts[0].shape[0]
+    radix = 1 if stage + 1 == len(stream.digits) else stream.digits[stage + 1][1]
+    size = rows // radix
+    return add([parts[0]] + received, *((e * size, (e + 1) * size, BF16) for e in range(radix)))
 
 
 def sum_rest(stream, value):
     stride = stream.count
     while stride < stream.row_devices:
-        value = (value.astype(F32) + stream.send(value, stride).astype(F32)).astype(BF16)
+        value = add([value, stream.send(value, stride)], (0, value.shape[0], BF16))[0]
         stride *= 2
     return value
 
@@ -216,9 +256,18 @@
     return kernel(functools.partial(place_kernel, streams, bounds), outs, [me], pieces, flops=start * columns)
 
 
-def history_kernel(mix_ref, history_ref, cot_ref, live_ref, running_ref, d_history_ref, d_mix_ref):
+def live_row(all_tokens, counts_ref, total_ref, width, first):
+    scale = jnp.full((1, width), all_tokens, F32) / (jnp.zeros((1, width), F32) + total_ref[0].astype(F32))
+    place = lax.broadcasted_iota(jnp.int32, (1, width), 1) + first
+    return jnp.where(place < counts_ref[0], scale, 0.0)
+
+
+def history_kernel(
+    all_tokens, mix_ref, counts_ref, total_ref, history_ref, cot_ref, running_ref, d_history_ref, d_mix_ref
+):
     layers = history_ref.shape[0]
     features, tokens = cot_ref.shape
+    live = live_row(all_tokens, counts_ref, total_ref, tokens, 0)
 
     @pl.when(pl.program_id(0) == 0)
     def _():
@@ -226,7 +275,7 @@
 
     for i in range(features // STEP):
         rows = slice(i * STEP, (i + 1) * STEP)
-        grad = cot_ref[rows].astype(F32) * live_ref[...]
+        grad = cot_ref[rows].astype(F32) * live
         running = jnp.zeros_like(grad)
         for j in range(layers):
             layer = history_ref[j, rows].astype(F32)
@@ -239,11 +288,11 @@
         running_ref[rows] = running
 
 
-def mix_history(mix_weights, history, cotangent, live):
+def mix_history(all_tokens, mix_weights, counts, total, history, cotangent):
     layers, features, tokens = history.shape
     block = 32
     return pl.pallas_call(
-        history_kernel,
+        functools.partial(history_kernel, all_tokens),
         grid=(features // block,),
         out_shape=(
             shape(features, tokens),
@@ -252,9 +301,10 @@
         ),
         in_specs=[
             pl.BlockSpec(memory_space=pltpu.SMEM),
+            pl.BlockSpec(memory_space=pltpu.SMEM),
+            pl.BlockSpec(memory_space=pltpu.SMEM),
             pl.BlockSpec((layers, block, tokens), lambda i: (0, i, 0)),
             pl.BlockSpec((block, tokens), lambda i: (i, 0)),
-            pl.BlockSpec((1, tokens), lambda i: (0, 0)),
         ],
         out_specs=(
             pl.BlockSpec((block, tokens), lambda i: (i, 0)),
@@ -263,7 +313,7 @@
         ),
         compiler_params=pltpu.CompilerParams(vmem_limit_bytes=12 * 1024 * 1024),
         cost_estimate=pl.CostEstimate(flops=1024, bytes_accessed=1024, transcendentals=0),
-    )(mix_weights, history, cotangent, live)
+    )(mix_weights, counts, total, history, cotangent)
 
 
 def spread_of(load, count, width):
@@ -277,16 +327,16 @@
     return mean, lax.rsqrt(column_sum(each_rows(count, squares, zero)) / count + EPSILON)
 
 
-def attention_kernel(
-    at_ref, x0, x1, x2, x3, norms, cosine, sine, w_qkv, w_out,
-    send, keep, x_half, x_all, normed, stats, qkv, heads_out, probs, project, scores,
+def project_kernel(
+    at_ref, x0, x1, x2, x3, n0, n1, n2, n3, cosine, sine, w_qkv, x_all, norms, normed, stats, qkv, project
 ):
     at = at_ref[0]
     part, tokens = x0.shape
-    model = w_out.shape[1]
-    half = tokens // 2
-    for e, piece in enumerate((x0, x1, x2, x3)):
-        x_all[pl.ds(pl.multiple_of((at ^ e) * part, 64), part), :] = piece[...]
+    model = w_qkv.shape[1]
+    for e, (piece, norm) in enumerate(((x0, n0), (x1, n1), (x2, n2), (x3, n3))):
+        rows = pl.ds(pl.multiple_of((at ^ e) * part, 64), part)
+        x_all[rows, :] = piece[...]
+        norms[rows, :] = norm[...].T[:part]
     mean, scale = spread_of(lambda i: x_all[rows_at(i), :].astype(F32), model, tokens)
     stats[0:1] = mean
     stats[1:2] = scale
@@ -306,6 +356,12 @@
             qkv[start : start + width] = (front * cos - back * sin).astype(BF16)
             qkv[start + width : start + HEAD_DIM] = (back * cos + front * sin).astype(BF16)
     qkv[2 * part :] = project[2 * part :].astype(BF16)
+
+
+def attention_kernel(at_ref, qkv, w_out, x_all, send, keep, x_half, heads_out, probs, scores):
+    at = at_ref[0]
+    part, tokens = heads_out.shape
+    half = tokens // 2
     for h in range(part // HEAD_DIM):
         head = slice(h * HEAD_DIM, (h + 1) * HEAD_DIM)
         for t in range(2):
@@ -349,7 +405,9 @@
     x_half[...] = x_all[:, pl.ds(own, half)]
 
 
-def output_gradient_kernel(at_ref, self_ref, c0, c1, c2, c3, live, w_down, g_out, d_active, cot_half, cot_all):
+def output_gradient_kernel(
+    all_tokens, at_ref, self_ref, counts_ref, total_ref, c0, c1, c2, c3, w_down, g_out, d_active, cot_half, cot_all
+):
     at = at_ref[0]
     part, tokens = c0.shape
     half = tokens // 2
@@ -357,7 +415,7 @@
         cot_all[pl.ds(pl.multiple_of((at ^ e) * part, 64), part), :] = piece[...]
     for place, side in enumerate((at % 2, 1 - at % 2)):
         now = pl.ds(pl.multiple_of(side * half, half), half)
-        factor = live[:, now]
+        factor = live_row(all_tokens, counts_ref, total_ref, half, side * half)
 
         def scale(i, _, now=now, factor=factor, place=place):
             rows = rows_at(i)
@@ -431,8 +489,17 @@
     store_blocks(at, total, part, send, keep)
 
 
+def fold_lanes(value):
+    return sum(value[:, k : k + 128] for k in range(0, value.shape[1], 128))
+
+
+def as_row(columns):
+    return column_sum(columns[...].T)
+
+
 def middle_gradient_kernel(
-    at_ref, self_ref, chip, received, middle, stats, cot_half, live, norms, d_middle, g_mid, d_gain, d_bias, d_normed
+    all_tokens, at_ref, self_ref, counts_ref, total_ref, chip, received, middle, stats, cot_half, norms,
+    d_middle, g_mid, gains, d_normed, gain_sums, bias_sums,
 ):
     model, half = chip.shape
     mean, scale = stats[0:1], stats[1:2]
@@ -444,14 +511,13 @@
         d_normed[rows, :] = grad
         xhat = (middle[rows, :] - mean) * scale
         both = grad * xhat
-        d_gain[rows, :] = jnp.sum(both, axis=1, keepdims=True)
-        d_bias[rows, :] = jnp.sum(grad, axis=1, keepdims=True)
+        gain_sums[rows, :] = fold_lanes(both)
+        bias_sums[rows, :] = fold_lanes(grad)
         gain = norms[rows, 2:3]
         return acc[0] + grad * gain, acc[1] + both * gain
 
     first, second = (column_sum(v) / model for v in each_rows(model, sums, (zero, zero)))
-    own = pl.ds(pl.multiple_of((at_ref[0] % 2) * half, half), half)
-    factor = self_ref[0] * live[:, own]
+    factor = self_ref[0] * live_row(all_tokens, counts_ref, total_ref, half, (at_ref[0] % 2) * half)
 
     def finish(i, _):
         rows = rows_at(i)
@@ -463,6 +529,8 @@
         g_mid[rows, :] = found.astype(BF16)
 
     each_rows(model, finish)
+    gains[0:1] = as_row(gain_sums)
+    gains[1:2] = as_row(bias_sums)
 
 
 def attention_gradient_kernel(
@@ -517,7 +585,7 @@
 
 
 def input_gradient_kernel(
-    at_ref, d_project, w_qkv, x_all, stats, d_middle, norms, send, keep, sums, d_gain, d_bias, total
+    at_ref, d_project, w_qkv, x_all, stats, d_middle, norms, gains, mix, send, keep, sums, total, gain_sums, bias_sums
 ):
     at = at_ref[0]
     model, half = d_middle.shape
@@ -533,8 +601,8 @@
         grad = total[rows, :]
         xhat = (x_all[rows, :].astype(F32) - mean) * scale
         both = grad * xhat
-        d_gain[rows, :] = jnp.sum(both, axis=1, keepdims=True)
-        d_bias[rows, :] = jnp.sum(grad, axis=1, keepdims=True)
+        gain_sums[rows, :] = fold_lanes(both)
+        bias_sums[rows, :] = fold_lanes(grad)
         gain = norms[rows, 0:1]
         lifted = grad * gain
         total[rows, :] = lifted * scale
@@ -542,9 +610,47 @@
         return acc[0] + lifted, acc[1] + both * gain
 
     first, second = each_rows(model, body, (zero, zero))
-    sums[0:1] = column_sum(first) / model
-    sums[1:2] = column_sum(second) / model
     store_blocks(at, total, part, send, keep)
+    sums[...] = jnp.zeros_like(sums)
+    sums[0:1] = as_row(gain_sums)
+    sums[1:2] = as_row(bias_sums)
+    sums[2:4] = 0.5 * gains[...]
+    sums[4:5, :tokens] = column_sum(first) / model
+    sums[5:6, :tokens] = column_sum(second) / model
+    sums[6:7, :128] = mix[...]
+
+
+def mixed_kernel(
+    all_tokens, self_ref, counts_ref, total_ref, chip, received, running, cotangent, d_mix, mixed, row, table
+):
+    layers = d_mix.shape[0]
+    part, tokens = chip.shape
+    live = live_row(all_tokens, counts_ref, total_ref, tokens, 0)
+
+    def body(i, acc):
+        rows = rows_at(i)
+        output = chip[rows, :] + received[rows, :].astype(F32)
+        mixed[rows, :] = (self_ref[0] * output + running[rows, :]).astype(BF16)
+        return acc + fold_lanes(cotangent[rows, :].astype(F32) * live * output)
+
+    found = each_rows(part, body, jnp.zeros((STEP, 128), F32))
+    table[...] = jnp.zeros_like(table)
+    table[:layers] = jnp.sum(d_mix[...], axis=1)
+    table[layers : layers + 1] = column_sum(found)
+    row[...] = as_row(table)
+
+
+def d_input_kernel(chip, received, x_in, stats, sums, d_input):
+    part, tokens = chip.shape
+    mean, scale = stats[0:1], stats[1:2]
+    first, second = sums[4:5, :tokens], sums[5:6, :tokens]
+
+    def body(i, _):
+        rows = rows_at(i)
+        xhat = (x_in[rows, :].astype(F32) - mean) * scale
+        d_input[rows, :] = chip[rows, :] + received[rows, :].astype(F32) - scale * (first + xhat * second)
+
+    each_rows(part, body)
 
 
 def local(
@@ -571,68 +677,71 @@
     hidden_units = w_up.shape[1]
     half = tokens // 2
     layers = mix_weights.shape[0]
+    all_tokens = float(tokens * row_devices)
     at_width = lax.axis_index("width")
     at = at_width.astype(jnp.int32)[None]
     me = lax.axis_index("rows").astype(jnp.int32)[None]
-    to_width = lambda value, offset: xor_send(value, "width", width, offset)
-    w_qkv = w_qkv.reshape(3 * part, model)
-
-    x_pieces = gather_width(x_in, width, ())
-    norms = jnp.stack([first_norm_gain, first_norm_bias, second_norm_gain, second_norm_bias])
-    norms = after(norms, x_in)
-    near = to_width(norms, 1)
-    pair = jnp.where(at_width % 2 == 1, jnp.concatenate([near, norms], 1), jnp.concatenate([norms, near], 1))
-    far = to_width(pair, 2)
-    norms = jnp.where(at_width // 2 == 1, jnp.concatenate([far, pair], 1), jnp.concatenate([pair, far], 1)).T
+    norms = jnp.pad(
+        jnp.stack([first_norm_gain, first_norm_bias, second_norm_gain, second_norm_bias]), ((0, 124), (0, -part % 128))
+    )
     inverse = 1.0 / 10000.0 ** (jnp.arange(HEAD_DIM // 2, dtype=F32) * 2.0 / HEAD_DIM)
     angles = positions[None, :].astype(F32) * inverse[:, None]
     cosine, sine = jnp.cos(angles), jnp.sin(angles)
-    live_total = counts
-    for stride, radix in reversed(digits_of(row_devices, "near")):
-        live_total = live_total + sum(
-            xor_send(live_total, "rows", row_devices, e * stride) for e in range(1, radix)
-        )
-    loss_scale = jnp.float32(tokens * row_devices) / live_total[0].astype(F32)
-    live = jnp.where(jnp.arange(tokens) < counts[0], loss_scale, 0.0)[None, :]
-
-    send, keep, x_half, x_all, normed_one, stats_one, qkv, heads_out, probs = kernel(
+    to_width = lambda value, offset: xor_send(value, "width", width, offset)
+    w_qkv = w_qkv.reshape(3 * part, model)
+    x_in, cotangent, counts = after((x_in, cotangent, counts), at, me)
+
+    x_far, x_near = to_width(x_in, 2), to_width(x_in, 1)
+    cot_far, cot_near = to_width(cotangent, 2), to_width(cotangent, 1)
+    norms = [norms[:8]] + [to_width(norms[:8], e) for e in range(1, width)]
+    total = sum_counts(counts, row_devices)
+    x_both, cot_both = to_width(x_far, 1), to_width(cot_far, 1)
+
+    x_all, norms, normed_one, stats_one, qkv = kernel(
+        project_kernel,
+        (
+            shape(model, tokens, kind=BF16),
+            shape(model, 8),
+            shape(model, tokens, kind=BF16),
+            shape(2, tokens),
+            shape(3 * part, tokens, kind=BF16),
+        ),
+        [at],
+        [x_in, x_near, x_far, x_both, *norms, cosine, sine, w_qkv],
+        [pltpu.VMEM((3 * part, tokens), F32)],
+    )
+    send, keep, x_half, heads_out, probs = kernel(
         attention_kernel,
         (
             shape(model, half, kind=BF16),
             shape(model, half),
             shape(model, half, kind=BF16),
-            shape(model, tokens, kind=BF16),
-            shape(model, tokens, kind=BF16),
-            shape(2, tokens),
-            shape(3 * part, tokens, kind=BF16),
             shape(part, tokens, kind=BF16),
             shape(part // HEAD_DIM, tokens, tokens, kind=BF16),
         ),
         [at],
-        [*x_pieces, after(norms, live), cosine, sine, w_qkv, w_out],
-        [pltpu.VMEM((3 * part, tokens), F32), pltpu.VMEM((tokens, half), F32)],
-        4 * 10**9,
-    )
-    chip = keep + to_width(send, 1).astype(F32)
-    received = to_width(chip.astype(BF16), 2)
-    cot_pieces = gather_width(after(cotangent, *x_pieces), width, (send,))
-
+        [after(qkv, cot_far, total), w_out, x_all],
+        [pltpu.VMEM((tokens, half), F32)],
+    )
+    chip, send = add([keep, to_width(send, 1)], (0, model, F32), (0, model, BF16))
+    received = to_width(send, 2)
+
+    running, d_history, d_mix = mix_history(
+        all_tokens, mix_weights, counts, total, history, after(cotangent, chip)
+    )
     g_out, d_active, cot_half = kernel(
-        output_gradient_kernel,
+        functools.partial(output_gradient_kernel, all_tokens),
         (shape(model, tokens, kind=BF16), shape(hidden_units, tokens), shape(model, half, kind=BF16)),
-        [at, self_weight],
-        [*cot_pieces, after(live, chip), w_down],
+        [at, self_weight, counts, total],
+        [cotangent, cot_near, cot_far, cot_both, after(w_down, running)],
         [pltpu.VMEM((model, tokens), BF16)],
-        10**9,
-    )
-    running, d_history, d_mix = mix_history(mix_weights, history, cotangent, after(live, d_active))
+    )
 
     middle, stats_two, normed_own = kernel(
         middle_kernel,
         (shape(model, half), shape(2, half), shape(model, half, kind=BF16)),
         [],
-        [x_half, chip, after(received, running), norms],
-        flops=10**8,
+        [x_half, chip, after(received, g_out), norms],
     )
     normed_two, active, d_hidden, send, keep = kernel(
         feed_forward_kernel,
@@ -646,15 +755,14 @@
         [],
         [normed_own, to_width(normed_own, 1), w_up, d_active],
         [pltpu.VMEM((hidden_units, tokens), F32)],
-        2 * 10**9,
     )
 
     down = Stream(row_devices, 0, hidden_units, "halving")
     up = Stream(row_devices, 0, model, "crossed")
     down_parts = weight_gradient(me, [down], active, after(g_out, send))[0]
     down_got = start_stage(down, down_parts, 0)
-    chip = keep + after(to_width(send, 1), *down_parts).astype(F32)
-    received = to_width(chip.astype(BF16), 2)
+    chip, send = add([keep, after(to_width(send, 1), *down_parts)], (0, model, F32), (0, model, BF16))
+    received = to_width(send, 2)
     up_parts = weight_gradient(me, [up], normed_two, after(d_hidden, chip))[0]
     up_got = start_stage(up, up_parts, 0)
 
@@ -665,29 +773,26 @@
         [at],
         [active, w_down, after(middle, *up_parts)],
         [pltpu.VMEM((model, tokens), F32)],
-        10**9,
-    )
-    out_chip = out_keep + to_width(out_send, 1).astype(F32)
-    output = out_chip[:part] + to_width(out_chip[part:].astype(BF16), 2).astype(F32)
-
-    d_middle, g_own, d_gain_two, d_bias_two = kernel(
-        middle_gradient_kernel,
-        (shape(model, half), shape(model, half, kind=BF16), shape(model, 1), shape(model, 1)),
-        [at, self_weight],
-        [chip, after(received, out_chip), middle, stats_two, cot_half, live, norms],
-        [pltpu.VMEM((model, half), F32)],
-        10**8,
+    )
+    out_near = to_width(out_send, 1)
+
+    d_middle, g_own, gains_two = kernel(
+        functools.partial(middle_gradient_kernel, all_tokens),
+        (shape(model, half), shape(model, half, kind=BF16), shape(2, model)),
+        [at, self_weight, counts, total],
+        [chip, after(received, out_keep), middle, stats_two, cot_half, norms],
+        [pltpu.VMEM((model, half), F32), pltpu.VMEM((model, 128), F32), pltpu.VMEM((model, 128), F32)],
     )
     g_other = to_width(g_own, 1)
     down_parts = add_stage(down, down_parts, [after(v, g_own) for v in down_got], 0)
     down_got = start_stage(down, down_parts, 1)
-    up_parts = add_stage(up, up_parts, [after(v, g_own) for v in up_got], 0)
+    up_parts = add_stage(up, up_parts, [after(v, down_parts[0]) for v in up_got], 0)
     up_got = start_stage(up, up_parts, 1)
     d_project, g_mid = kernel(
         attention_gradient_kernel,
         (shape(3 * part, tokens, kind=BF16), shape(model, tokens, kind=BF16)),
         [at],
-        [g_own, after(g_other, *down_parts, *up_parts), w_out, qkv, probs, cosine, sine],
+        [g_own, after(g_other, *up_parts), w_out, qkv, probs, cosine, sine],
         [
             pltpu.VMEM((part, tokens), BF16),
             pltpu.VMEM((tokens, half), BF16),
@@ -696,7 +801,6 @@
             pltpu.VMEM((HEAD_DIM, tokens), F32),
             pltpu.VMEM((HEAD_DIM, tokens), F32),
         ],
-        4 * 10**9,
     )
     tail_rows = 4 * part
     tail = [
@@ -706,64 +810,70 @@
     tail_parts = weight_gradient(me, tail, d_project, normed_one, heads_out, g_mid)
     tail_got = [start_stage(s, p, 0) for s, p in zip(tail, tail_parts)]
 
-    in_send, in_keep, sums, d_gain_one, d_bias_one = kernel(
+    out_chip, out_send = add(
+        [out_keep, after(out_near, *tail_parts[0])], (0, part, F32), (part, 2 * part, BF16)
+    )
+    out_far = to_width(out_send, 2)
+    down_parts = add_stage(down, down_parts, [after(v, out_send) for v in down_got], 1)
+    down_got = start_stage(down, down_parts, 2)
+    up_parts = add_stage(up, up_parts, [after(v, down_parts[0]) for v in up_got], 1)
+    up_got = start_stage(up, up_parts, 2)
+    mixed, mix_row = kernel(
+        functools.partial(mixed_kernel, all_tokens),
+        (shape(part, tokens, kind=BF16), shape(1, 128)),
+        [self_weight, counts, total],
+        [out_chip, after(out_far, up_parts[0]), running, cotangent, d_mix],
+        [pltpu.VMEM((128, 128), F32)],
+    )
+    in_send, in_keep, sums = kernel(
         input_gradient_kernel,
-        blocks + (shape(2, tokens), shape(model, 1), shape(model, 1)),
+        blocks + (shape(8, model),),
         [at],
-        [after(d_project, *tail_parts[0]), w_qkv, x_all, stats_one, d_middle, norms],
-        [pltpu.VMEM((model, tokens), F32)],
-        10**9,
+        [d_project, w_qkv, x_all, stats_one, d_middle, norms, gains_two, mix_row],
+        [pltpu.VMEM((model, tokens), F32), pltpu.VMEM((model, 128), F32), pltpu.VMEM((model, 128), F32)],
     )
     in_near = to_width(in_send, 1)
-
-    down_parts = add_stage(down, down_parts, [after(v, in_send) for v in down_got], 1)
-    down_got = start_stage(down, down_parts, 2)
-    up_parts = add_stage(up, up_parts, [after(v, in_send) for v in up_got], 1)
-    up_got = start_stage(up, up_parts, 2)
-
-    cot_wide = cotangent.astype(F32) * live
-    mixed = (self_weight[0] * output + running).astype(BF16)
-    d_mix = jnp.concatenate([jnp.sum(d_mix, axis=(1, 2)), jnp.sum(cot_wide * output)[None]])
-    flat = jnp.concatenate(
-        [d_gain_one[:, 0], d_bias_one[:, 0], 0.5 * d_gain_two[:, 0], 0.5 * d_bias_two[:, 0], sums[0], sums[1], d_mix]
-    )
-    flat = sum_small(flat, "width", width)
-    in_chip = in_keep + in_near.astype(F32)
-    in_total = in_chip[:part] + to_width(in_chip[part:].astype(BF16), 2).astype(F32)
-    scale_one = stats_one[1:2]
-    own_xhat = (x_in.astype(F32) - stats_one[0:1]) * scale_one
-    d_input = in_total - scale_one * (
-        flat[4 * model : 4 * model + tokens] + own_xhat * flat[4 * model + tokens : 4 * model + 2 * tokens]
-    )
-    ends = [lax.dynamic_slice_in_dim(flat, i * model + at_width * part, part) for i in range(4)]
-    small = sum_small(jnp.concatenate([flat[4 * model + 2 * tokens :]] + ends), "rows", row_devices)
-    ends = [small[layers + 1 + i * part : layers + 1 + (i + 1) * part] for i in range(4)]
-
-    tail_parts = [add_stage(s, p, g, 0) for s, p, g in zip(tail, tail_parts, tail_got)]
+    tail_parts = [
+        add_stage(s, p, [after(v, in_send) for v in g], 0) for s, p, g in zip(tail, tail_parts, tail_got)
+    ]
     tail_got = [start_stage(s, p, 1) for s, p in zip(tail, tail_parts)]
-    down_value = sum_rest(down, add_stage(down, down_parts, [after(v, *tail_parts[0]) for v in down_got], 2)[0])
-    up_value = sum_rest(up, add_stage(up, up_parts, [after(v, *tail_parts[0]) for v in up_got], 2)[0])
+    in_chip, in_send = add(
+        [in_keep, after(in_near, *tail_parts[0], *tail_parts[1])], (0, part, F32), (part, 2 * part, BF16)
+    )
+    in_far = to_width(in_send, 2)
+    sums = sum_small(after(sums, in_send), "width", width)
+    down_value = sum_rest(down, add_stage(down, down_parts, [after(v, in_send) for v in down_got], 2)[0])
+    up_value = sum_rest(up, add_stage(up, up_parts, [after(v, down_value) for v in up_got], 2)[0])
     for stage in range(len(down.digits) - 1, 0, -1):
-        down_value = jnp.concatenate(gather_stage(down, down_value, stage))
-        up_value = jnp.concatenate(gather_stage(up, up_value, stage))
+        down_value = join(gather_stage(down, down_value, stage))
+        up_value = join(gather_stage(up, up_value, stage))
         if stage == len(down.digits) - 1:
+            d_input = kernel(
+                d_input_kernel,
+                shape(part, tokens),
+                [],
+                [in_chip, after(in_far, down_value), x_in, stats_one, sums],
+            )
             tail_values = [
-                sum_rest(s, add_stage(s, p, [after(v, down_value) for v in g], 1)[0])
+                sum_rest(s, add_stage(s, p, [after(v, d_input) for v in g], 1)[0])
                 for s, p, g in zip(tail, tail_parts, tail_got)
             ]
-            tail_values = [jnp.concatenate(gather_stage(s, v, 1)) for s, v in zip(tail, tail_values)]
+            tail_values = [join(gather_stage(s, v, 1)) for s, v in zip(tail, tail_values)]
+            small = sum_small(after(sums, d_input), "rows", row_devices)
     down_pieces = gather_stage(down, down_value, 0)
     up_pieces = gather_stage(up, up_value, 0)
     tail_pieces = [piece for s, v in zip(tail, tail_values) for piece in gather_stage(s, v, 0)]
     d_w_down = place(me, [down], down_pieces, (hidden_units,))[0]
     d_w_up = place(me, [up], up_pieces, (model,))[0]
     d_w_qkv, d_w_out = place(me, tail, tail_pieces, (3 * part, part))
+    small = after(small, d_w_qkv)
+    ends = [lax.dynamic_slice(small, (i, at_width * part), (1, part))[0] for i in range(4)]
     return (
         mixed,
         d_input,
         d_history,
-        small[:layers],
-        small[layers : layers + 1],
+        small[6, :layers],
+        small[6, layers : layers + 1],
         ends[0],
         ends[1],
         d_w_qkv.reshape(3, part, model),

time: 213 us -> 202 us (0.948)
  starting transfers between devices: 53.7 us -> 69.1 us
  other arithmetic: 15 us -> 1.74 us
  local copies, waits for them, and re-layouts: 18.6 us -> 9.22 us
  waiting for transfers between devices: 80.6 us -> 73.2 us
  Pallas kernels: 39.6 us -> 45.6 us
  between operations: 5.26 us -> 2.46 us
    ppermute x55 -> x56, starting transfers between devices: 53.7 us -> 69.1 us  [xor_send(): return lax.ppermute(value, axis, [(i, i ^ offset) for i in range(size)])]
    ppermute x55 -> x56, waiting for transfers between devices: 80.6 us -> 73.2 us  [xor_send(): return lax.ppermute(value, axis, [(i, i ^ offset) for i in range(size)])]
    convert_element_type x12 -> x0, other arithmetic: 5.2 us -> none  [the longest x10 2.81 us: add_stage(): tree_sum([part.astype(F32) for part in [parts[0]] + received]).astype(BF16)]
    pallas_call x1 -> x3, Pallas kernels: 5.37 us -> 10.3 us  [the longest x1 6.14 us: mix_history(): pl.pallas_call(functools.partial(history_kernel, all_tokens), grid=(featu...]
    unnamed x108 -> x28, local copies, waits for them, and re-layouts: 12.4 us -> 7.48 us
    slice x15 -> x1, local copies, waits for them, and re-layouts: 3.43 us -> 0.58 us  [local(): small[6, layers:layers + 1]]
    concatenate x4 -> x0, local copies, waits for them, and re-layouts: 2.69 us -> none  [the longest x1 0.94 us: local(): jnp.concatenate([pair, far], 1)]
    reduce_sum x2 -> x0, other arithmetic: 2.62 us -> none  [the longest x1 1.41 us: local(): jnp.sum(cot_wide * output)[None]]
  transfers between devices with their start and end apart: 55 -> 56, of which waited for: 22 -> 24; matrix products, arithmetic and copies ran while one was open for 8% -> 2% of each run, Pallas kernels for 7% -> 17%
where the time goes in v3:
time: 202 us; the launch traced here: 201 us
  waiting for transfers between devices  73.2 us (36%)
  starting transfers between devices  69.1 us (34%)
  Pallas kernels  45.6 us (23%)
  local copies, waits for them, and re-layouts  9.22 us (5%)
  between operations  2.46 us (1%)
    ppermute x56, waiting for transfers between devices, xor_send(): return lax.ppermute(value, axis, [(i, i ^ offset) for i in range(size)])  73.2 us
    ppermute x56, starting transfers between devices, xor_send(): return lax.ppermute(value, axis, [(i, i ^ offset) for i in range(size)])  69.1 us
    pallas_call x42, Pallas kernels, kernel(): pl.pallas_call(body, out_shape=outs, in_specs=[pl.BlockSpec(memory_space=...  35.3 us
    unnamed x28, local copies, waits for them, and re-layouts  7.48 us
    pallas_call x1, Pallas kernels, mix_history(): pl.pallas_call(functools.partial(history_kernel, all_tokens), grid=(featu...  6.14 us
    pallas_call x2, Pallas kernels, sum_counts(): pl.pallas_call(count_kernel, out_shape=jax.ShapeDtypeStruct((1,), jnp.int...  4.13 us
  transfers between devices with their start and end apart: 56, of which 24 were waited for; matrix products, arithmetic and copies ran while one was open for 2% of the time, Pallas kernels for 17%

profile of v3, /device:TPU:0, one launch (start us, length us, event | category | flops | bytes accessed | tf_op | source)
XLA Modules:
  0.0 201.3 jit_solution(16328382358498470658)
XLA Ops:
  0.7 3.1 %collective-permute-start = (s32[1]{0:T(128)}, s32[1]{0:T(128)}, u32[]{:S(2)}, u32[]{:S(2)}) collective-permute-start(s32[1]{0:T(128)} %param.18), channel_id=1, source_target_pairs={{0,8},{4,12},{8,0},{12,4},{16,24},{20,28},{24,16},{28,20},{1,9},{5... | collective-permute-start | bytes 20 | tf_op jit(solution)/shard_map/ppermute | solution.py:55
  3.7 2.6 %collective-permute-start.1 = (s32[1]{0:T(128)}, s32[1]{0:T(128)}, u32[]{:S(2)}, u32[]{:S(2)}) collective-permute-start(s32[1]{0:T(128)} %param.18), channel_id=1, source_target_pairs={{0,16},{4,20},{8,24},{12,28},{16,0},{20,4},{24,8},{28,12},{1,17},{... | collective-permute-start | bytes 20 | tf_op jit(solution)/shard_map/ppermute | solution.py:55
  6.3 1.7 collective-permute-start.5
  11.9 2.3 %shard_map.246.refs_0_ = s32[1]{0:T(128)} custom-call(s32[1]{0:T(128)S(6)} %copy.28.refs_0_.counts_ref, s32[1]{0:T(128)} %collective-permute-done.refs_1_, s32[1]{0:T(128)} %collective-permute-done.1.refs_2_, s32[1]{0:T(128)} %collective-permute-done.2.refs_3_), custom_call_target="tpu_custom_call" | custom-call | tf_op jit(solution)/shard_map/pallas_call | solution.py:111
  15.8 2.3 %collective-permute-done.3.refs_1_ = s32[1]{0:T(128)} collective-permute-done((s32[1]{0:T(128)}, s32[1]{0:T(128)}, u32[]{:S(2)}, u32[]{:S(2)}) %collective-permute-start.3) | collective-permute-done | bytes 36 | tf_op jit(solution)/shard_map/ppermute | solution.py:55
  20.3 1.8 shard_map.247.total_ref
  24.2 2.3 %shard_map.248 = (bf16[768,512]{1,0:T(8,128)(2,1)S(1)}, f32[768,8]{1,0:T(8,128)S(1)}, bf16[768,512]{1,0:T(8,128)(2,1)S(1)}, f32[2,512]{1,0:T(2,128)S(1)}, bf16[576,512]{1,0:T(8,128)(2,1)S(1)}) custom-call(s32[1]{0:T(128)} %bitcast.at_ref, bf16[192,512]{1,0:T(8,128)(2,1)S(1)} %copy-done.7, bf16[192,512]{1,0:T(8,128)(2,1)S(1)} %collective-permute-done.4.x1, ...), custom_call_target="tpu_custom_call" | custom-call | flops 1024 | bytes 1024 | tf_op jit(solution)/shard_map/pallas_call | solution.py:22
  26.6 4.7 %shard_map.249 = (bf16[768,256]{1,0:T(8,128)(2,1)S(1)}, f32[768,256]{1,0:T(8,128)S(1)}, bf16[768,256]{1,0:T(8,128)(2,1)S(1)}, bf16[192,512]{1,0:T(8,128)(2,1)S(1)}, bf16[3,512,512]{2,1,0:T(8,128)(2,1)S(1)}) custom-call(s32[1]{0:T(128)} %bitcast.at_ref, bf16[576,512]{1,0:T(8,128)(2,1)S(1)} %get-tuple-element.121.qkv, bf16[192,768]{1,0:T(8,128)(2,1)S(1)} %copy-done.6, ...), custom_call_target="tpu_custom_call" | custom-call | flops 1024 | bytes 1024 | tf_op jit(solution)/shard_map/pallas_call | solution.py:22
  33.4 1.6 collective-permute-start.12
  36.2 2.7 %copy-done = bf16[30,192,512]{2,1,0:T(8,128)(2,1)S(1)} copy-done((bf16[30,192,512]{2,1,0:T(8,128)(2,1)S(1)}, bf16[30,192,512]{2,1,0:T(8,128)(2,1)}, u32[]{:S(2)}) %copy-start) | copy-done | bytes 5898264
  38.9 6.1 %shard_map.251 = (f32[192,512]{1,0:T(8,128)S(1)}, bf16[30,192,512]{2,1,0:T(8,128)(2,1)}, f32[30,8,128]{2,1,0:T(8,128)S(1)}) custom-call(f32[30]{0:T(128)S(1)} %copy-done.13, s32[1]{0:T(128)S(6)} %copy.28.refs_0_.counts_ref, s32[1]{0:T(128)} %shard_map.247.total_ref, bf16[30,192,512]{2,1,0:T(8,128)(2,1)S(1)} %copy-done, bf16[192,512]{1,0:T(8,128)(2,1)S(1)} %copy-done.4), custom_call_target="tpu_custom_call" | custom-call | flops 1024 | bytes 1024 | tf_op jit(solution)/shard_map/pallas_call | solution.py:294
  45.0 1.9 shard_map.252
  48.6 1.7 collective-permute-done.15.other
  50.3 2.7 %shard_map.254 = (bf16[768,512]{1,0:T(8,128)(2,1)S(1)}, bf16[768,512]{1,0:T(8,128)(2,1)S(1)}, bf16[768,512]{1,0:T(8,128)(2,1)S(1)}, bf16[768,256]{1,0:T(8,128)(2,1)S(1)}, f32[768,256]{1,0:T(8,128)S(1)}) custom-call(bf16[768,256]{1,0:T(8,128)(2,1)S(1)} %get-tuple-element.134.own, bf16[768,256]{1,0:T(8,128)(2,1)S(1)} %collective-permute-done.15.other, ...), custom_call_target="tpu_custom_call" | custom-call | flops 1024 | bytes 1024 | tf_op jit(solution)/shard_map/pallas_call | solution.py:22
  59.0 7.3 %collective-permute-done.18.received = bf16[768,256]{1,0:T(8,128)(2,1)S(1)} collective-permute-done((bf16[768,256]{1,0:T(8,128)(2,1)S(1)}, bf16[768,256]{1,0:T(8,128)(2,1)S(1)}, u32[]{:S(2)}, u32[]{:S(2)}) %collective-permute-start.18) | collective-permute-done | bytes 393248 | tf_op jit(solution)/shard_map/ppermute | solution.py:55
  66.3 2.9 %shard_map.259 = (f32[768,256]{1,0:T(8,128)S(1)}, bf16[768,256]{1,0:T(8,128)(2,1)S(1)}, f32[2,768]{1,0:T(2,128)S(1)}) custom-call(s32[1]{0:T(128)} %bitcast.at_ref, f32[1]{0:T(128)S(6)} %copy.29.self_ref, s32[1]{0:T(128)S(6)} %copy.28.refs_0_.counts_ref, s32[1]{0:T(128)} %shard_map.247.total_ref, f32[768,256]{1,0:T(8,128)S(1)} %get-tuple-element.146.chip, ...), custom_call_target="tpu_custom_call" | custom-call | flops 1024 | bytes 1024 | tf_op jit(solution)/shard_map/pallas_call | solution.py:22
  71.0 2.0 collective-permute-done.20.refs_1_
  73.7 3.6 %shard_map.262 = (bf16[576,512]{1,0:T(8,128)(2,1)S(1)}, bf16[768,512]{1,0:T(8,128)(2,1)S(1)}) custom-call(s32[1]{0:T(128)} %bitcast.at_ref, bf16[768,256]{1,0:T(8,128)(2,1)S(1)} %get-tuple-element.157.own, bf16[768,256]{1,0:T(8,128)(2,1)S(1)} %collective-permute-done.19.other, bf16[192,768]{1,0:T(8,128)(2,1)S(1)} %copy-done.6, ...), custom_call_target="tpu_custom_call" | custom-call | flops 1024 | bytes 1024 | tf_op jit(solution)/shard_map/pallas_call | solution.py:22
  78.4 1.6 collective-permute-start.22
  80.0 1.8 collective-permute-start.26
  82.0 2.2 %collective-permute-done.22.received = bf16[192,512]{1,0:T(8,128)(2,1)S(1)} collective-permute-done((bf16[192,512]{1,0:T(8,128)(2,1)S(1)}, bf16[192,512]{1,0:T(8,128)(2,1)S(1)}, u32[]{:S(2)}, u32[]{:S(2)}) %collective-permute-start.22) | collective-permute-done | bytes 196640 | tf_op jit(solution)/shard_map/ppermute | solution.py:55
  85.6 2.8 %shard_map.268 = (bf16[384,512]{1,0:T(8,128)(2,1)S(1)}, f32[384,512]{1,0:T(8,128)S(1)}, f32[8,768]{1,0:T(8,128)S(1)}) custom-call(s32[1]{0:T(128)} %bitcast.at_ref, bf16[576,512]{1,0:T(8,128)(2,1)S(1)} %get-tuple-element.165.refs_0_.d_project, bf16[576,768]{1,0:T(8,128)(2,1)S(1)} %bitcast.16, bf16[768,512]{1,0:T(8,128)(2,1)S(1)} %get-tuple-element.122.x_all, ...), custom_call_target="tpu_custom_call" | custom-call | flops 1024 | bytes 1024 | tf_op jit(solution)/shard_map/pallas_call | solution.py:22
  88.5 3.0 %collective-permute-start.29 = (bf16[64,768]{1,0:T(8,128)(2,1)S(1)}, bf16[64,768]{1,0:T(8,128)(2,1)S(1)}, u32[]{:S(2)}, u32[]{:S(2)}) collective-permute-start(bf16[64,768]{1,0:T(8,128)(2,1)S(1)} %get-tuple-element.198), channel_id=1, source_target_pairs={{0,24},{4,28},{8,16},{12,20},{16,8},{20,12},{24,0},{28,4},{1,25},{... | collective-permute-start | bytes 294920 | tf_op jit(solution)/shard_map/ppermute | solution.py:55
  91.5 2.9 %collective-permute-start.31 = (bf16[96,768]{1,0:T(8,128)(2,1)S(1)}, bf16[96,768]{1,0:T(8,128)(2,1)S(1)}, u32[]{:S(2)}, u32[]{:S(2)}) collective-permute-start(bf16[96,768]{1,0:T(8,128)(2,1)S(1)} %get-tuple-element.205), channel_id=1, source_target_pairs={{0,16},{4,20},{8,24},{12,28},{16,0},{20,4},{24,8},{28,12},{1,17},{... | collective-permute-start | bytes 442376 | tf_op jit(solution)/shard_map/ppermute | solution.py:55
  94.4 1.6 collective-permute-done.29.refs_3_
  96.0 6.6 %collective-permute-start.27 = (bf16[64,768]{1,0:T(8,128)(2,1)S(1)}, bf16[64,768]{1,0:T(8,128)(2,1)S(1)}, u32[]{:S(2)}, u32[]{:S(2)}) collective-permute-start(bf16[64,768]{1,0:T(8,128)(2,1)S(1)} %get-tuple-element.194), channel_id=1, source_target_pairs={{0,8},{4,12},{8,0},{12,4},{16,24},{20,28},{24,16},{28,20},{1,9},{5... | collective-permute-start | bytes 294920 | tf_op jit(solution)/shard_map/ppermute | solution.py:55
  102.7 1.6 collective-permute-done.28.refs_2_
  104.3 5.9 %collective-permute-done.27.refs_1_ = bf16[64,768]{1,0:T(8,128)(2,1)S(1)} collective-permute-done((bf16[64,768]{1,0:T(8,128)(2,1)S(1)}, bf16[64,768]{1,0:T(8,128)(2,1)S(1)}, u32[]{:S(2)}, u32[]{:S(2)}) %collective-permute-start.27) | collective-permute-done | bytes 98336 | tf_op jit(solution)/shard_map/ppermute | solution.py:55
  110.6 1.6 collective-permute-start.30
  113.6 1.7 collective-permute-start.51
  117.0 8.7 %collective-permute-start.40 = (bf16[64,768]{1,0:T(8,128)(2,1)S(1)}, bf16[64,768]{1,0:T(8,128)(2,1)S(1)}, u32[]{:S(2)}, u32[]{:S(2)}) collective-permute-start(bf16[64,768]{1,0:T(8,128)(2,1)S(1)} %get-tuple-element.192), channel_id=1, source_target_pairs={{0,24},{4,28},{8,16},{12,20},{16,8},{20,12},{24,0},{28,4},{1,25},{... | collective-permute-start | bytes 294920 | tf_op jit(solution)/shard_map/ppermute | solution.py:55
  125.7 1.9 collective-permute-start.39
  131.8 3.9 %collective-permute-done.39.refs_2_ = bf16[64,768]{1,0:T(8,128)(2,1)S(1)} collective-permute-done((bf16[64,768]{1,0:T(8,128)(2,1)S(1)}, bf16[64,768]{1,0:T(8,128)(2,1)S(1)}, u32[]{:S(2)}, u32[]{:S(2)}) %collective-permute-start.39) | collective-permute-done | bytes 98336 | tf_op jit(solution)/shard_map/ppermute | solution.py:55
  135.8 3.1 %collective-permute-start.42 = (bf16[64,768]{1,0:T(8,128)(2,1)S(1)}, bf16[64,768]{1,0:T(8,128)(2,1)S(1)}, u32[]{:S(2)}, u32[]{:S(2)}) collective-permute-start(bf16[64,768]{1,0:T(8,128)(2,1)S(1)} %shard_map.280.refs_0_), channel_id=1, source_target_pairs={{0,16},{4,20},{8,24},{12,28},{16,0},{20,4},{24,8},{28,12},{1,17},{... | collective-permute-start | bytes 294920 | tf_op jit(solution)/shard_map/ppermute | solution.py:55
  140.2 5.8 %collective-permute-done.41.refs_1_ = bf16[64,768]{1,0:T(8,128)(2,1)S(1)} collective-permute-done((bf16[64,768]{1,0:T(8,128)(2,1)S(1)}, bf16[64,768]{1,0:T(8,128)(2,1)S(1)}, u32[]{:S(2)}, u32[]{:S(2)}) %collective-permute-start.41) | collective-permute-done | bytes 98336 | tf_op jit(solution)/shard_map/ppermute | solution.py:55
  150.8 9.6 %collective-permute-done.45.refs_1_ = bf16[32,768]{1,0:T(8,128)(2,1)S(1)} collective-permute-done((bf16[32,768]{1,0:T(8,128)(2,1)S(1)}, bf16[32,768]{1,0:T(8,128)(2,1)S(1)}, u32[]{:S(2)}, u32[]{:S(2)}) %collective-permute-start.45) | collective-permute-done | bytes 49184 | tf_op jit(solution)/shard_map/ppermute | solution.py:55
  161.4 9.8 %collective-permute-done.46.refs_1_ = bf16[32,768]{1,0:T(8,128)(2,1)S(1)} collective-permute-done((bf16[32,768]{1,0:T(8,128)(2,1)S(1)}, bf16[32,768]{1,0:T(8,128)(2,1)S(1)}, u32[]{:S(2)}, u32[]{:S(2)}) %collective-permute-start.46) | collective-permute-done | bytes 49184 | tf_op jit(solution)/shard_map/ppermute | solution.py:55
  172.2 3.0 %collective-permute-done.35.refs_1_ = f32[8,768]{1,0:T(8,128)S(1)} collective-permute-done((f32[8,768]{1,0:T(8,128)S(1)}, f32[8,768]{1,0:T(8,128)S(1)}, u32[]{:S(2)}, u32[]{:S(2)}) %collective-permute-start.35) | collective-permute-done | bytes 24608 | tf_op jit(solution)/shard_map/ppermute | solution.py:55
  175.2 1.9 collective-permute-start.36
  177.2 2.0 %collective-permute-done.36.refs_1_ = f32[8,768]{1,0:T(8,128)S(1)} collective-permute-done((f32[8,768]{1,0:T(8,128)S(1)}, f32[8,768]{1,0:T(8,128)S(1)}, u32[]{:S(2)}, u32[]{:S(2)}) %collective-permute-start.36) | collective-permute-done | bytes 24608 | tf_op jit(solution)/shard_map/ppermute | solution.py:55
  179.2 3.1 %collective-permute-start.37 = (f32[8,768]{1,0:T(8,128)S(1)}, f32[8,768]{1,0:T(8,128)S(1)}, u32[]{:S(2)}, u32[]{:S(2)}) collective-permute-start(f32[8,768]{1,0:T(8,128)S(1)} %shard_map.278.refs_0_), channel_id=1, source_target_pairs={{0,16},{4,20},{8,24},{12,28},{16,0},{20,4},{24,8},{28,12},{1,17},{... | collective-permute-start | bytes 73736 | tf_op jit(solution)/shard_map/ppermute | solution.py:55
  183.0 2.3 %collective-permute-done.37.refs_1_ = f32[8,768]{1,0:T(8,128)S(1)} collective-permute-done((f32[8,768]{1,0:T(8,128)S(1)}, f32[8,768]{1,0:T(8,128)S(1)}, u32[]{:S(2)}, u32[]{:S(2)}) %collective-permute-start.37) | collective-permute-done | bytes 24608 | tf_op jit(solution)/shard_map/ppermute | solution.py:55
  185.9 2.2 %collective-permute-start.48 = (bf16[64,768]{1,0:T(8,128)(2,1)S(1)}, bf16[64,768]{1,0:T(8,128)(2,1)S(1)}, u32[]{:S(2)}, u32[]{:S(2)}) collective-permute-start(bf16[64,768]{1,0:T(8,128)(2,1)S(1)} %shard_map.283.refs_2_), channel_id=1, source_target_pairs={{0,16},{4,20},{8,24},{12,28},{16,0},{20,4},{24,8},{28,12},{1,17},{... | collective-permute-start | bytes 294920 | tf_op jit(solution)/shard_map/ppermute | solution.py:55
  188.0 2.0 collective-permute-start.49
  191.5 3.1 %collective-permute-done.49.refs_5_ = bf16[64,768]{1,0:T(8,128)(2,1)S(1)} collective-permute-done((bf16[64,768]{1,0:T(8,128)(2,1)S(1)}, bf16[64,768]{1,0:T(8,128)(2,1)S(1)}, u32[]{:S(2)}, u32[]{:S(2)}) %collective-permute-start.49) | collective-permute-done | bytes 98336 | tf_op jit(solution)/shard_map/ppermute | solution.py:55
  194.6 1.8 shard_map.284
  198.1 1.6 shard_map.290
  199.7 1.6 shard_map.288
  (144 shorter events, 44.7 us)
Async XLA Ops:
  0.7 9.6 %collective-permute-start = (s32[1]{0:T(128)}, s32[1]{0:T(128)}, u32[]{:S(2)}, u32[]{:S(2)}) collective-permute-start(s32[1]{0:T(128)} %param.18), channel_id=1, source_target_pairs={{0,8},{4,12},{8,0},{12,4},{16,24},{20,28},{24,16},{28,20},{1,9},{5... | collective-permute-start | bytes 20 | tf_op jit(solution)/shard_map/ppermute | solution.py:55
  3.7 7.0 %collective-permute-start.1 = (s32[1]{0:T(128)}, s32[1]{0:T(128)}, u32[]{:S(2)}, u32[]{:S(2)}) collective-permute-start(s32[1]{0:T(128)} %param.18), channel_id=1, source_target_pairs={{0,16},{4,20},{8,24},{12,28},{16,0},{20,4},{24,8},{28,12},{1,17},{... | collective-permute-start | bytes 20 | tf_op jit(solution)/shard_map/ppermute | solution.py:55
  6.3 5.6 %collective-permute-start.2 = (s32[1]{0:T(128)}, s32[1]{0:T(128)}, u32[]{:S(2)}, u32[]{:S(2)}) collective-permute-start(s32[1]{0:T(128)} %param.18), channel_id=1, source_target_pairs={{0,24},{4,28},{8,16},{12,20},{16,8},{20,12},{24,0},{28,4},{1,25},{... | collective-permute-start | bytes 20 | tf_op jit(solution)/shard_map/ppermute | solution.py:55
  6.3 13.3 %collective-permute-start.5 = (bf16[192,512]{1,0:T(8,128)(2,1)}, bf16[192,512]{1,0:T(8,128)(2,1)S(1)}, u32[]{:S(2)}, u32[]{:S(2)}) collective-permute-start(bf16[192,512]{1,0:T(8,128)(2,1)} %x_in), channel_id=1, source_target_pairs={{0,2},{1,3},{2,0},{3,1},{4,6},{5,7},{6,4},{7,5},{8,10},{9,11},{10,... | collective-permute-start | bytes 589832 | tf_op jit(solution)/shard_map/ppermute | solution.py:55
  8.8 9.3 %collective-permute-start.7 = (f32[8,256]{1,0:T(8,128)S(1)}, f32[8,256]{1,0:T(8,128)S(1)}, u32[]{:S(2)}, u32[]{:S(2)}) collective-permute-start(f32[8,256]{1,0:T(8,128)S(1)} %fusion.1.n0), channel_id=1, source_target_pairs={{0,1},{1,0},{2,3},{3,2},{4,5},{5,4},{6,7},{7,6},{8,9},{9,8},{10,11... | collective-permute-start | bytes 24584 | tf_op jit(solution)/shard_map/ppermute | solution.py:55
  10.3 11.8 %collective-permute-start.4 = (bf16[192,512]{1,0:T(8,128)(2,1)}, bf16[192,512]{1,0:T(8,128)(2,1)S(1)}, u32[]{:S(2)}, u32[]{:S(2)}) collective-permute-start(bf16[192,512]{1,0:T(8,128)(2,1)} %x_in), channel_id=1, source_target_pairs={{0,1},{1,0},{2,3},{3,2},{4,5},{5,4},{6,7},{7,6},{8,9},{9,8},{10,11... | collective-permute-start | bytes 589832 | tf_op jit(solution)/shard_map/ppermute | solution.py:55
  10.8 11.3 %collective-permute-start.8 = (f32[8,256]{1,0:T(8,128)S(1)}, f32[8,256]{1,0:T(8,128)S(1)}, u32[]{:S(2)}, u32[]{:S(2)}) collective-permute-start(f32[8,256]{1,0:T(8,128)S(1)} %fusion.1.n0), channel_id=1, source_target_pairs={{0,2},{1,3},{2,0},{3,1},{4,6},{5,7},{6,4},{7,5},{8,10},{9,11},{10,... | collective-permute-start | bytes 24584 | tf_op jit(solution)/shard_map/ppermute | solution.py:55
  18.1 4.0 %collective-permute-start.9 = (f32[8,256]{1,0:T(8,128)S(1)}, f32[8,256]{1,0:T(8,128)S(1)}, u32[]{:S(2)}, u32[]{:S(2)}) collective-permute-start(f32[8,256]{1,0:T(8,128)S(1)} %fusion.1.n0), channel_id=1, source_target_pairs={{0,3},{1,2},{2,1},{3,0},{4,7},{5,6},{6,5},{7,4},{8,11},{9,10},{10,... | collective-permute-start | bytes 24584 | tf_op jit(solution)/shard_map/ppermute | solution.py:55
  18.1 8.5 %collective-permute-start.10 = (bf16[192,512]{1,0:T(8,128)(2,1)}, bf16[192,512]{1,0:T(8,128)(2,1)S(1)}, u32[]{:S(2)}, u32[]{:S(2)}) collective-permute-start(bf16[192,512]{1,0:T(8,128)(2,1)} %cotangent), channel_id=1, source_target_pairs={{0,2},{1,3},{2,0},{3,1},{4,6},{5,7},{6,4},{7,5},{8,10},{9,11},{10,... | collective-permute-start | bytes 589832 | tf_op jit(solution)/shard_map/ppermute | solution.py:55
  33.4 13.5 %collective-permute-start.12 = (bf16[768,256]{1,0:T(8,128)(2,1)S(1)}, bf16[768,256]{1,0:T(8,128)(2,1)S(1)}, u32[]{:S(2)}, u32[]{:S(2)}) collective-permute-start(bf16[768,256]{1,0:T(8,128)(2,1)S(1)} %get-tuple-element.127), channel_id=1, source_target_pairs={{0,2},{1,3},{2,0},{3,1},{4,6},{5,7},{6,4},{7,5},{8,10},{9,11},{10,... | collective-permute-start | bytes 1179656 | tf_op jit(solution)/shard_map/ppermute | solution.py:55
  35.0 10.0 %collective-permute-start.13 = (bf16[192,512]{1,0:T(8,128)(2,1)S(1)}, bf16[192,512]{1,0:T(8,128)(2,1)S(1)}, u32[]{:S(2)}, u32[]{:S(2)}) collective-permute-start(bf16[192,512]{1,0:T(8,128)(2,1)S(1)} %copy-done.4), channel_id=1, source_target_pairs={{0,1},{1,0},{2,3},{3,2},{4,5},{5,4},{6,7},{7,6},{8,9},{9,8},{10,11... | collective-permute-start | bytes 589832 | tf_op jit(solution)/shard_map/ppermute | solution.py:55
  35.0 10.0 %collective-permute-start.14 = (bf16[192,512]{1,0:T(8,128)(2,1)S(1)}, bf16[192,512]{1,0:T(8,128)(2,1)S(1)}, u32[]{:S(2)}, u32[]{:S(2)}) collective-permute-start(bf16[192,512]{1,0:T(8,128)(2,1)S(1)} %collective-permute-done.10.c2), channel_id=1, source_target_pairs={{0,1},{1,0},{2,3},{3,2},{4,5},{5,4},{6,7},{7,6},{8,9},{9,8},{10,11... | collective-permute-start | bytes 589832 | tf_op jit(solution)/shard_map/ppermute | solution.py:55
  55.1 11.2 %collective-permute-start.18 = (bf16[768,256]{1,0:T(8,128)(2,1)S(1)}, bf16[768,256]{1,0:T(8,128)(2,1)S(1)}, u32[]{:S(2)}, u32[]{:S(2)}) collective-permute-start(bf16[768,256]{1,0:T(8,128)(2,1)S(1)} %get-tuple-element.153), channel_id=1, source_target_pairs={{0,2},{1,3},{2,0},{3,1},{4,6},{5,7},{6,4},{7,5},{8,10},{9,11},{10,... | collective-permute-start | bytes 1179656 | tf_op jit(solution)/shard_map/ppermute | solution.py:55
  55.7 15.1 %collective-permute-start.21 = (bf16[384,768]{1,0:T(8,128)(2,1)S(1)}, bf16[384,768]{1,0:T(8,128)(2,1)S(1)}, u32[]{:S(2)}, u32[]{:S(2)}) collective-permute-start(bf16[384,768]{1,0:T(8,128)(2,1)S(1)} %get-tuple-element.144), channel_id=1, source_target_pairs={{0,4},{4,0},{8,12},{12,8},{16,20},{20,16},{24,28},{28,24},{1,5},{5... | collective-permute-start | bytes 1769480 | tf_op jit(solution)/shard_map/ppermute | solution.py:55
  58.0 15.0 %collective-permute-start.20 = (bf16[384,768]{1,0:T(8,128)(2,1)S(1)}, bf16[384,768]{1,0:T(8,128)(2,1)S(1)}, u32[]{:S(2)}, u32[]{:S(2)}) collective-permute-start(bf16[384,768]{1,0:T(8,128)(2,1)S(1)} %get-tuple-element.149), channel_id=1, source_target_pairs={{0,8},{4,12},{8,0},{12,4},{16,24},{20,28},{24,16},{28,20},{1,9},{5... | collective-permute-start | bytes 1769480 | tf_op jit(solution)/shard_map/ppermute | solution.py:55
  69.2 4.5 %collective-permute-start.19 = (bf16[768,256]{1,0:T(8,128)(2,1)S(1)}, bf16[768,256]{1,0:T(8,128)(2,1)S(1)}, u32[]{:S(2)}, u32[]{:S(2)}) collective-permute-start(bf16[768,256]{1,0:T(8,128)(2,1)S(1)} %get-tuple-element.157.own), channel_id=1, source_target_pairs={{0,1},{1,0},{2,3},{3,2},{4,5},{5,4},{6,7},{7,6},{8,9},{9,8},{10,11... | collective-permute-start | bytes 1179656 | tf_op jit(solution)/shard_map/ppermute | solution.py:55
  69.3 8.9 %collective-permute-start.17 = (bf16[384,512]{1,0:T(8,128)(2,1)S(1)}, bf16[384,512]{1,0:T(8,128)(2,1)S(1)}, u32[]{:S(2)}, u32[]{:S(2)}) collective-permute-start(bf16[384,512]{1,0:T(8,128)(2,1)S(1)} %get-tuple-element.152), channel_id=1, source_target_pairs={{0,1},{1,0},{2,3},{3,2},{4,5},{5,4},{6,7},{7,6},{8,9},{9,8},{10,11... | collective-permute-start | bytes 1179656 | tf_op jit(solution)/shard_map/ppermute | solution.py:55
  70.9 10.8 %collective-permute-start.24 = (bf16[192,768]{1,0:T(8,128)(2,1)S(1)}, bf16[192,768]{1,0:T(8,128)(2,1)S(1)}, u32[]{:S(2)}, u32[]{:S(2)}) collective-permute-start(bf16[192,768]{1,0:T(8,128)(2,1)S(1)} %get-tuple-element.174), channel_id=1, source_target_pairs={{0,8},{4,12},{8,0},{12,4},{16,24},{20,28},{24,16},{28,20},{1,9},{5... | collective-permute-start | bytes 884744 | tf_op jit(solution)/shard_map/ppermute | solution.py:55
  73.2 8.6 %collective-permute-start.23 = (bf16[192,768]{1,0:T(8,128)(2,1)S(1)}, bf16[192,768]{1,0:T(8,128)(2,1)S(1)}, u32[]{:S(2)}, u32[]{:S(2)}) collective-permute-start(bf16[192,768]{1,0:T(8,128)(2,1)S(1)} %get-tuple-element.162), channel_id=1, source_target_pairs={{0,4},{4,0},{8,12},{12,8},{16,20},{20,16},{24,28},{28,24},{1,5},{5... | collective-permute-start | bytes 884744 | tf_op jit(solution)/shard_map/ppermute | solution.py:55
  78.4 5.7 %collective-permute-start.22 = (bf16[192,512]{1,0:T(8,128)(2,1)S(1)}, bf16[192,512]{1,0:T(8,128)(2,1)S(1)}, u32[]{:S(2)}, u32[]{:S(2)}) collective-permute-start(bf16[192,512]{1,0:T(8,128)(2,1)S(1)} %get-tuple-element.173), channel_id=1, source_target_pairs={{0,2},{1,3},{2,0},{3,1},{4,6},{5,7},{6,4},{7,5},{8,10},{9,11},{10,... | collective-permute-start | bytes 589832 | tf_op jit(solution)/shard_map/ppermute | solution.py:55
  80.0 30.3 %collective-permute-start.26 = (bf16[256,768]{1,0:T(8,128)(2,1)S(1)}, bf16[256,768]{1,0:T(8,128)(2,1)S(1)}, u32[]{:S(2)}, u32[]{:S(2)}) collective-permute-start(bf16[256,768]{1,0:T(8,128)(2,1)S(1)} %get-tuple-element.170), channel_id=1, source_target_pairs={{0,4},{4,0},{8,12},{12,8},{16,20},{20,16},{24,28},{28,24},{1,5},{5... | collective-permute-start | bytes 1179656 | tf_op jit(solution)/shard_map/ppermute | solution.py:55
  88.4 22.0 %collective-permute-start.25 = (bf16[384,512]{1,0:T(8,128)(2,1)S(1)}, bf16[384,512]{1,0:T(8,128)(2,1)S(1)}, u32[]{:S(2)}, u32[]{:S(2)}) collective-permute-start(bf16[384,512]{1,0:T(8,128)(2,1)S(1)} %get-tuple-element.187), channel_id=1, source_target_pairs={{0,1},{1,0},{2,3},{3,2},{4,5},{5,4},{6,7},{7,6},{8,9},{9,8},{10,11... | collective-permute-start | bytes 1179656 | tf_op jit(solution)/shard_map/ppermute | solution.py:55
  88.5 7.6 %collective-permute-start.29 = (bf16[64,768]{1,0:T(8,128)(2,1)S(1)}, bf16[64,768]{1,0:T(8,128)(2,1)S(1)}, u32[]{:S(2)}, u32[]{:S(2)}) collective-permute-start(bf16[64,768]{1,0:T(8,128)(2,1)S(1)} %get-tuple-element.198), channel_id=1, source_target_pairs={{0,24},{4,28},{8,16},{12,20},{16,8},{20,12},{24,0},{28,4},{1,25},{... | collective-permute-start | bytes 294920 | tf_op jit(solution)/shard_map/ppermute | solution.py:55
  91.5 12.8 %collective-permute-start.28 = (bf16[64,768]{1,0:T(8,128)(2,1)S(1)}, bf16[64,768]{1,0:T(8,128)(2,1)S(1)}, u32[]{:S(2)}, u32[]{:S(2)}) collective-permute-start(bf16[64,768]{1,0:T(8,128)(2,1)S(1)} %get-tuple-element.196), channel_id=1, source_target_pairs={{0,16},{4,20},{8,24},{12,28},{16,0},{20,4},{24,8},{28,12},{1,17},{... | collective-permute-start | bytes 294920 | tf_op jit(solution)/shard_map/ppermute | solution.py:55
  91.5 20.6 %collective-permute-start.31 = (bf16[96,768]{1,0:T(8,128)(2,1)S(1)}, bf16[96,768]{1,0:T(8,128)(2,1)S(1)}, u32[]{:S(2)}, u32[]{:S(2)}) collective-permute-start(bf16[96,768]{1,0:T(8,128)(2,1)S(1)} %get-tuple-element.205), channel_id=1, source_target_pairs={{0,16},{4,20},{8,24},{12,28},{16,0},{20,4},{24,8},{28,12},{1,17},{... | collective-permute-start | bytes 442376 | tf_op jit(solution)/shard_map/ppermute | solution.py:55
  96.0 14.2 %collective-permute-start.27 = (bf16[64,768]{1,0:T(8,128)(2,1)S(1)}, bf16[64,768]{1,0:T(8,128)(2,1)S(1)}, u32[]{:S(2)}, u32[]{:S(2)}) collective-permute-start(bf16[64,768]{1,0:T(8,128)(2,1)S(1)} %get-tuple-element.194), channel_id=1, source_target_pairs={{0,8},{4,12},{8,0},{12,4},{16,24},{20,28},{24,16},{28,20},{1,9},{5... | collective-permute-start | bytes 294920 | tf_op jit(solution)/shard_map/ppermute | solution.py:55
  104.3 9.2 %collective-permute-start.50 = (bf16[96,768]{1,0:T(8,128)(2,1)S(1)}, bf16[96,768]{1,0:T(8,128)(2,1)S(1)}, u32[]{:S(2)}, u32[]{:S(2)}) collective-permute-start(bf16[96,768]{1,0:T(8,128)(2,1)S(1)} %get-tuple-element.219), channel_id=1, source_target_pairs={{0,16},{4,20},{8,24},{12,28},{16,0},{20,4},{24,8},{28,12},{1,17},{... | collective-permute-start | bytes 442376 | tf_op jit(solution)/shard_map/ppermute | solution.py:55
  110.6 19.2 %collective-permute-start.30 = (bf16[192,512]{1,0:T(8,128)(2,1)S(1)}, bf16[192,512]{1,0:T(8,128)(2,1)S(1)}, u32[]{:S(2)}, u32[]{:S(2)}) collective-permute-start(bf16[192,512]{1,0:T(8,128)(2,1)S(1)} %get-tuple-element.204), channel_id=1, source_target_pairs={{0,2},{1,3},{2,0},{3,1},{4,6},{5,7},{6,4},{7,5},{8,10},{9,11},{10,... | collective-permute-start | bytes 589832 | tf_op jit(solution)/shard_map/ppermute | solution.py:55
  112.2 15.4 %collective-permute-start.32 = (bf16[96,768]{1,0:T(8,128)(2,1)S(1)}, bf16[96,768]{1,0:T(8,128)(2,1)S(1)}, u32[]{:S(2)}, u32[]{:S(2)}) collective-permute-start(bf16[96,768]{1,0:T(8,128)(2,1)S(1)} %shard_map.272.refs_0_), channel_id=1, source_target_pairs={{0,16},{4,20},{8,24},{12,28},{16,0},{20,4},{24,8},{28,12},{1,17},{... | collective-permute-start | bytes 442376 | tf_op jit(solution)/shard_map/ppermute | solution.py:55
  113.6 15.7 %collective-permute-start.51 = (bf16[96,768]{1,0:T(8,128)(2,1)S(1)}, bf16[96,768]{1,0:T(8,128)(2,1)S(1)}, u32[]{:S(2)}, u32[]{:S(2)}) collective-permute-start(bf16[96,768]{1,0:T(8,128)(2,1)S(1)} %shard_map.285.refs_0_), channel_id=1, source_target_pairs={{0,16},{4,20},{8,24},{12,28},{16,0},{20,4},{24,8},{28,12},{1,17},{... | collective-permute-start | bytes 442376 | tf_op jit(solution)/shard_map/ppermute | solution.py:55
  116.5 9.2 %collective-permute-start.34 = (f32[8,768]{1,0:T(8,128)S(1)}, f32[8,768]{1,0:T(8,128)S(1)}, u32[]{:S(2)}, u32[]{:S(2)}) collective-permute-start(f32[8,768]{1,0:T(8,128)S(1)} %shard_map.274.refs_0_), channel_id=1, source_target_pairs={{0,2},{1,3},{2,0},{3,1},{4,6},{5,7},{6,4},{7,5},{8,10},{9,11},{10,... | collective-permute-start | bytes 73736 | tf_op jit(solution)/shard_map/ppermute | solution.py:55
  117.0 14.8 %collective-permute-start.40 = (bf16[64,768]{1,0:T(8,128)(2,1)S(1)}, bf16[64,768]{1,0:T(8,128)(2,1)S(1)}, u32[]{:S(2)}, u32[]{:S(2)}) collective-permute-start(bf16[64,768]{1,0:T(8,128)(2,1)S(1)} %get-tuple-element.192), channel_id=1, source_target_pairs={{0,24},{4,28},{8,16},{12,20},{16,8},{20,12},{24,0},{28,4},{1,25},{... | collective-permute-start | bytes 294920 | tf_op jit(solution)/shard_map/ppermute | solution.py:55
  125.7 10.0 %collective-permute-start.39 = (bf16[64,768]{1,0:T(8,128)(2,1)S(1)}, bf16[64,768]{1,0:T(8,128)(2,1)S(1)}, u32[]{:S(2)}, u32[]{:S(2)}) collective-permute-start(bf16[64,768]{1,0:T(8,128)(2,1)S(1)} %get-tuple-element.191), channel_id=1, source_target_pairs={{0,16},{4,20},{8,24},{12,28},{16,0},{20,4},{24,8},{28,12},{1,17},{... | collective-permute-start | bytes 294920 | tf_op jit(solution)/shard_map/ppermute | solution.py:55
  127.6 8.0 %collective-permute-start.38 = (bf16[64,768]{1,0:T(8,128)(2,1)S(1)}, bf16[64,768]{1,0:T(8,128)(2,1)S(1)}, u32[]{:S(2)}, u32[]{:S(2)}) collective-permute-start(bf16[64,768]{1,0:T(8,128)(2,1)S(1)} %get-tuple-element.190), channel_id=1, source_target_pairs={{0,8},{4,12},{8,0},{12,4},{16,24},{20,28},{24,16},{28,20},{1,9},{5... | collective-permute-start | bytes 294920 | tf_op jit(solution)/shard_map/ppermute | solution.py:55
  129.3 20.0 %collective-permute-start.54 = (bf16[192,768]{1,0:T(8,128)(2,1)S(1)}, bf16[192,768]{1,0:T(8,128)(2,1)S(1)}, u32[]{:S(2)}, u32[]{:S(2)}) collective-permute-start(bf16[192,768]{1,0:T(8,128)(2,1)S(1)} %shard_map.273.refs_0_), channel_id=1, source_target_pairs={{0,8},{4,12},{8,0},{12,4},{16,24},{20,28},{24,16},{28,20},{1,9},{5... | collective-permute-start | bytes 884744 | tf_op jit(solution)/shard_map/ppermute | solution.py:55
  129.8 20.5 %collective-permute-start.52 = (bf16[192,768]{1,0:T(8,128)(2,1)S(1)}, bf16[192,768]{1,0:T(8,128)(2,1)S(1)}, u32[]{:S(2)}, u32[]{:S(2)}) collective-permute-start(bf16[192,768]{1,0:T(8,128)(2,1)S(1)} %shard_map.286.refs_0_), channel_id=1, source_target_pairs={{0,4},{4,0},{8,12},{12,8},{16,20},{20,16},{24,28},{28,24},{1,5},{5... | collective-permute-start | bytes 884744 | tf_op jit(solution)/shard_map/ppermute | solution.py:55
  135.7 10.2 %collective-permute-start.41 = (bf16[64,768]{1,0:T(8,128)(2,1)S(1)}, bf16[64,768]{1,0:T(8,128)(2,1)S(1)}, u32[]{:S(2)}, u32[]{:S(2)}) collective-permute-start(bf16[64,768]{1,0:T(8,128)(2,1)S(1)} %shard_map.280.refs_0_), channel_id=1, source_target_pairs={{0,8},{4,12},{8,0},{12,4},{16,24},{20,28},{24,16},{28,20},{1,9},{5... | collective-permute-start | bytes 294920 | tf_op jit(solution)/shard_map/ppermute | solution.py:55
  135.8 10.2 %collective-permute-start.42 = (bf16[64,768]{1,0:T(8,128)(2,1)S(1)}, bf16[64,768]{1,0:T(8,128)(2,1)S(1)}, u32[]{:S(2)}, u32[]{:S(2)}) collective-permute-start(bf16[64,768]{1,0:T(8,128)(2,1)S(1)} %shard_map.280.refs_0_), channel_id=1, source_target_pairs={{0,16},{4,20},{8,24},{12,28},{16,0},{20,4},{24,8},{28,12},{1,17},{... | collective-permute-start | bytes 294920 | tf_op jit(solution)/shard_map/ppermute | solution.py:55
  138.9 8.3 %collective-permute-start.43 = (bf16[64,768]{1,0:T(8,128)(2,1)S(1)}, bf16[64,768]{1,0:T(8,128)(2,1)S(1)}, u32[]{:S(2)}, u32[]{:S(2)}) collective-permute-start(bf16[64,768]{1,0:T(8,128)(2,1)S(1)} %shard_map.280.refs_0_), channel_id=1, source_target_pairs={{0,24},{4,28},{8,16},{12,20},{16,8},{20,12},{24,0},{28,4},{1,25},{... | collective-permute-start | bytes 294920 | tf_op jit(solution)/shard_map/ppermute | solution.py:55
  147.2 47.3 %collective-permute-start.44 = (bf16[256,768]{1,0:T(8,128)(2,1)S(1)}, bf16[256,768]{1,0:T(8,128)(2,1)S(1)}, u32[]{:S(2)}, u32[]{:S(2)}) collective-permute-start(bf16[256,768]{1,0:T(8,128)(2,1)S(1)} %shard_map.281.refs_0_), channel_id=1, source_target_pairs={{0,4},{4,0},{8,12},{12,8},{16,20},{20,16},{24,28},{28,24},{1,5},{5... | collective-permute-start | bytes 1179656 | tf_op jit(solution)/shard_map/ppermute | solution.py:55
  148.2 12.2 %collective-permute-start.45 = (bf16[32,768]{1,0:T(8,128)(2,1)S(1)}, bf16[32,768]{1,0:T(8,128)(2,1)S(1)}, u32[]{:S(2)}, u32[]{:S(2)}) collective-permute-start(bf16[32,768]{1,0:T(8,128)(2,1)S(1)} %get-tuple-element.201), channel_id=1, source_target_pairs={{0,4},{4,0},{8,12},{12,8},{16,20},{20,16},{24,28},{28,24},{1,5},{5... | collective-permute-start | bytes 147464 | tf_op jit(solution)/shard_map/ppermute | solution.py:55
  149.4 48.8 %collective-permute-start.55 = (bf16[384,768]{1,0:T(8,128)(2,1)S(1)}, bf16[384,768]{1,0:T(8,128)(2,1)S(1)}, u32[]{:S(2)}, u32[]{:S(2)}) collective-permute-start(bf16[384,768]{1,0:T(8,128)(2,1)S(1)} %shard_map.289.refs_0_), channel_id=1, source_target_pairs={{0,4},{4,0},{8,12},{12,8},{16,20},{20,16},{24,28},{28,24},{1,5},{5... | collective-permute-start | bytes 1769480 | tf_op jit(solution)/shard_map/ppermute | solution.py:55
  150.4 49.3 %collective-permute-start.53 = (bf16[384,768]{1,0:T(8,128)(2,1)S(1)}, bf16[384,768]{1,0:T(8,128)(2,1)S(1)}, u32[]{:S(2)}, u32[]{:S(2)}) collective-permute-start(bf16[384,768]{1,0:T(8,128)(2,1)S(1)} %shard_map.287.refs_0_), channel_id=1, source_target_pairs={{0,8},{4,12},{8,0},{12,4},{16,24},{20,28},{24,16},{28,20},{1,9},{5... | collective-permute-start | bytes 1769480 | tf_op jit(solution)/shard_map/ppermute | solution.py:55
  160.4 10.8 %collective-permute-start.46 = (bf16[32,768]{1,0:T(8,128)(2,1)S(1)}, bf16[32,768]{1,0:T(8,128)(2,1)S(1)}, u32[]{:S(2)}, u32[]{:S(2)}) collective-permute-start(bf16[32,768]{1,0:T(8,128)(2,1)S(1)} %shard_map.282.refs_0_), channel_id=1, source_target_pairs={{0,4},{4,0},{8,12},{12,8},{16,20},{20,16},{24,28},{28,24},{1,5},{5... | collective-permute-start | bytes 147464 | tf_op jit(solution)/shard_map/ppermute | solution.py:55
  171.3 16.8 %collective-permute-start.47 = (bf16[64,768]{1,0:T(8,128)(2,1)S(1)}, bf16[64,768]{1,0:T(8,128)(2,1)S(1)}, u32[]{:S(2)}, u32[]{:S(2)}) collective-permute-start(bf16[64,768]{1,0:T(8,128)(2,1)S(1)} %shard_map.283.refs_2_), channel_id=1, source_target_pairs={{0,8},{4,12},{8,0},{12,4},{16,24},{20,28},{24,16},{28,20},{1,9},{5... | collective-permute-start | bytes 294920 | tf_op jit(solution)/shard_map/ppermute | solution.py:55
  179.2 6.0 %collective-permute-start.37 = (f32[8,768]{1,0:T(8,128)S(1)}, f32[8,768]{1,0:T(8,128)S(1)}, u32[]{:S(2)}, u32[]{:S(2)}) collective-permute-start(f32[8,768]{1,0:T(8,128)S(1)} %shard_map.278.refs_0_), channel_id=1, source_target_pairs={{0,16},{4,20},{8,24},{12,28},{16,0},{20,4},{24,8},{28,12},{1,17},{... | collective-permute-start | bytes 73736 | tf_op jit(solution)/shard_map/ppermute | solution.py:55
  185.9 5.6 %collective-permute-start.48 = (bf16[64,768]{1,0:T(8,128)(2,1)S(1)}, bf16[64,768]{1,0:T(8,128)(2,1)S(1)}, u32[]{:S(2)}, u32[]{:S(2)}) collective-permute-start(bf16[64,768]{1,0:T(8,128)(2,1)S(1)} %shard_map.283.refs_2_), channel_id=1, source_target_pairs={{0,16},{4,20},{8,24},{12,28},{16,0},{20,4},{24,8},{28,12},{1,17},{... | collective-permute-start | bytes 294920 | tf_op jit(solution)/shard_map/ppermute | solution.py:55
  188.0 6.5 %collective-permute-start.49 = (bf16[64,768]{1,0:T(8,128)(2,1)S(1)}, bf16[64,768]{1,0:T(8,128)(2,1)S(1)}, u32[]{:S(2)}, u32[]{:S(2)}) collective-permute-start(bf16[64,768]{1,0:T(8,128)(2,1)S(1)} %shard_map.283.refs_2_), channel_id=1, source_target_pairs={{0,24},{4,28},{8,16},{12,20},{16,8},{20,12},{24,0},{28,4},{1,25},{... | collective-permute-start | bytes 294920 | tf_op jit(solution)/shard_map/ppermute | solution.py:55
  (22 other events, 87.9 us)

commit v4 on v3

--- a/solution.py
+++ b/solution.py
@@ -2,6 +2,7 @@
 
 import jax
 import jax.numpy as jnp
+import numpy as np
 from jax import lax
 from jax.experimental import pallas as pl
 from jax.experimental.pallas import tpu as pltpu
@@ -18,8 +19,16 @@
     return jax.ShapeDtypeStruct(dims, kind)
 
 
-def kernel(body, outs, scalars, arrays, scratch=(), flops=0, limit=12):
-    return pl.pallas_call(
+class Order:
+    last = None
+    cost = 10**9
+
+
+def kernel(body, outs, scalars, arrays, scratch=(), limit=12):
+    arrays = list(arrays)
+    if Order.last is not None:
+        arrays[0] = after(arrays[0], Order.last)
+    found = pl.pallas_call(
         body,
         out_shape=outs,
         in_specs=[pl.BlockSpec(memory_space=pltpu.SMEM)] * len(scalars)
@@ -27,8 +36,10 @@
         out_specs=jax.tree.map(lambda _: pl.BlockSpec(memory_space=pltpu.VMEM), outs),
         scratch_shapes=list(scratch),
         compiler_params=pltpu.CompilerParams(vmem_limit_bytes=limit * 1024 * 1024),
-        cost_estimate=pl.CostEstimate(flops=1024, bytes_accessed=1024, transcendentals=0),
+        cost_estimate=pl.CostEstimate(flops=Order.cost, bytes_accessed=1024, transcendentals=0),
     )(*scalars, *arrays)
+    Order.last = jax.tree.leaves(found)[0]
+    return found
 
 
 def after(value, *others):
@@ -101,24 +112,8 @@
     return kernel(join_kernel, shape(rows, pieces[0].shape[1], kind=pieces[0].dtype), [], pieces)
 
 
-def count_kernel(*refs):
-    refs[-1][0] = sum((ref[0] for ref in refs[1:-1]), refs[0][0])
-
-
-def sum_counts(counts, row_devices):
-    for stride, radix in reversed(digits_of(row_devices, "near")):
-        parts = [counts] + [xor_send(counts, "rows", row_devices, e * stride) for e in range(1, radix)]
-        counts = pl.pallas_call(
-            count_kernel,
-            out_shape=jax.ShapeDtypeStruct((1,), jnp.int32),
-            in_specs=[pl.BlockSpec(memory_space=pltpu.SMEM)] * len(parts),
-            out_specs=pl.BlockSpec(memory_space=pltpu.SMEM),
-            compiler_params=pltpu.CompilerParams(vmem_limit_bytes=1024 * 1024),
-        )(*parts)
-    return counts
-
-
 def chunks_of(count, rows):
+    count = min(count, 8)
     while rows % (16 * count):
         count //= 2
     return count
@@ -132,12 +127,8 @@
             strides.append((stride, 2))
             stride *= 2
         return strides
-    if kind == "crossed":
-        strides = digits_of(count, "halving")
-        return [strides[1], strides[0]] + strides[2:]
-    if kind == "near":
-        return [(1, 2), (2, count // 2)]
-    return [(2, count // 2), (1, 2)]
+    strides = digits_of(count, "halving")
+    return [strides[1], strides[0]] + strides[2:]
 
 
 def offsets_of(digits):
@@ -184,7 +175,7 @@
 def weight_gradient(me, streams, *operands):
     pairs = len(operands) // 2
     total = sum(operands[2 * i].shape[0] for i in range(pairs))
-    columns, tokens = operands[1].shape
+    columns = operands[1].shape[0]
     outs = tuple(
         shape(len(offsets) * stream.chunk, columns, kind=BF16) for stream in streams for offsets in stream.parts()
     )
@@ -195,7 +186,6 @@
             [me],
             operands,
             [pltpu.VMEM((total, columns), BF16)],
-            2 * total * columns * tokens,
         )
     )
     return [[found.pop(0) for _ in stream.parts()] for stream in streams]
@@ -253,27 +243,18 @@
         bounds.append((start, start + size))
         start += size
     outs = tuple(shape(size, columns) for size in sizes)
-    return kernel(functools.partial(place_kernel, streams, bounds), outs, [me], pieces, flops=start * columns)
+    return kernel(functools.partial(place_kernel, streams, bounds), outs, [me], pieces)
 
 
 def live_row(all_tokens, counts_ref, total_ref, width, first):
-    scale = jnp.full((1, width), all_tokens, F32) / (jnp.zeros((1, width), F32) + total_ref[0].astype(F32))
+    scale = jnp.full((1, width), all_tokens, F32) / jnp.broadcast_to(total_ref[0:1, 0:1], (1, width))
     place = lax.broadcasted_iota(jnp.int32, (1, width), 1) + first
     return jnp.where(place < counts_ref[0], scale, 0.0)
 
 
-def history_kernel(
-    all_tokens, mix_ref, counts_ref, total_ref, history_ref, cot_ref, running_ref, d_history_ref, d_mix_ref
-):
-    layers = history_ref.shape[0]
-    features, tokens = cot_ref.shape
-    live = live_row(all_tokens, counts_ref, total_ref, tokens, 0)
-
-    @pl.when(pl.program_id(0) == 0)
-    def _():
-        d_mix_ref[...] = jnp.zeros_like(d_mix_ref)
-
-    for i in range(features // STEP):
+def history_block(live, mix_ref, d_mix_ref, history_ref, cot_ref, running_ref, d_history_ref):
+    layers, block, tokens = history_ref.shape
+    for i in range(block // STEP):
         rows = slice(i * STEP, (i + 1) * STEP)
         grad = cot_ref[rows].astype(F32) * live
         running = jnp.zeros_like(grad)
@@ -288,32 +269,44 @@
         running_ref[rows] = running
 
 
+def history_kernel(
+    all_tokens, block, mix_ref, counts_ref, cot_ref, total_ref, history_ref, running_ref, d_history_ref, d_mix_ref
+):
+    layers, features, tokens = history_ref.shape
+    live = live_row(all_tokens, counts_ref, total_ref, tokens, 0)
+    d_mix_ref[...] = jnp.zeros_like(d_mix_ref)
+
+    def body(history_part, d_history_part):
+        at = pl.multiple_of(pl.program_id(0) * block, block)
+        history_block(
+            live, mix_ref, d_mix_ref, history_part, cot_ref.at[pl.ds(at, block)], running_ref.at[pl.ds(at, block)],
+            d_history_part,
+        )
+
+    whole = pl.BlockSpec((layers, block, tokens), lambda i: (0, i, 0))
+    pltpu.emit_pipeline(body, grid=(features // block,), in_specs=[whole], out_specs=[whole])(
+        history_ref, d_history_ref
+    )
+
+
 def mix_history(all_tokens, mix_weights, counts, total, history, cotangent):
     layers, features, tokens = history.shape
-    block = 32
-    return pl.pallas_call(
-        functools.partial(history_kernel, all_tokens),
-        grid=(features // block,),
+    vmem, hbm = pl.BlockSpec(memory_space=pltpu.VMEM), pl.BlockSpec(memory_space=pltpu.HBM)
+    smem = pl.BlockSpec(memory_space=pltpu.SMEM)
+    found = pl.pallas_call(
+        functools.partial(history_kernel, all_tokens, 32),
         out_shape=(
             shape(features, tokens),
             shape(*history.shape, kind=BF16),
             shape(layers, STEP // 2, 128),
         ),
-        in_specs=[
-            pl.BlockSpec(memory_space=pltpu.SMEM),
-            pl.BlockSpec(memory_space=pltpu.SMEM),
-            pl.BlockSpec(memory_space=pltpu.SMEM),
-            pl.BlockSpec((layers, block, tokens), lambda i: (0, i, 0)),
-            pl.BlockSpec((block, tokens), lambda i: (i, 0)),
-        ],
-        out_specs=(
-            pl.BlockSpec((block, tokens), lambda i: (i, 0)),
-            pl.BlockSpec((layers, block, tokens), lambda i: (0, i, 0)),
-            pl.BlockSpec((layers, STEP // 2, 128), lambda i: (0, 0, 0)),
-        ),
+        in_specs=[smem, smem, vmem, vmem, hbm],
+        out_specs=(vmem, hbm, vmem),
         compiler_params=pltpu.CompilerParams(vmem_limit_bytes=12 * 1024 * 1024),
-        cost_estimate=pl.CostEstimate(flops=1024, bytes_accessed=1024, transcendentals=0),
-    )(mix_weights, counts, total, history, cotangent)
+        cost_estimate=pl.CostEstimate(flops=Order.cost, bytes_accessed=1024, transcendentals=0),
+    )(mix_weights, counts, after(cotangent, Order.last), total, history)
+    Order.last = found[0]
+    return found
 
 
 def spread_of(load, count, width):
@@ -327,16 +320,27 @@
     return mean, lax.rsqrt(column_sum(each_rows(count, squares, zero)) / count + EPSILON)
 
 
+def prepare_kernel(counts_ref, positions, rates, g1, b1, g2, b2, count, norms, cosine, sine):
+    count[...] = jnp.zeros(count.shape, F32) + counts_ref[0].astype(F32)
+    norms[...] = jnp.zeros_like(norms)
+    for i, ref in enumerate((g1, b1, g2, b2)):
+        norms[i : i + 1, : ref.shape[1]] = ref[...]
+    angles = positions[...].astype(F32) * rates[...]
+    cosine[...] = jnp.cos(angles)
+    sine[...] = jnp.sin(angles)
+
+
 def project_kernel(
-    at_ref, x0, x1, x2, x3, n0, n1, n2, n3, cosine, sine, w_qkv, x_all, norms, normed, stats, qkv, project
+    at_ref, x0, x1, x2, x3, n01, n23, cosine, sine, w_qkv, x_all, norms, normed, stats, qkv, project
 ):
     at = at_ref[0]
     part, tokens = x0.shape
     model = w_qkv.shape[1]
-    for e, (piece, norm) in enumerate(((x0, n0), (x1, n1), (x2, n2), (x3, n3))):
+    near, far = n01[...].T, n23[...].T
+    for e, (piece, norm) in enumerate(((x0, near), (x1, near), (x2, far), (x3, far))):
         rows = pl.ds(pl.multiple_of((at ^ e) * part, 64), part)
         x_all[rows, :] = piece[...]
-        norms[rows, :] = norm[...].T[:part]
+        norms[rows, :] = norm[:part, 8 * (e % 2) : 8 * (e % 2) + 8]
     mean, scale = spread_of(lambda i: x_all[rows_at(i), :].astype(F32), model, tokens)
     stats[0:1] = mean
     stats[1:2] = scale
@@ -406,7 +410,7 @@
 
 
 def output_gradient_kernel(
-    all_tokens, at_ref, self_ref, counts_ref, total_ref, c0, c1, c2, c3, w_down, g_out, d_active, cot_half, cot_all
+    all_tokens, at_ref, self_ref, counts_ref, c0, c1, c2, c3, total_ref, w_down, g_out, d_active, cot_half, cot_all
 ):
     at = at_ref[0]
     part, tokens = c0.shape
@@ -498,7 +502,7 @@
 
 
 def middle_gradient_kernel(
-    all_tokens, at_ref, self_ref, counts_ref, total_ref, chip, received, middle, stats, cot_half, norms,
+    all_tokens, at_ref, self_ref, counts_ref, chip, received, total_ref, middle, stats, cot_half, norms,
     d_middle, g_mid, gains, d_normed, gain_sums, bias_sums,
 ):
     model, half = chip.shape
@@ -621,7 +625,7 @@
 
 
 def mixed_kernel(
-    all_tokens, self_ref, counts_ref, total_ref, chip, received, running, cotangent, d_mix, mixed, row, table
+    all_tokens, self_ref, counts_ref, chip, received, total_ref, running, cotangent, d_mix, mixed, row, table
 ):
     layers = d_mix.shape[0]
     part, tokens = chip.shape
@@ -638,6 +642,17 @@
     table[:layers] = jnp.sum(d_mix[...], axis=1)
     table[layers : layers + 1] = column_sum(found)
     row[...] = as_row(table)
+
+
+def ends_kernel(layers, width, at_ref, sums, d_mix, d_self, *ends):
+    part = ends[0].shape[1]
+    d_mix[...] = sums[6:7, :layers]
+    d_self[...] = sums[6:7, layers : layers + 1]
+    for i, end in enumerate(ends):
+        found = sums[i : i + 1, :part]
+        for w in range(1, width):
+            found = jnp.where(at_ref[0] == w, sums[i : i + 1, w * part : (w + 1) * part], found)
+        end[...] = found
 
 
 def d_input_kernel(chip, received, x_in, stats, sums, d_input):
@@ -678,25 +693,46 @@
     half = tokens // 2
     layers = mix_weights.shape[0]
     all_tokens = float(tokens * row_devices)
-    at_width = lax.axis_index("width")
-    at = at_width.astype(jnp.int32)[None]
+    at = lax.axis_index("width").astype(jnp.int32)[None]
     me = lax.axis_index("rows").astype(jnp.int32)[None]
-    norms = jnp.pad(
-        jnp.stack([first_norm_gain, first_norm_bias, second_norm_gain, second_norm_bias]), ((0, 124), (0, -part % 128))
-    )
-    inverse = 1.0 / 10000.0 ** (jnp.arange(HEAD_DIM // 2, dtype=F32) * 2.0 / HEAD_DIM)
-    angles = positions[None, :].astype(F32) * inverse[:, None]
-    cosine, sine = jnp.cos(angles), jnp.sin(angles)
+    Order.last, Order.cost = None, 10**9
     to_width = lambda value, offset: xor_send(value, "width", width, offset)
+    to_row = lambda value, offset: xor_send(value, "rows", row_devices, offset)
     w_qkv = w_qkv.reshape(3 * part, model)
+    rates = 1.0 / 10000.0 ** (np.arange(HEAD_DIM // 2) * 2.0 / HEAD_DIM)
     x_in, cotangent, counts = after((x_in, cotangent, counts), at, me)
 
     x_far, x_near = to_width(x_in, 2), to_width(x_in, 1)
-    cot_far, cot_near = to_width(cotangent, 2), to_width(cotangent, 1)
-    norms = [norms[:8]] + [to_width(norms[:8], e) for e in range(1, width)]
-    total = sum_counts(counts, row_devices)
-    x_both, cot_both = to_width(x_far, 1), to_width(cot_far, 1)
-
+    cot_now = after(cotangent, x_near)
+    cot_far, cot_near = to_width(cot_now, 2), to_width(cot_now, 1)
+    live_total, norms, cosine, sine = kernel(
+        prepare_kernel,
+        (
+            shape(8, 128),
+            shape(8, -(-part // 128) * 128),
+            shape(HEAD_DIM // 2, tokens),
+            shape(HEAD_DIM // 2, tokens),
+        ),
+        [counts],
+        [
+            after(positions[None, :], x_near),
+            jnp.asarray(rates[:, None], F32),
+            *(v[None, :] for v in (first_norm_gain, first_norm_bias, second_norm_gain, second_norm_bias)),
+        ],
+    )
+    strides = [1 << i for i in range(row_devices.bit_length() - 1)]
+
+    def grow_total(value, stride):
+        return add([value, to_row(value, stride)], (0, 8, F32))[0]
+
+    Order.cost = 10**9
+    norms_near = join([norms, to_width(norms, 1)])
+    norms_far = to_width(norms_near, 2)
+    Order.cost = 10**10
+    live_total = grow_total(live_total, strides[0])
+    x_both = to_width(after(x_far, norms_near), 1)
+
+    Order.cost = 10**8
     x_all, norms, normed_one, stats_one, qkv = kernel(
         project_kernel,
         (
@@ -707,9 +743,13 @@
             shape(3 * part, tokens, kind=BF16),
         ),
         [at],
-        [x_in, x_near, x_far, x_both, *norms, cosine, sine, w_qkv],
+        [x_in, x_near, x_far, x_both, norms_near, norms_far, cosine, sine, w_qkv],
         [pltpu.VMEM((3 * part, tokens), F32)],
     )
+    Order.cost = 10**9
+    for stride in strides[1:-1]:
+        live_total = grow_total(live_total, stride)
+    cot_both = to_width(cot_far, 1)
     send, keep, x_half, heads_out, probs = kernel(
         attention_kernel,
         (
@@ -720,20 +760,19 @@
             shape(part // HEAD_DIM, tokens, tokens, kind=BF16),
         ),
         [at],
-        [after(qkv, cot_far, total), w_out, x_all],
+        [after(qkv, cot_far), w_out, x_all],
         [pltpu.VMEM((tokens, half), F32)],
     )
     chip, send = add([keep, to_width(send, 1)], (0, model, F32), (0, model, BF16))
     received = to_width(send, 2)
 
-    running, d_history, d_mix = mix_history(
-        all_tokens, mix_weights, counts, total, history, after(cotangent, chip)
-    )
+    live_total = grow_total(live_total, strides[-1])
+    running, d_history, d_mix = mix_history(all_tokens, mix_weights, counts, live_total, history, cotangent)
     g_out, d_active, cot_half = kernel(
         functools.partial(output_gradient_kernel, all_tokens),
         (shape(model, tokens, kind=BF16), shape(hidden_units, tokens), shape(model, half, kind=BF16)),
-        [at, self_weight, counts, total],
-        [cotangent, cot_near, cot_far, cot_both, after(w_down, running)],
+        [at, self_weight, counts],
+        [cotangent, cot_near, cot_far, cot_both, live_total, w_down],
         [pltpu.VMEM((model, tokens), BF16)],
     )
 
@@ -741,7 +780,7 @@
         middle_kernel,
         (shape(model, half), shape(2, half), shape(model, half, kind=BF16)),
         [],
-        [x_half, chip, after(received, g_out), norms],
+        [x_half, chip, received, norms],
     )
     normed_two, active, d_hidden, send, keep = kernel(
         feed_forward_kernel,
@@ -759,40 +798,37 @@
 
     down = Stream(row_devices, 0, hidden_units, "halving")
     up = Stream(row_devices, 0, model, "crossed")
-    down_parts = weight_gradient(me, [down], active, after(g_out, send))[0]
+    down_parts = weight_gradient(me, [down], active, g_out)[0]
     down_got = start_stage(down, down_parts, 0)
-    chip, send = add([keep, after(to_width(send, 1), *down_parts)], (0, model, F32), (0, model, BF16))
+    chip, send = add([keep, to_width(send, 1)], (0, model, F32), (0, model, BF16))
     received = to_width(send, 2)
-    up_parts = weight_gradient(me, [up], normed_two, after(d_hidden, chip))[0]
+    up_parts = weight_gradient(me, [up], normed_two, d_hidden)[0]
     up_got = start_stage(up, up_parts, 0)
-
     blocks = (shape(2 * part, tokens, kind=BF16), shape(2 * part, tokens))
     out_send, out_keep = kernel(
-        output_kernel,
-        blocks,
-        [at],
-        [active, w_down, after(middle, *up_parts)],
-        [pltpu.VMEM((model, tokens), F32)],
+        output_kernel, blocks, [at], [active, w_down, middle], [pltpu.VMEM((model, tokens), F32)]
     )
     out_near = to_width(out_send, 1)
 
     d_middle, g_own, gains_two = kernel(
         functools.partial(middle_gradient_kernel, all_tokens),
         (shape(model, half), shape(model, half, kind=BF16), shape(2, model)),
-        [at, self_weight, counts, total],
-        [chip, after(received, out_keep), middle, stats_two, cot_half, norms],
+        [at, self_weight, counts],
+        [chip, received, live_total, middle, stats_two, cot_half, norms],
         [pltpu.VMEM((model, half), F32), pltpu.VMEM((model, 128), F32), pltpu.VMEM((model, 128), F32)],
     )
     g_other = to_width(g_own, 1)
-    down_parts = add_stage(down, down_parts, [after(v, g_own) for v in down_got], 0)
+    out_chip, out_send = add([out_keep, out_near], (0, part, F32), (part, 2 * part, BF16))
+    out_far = to_width(out_send, 2)
+    down_parts = add_stage(down, down_parts, down_got, 0)
     down_got = start_stage(down, down_parts, 1)
-    up_parts = add_stage(up, up_parts, [after(v, down_parts[0]) for v in up_got], 0)
+    up_parts = add_stage(up, up_parts, up_got, 0)
     up_got = start_stage(up, up_parts, 1)
     d_project, g_mid = kernel(
         attention_gradient_kernel,
         (shape(3 * part, tokens, kind=BF16), shape(model, tokens, kind=BF16)),
         [at],
-        [g_own, after(g_other, *up_parts), w_out, qkv, probs, cosine, sine],
+        [g_own, g_other, w_out, qkv, probs, cosine, sine],
         [
             pltpu.VMEM((part, tokens), BF16),
             pltpu.VMEM((tokens, half), BF16),
@@ -804,27 +840,25 @@
     )
     tail_rows = 4 * part
     tail = [
-        Stream(row_devices, 0, tail_rows * 2 // 3, "near"),
-        Stream(row_devices, tail_rows * 2 // 3, tail_rows // 3, "far"),
+        Stream(row_devices, 0, tail_rows // 2, "halving"),
+        Stream(row_devices, tail_rows // 2, tail_rows // 2, "crossed"),
     ]
-    tail_parts = weight_gradient(me, tail, d_project, normed_one, heads_out, g_mid)
-    tail_got = [start_stage(s, p, 0) for s, p in zip(tail, tail_parts)]
-
-    out_chip, out_send = add(
-        [out_keep, after(out_near, *tail_parts[0])], (0, part, F32), (part, 2 * part, BF16)
-    )
-    out_far = to_width(out_send, 2)
-    down_parts = add_stage(down, down_parts, [after(v, out_send) for v in down_got], 1)
-    down_got = start_stage(down, down_parts, 2)
-    up_parts = add_stage(up, up_parts, [after(v, down_parts[0]) for v in up_got], 1)
-    up_got = start_stage(up, up_parts, 2)
+    first, second = tail
+    first_parts, second_parts = weight_gradient(me, tail, d_project, normed_one, heads_out, g_mid)
+    first_got = start_stage(first, first_parts, 0)
+    second_got = start_stage(second, second_parts, 0)
+
+    Order.cost = 6 * 10**9
     mixed, mix_row = kernel(
         functools.partial(mixed_kernel, all_tokens),
         (shape(part, tokens, kind=BF16), shape(1, 128)),
-        [self_weight, counts, total],
-        [out_chip, after(out_far, up_parts[0]), running, cotangent, d_mix],
+        [self_weight, counts],
+        [out_chip, out_far, live_total, running, cotangent, d_mix],
         [pltpu.VMEM((128, 128), F32)],
     )
+    Order.cost = 10**8
+    down_parts = add_stage(down, down_parts, down_got, 1)
+    down_got = start_stage(down, down_parts, 2)
     in_send, in_keep, sums = kernel(
         input_gradient_kernel,
         blocks + (shape(8, model),),
@@ -833,53 +867,70 @@
         [pltpu.VMEM((model, tokens), F32), pltpu.VMEM((model, 128), F32), pltpu.VMEM((model, 128), F32)],
     )
     in_near = to_width(in_send, 1)
-    tail_parts = [
-        add_stage(s, p, [after(v, in_send) for v in g], 0) for s, p, g in zip(tail, tail_parts, tail_got)
-    ]
-    tail_got = [start_stage(s, p, 1) for s, p in zip(tail, tail_parts)]
-    in_chip, in_send = add(
-        [in_keep, after(in_near, *tail_parts[0], *tail_parts[1])], (0, part, F32), (part, 2 * part, BF16)
-    )
+    sums_got = to_width(sums, 1)
+    up_parts = add_stage(up, up_parts, up_got, 1)
+    up_got = start_stage(up, up_parts, 2)
+    first_parts = add_stage(first, first_parts, first_got, 0)
+    first_got = start_stage(first, first_parts, 1)
+    Order.cost = 2 * 10**10
+    second_parts = add_stage(second, second_parts, second_got, 0)
+    second_got = start_stage(second, second_parts, 1)
+    Order.cost = 10**9
+    in_chip, in_send = add([in_keep, in_near], (0, part, F32), (part, 2 * part, BF16))
     in_far = to_width(in_send, 2)
-    sums = sum_small(after(sums, in_send), "width", width)
-    down_value = sum_rest(down, add_stage(down, down_parts, [after(v, in_send) for v in down_got], 2)[0])
-    up_value = sum_rest(up, add_stage(up, up_parts, [after(v, down_value) for v in up_got], 2)[0])
-    for stage in range(len(down.digits) - 1, 0, -1):
-        down_value = join(gather_stage(down, down_value, stage))
-        up_value = join(gather_stage(up, up_value, stage))
-        if stage == len(down.digits) - 1:
-            d_input = kernel(
-                d_input_kernel,
-                shape(part, tokens),
-                [],
-                [in_chip, after(in_far, down_value), x_in, stats_one, sums],
-            )
-            tail_values = [
-                sum_rest(s, add_stage(s, p, [after(v, d_input) for v in g], 1)[0])
-                for s, p, g in zip(tail, tail_parts, tail_got)
-            ]
-            tail_values = [join(gather_stage(s, v, 1)) for s, v in zip(tail, tail_values)]
-            small = sum_small(after(sums, d_input), "rows", row_devices)
-    down_pieces = gather_stage(down, down_value, 0)
-    up_pieces = gather_stage(up, up_value, 0)
-    tail_pieces = [piece for s, v in zip(tail, tail_values) for piece in gather_stage(s, v, 0)]
+    sums = add([sums, sums_got], (0, 8, F32))[0]
+    sums_got = to_width(sums, 2)
+    last = len(down.digits) - 1
+    down_value = sum_rest(down, add_stage(down, down_parts, down_got, 2)[0])
+    down_pieces = gather_stage(down, down_value, last)
+    up_value = sum_rest(up, add_stage(up, up_parts, up_got, 2)[0])
+    up_pieces = gather_stage(up, up_value, last)
+    first_parts = add_stage(first, first_parts, first_got, 1)
+    first_got = start_stage(first, first_parts, 2)
+    second_parts = add_stage(second, second_parts, second_got, 1)
+    second_got = start_stage(second, second_parts, 2)
+    sums = add([sums, sums_got], (0, 8, F32))[0]
+    sums_got = to_row(sums, strides[0])
+    d_input = kernel(d_input_kernel, shape(part, tokens), [], [in_chip, in_far, x_in, stats_one, sums])
+    down_pieces = gather_stage(down, join(down_pieces), last - 1)
+    up_pieces = gather_stage(up, join(up_pieces), last - 1)
+    first_value = sum_rest(first, add_stage(first, first_parts, first_got, 2)[0])
+    first_pieces = gather_stage(first, first_value, last)
+    second_value = sum_rest(second, add_stage(second, second_parts, second_got, 2)[0])
+    second_pieces = gather_stage(second, second_value, last)
+    for stride in strides[1:-1]:
+        sums = add([sums, sums_got], (0, 8, F32))[0]
+        sums_got = to_row(sums, stride)
+    first_pieces = gather_stage(first, join(first_pieces), last - 1)
+    second_pieces = gather_stage(second, join(second_pieces), last - 1)
+    down_pieces = gather_stage(down, join(down_pieces), 0)
+    up_pieces = gather_stage(up, join(up_pieces), 0)
+    sums = add([sums, sums_got], (0, 8, F32))[0]
+    sums_got = to_row(sums, strides[-1])
+    first_pieces = gather_stage(first, join(first_pieces), 0)
+    second_pieces = gather_stage(second, join(second_pieces), 0)
+    sums = add([sums, sums_got], (0, 8, F32))[0]
+    d_mix, d_self, *ends = kernel(
+        functools.partial(ends_kernel, layers, width),
+        (shape(1, layers), shape(1, 1)) + (shape(1, part),) * 4,
+        [at],
+        [sums],
+    )
     d_w_down = place(me, [down], down_pieces, (hidden_units,))[0]
     d_w_up = place(me, [up], up_pieces, (model,))[0]
-    d_w_qkv, d_w_out = place(me, tail, tail_pieces, (3 * part, part))
-    small = after(small, d_w_qkv)
-    ends = [lax.dynamic_slice(small, (i, at_width * part), (1, part))[0] for i in range(4)]
+    d_w_qkv, d_w_out = place(me, tail, first_pieces + second_pieces, (3 * part, part))
     return (
         mixed,
         d_input,
         d_history,
-        small[6, :layers],
-        small[6, layers : layers + 1],
-        ends[0],
-        ends[1],
+        d_mix[0],
+        d_self[0],
+        ends[0][0],
+        ends[1][0],
         d_w_qkv.reshape(3, part, model),
         d_w_out,
-        ends[2],
-        ends[3],
+        ends[2][0],
+        ends[3][0],
         d_w_up,
         d_w_down,
     )

time: 202 us -> 157 us (0.78)
  starting transfers between devices: 69.1 us -> 49.9 us
  waiting for transfers between devices: 73.2 us -> 58.5 us
  Pallas kernels: 45.6 us -> 40.9 us
  local copies, waits for them, and re-layouts: 9.22 us -> 5.08 us
    ppermute x56 -> x50, starting transfers between devices: 69.1 us -> 49.9 us  [xor_send(): return lax.ppermute(value, axis, [(i, i ^ offset) for i in range(size)])]
    ppermute x56 -> x50, waiting for transfers between devices: 73.2 us -> 58.5 us  [xor_send(): return lax.ppermute(value, axis, [(i, i ^ offset) for i in range(size)])]
    pallas_call x3 -> x1, Pallas kernels: 10.3 us -> 5.91 us  [mix_history(): pl.pallas_call(functools.partial(history_kernel, all_tokens, 32), out_sha...]
    unnamed x28 -> x30, local copies, waits for them, and re-layouts: 7.48 us -> 5.08 us
    pallas_call x42 -> x52, Pallas kernels: 35.3 us -> 34.9 us  [kernel(): pl.pallas_call(body, out_shape=outs, in_specs=[pl.BlockSpec(memory_space=...]
  transfers between devices with their start and end apart: 56 -> 50, of which waited for: 24 -> 16; matrix products, arithmetic and copies ran while one was open for 2% -> 0% of each run, Pallas kernels for 17% -> 19%
where the time goes in v4:
time: 157 us
  waiting for transfers between devices  58.5 us (37%)
  starting transfers between devices  49.9 us (32%)
  Pallas kernels  40.9 us (26%)
  local copies, waits for them, and re-layouts  5.08 us (3%)
  between operations  2.56 us (2%)
    ppermute x50, waiting for transfers between devices, xor_send(): return lax.ppermute(value, axis, [(i, i ^ offset) for i in range(size)])  58.5 us
    ppermute x50, starting transfers between devices, xor_send(): return lax.ppermute(value, axis, [(i, i ^ offset) for i in range(size)])  49.9 us
    pallas_call x52, Pallas kernels, kernel(): pl.pallas_call(body, out_shape=outs, in_specs=[pl.BlockSpec(memory_space=...  34.9 us
    pallas_call x1, Pallas kernels, mix_history(): pl.pallas_call(functools.partial(history_kernel, all_tokens, 32), out_sha...  5.91 us
    unnamed x30, local copies, waits for them, and re-layouts  5.08 us
  transfers between devices with their start and end apart: 50, of which 16 were waited for; matrix products, arithmetic and copies ran while one was open for 0% of the time, Pallas kernels for 19%

profile of v4, /device:TPU:0, one launch (start us, length us, event | category | flops | bytes accessed | tf_op | source)
XLA Modules:
  0.0 156.8 jit_solution(2286069570071003572)
XLA Ops:
  1.2 2.6 %collective-permute-start.3 = (bf16[192,512]{1,0:T(8,128)(2,1)}, bf16[192,512]{1,0:T(8,128)(2,1)S(1)}, u32[]{:S(2)}, u32[]{:S(2)}) collective-permute-start(bf16[192,512]{1,0:T(8,128)(2,1)} %x_in), channel_id=1, source_target_pairs={{0,2},{1,3},{2,0},{3,1},{4,6},{5,7},{6,4},{7,5},{8,10},{9,11},{10,... | collective-permute-start | bytes 589832 | tf_op jit(solution)/shard_map/ppermute | solution.py:66
  9.1 1.5 collective-permute-start.2
  11.5 1.2 collective-permute-start.5
  12.7 1.6 %collective-permute-start.7 = (f32[8,128]{1,0:T(8,128)S(1)}, f32[8,128]{1,0:T(8,128)S(1)}, u32[]{:S(2)}, u32[]{:S(2)}) collective-permute-start(f32[8,128]{1,0:T(8,128)S(1)} %shard_map.257.refs_0_), channel_id=1, source_target_pairs={{0,8},{4,12},{8,0},{12,4},{16,24},{20,28},{24,16},{28,20},{1,9},{5... | collective-permute-start | bytes 12296 | tf_op jit(solution)/shard_map/ppermute | solution.py:66
  14.4 3.5 %collective-permute-done.5.n23 = f32[16,256]{1,0:T(8,128)S(1)} collective-permute-done((f32[16,256]{1,0:T(8,128)S(1)}, f32[16,256]{1,0:T(8,128)S(1)}, u32[]{:S(2)}, u32[]{:S(2)}) %collective-permute-start.5) | collective-permute-done | bytes 16416 | tf_op jit(solution)/shard_map/ppermute | solution.py:66
  17.8 2.4 %shard_map.258 = (bf16[768,512]{1,0:T(8,128)(2,1)S(1)}, f32[768,8]{1,0:T(8,128)S(1)}, bf16[768,512]{1,0:T(8,128)(2,1)S(1)}, f32[2,512]{1,0:T(2,128)S(1)}, bf16[576,512]{1,0:T(8,128)(2,1)S(1)}) custom-call(s32[1]{0:T(128)} %bitcast.at_ref, bf16[192,512]{1,0:T(8,128)(2,1)S(1)} %copy-done.2, bf16[192,512]{1,0:T(8,128)(2,1)S(1)} %collective-permute-done.x1, ...), custom_call_target="tpu_custom_call" | custom-call | flops 100000000 | bytes 1024 | tf_op jit(solution)/shard_map/pallas_call | solution.py:31
  21.2 4.7 %shard_map.260 = (bf16[768,256]{1,0:T(8,128)(2,1)S(1)}, f32[768,256]{1,0:T(8,128)S(1)}, bf16[768,256]{1,0:T(8,128)(2,1)S(1)}, bf16[192,512]{1,0:T(8,128)(2,1)S(1)}, bf16[3,512,512]{2,1,0:T(8,128)(2,1)S(1)}) custom-call(s32[1]{0:T(128)} %bitcast.at_ref, bf16[576,512]{1,0:T(8,128)(2,1)S(1)} %get-tuple-element.168.qkv, bf16[192,768]{1,0:T(8,128)(2,1)S(1)} %copy-done.6, ...), custom_call_target="tpu_custom_call" | custom-call | flops 1000000000 | bytes 1024 | tf_op jit(solution)/shard_map/pallas_call | solution.py:31
  26.0 1.7 %collective-permute-done.8.refs_1_ = bf16[768,256]{1,0:T(8,128)(2,1)S(1)} collective-permute-done((bf16[768,256]{1,0:T(8,128)(2,1)S(1)}, bf16[768,256]{1,0:T(8,128)(2,1)S(1)}, u32[]{:S(2)}, u32[]{:S(2)}) %collective-permute-start.8) | collective-permute-done | bytes 393248 | tf_op jit(solution)/shard_map/ppermute | solution.py:66
  29.5 2.6 %collective-permute-start.9 = (f32[8,128]{1,0:T(8,128)S(1)}, f32[8,128]{1,0:T(8,128)S(1)}, u32[]{:S(2)}, u32[]{:S(2)}) collective-permute-start(f32[8,128]{1,0:T(8,128)S(1)} %shard_map.259.refs_0_), channel_id=1, source_target_pairs={{0,16},{4,20},{8,24},{12,28},{16,0},{20,4},{24,8},{28,12},{1,17},{... | collective-permute-start | bytes 12296 | tf_op jit(solution)/shard_map/ppermute | solution.py:66
  32.7 1.3 collective-permute-done.9.refs_1_
  34.0 5.9 %shard_map.263 = (f32[192,512]{1,0:T(8,128)S(1)}, bf16[30,192,512]{2,1,0:T(8,128)(2,1)}, f32[30,8,128]{2,1,0:T(8,128)S(1)}) custom-call(f32[30]{0:T(128)S(1)} %copy-done.3, s32[1]{0:T(128)S(6)} %copy.29.counts_ref, bf16[192,512]{1,0:T(8,128)(2,1)S(1)} %copy-done.1, f32[8,128]{1,0:T(8,128)S(1)} %shard_map.262.total_ref, bf16[30,192,512]{2,1,0:T(8,128)(2,1)S(1)} %bitcast.16), custom_call_target="tpu_custom_call" | custom-call | flops 1000000000 | bytes 1024 | tf_op jit(solution)/shard_map/pallas_call | solution.py:296
  40.0 1.3 shard_map.264
  41.3 1.6 shard_map.265
  42.9 1.7 %collective-permute-done.13.other = bf16[768,256]{1,0:T(8,128)(2,1)S(1)} collective-permute-done((bf16[768,256]{1,0:T(8,128)(2,1)S(1)}, bf16[768,256]{1,0:T(8,128)(2,1)S(1)}, u32[]{:S(2)}, u32[]{:S(2)}) %collective-permute-start.13) | collective-permute-done | bytes 393248 | tf_op jit(solution)/shard_map/ppermute | solution.py:66
  44.6 2.6 %shard_map.266 = (bf16[768,512]{1,0:T(8,128)(2,1)S(1)}, bf16[768,512]{1,0:T(8,128)(2,1)S(1)}, bf16[768,512]{1,0:T(8,128)(2,1)S(1)}, bf16[768,256]{1,0:T(8,128)(2,1)S(1)}, f32[768,256]{1,0:T(8,128)S(1)}) custom-call(bf16[768,256]{1,0:T(8,128)(2,1)S(1)} %get-tuple-element.184.own, bf16[768,256]{1,0:T(8,128)(2,1)S(1)} %collective-permute-done.13.other, ...), custom_call_target="tpu_custom_call" | custom-call | flops 1000000000 | bytes 1024 | tf_op jit(solution)/shard_map/pallas_call | solution.py:31
  49.4 1.2 collective-permute-start.15
  52.0 1.6 %collective-permute-start.18 = (bf16[384,768]{1,0:T(8,128)(2,1)S(1)}, bf16[384,768]{1,0:T(8,128)(2,1)S(1)}, u32[]{:S(2)}, u32[]{:S(2)}) collective-permute-start(bf16[384,768]{1,0:T(8,128)(2,1)S(1)} %get-tuple-element.212), channel_id=1, source_target_pairs={{0,8},{4,12},{8,0},{12,4},{16,24},{20,28},{24,16},{28,20},{1,9},{5... | collective-permute-start | bytes 1769480 | tf_op jit(solution)/shard_map/ppermute | solution.py:66
  54.6 6.0 %collective-permute-done.15.received = bf16[768,256]{1,0:T(8,128)(2,1)S(1)} collective-permute-done((bf16[768,256]{1,0:T(8,128)(2,1)S(1)}, bf16[768,256]{1,0:T(8,128)(2,1)S(1)}, u32[]{:S(2)}, u32[]{:S(2)}) %collective-permute-start.15) | collective-permute-done | bytes 393248 | tf_op jit(solution)/shard_map/ppermute | solution.py:66
  60.6 2.4 %shard_map.271 = (f32[768,256]{1,0:T(8,128)S(1)}, bf16[768,256]{1,0:T(8,128)(2,1)S(1)}, f32[2,768]{1,0:T(2,128)S(1)}) custom-call(s32[1]{0:T(128)} %bitcast.at_ref, f32[1]{0:T(128)S(6)} %copy.30.self_ref, s32[1]{0:T(128)S(6)} %copy.29.counts_ref, f32[768,256]{1,0:T(8,128)S(1)} %get-tuple-element.200.chip, ...), custom_call_target="tpu_custom_call" | custom-call | flops 1000000000 | bytes 1024 | tf_op jit(solution)/shard_map/pallas_call | solution.py:31
  63.2 1.2 collective-permute-start.20
  64.4 1.3 collective-permute-done.17.refs_1_
  65.8 1.6 %collective-permute-start.21 = (bf16[192,768]{1,0:T(8,128)(2,1)S(1)}, bf16[192,768]{1,0:T(8,128)(2,1)S(1)}, u32[]{:S(2)}, u32[]{:S(2)}) collective-permute-start(bf16[192,768]{1,0:T(8,128)(2,1)S(1)} %get-tuple-element.227), channel_id=1, source_target_pairs={{0,8},{4,12},{8,0},{12,4},{16,24},{20,28},{24,16},{28,20},{1,9},{5... | collective-permute-start | bytes 884744 | tf_op jit(solution)/shard_map/ppermute | solution.py:66
  67.6 1.2 collective-permute-start.22
  68.9 3.6 %shard_map.275 = (bf16[576,512]{1,0:T(8,128)(2,1)S(1)}, bf16[768,512]{1,0:T(8,128)(2,1)S(1)}) custom-call(s32[1]{0:T(128)} %bitcast.at_ref, bf16[768,256]{1,0:T(8,128)(2,1)S(1)} %get-tuple-element.214.own, bf16[768,256]{1,0:T(8,128)(2,1)S(1)} %collective-permute-done.19.other, bf16[192,768]{1,0:T(8,128)(2,1)S(1)} %copy-done.6, ...), custom_call_target="tpu_custom_call" | custom-call | flops 1000000000 | bytes 1024 | tf_op jit(solution)/shard_map/pallas_call | solution.py:31
  76.3 2.8 %shard_map.279 = (bf16[384,512]{1,0:T(8,128)(2,1)S(1)}, f32[384,512]{1,0:T(8,128)S(1)}, f32[8,768]{1,0:T(8,128)S(1)}) custom-call(s32[1]{0:T(128)} %bitcast.at_ref, bf16[576,512]{1,0:T(8,128)(2,1)S(1)} %get-tuple-element.229.refs_0_.d_project, bf16[576,768]{1,0:T(8,128)(2,1)S(1)} %bitcast.18, bf16[768,512]{1,0:T(8,128)(2,1)S(1)} %get-tuple-element.166.x_all, ...), custom_call_target="tpu_custom_call" | custom-call | flops 100000000 | bytes 1024 | tf_op jit(solution)/shard_map/pallas_call | solution.py:31
  79.7 2.6 %collective-permute-start.27 = (bf16[96,768]{1,0:T(8,128)(2,1)S(1)}, bf16[96,768]{1,0:T(8,128)(2,1)S(1)}, u32[]{:S(2)}, u32[]{:S(2)}) collective-permute-start(bf16[96,768]{1,0:T(8,128)(2,1)S(1)} %get-tuple-element.250), channel_id=1, source_target_pairs={{0,16},{4,20},{8,24},{12,28},{16,0},{20,4},{24,8},{28,12},{1,17},{... | collective-permute-start | bytes 442376 | tf_op jit(solution)/shard_map/ppermute | solution.py:66
  82.4 1.8 %collective-permute-start.28 = (bf16[96,768]{1,0:T(8,128)(2,1)S(1)}, bf16[96,768]{1,0:T(8,128)(2,1)S(1)}, u32[]{:S(2)}, u32[]{:S(2)}) collective-permute-start(bf16[96,768]{1,0:T(8,128)(2,1)S(1)} %get-tuple-element.252), channel_id=1, source_target_pairs={{0,16},{4,20},{8,24},{12,28},{16,0},{20,4},{24,8},{28,12},{1,17},{... | collective-permute-start | bytes 442376 | tf_op jit(solution)/shard_map/ppermute | solution.py:66
  85.4 1.6 %collective-permute-start.29 = (bf16[96,768]{1,0:T(8,128)(2,1)S(1)}, bf16[96,768]{1,0:T(8,128)(2,1)S(1)}, u32[]{:S(2)}, u32[]{:S(2)}) collective-permute-start(bf16[96,768]{1,0:T(8,128)(2,1)S(1)} %get-tuple-element.254), channel_id=1, source_target_pairs={{0,8},{4,12},{8,0},{12,4},{16,24},{20,28},{24,16},{28,20},{1,9},{5... | collective-permute-start | bytes 442376 | tf_op jit(solution)/shard_map/ppermute | solution.py:66
  88.1 5.4 %collective-permute-done.27.refs_1_ = bf16[96,768]{1,0:T(8,128)(2,1)S(1)} collective-permute-done((bf16[96,768]{1,0:T(8,128)(2,1)S(1)}, bf16[96,768]{1,0:T(8,128)(2,1)S(1)}, u32[]{:S(2)}, u32[]{:S(2)}) %collective-permute-start.27) | collective-permute-done | bytes 147488 | tf_op jit(solution)/shard_map/ppermute | solution.py:66
  93.5 2.6 %collective-permute-done.28.refs_1_ = bf16[96,768]{1,0:T(8,128)(2,1)S(1)} collective-permute-done((bf16[96,768]{1,0:T(8,128)(2,1)S(1)}, bf16[96,768]{1,0:T(8,128)(2,1)S(1)}, u32[]{:S(2)}, u32[]{:S(2)}) %collective-permute-start.28) | collective-permute-done | bytes 147488 | tf_op jit(solution)/shard_map/ppermute | solution.py:66
  96.2 2.9 %collective-permute-start.33 = (bf16[96,768]{1,0:T(8,128)(2,1)S(1)}, bf16[96,768]{1,0:T(8,128)(2,1)S(1)}, u32[]{:S(2)}, u32[]{:S(2)}) collective-permute-start(bf16[96,768]{1,0:T(8,128)(2,1)S(1)} %shard_map.285.refs_0_), channel_id=1, source_target_pairs={{0,16},{4,20},{8,24},{12,28},{16,0},{20,4},{24,8},{28,12},{1,17},{... | collective-permute-start | bytes 442376 | tf_op jit(solution)/shard_map/ppermute | solution.py:66
  100.2 1.7 %collective-permute-start.37 = (f32[8,768]{1,0:T(8,128)S(1)}, f32[8,768]{1,0:T(8,128)S(1)}, u32[]{:S(2)}, u32[]{:S(2)}) collective-permute-start(f32[8,768]{1,0:T(8,128)S(1)} %shard_map.289.sums.refs_0_), channel_id=1, source_target_pairs={{0,4},{4,0},{8,12},{12,8},{16,20},{20,16},{24,28},{28,24},{1,5},{5... | collective-permute-start | bytes 73736 | tf_op jit(solution)/shard_map/ppermute | solution.py:66
  102.0 2.9 %collective-permute-done.32.received = bf16[192,512]{1,0:T(8,128)(2,1)S(1)} collective-permute-done((bf16[192,512]{1,0:T(8,128)(2,1)S(1)}, bf16[192,512]{1,0:T(8,128)(2,1)S(1)}, u32[]{:S(2)}, u32[]{:S(2)}) %collective-permute-start.32) | collective-permute-done | bytes 196640 | tf_op jit(solution)/shard_map/ppermute | solution.py:66
  106.1 9.5 %collective-permute-done.33.refs_1_ = bf16[96,768]{1,0:T(8,128)(2,1)S(1)} collective-permute-done((bf16[96,768]{1,0:T(8,128)(2,1)S(1)}, bf16[96,768]{1,0:T(8,128)(2,1)S(1)}, u32[]{:S(2)}, u32[]{:S(2)}) %collective-permute-start.33) | collective-permute-done | bytes 147488 | tf_op jit(solution)/shard_map/ppermute | solution.py:66
  115.7 2.5 %collective-permute-done.35.refs_1_ = bf16[48,768]{1,0:T(8,128)(2,1)S(1)} collective-permute-done((bf16[48,768]{1,0:T(8,128)(2,1)S(1)}, bf16[48,768]{1,0:T(8,128)(2,1)S(1)}, u32[]{:S(2)}, u32[]{:S(2)}) %collective-permute-start.35) | collective-permute-done | bytes 73760 | tf_op jit(solution)/shard_map/ppermute | solution.py:66
  118.4 2.9 %collective-permute-start.38 = (bf16[48,768]{1,0:T(8,128)(2,1)S(1)}, bf16[48,768]{1,0:T(8,128)(2,1)S(1)}, u32[]{:S(2)}, u32[]{:S(2)}) collective-permute-start(bf16[48,768]{1,0:T(8,128)(2,1)S(1)} %shard_map.293.refs_0_), channel_id=1, source_target_pairs={{0,16},{4,20},{8,24},{12,28},{16,0},{20,4},{24,8},{28,12},{1,17},{... | collective-permute-start | bytes 221192 | tf_op jit(solution)/shard_map/ppermute | solution.py:66
  121.3 1.2 collective-permute-start.41
  122.5 5.2 %collective-permute-done.38.refs_1_ = bf16[48,768]{1,0:T(8,128)(2,1)S(1)} collective-permute-done((bf16[48,768]{1,0:T(8,128)(2,1)S(1)}, bf16[48,768]{1,0:T(8,128)(2,1)S(1)}, u32[]{:S(2)}, u32[]{:S(2)}) %collective-permute-start.38) | collective-permute-done | bytes 73760 | tf_op jit(solution)/shard_map/ppermute | solution.py:66
  127.8 1.8 %collective-permute-start.46 = (bf16[384,768]{1,0:T(8,128)(2,1)S(1)}, bf16[384,768]{1,0:T(8,128)(2,1)S(1)}, u32[]{:S(2)}, u32[]{:S(2)}) collective-permute-start(bf16[384,768]{1,0:T(8,128)(2,1)S(1)} %shard_map.298.refs_0_), channel_id=1, source_target_pairs={{0,4},{4,0},{8,12},{12,8},{16,20},{20,16},{24,28},{28,24},{1,5},{5... | collective-permute-start | bytes 1769480 | tf_op jit(solution)/shard_map/ppermute | solution.py:66
  129.6 2.1 %collective-permute-start.47 = (bf16[384,768]{1,0:T(8,128)(2,1)S(1)}, bf16[384,768]{1,0:T(8,128)(2,1)S(1)}, u32[]{:S(2)}, u32[]{:S(2)}) collective-permute-start(bf16[384,768]{1,0:T(8,128)(2,1)S(1)} %shard_map.299.refs_0_), channel_id=1, source_target_pairs={{0,8},{4,12},{8,0},{12,4},{16,24},{20,28},{24,16},{28,20},{1,9},{5... | collective-permute-start | bytes 1769480 | tf_op jit(solution)/shard_map/ppermute | solution.py:66
  131.8 1.1 collective-permute-start.44
  132.9 12.9 %collective-permute-done.42.refs_1_ = f32[8,768]{1,0:T(8,128)S(1)} collective-permute-done((f32[8,768]{1,0:T(8,128)S(1)}, f32[8,768]{1,0:T(8,128)S(1)}, u32[]{:S(2)}, u32[]{:S(2)}) %collective-permute-start.42) | collective-permute-done | bytes 24608 | tf_op jit(solution)/shard_map/ppermute | solution.py:66
  146.3 1.9 %collective-permute-start.49 = (bf16[192,768]{1,0:T(8,128)(2,1)S(1)}, bf16[192,768]{1,0:T(8,128)(2,1)S(1)}, u32[]{:S(2)}, u32[]{:S(2)}) collective-permute-start(bf16[192,768]{1,0:T(8,128)(2,1)S(1)} %shard_map.302.refs_2_), channel_id=1, source_target_pairs={{0,8},{4,12},{8,0},{12,4},{16,24},{20,28},{24,16},{28,20},{1,9},{5... | collective-permute-start | bytes 884744 | tf_op jit(solution)/shard_map/ppermute | solution.py:66
  148.2 1.2 collective-permute-start.48
  149.5 1.3 collective-permute-done.45.refs_1_
  151.6 1.6 shard_map.305
  153.2 1.6 shard_map.306
  155.0 1.8 %shard_map.307 = (f32[576,768]{1,0:T(8,128)}, f32[192,768]{1,0:T(8,128)}) custom-call(s32[1]{0:T(128)} %bitcast.1.me_ref, bf16[192,768]{1,0:T(8,128)(2,1)S(1)} %shard_map.301.refs_0_, bf16[192,768]{1,0:T(8,128)(2,1)S(1)} %collective-permute-done.48.refs_1_, bf16[192,768]{1,0:T(8,128)(2,1)S(1)} %shard_map.302.refs_2_, ...), custom_call_target="tpu_custom_call" | custom-call | flops 1000000000 | bytes 1024 | tf_op jit(solution)/shard_map/pallas_call | solution.py:31
  (136 shorter events, 25.5 us)
Async XLA Ops:
  0.7 3.8 %collective-permute-start = (bf16[192,512]{1,0:T(8,128)(2,1)}, bf16[192,512]{1,0:T(8,128)(2,1)S(1)}, u32[]{:S(2)}, u32[]{:S(2)}) collective-permute-start(bf16[192,512]{1,0:T(8,128)(2,1)} %x_in), channel_id=1, source_target_pairs={{0,1},{1,0},{2,3},{3,2},{4,5},{5,4},{6,7},{7,6},{8,9},{9,8},{10,11... | collective-permute-start | bytes 589832 | tf_op jit(solution)/shard_map/ppermute | solution.py:66
  1.2 11.5 %collective-permute-start.3 = (bf16[192,512]{1,0:T(8,128)(2,1)}, bf16[192,512]{1,0:T(8,128)(2,1)S(1)}, u32[]{:S(2)}, u32[]{:S(2)}) collective-permute-start(bf16[192,512]{1,0:T(8,128)(2,1)} %x_in), channel_id=1, source_target_pairs={{0,2},{1,3},{2,0},{3,1},{4,6},{5,7},{6,4},{7,5},{8,10},{9,11},{10,... | collective-permute-start | bytes 589832 | tf_op jit(solution)/shard_map/ppermute | solution.py:66
  8.9 2.6 %collective-permute-start.1 = (f32[8,256]{1,0:T(8,128)S(1)}, f32[8,256]{1,0:T(8,128)S(1)}, u32[]{:S(2)}, u32[]{:S(2)}) collective-permute-start(f32[8,256]{1,0:T(8,128)S(1)} %get-tuple-element.156.refs_0_), channel_id=1, source_target_pairs={{0,1},{1,0},{2,3},{3,2},{4,5},{5,4},{6,7},{7,6},{8,9},{9,8},{10,11... | collective-permute-start | bytes 24584 | tf_op jit(solution)/shard_map/ppermute | solution.py:66
  9.1 3.6 %collective-permute-start.2 = (f32[8,128]{1,0:T(8,128)S(1)}, f32[8,128]{1,0:T(8,128)S(1)}, u32[]{:S(2)}, u32[]{:S(2)}) collective-permute-start(f32[8,128]{1,0:T(8,128)S(1)} %get-tuple-element.157.refs_0_), channel_id=1, source_target_pairs={{0,4},{4,0},{8,12},{12,8},{16,20},{20,16},{24,28},{28,24},{1,5},{5... | collective-permute-start | bytes 12296 | tf_op jit(solution)/shard_map/ppermute | solution.py:66
  10.6 9.6 %collective-permute-start.6 = (bf16[192,512]{1,0:T(8,128)(2,1)S(1)}, bf16[192,512]{1,0:T(8,128)(2,1)S(1)}, u32[]{:S(2)}, u32[]{:S(2)}) collective-permute-start(bf16[192,512]{1,0:T(8,128)(2,1)S(1)} %copy-done.1), channel_id=1, source_target_pairs={{0,2},{1,3},{2,0},{3,1},{4,6},{5,7},{6,4},{7,5},{8,10},{9,11},{10,... | collective-permute-start | bytes 589832 | tf_op jit(solution)/shard_map/ppermute | solution.py:66
  11.5 6.3 %collective-permute-start.5 = (f32[16,256]{1,0:T(8,128)S(1)}, f32[16,256]{1,0:T(8,128)S(1)}, u32[]{:S(2)}, u32[]{:S(2)}) collective-permute-start(f32[16,256]{1,0:T(8,128)S(1)} %shard_map.256.n01), channel_id=1, source_target_pairs={{0,2},{1,3},{2,0},{3,1},{4,6},{5,7},{6,4},{7,5},{8,10},{9,11},{10,... | collective-permute-start | bytes 49160 | tf_op jit(solution)/shard_map/ppermute | solution.py:66
  12.7 5.1 %collective-permute-start.4 = (bf16[192,512]{1,0:T(8,128)(2,1)S(1)}, bf16[192,512]{1,0:T(8,128)(2,1)S(1)}, u32[]{:S(2)}, u32[]{:S(2)}) collective-permute-start(bf16[192,512]{1,0:T(8,128)(2,1)S(1)} %collective-permute-done.3.x2), channel_id=1, source_target_pairs={{0,1},{1,0},{2,3},{3,2},{4,5},{5,4},{6,7},{7,6},{8,9},{9,8},{10,11... | collective-permute-start | bytes 589832 | tf_op jit(solution)/shard_map/ppermute | solution.py:66
  12.7 7.5 %collective-permute-start.7 = (f32[8,128]{1,0:T(8,128)S(1)}, f32[8,128]{1,0:T(8,128)S(1)}, u32[]{:S(2)}, u32[]{:S(2)}) collective-permute-start(f32[8,128]{1,0:T(8,128)S(1)} %shard_map.257.refs_0_), channel_id=1, source_target_pairs={{0,8},{4,12},{8,0},{12,4},{16,24},{20,28},{24,16},{28,20},{1,9},{5... | collective-permute-start | bytes 12296 | tf_op jit(solution)/shard_map/ppermute | solution.py:66
  25.9 1.8 %collective-permute-start.8 = (bf16[768,256]{1,0:T(8,128)(2,1)S(1)}, bf16[768,256]{1,0:T(8,128)(2,1)S(1)}, u32[]{:S(2)}, u32[]{:S(2)}) collective-permute-start(bf16[768,256]{1,0:T(8,128)(2,1)S(1)} %get-tuple-element.171), channel_id=1, source_target_pairs={{0,1},{1,0},{2,3},{3,2},{4,5},{5,4},{6,7},{7,6},{8,9},{9,8},{10,11... | collective-permute-start | bytes 1179656 | tf_op jit(solution)/shard_map/ppermute | solution.py:66
  28.0 13.2 %collective-permute-start.12 = (bf16[768,256]{1,0:T(8,128)(2,1)S(1)}, bf16[768,256]{1,0:T(8,128)(2,1)S(1)}, u32[]{:S(2)}, u32[]{:S(2)}) collective-permute-start(bf16[768,256]{1,0:T(8,128)(2,1)S(1)} %get-tuple-element.180), channel_id=1, source_target_pairs={{0,2},{1,3},{2,0},{3,1},{4,6},{5,7},{6,4},{7,5},{8,10},{9,11},{10,... | collective-permute-start | bytes 1179656 | tf_op jit(solution)/shard_map/ppermute | solution.py:66
  29.0 11.0 %collective-permute-start.10 = (bf16[192,512]{1,0:T(8,128)(2,1)S(1)}, bf16[192,512]{1,0:T(8,128)(2,1)S(1)}, u32[]{:S(2)}, u32[]{:S(2)}) collective-permute-start(bf16[192,512]{1,0:T(8,128)(2,1)S(1)} %copy-done.1), channel_id=1, source_target_pairs={{0,1},{1,0},{2,3},{3,2},{4,5},{5,4},{6,7},{7,6},{8,9},{9,8},{10,11... | collective-permute-start | bytes 589832 | tf_op jit(solution)/shard_map/ppermute | solution.py:66
  29.0 11.0 %collective-permute-start.11 = (bf16[192,512]{1,0:T(8,128)(2,1)S(1)}, bf16[192,512]{1,0:T(8,128)(2,1)S(1)}, u32[]{:S(2)}, u32[]{:S(2)}) collective-permute-start(bf16[192,512]{1,0:T(8,128)(2,1)S(1)} %collective-permute-done.6.c2), channel_id=1, source_target_pairs={{0,1},{1,0},{2,3},{3,2},{4,5},{5,4},{6,7},{7,6},{8,9},{9,8},{10,11... | collective-permute-start | bytes 589832 | tf_op jit(solution)/shard_map/ppermute | solution.py:66
  29.5 4.5 %collective-permute-start.9 = (f32[8,128]{1,0:T(8,128)S(1)}, f32[8,128]{1,0:T(8,128)S(1)}, u32[]{:S(2)}, u32[]{:S(2)}) collective-permute-start(f32[8,128]{1,0:T(8,128)S(1)} %shard_map.259.refs_0_), channel_id=1, source_target_pairs={{0,16},{4,20},{8,24},{12,28},{16,0},{20,4},{24,8},{28,12},{1,17},{... | collective-permute-start | bytes 12296 | tf_op jit(solution)/shard_map/ppermute | solution.py:66
  49.4 11.2 %collective-permute-start.15 = (bf16[768,256]{1,0:T(8,128)(2,1)S(1)}, bf16[768,256]{1,0:T(8,128)(2,1)S(1)}, u32[]{:S(2)}, u32[]{:S(2)}) collective-permute-start(bf16[768,256]{1,0:T(8,128)(2,1)S(1)} %get-tuple-element.201), channel_id=1, source_target_pairs={{0,2},{1,3},{2,0},{3,1},{4,6},{5,7},{6,4},{7,5},{8,10},{9,11},{10,... | collective-permute-start | bytes 1179656 | tf_op jit(solution)/shard_map/ppermute | solution.py:66
  50.5 15.1 %collective-permute-start.17 = (bf16[384,768]{1,0:T(8,128)(2,1)S(1)}, bf16[384,768]{1,0:T(8,128)(2,1)S(1)}, u32[]{:S(2)}, u32[]{:S(2)}) collective-permute-start(bf16[384,768]{1,0:T(8,128)(2,1)S(1)} %get-tuple-element.209), channel_id=1, source_target_pairs={{0,4},{4,0},{8,12},{12,8},{16,20},{20,16},{24,28},{28,24},{1,5},{5... | collective-permute-start | bytes 1769480 | tf_op jit(solution)/shard_map/ppermute | solution.py:66
  52.0 15.5 %collective-permute-start.18 = (bf16[384,768]{1,0:T(8,128)(2,1)S(1)}, bf16[384,768]{1,0:T(8,128)(2,1)S(1)}, u32[]{:S(2)}, u32[]{:S(2)}) collective-permute-start(bf16[384,768]{1,0:T(8,128)(2,1)S(1)} %get-tuple-element.212), channel_id=1, source_target_pairs={{0,8},{4,12},{8,0},{12,4},{16,24},{20,28},{24,16},{28,20},{1,9},{5... | collective-permute-start | bytes 1769480 | tf_op jit(solution)/shard_map/ppermute | solution.py:66
  54.5 8.5 %collective-permute-start.16 = (bf16[384,512]{1,0:T(8,128)(2,1)S(1)}, bf16[384,512]{1,0:T(8,128)(2,1)S(1)}, u32[]{:S(2)}, u32[]{:S(2)}) collective-permute-start(bf16[384,512]{1,0:T(8,128)(2,1)S(1)} %get-tuple-element.199), channel_id=1, source_target_pairs={{0,1},{1,0},{2,3},{3,2},{4,5},{5,4},{6,7},{7,6},{8,9},{9,8},{10,11... | collective-permute-start | bytes 1179656 | tf_op jit(solution)/shard_map/ppermute | solution.py:66
  63.0 5.9 %collective-permute-start.19 = (bf16[768,256]{1,0:T(8,128)(2,1)S(1)}, bf16[768,256]{1,0:T(8,128)(2,1)S(1)}, u32[]{:S(2)}, u32[]{:S(2)}) collective-permute-start(bf16[768,256]{1,0:T(8,128)(2,1)S(1)} %get-tuple-element.214.own), channel_id=1, source_target_pairs={{0,1},{1,0},{2,3},{3,2},{4,5},{5,4},{6,7},{7,6},{8,9},{9,8},{10,11... | collective-permute-start | bytes 1179656 | tf_op jit(solution)/shard_map/ppermute | solution.py:66
  63.2 12.1 %collective-permute-start.20 = (bf16[192,512]{1,0:T(8,128)(2,1)S(1)}, bf16[192,512]{1,0:T(8,128)(2,1)S(1)}, u32[]{:S(2)}, u32[]{:S(2)}) collective-permute-start(bf16[192,512]{1,0:T(8,128)(2,1)S(1)} %get-tuple-element.223), channel_id=1, source_target_pairs={{0,2},{1,3},{2,0},{3,1},{4,6},{5,7},{6,4},{7,5},{8,10},{9,11},{10,... | collective-permute-start | bytes 589832 | tf_op jit(solution)/shard_map/ppermute | solution.py:66
  65.8 10.4 %collective-permute-start.21 = (bf16[192,768]{1,0:T(8,128)(2,1)S(1)}, bf16[192,768]{1,0:T(8,128)(2,1)S(1)}, u32[]{:S(2)}, u32[]{:S(2)}) collective-permute-start(bf16[192,768]{1,0:T(8,128)(2,1)S(1)} %get-tuple-element.227), channel_id=1, source_target_pairs={{0,8},{4,12},{8,0},{12,4},{16,24},{20,28},{24,16},{28,20},{1,9},{5... | collective-permute-start | bytes 884744 | tf_op jit(solution)/shard_map/ppermute | solution.py:66
  67.6 12.1 %collective-permute-start.22 = (bf16[192,768]{1,0:T(8,128)(2,1)S(1)}, bf16[192,768]{1,0:T(8,128)(2,1)S(1)}, u32[]{:S(2)}, u32[]{:S(2)}) collective-permute-start(bf16[192,768]{1,0:T(8,128)(2,1)S(1)} %get-tuple-element.237), channel_id=1, source_target_pairs={{0,4},{4,0},{8,12},{12,8},{16,20},{20,16},{24,28},{28,24},{1,5},{5... | collective-permute-start | bytes 884744 | tf_op jit(solution)/shard_map/ppermute | solution.py:66
  73.4 9.0 %collective-permute-start.23 = (bf16[192,768]{1,0:T(8,128)(2,1)S(1)}, bf16[192,768]{1,0:T(8,128)(2,1)S(1)}, u32[]{:S(2)}, u32[]{:S(2)}) collective-permute-start(bf16[192,768]{1,0:T(8,128)(2,1)S(1)} %get-tuple-element.240), channel_id=1, source_target_pairs={{0,4},{4,0},{8,12},{12,8},{16,20},{20,16},{24,28},{28,24},{1,5},{5... | collective-permute-start | bytes 884744 | tf_op jit(solution)/shard_map/ppermute | solution.py:66
  74.3 10.0 %collective-permute-start.24 = (bf16[192,768]{1,0:T(8,128)(2,1)S(1)}, bf16[192,768]{1,0:T(8,128)(2,1)S(1)}, u32[]{:S(2)}, u32[]{:S(2)}) collective-permute-start(bf16[192,768]{1,0:T(8,128)(2,1)S(1)} %get-tuple-element.243), channel_id=1, source_target_pairs={{0,8},{4,12},{8,0},{12,4},{16,24},{20,28},{24,16},{28,20},{1,9},{5... | collective-permute-start | bytes 884744 | tf_op jit(solution)/shard_map/ppermute | solution.py:66
  79.1 6.2 %collective-permute-start.25 = (bf16[384,512]{1,0:T(8,128)(2,1)S(1)}, bf16[384,512]{1,0:T(8,128)(2,1)S(1)}, u32[]{:S(2)}, u32[]{:S(2)}) collective-permute-start(bf16[384,512]{1,0:T(8,128)(2,1)S(1)} %get-tuple-element.235), channel_id=1, source_target_pairs={{0,1},{1,0},{2,3},{3,2},{4,5},{5,4},{6,7},{7,6},{8,9},{9,8},{10,11... | collective-permute-start | bytes 1179656 | tf_op jit(solution)/shard_map/ppermute | solution.py:66
  79.2 7.8 %collective-permute-start.26 = (f32[8,768]{1,0:T(8,128)S(1)}, f32[8,768]{1,0:T(8,128)S(1)}, u32[]{:S(2)}, u32[]{:S(2)}) collective-permute-start(f32[8,768]{1,0:T(8,128)S(1)} %get-tuple-element.248.refs_0_), channel_id=1, source_target_pairs={{0,1},{1,0},{2,3},{3,2},{4,5},{5,4},{6,7},{7,6},{8,9},{9,8},{10,11... | collective-permute-start | bytes 73736 | tf_op jit(solution)/shard_map/ppermute | solution.py:66
  79.7 13.7 %collective-permute-start.27 = (bf16[96,768]{1,0:T(8,128)(2,1)S(1)}, bf16[96,768]{1,0:T(8,128)(2,1)S(1)}, u32[]{:S(2)}, u32[]{:S(2)}) collective-permute-start(bf16[96,768]{1,0:T(8,128)(2,1)S(1)} %get-tuple-element.250), channel_id=1, source_target_pairs={{0,16},{4,20},{8,24},{12,28},{16,0},{20,4},{24,8},{28,12},{1,17},{... | collective-permute-start | bytes 442376 | tf_op jit(solution)/shard_map/ppermute | solution.py:66
  82.4 13.6 %collective-permute-start.28 = (bf16[96,768]{1,0:T(8,128)(2,1)S(1)}, bf16[96,768]{1,0:T(8,128)(2,1)S(1)}, u32[]{:S(2)}, u32[]{:S(2)}) collective-permute-start(bf16[96,768]{1,0:T(8,128)(2,1)S(1)} %get-tuple-element.252), channel_id=1, source_target_pairs={{0,16},{4,20},{8,24},{12,28},{16,0},{20,4},{24,8},{28,12},{1,17},{... | collective-permute-start | bytes 442376 | tf_op jit(solution)/shard_map/ppermute | solution.py:66
  84.5 15.6 %collective-permute-start.30 = (bf16[96,768]{1,0:T(8,128)(2,1)S(1)}, bf16[96,768]{1,0:T(8,128)(2,1)S(1)}, u32[]{:S(2)}, u32[]{:S(2)}) collective-permute-start(bf16[96,768]{1,0:T(8,128)(2,1)S(1)} %get-tuple-element.257), channel_id=1, source_target_pairs={{0,4},{4,0},{8,12},{12,8},{16,20},{20,16},{24,28},{28,24},{1,5},{5... | collective-permute-start | bytes 442376 | tf_op jit(solution)/shard_map/ppermute | solution.py:66
  85.4 13.7 %collective-permute-start.29 = (bf16[96,768]{1,0:T(8,128)(2,1)S(1)}, bf16[96,768]{1,0:T(8,128)(2,1)S(1)}, u32[]{:S(2)}, u32[]{:S(2)}) collective-permute-start(bf16[96,768]{1,0:T(8,128)(2,1)S(1)} %get-tuple-element.254), channel_id=1, source_target_pairs={{0,8},{4,12},{8,0},{12,4},{16,24},{20,28},{24,16},{28,20},{1,9},{5... | collective-permute-start | bytes 442376 | tf_op jit(solution)/shard_map/ppermute | solution.py:66
  87.1 13.1 %collective-permute-start.31 = (f32[8,768]{1,0:T(8,128)S(1)}, f32[8,768]{1,0:T(8,128)S(1)}, u32[]{:S(2)}, u32[]{:S(2)}) collective-permute-start(f32[8,768]{1,0:T(8,128)S(1)} %shard_map.284.refs_0_), channel_id=1, source_target_pairs={{0,2},{1,3},{2,0},{3,1},{4,6},{5,7},{6,4},{7,5},{8,10},{9,11},{10,... | collective-permute-start | bytes 73736 | tf_op jit(solution)/shard_map/ppermute | solution.py:66
  96.1 19.6 %collective-permute-start.34 = (bf16[96,768]{1,0:T(8,128)(2,1)S(1)}, bf16[96,768]{1,0:T(8,128)(2,1)S(1)}, u32[]{:S(2)}, u32[]{:S(2)}) collective-permute-start(bf16[96,768]{1,0:T(8,128)(2,1)S(1)} %shard_map.286.refs_0_), channel_id=1, source_target_pairs={{0,16},{4,20},{8,24},{12,28},{16,0},{20,4},{24,8},{28,12},{1,17},{... | collective-permute-start | bytes 442376 | tf_op jit(solution)/shard_map/ppermute | solution.py:66
  96.2 19.4 %collective-permute-start.33 = (bf16[96,768]{1,0:T(8,128)(2,1)S(1)}, bf16[96,768]{1,0:T(8,128)(2,1)S(1)}, u32[]{:S(2)}, u32[]{:S(2)}) collective-permute-start(bf16[96,768]{1,0:T(8,128)(2,1)S(1)} %shard_map.285.refs_0_), channel_id=1, source_target_pairs={{0,16},{4,20},{8,24},{12,28},{16,0},{20,4},{24,8},{28,12},{1,17},{... | collective-permute-start | bytes 442376 | tf_op jit(solution)/shard_map/ppermute | solution.py:66
  99.1 5.7 %collective-permute-start.32 = (bf16[192,512]{1,0:T(8,128)(2,1)S(1)}, bf16[192,512]{1,0:T(8,128)(2,1)S(1)}, u32[]{:S(2)}, u32[]{:S(2)}) collective-permute-start(bf16[192,512]{1,0:T(8,128)(2,1)S(1)} %get-tuple-element.261), channel_id=1, source_target_pairs={{0,2},{1,3},{2,0},{3,1},{4,6},{5,7},{6,4},{7,5},{8,10},{9,11},{10,... | collective-permute-start | bytes 589832 | tf_op jit(solution)/shard_map/ppermute | solution.py:66
  100.2 22.3 %collective-permute-start.37 = (f32[8,768]{1,0:T(8,128)S(1)}, f32[8,768]{1,0:T(8,128)S(1)}, u32[]{:S(2)}, u32[]{:S(2)}) collective-permute-start(f32[8,768]{1,0:T(8,128)S(1)} %shard_map.289.sums.refs_0_), channel_id=1, source_target_pairs={{0,4},{4,0},{8,12},{12,8},{16,20},{20,16},{24,28},{28,24},{1,5},{5... | collective-permute-start | bytes 73736 | tf_op jit(solution)/shard_map/ppermute | solution.py:66
  101.9 16.3 %collective-permute-start.36 = (bf16[48,768]{1,0:T(8,128)(2,1)S(1)}, bf16[48,768]{1,0:T(8,128)(2,1)S(1)}, u32[]{:S(2)}, u32[]{:S(2)}) collective-permute-start(bf16[48,768]{1,0:T(8,128)(2,1)S(1)} %get-tuple-element.268), channel_id=1, source_target_pairs={{0,16},{4,20},{8,24},{12,28},{16,0},{20,4},{24,8},{28,12},{1,17},{... | collective-permute-start | bytes 221192 | tf_op jit(solution)/shard_map/ppermute | solution.py:66
  104.8 13.4 %collective-permute-start.35 = (bf16[48,768]{1,0:T(8,128)(2,1)S(1)}, bf16[48,768]{1,0:T(8,128)(2,1)S(1)}, u32[]{:S(2)}, u32[]{:S(2)}) collective-permute-start(bf16[48,768]{1,0:T(8,128)(2,1)S(1)} %get-tuple-element.266), channel_id=1, source_target_pairs={{0,16},{4,20},{8,24},{12,28},{16,0},{20,4},{24,8},{28,12},{1,17},{... | collective-permute-start | bytes 221192 | tf_op jit(solution)/shard_map/ppermute | solution.py:66
  115.6 12.2 %collective-permute-start.40 = (bf16[192,768]{1,0:T(8,128)(2,1)S(1)}, bf16[192,768]{1,0:T(8,128)(2,1)S(1)}, u32[]{:S(2)}, u32[]{:S(2)}) collective-permute-start(bf16[192,768]{1,0:T(8,128)(2,1)S(1)} %shard_map.291.refs_0_), channel_id=1, source_target_pairs={{0,8},{4,12},{8,0},{12,4},{16,24},{20,28},{24,16},{28,20},{1,9},{5... | collective-permute-start | bytes 884744 | tf_op jit(solution)/shard_map/ppermute | solution.py:66
  118.3 9.5 %collective-permute-start.39 = (bf16[48,768]{1,0:T(8,128)(2,1)S(1)}, bf16[48,768]{1,0:T(8,128)(2,1)S(1)}, u32[]{:S(2)}, u32[]{:S(2)}) collective-permute-start(bf16[48,768]{1,0:T(8,128)(2,1)S(1)} %shard_map.294.refs_0_), channel_id=1, source_target_pairs={{0,16},{4,20},{8,24},{12,28},{16,0},{20,4},{24,8},{28,12},{1,17},{... | collective-permute-start | bytes 221192 | tf_op jit(solution)/shard_map/ppermute | solution.py:66
  118.4 9.3 %collective-permute-start.38 = (bf16[48,768]{1,0:T(8,128)(2,1)S(1)}, bf16[48,768]{1,0:T(8,128)(2,1)S(1)}, u32[]{:S(2)}, u32[]{:S(2)}) collective-permute-start(bf16[48,768]{1,0:T(8,128)(2,1)S(1)} %shard_map.293.refs_0_), channel_id=1, source_target_pairs={{0,16},{4,20},{8,24},{12,28},{16,0},{20,4},{24,8},{28,12},{1,17},{... | collective-permute-start | bytes 221192 | tf_op jit(solution)/shard_map/ppermute | solution.py:66
  121.3 8.3 %collective-permute-start.41 = (bf16[192,768]{1,0:T(8,128)(2,1)S(1)}, bf16[192,768]{1,0:T(8,128)(2,1)S(1)}, u32[]{:S(2)}, u32[]{:S(2)}) collective-permute-start(bf16[192,768]{1,0:T(8,128)(2,1)S(1)} %shard_map.292.refs_0_), channel_id=1, source_target_pairs={{0,4},{4,0},{8,12},{12,8},{16,20},{20,16},{24,28},{28,24},{1,5},{5... | collective-permute-start | bytes 884744 | tf_op jit(solution)/shard_map/ppermute | solution.py:66
  127.7 18.6 %collective-permute-start.43 = (bf16[96,768]{1,0:T(8,128)(2,1)S(1)}, bf16[96,768]{1,0:T(8,128)(2,1)S(1)}, u32[]{:S(2)}, u32[]{:S(2)}) collective-permute-start(bf16[96,768]{1,0:T(8,128)(2,1)S(1)} %shard_map.296.refs_0_), channel_id=1, source_target_pairs={{0,8},{4,12},{8,0},{12,4},{16,24},{20,28},{24,16},{28,20},{1,9},{5... | collective-permute-start | bytes 442376 | tf_op jit(solution)/shard_map/ppermute | solution.py:66
  127.8 23.8 %collective-permute-start.46 = (bf16[384,768]{1,0:T(8,128)(2,1)S(1)}, bf16[384,768]{1,0:T(8,128)(2,1)S(1)}, u32[]{:S(2)}, u32[]{:S(2)}) collective-permute-start(bf16[384,768]{1,0:T(8,128)(2,1)S(1)} %shard_map.298.refs_0_), channel_id=1, source_target_pairs={{0,4},{4,0},{8,12},{12,8},{16,20},{20,16},{24,28},{28,24},{1,5},{5... | collective-permute-start | bytes 1769480 | tf_op jit(solution)/shard_map/ppermute | solution.py:66
  129.6 23.5 %collective-permute-start.47 = (bf16[384,768]{1,0:T(8,128)(2,1)S(1)}, bf16[384,768]{1,0:T(8,128)(2,1)S(1)}, u32[]{:S(2)}, u32[]{:S(2)}) collective-permute-start(bf16[384,768]{1,0:T(8,128)(2,1)S(1)} %shard_map.299.refs_0_), channel_id=1, source_target_pairs={{0,8},{4,12},{8,0},{12,4},{16,24},{20,28},{24,16},{28,20},{1,9},{5... | collective-permute-start | bytes 1769480 | tf_op jit(solution)/shard_map/ppermute | solution.py:66
  131.7 14.1 %collective-permute-start.42 = (f32[8,768]{1,0:T(8,128)S(1)}, f32[8,768]{1,0:T(8,128)S(1)}, u32[]{:S(2)}, u32[]{:S(2)}) collective-permute-start(f32[8,768]{1,0:T(8,128)S(1)} %shard_map.295.refs_0_), channel_id=1, source_target_pairs={{0,8},{4,12},{8,0},{12,4},{16,24},{20,28},{24,16},{28,20},{1,9},{5... | collective-permute-start | bytes 73736 | tf_op jit(solution)/shard_map/ppermute | solution.py:66
  131.8 14.5 %collective-permute-start.44 = (bf16[96,768]{1,0:T(8,128)(2,1)S(1)}, bf16[96,768]{1,0:T(8,128)(2,1)S(1)}, u32[]{:S(2)}, u32[]{:S(2)}) collective-permute-start(bf16[96,768]{1,0:T(8,128)(2,1)S(1)} %shard_map.297.refs_0_), channel_id=1, source_target_pairs={{0,4},{4,0},{8,12},{12,8},{16,20},{20,16},{24,28},{28,24},{1,5},{5... | collective-permute-start | bytes 442376 | tf_op jit(solution)/shard_map/ppermute | solution.py:66
  145.8 5.0 %collective-permute-start.45 = (f32[8,768]{1,0:T(8,128)S(1)}, f32[8,768]{1,0:T(8,128)S(1)}, u32[]{:S(2)}, u32[]{:S(2)}) collective-permute-start(f32[8,768]{1,0:T(8,128)S(1)} %shard_map.300.refs_0_), channel_id=1, source_target_pairs={{0,16},{4,20},{8,24},{12,28},{16,0},{20,4},{24,8},{28,12},{1,17},{... | collective-permute-start | bytes 73736 | tf_op jit(solution)/shard_map/ppermute | solution.py:66
  146.3 8.4 %collective-permute-start.49 = (bf16[192,768]{1,0:T(8,128)(2,1)S(1)}, bf16[192,768]{1,0:T(8,128)(2,1)S(1)}, u32[]{:S(2)}, u32[]{:S(2)}) collective-permute-start(bf16[192,768]{1,0:T(8,128)(2,1)S(1)} %shard_map.302.refs_2_), channel_id=1, source_target_pairs={{0,8},{4,12},{8,0},{12,4},{16,24},{20,28},{24,16},{28,20},{1,9},{5... | collective-permute-start | bytes 884744 | tf_op jit(solution)/shard_map/ppermute | solution.py:66
  148.2 6.8 %collective-permute-start.48 = (bf16[192,768]{1,0:T(8,128)(2,1)S(1)}, bf16[192,768]{1,0:T(8,128)(2,1)S(1)}, u32[]{:S(2)}, u32[]{:S(2)}) collective-permute-start(bf16[192,768]{1,0:T(8,128)(2,1)S(1)} %shard_map.301.refs_0_), channel_id=1, source_target_pairs={{0,4},{4,0},{8,12},{12,8},{16,20},{20,16},{24,28},{28,24},{1,5},{5... | collective-permute-start | bytes 884744 | tf_op jit(solution)/shard_map/ppermute | solution.py:66
  (17 other events, 62.9 us)

commit v5 on v4

--- a/solution.py
+++ b/solution.py
@@ -216,8 +216,9 @@
     return [value] + [stream.send(value, e * stride) for e in range(1, radix)]
 
 
-def place_kernel(streams, bounds, me_ref, *refs):
+def place_kernel(all_tokens, streams, bounds, me_ref, sums, *refs):
     pieces, outs = list(refs[: -len(bounds)]), refs[-len(bounds) :]
+    scale = loss_scale(all_tokens, sums, outs[0].shape[1])
     for stream in streams:
         for offsets in stream.parts():
             piece = pieces.pop(0)
@@ -228,7 +229,9 @@
 
                     def store(out=out, first=first, piece=piece, place=place, row=row, size=stream.chunk):
                         at = pl.multiple_of(row - first, 16)
-                        out[pl.ds(at, size), :] = piece[place * size : (place + 1) * size].astype(F32)
+                        out[pl.ds(at, size), :] = (
+                            piece[place * size : (place + 1) * size].astype(F32) * scale
+                        )
 
                     if len(bounds) == 1:
                         store()
@@ -236,75 +239,75 @@
                         pl.when((row >= first) & (row < last))(store)
 
 
-def place(me, streams, pieces, sizes):
+def place(all_tokens, me, sums, streams, pieces, sizes):
     columns = pieces[0].shape[1]
     bounds, start = [], 0
     for size in sizes:
         bounds.append((start, start + size))
         start += size
     outs = tuple(shape(size, columns) for size in sizes)
-    return kernel(functools.partial(place_kernel, streams, bounds), outs, [me], pieces)
-
-
-def live_row(all_tokens, counts_ref, total_ref, width, first):
-    scale = jnp.full((1, width), all_tokens, F32) / jnp.broadcast_to(total_ref[0:1, 0:1], (1, width))
+    return kernel(functools.partial(place_kernel, all_tokens, streams, bounds), outs, [me], [sums, *pieces])
+
+
+def live_row(counts_ref, width, first):
     place = lax.broadcasted_iota(jnp.int32, (1, width), 1) + first
-    return jnp.where(place < counts_ref[0], scale, 0.0)
-
-
-def history_block(live, mix_ref, d_mix_ref, history_ref, cot_ref, running_ref, d_history_ref):
-    layers, block, tokens = history_ref.shape
-    for i in range(block // STEP):
-        rows = slice(i * STEP, (i + 1) * STEP)
-        grad = cot_ref[rows].astype(F32) * live
-        running = jnp.zeros_like(grad)
-        for j in range(layers):
-            layer = history_ref[j, rows].astype(F32)
-            weight = mix_ref[j]
-            running = running + weight * layer
-            d_history_ref[j, rows] = (weight * grad).astype(BF16)
-            terms = grad * layer
-            terms = terms[: STEP // 2] + terms[STEP // 2 :]
-            d_mix_ref[j] += sum(terms[:, k : k + 128] for k in range(0, tokens, 128))
-        running_ref[rows] = running
-
-
-def history_kernel(
-    all_tokens, block, mix_ref, counts_ref, cot_ref, total_ref, history_ref, running_ref, d_history_ref, d_mix_ref
-):
+    return jnp.where(place < counts_ref[0], 1.0, 0.0)
+
+
+def loss_scale(all_tokens, sums, width):
+    return jnp.full((1, width), all_tokens, F32) / jnp.broadcast_to(sums[7:8, 0:1], (1, width))
+
+
+def history_kernel(block, mix_ref, counts_ref, cot_ref, history_ref, running_ref, d_mix_ref):
     layers, features, tokens = history_ref.shape
-    live = live_row(all_tokens, counts_ref, total_ref, tokens, 0)
+    live = live_row(counts_ref, tokens, 0)
     d_mix_ref[...] = jnp.zeros_like(d_mix_ref)
 
-    def body(history_part, d_history_part):
-        at = pl.multiple_of(pl.program_id(0) * block, block)
-        history_block(
-            live, mix_ref, d_mix_ref, history_part, cot_ref.at[pl.ds(at, block)], running_ref.at[pl.ds(at, block)],
-            d_history_part,
-        )
+    def body(history_part):
+        for i in range(block // STEP):
+            rows = slice(i * STEP, (i + 1) * STEP)
+            own = pl.ds(pl.multiple_of(pl.program_id(0) * block + i * STEP, STEP), STEP)
+            grad = cot_ref[own].astype(F32) * live
+            running = jnp.zeros_like(grad)
+            for j in range(layers):
+                layer = history_part[j, rows].astype(F32)
+                running = running + mix_ref[j] * layer
+                terms = grad * layer
+                terms = terms[: STEP // 2] + terms[STEP // 2 :]
+                d_mix_ref[j] += sum(terms[:, k : k + 128] for k in range(0, tokens, 128))
+            running_ref[own] = running
 
     whole = pl.BlockSpec((layers, block, tokens), lambda i: (0, i, 0))
-    pltpu.emit_pipeline(body, grid=(features // block,), in_specs=[whole], out_specs=[whole])(
-        history_ref, d_history_ref
-    )
-
-
-def mix_history(all_tokens, mix_weights, counts, total, history, cotangent):
-    layers, features, tokens = history.shape
+    pltpu.emit_pipeline(body, grid=(features // block,), in_specs=[whole])(history_ref)
+
+
+def d_history_kernel(all_tokens, block, mix_ref, counts_ref, cot_ref, sums, d_history_ref):
+    layers, features, tokens = d_history_ref.shape
+    factor = live_row(counts_ref, tokens, 0) * loss_scale(all_tokens, sums, tokens)
+
+    def body(part):
+        for i in range(block // STEP):
+            rows = slice(i * STEP, (i + 1) * STEP)
+            own = pl.ds(pl.multiple_of(pl.program_id(0) * block + i * STEP, STEP), STEP)
+            grad = cot_ref[own].astype(F32) * factor
+            for j in range(layers):
+                part[j, rows] = (mix_ref[j] * grad).astype(BF16)
+
+    whole = pl.BlockSpec((layers, block, tokens), lambda i: (0, i, 0))
+    pltpu.emit_pipeline(body, grid=(features // block,), out_specs=[whole])(d_history_ref)
+
+
+def history_call(body, outs, in_hbm, out_hbm, scalars, arrays):
     vmem, hbm = pl.BlockSpec(memory_space=pltpu.VMEM), pl.BlockSpec(memory_space=pltpu.HBM)
-    smem = pl.BlockSpec(memory_space=pltpu.SMEM)
+    arrays = [after(arrays[0], Order.last), *arrays[1:]]
     found = pl.pallas_call(
-        functools.partial(history_kernel, all_tokens, 32),
-        out_shape=(
-            shape(features, tokens),
-            shape(*history.shape, kind=BF16),
-            shape(layers, STEP // 2, 128),
-        ),
-        in_specs=[smem, smem, vmem, vmem, hbm],
-        out_specs=(vmem, hbm, vmem),
+        body,
+        out_shape=outs,
+        in_specs=[pl.BlockSpec(memory_space=pltpu.SMEM)] * len(scalars) + [hbm if h else vmem for h in in_hbm],
+        out_specs=tuple(hbm if h else vmem for h in out_hbm),
         compiler_params=pltpu.CompilerParams(vmem_limit_bytes=12 * 1024 * 1024),
         cost_estimate=pl.CostEstimate(flops=Order.cost, bytes_accessed=1024, transcendentals=0),
-    )(mix_weights, counts, after(cotangent, Order.last), total, history)
+    )(*scalars, *arrays)
     Order.last = found[0]
     return found
 
@@ -320,27 +323,55 @@
     return mean, lax.rsqrt(column_sum(each_rows(count, squares, zero)) / count + EPSILON)
 
 
-def prepare_kernel(counts_ref, positions, rates, g1, b1, g2, b2, count, norms, cosine, sine):
-    count[...] = jnp.zeros(count.shape, F32) + counts_ref[0].astype(F32)
+def prepare_kernel(now, *refs):
+    sources, (norms, cosine, sine), places, sem = refs[:6], refs[6:9], refs[9:15], refs[15]
+    copies = [pltpu.make_async_copy(*pair, sem.at[i]) for i, pair in enumerate(zip(sources, places))]
+    for copy in copies:
+        copy.start()
     norms[...] = jnp.zeros_like(norms)
-    for i, ref in enumerate((g1, b1, g2, b2)):
+    for copy in copies:
+        copy.wait()
+    positions, rates, *vectors = places
+    for i, ref in enumerate(vectors):
         norms[i : i + 1, : ref.shape[1]] = ref[...]
     angles = positions[...].astype(F32) * rates[...]
     cosine[...] = jnp.cos(angles)
     sine[...] = jnp.sin(angles)
 
 
+def prepare(now, *sources):
+    tokens, part = sources[0].shape[1], sources[2].shape[1]
+    rates = sources[1].shape[0]
+    vmem = pl.BlockSpec(memory_space=pltpu.VMEM)
+    found = pl.pallas_call(
+        prepare_kernel,
+        out_shape=(shape(8, -(-part // 128) * 128), shape(rates, tokens), shape(rates, tokens)),
+        in_specs=[vmem] + [pl.BlockSpec(memory_space=pltpu.HBM)] * len(sources),
+        out_specs=(vmem,) * 3,
+        scratch_shapes=[pltpu.VMEM(v.shape, v.dtype) for v in sources] + [pltpu.SemaphoreType.DMA((len(sources),))],
+        compiler_params=pltpu.CompilerParams(vmem_limit_bytes=4 * 1024 * 1024),
+        cost_estimate=pl.CostEstimate(flops=Order.cost, bytes_accessed=1024, transcendentals=0),
+    )(now, *(pltpu.with_memory_space_constraint(v, pltpu.HBM) for v in sources))
+    Order.last = found[0]
+    return found
+
+
+def norms_kernel(at_ref, n01, n23, norms):
+    part = norms.shape[0] // 4
+    near, far = n01[...].T, n23[...].T
+    for e, norm in enumerate((near, near, far, far)):
+        rows = pl.ds(pl.multiple_of((at_ref[0] ^ e) * part, 64), part)
+        norms[rows, :] = norm[:part, 8 * (e % 2) : 8 * (e % 2) + 8]
+
+
 def project_kernel(
-    at_ref, x0, x1, x2, x3, n01, n23, cosine, sine, w_qkv, x_all, norms, normed, stats, qkv, project
+    at_ref, x0, x1, x2, x3, norms, cosine, sine, w_qkv, w_out, x_all, normed, stats, qkv, project
 ):
     at = at_ref[0]
     part, tokens = x0.shape
     model = w_qkv.shape[1]
-    near, far = n01[...].T, n23[...].T
-    for e, (piece, norm) in enumerate(((x0, near), (x1, near), (x2, far), (x3, far))):
-        rows = pl.ds(pl.multiple_of((at ^ e) * part, 64), part)
-        x_all[rows, :] = piece[...]
-        norms[rows, :] = norm[:part, 8 * (e % 2) : 8 * (e % 2) + 8]
+    for e, piece in enumerate((x0, x1, x2, x3)):
+        x_all[pl.ds(pl.multiple_of((at ^ e) * part, 64), part), :] = piece[...]
     mean, scale = spread_of(lambda i: x_all[rows_at(i), :].astype(F32), model, tokens)
     stats[0:1] = mean
     stats[1:2] = scale
@@ -410,7 +441,7 @@
 
 
 def output_gradient_kernel(
-    all_tokens, at_ref, self_ref, counts_ref, c0, c1, c2, c3, total_ref, w_down, g_out, d_active, cot_half, cot_all
+    at_ref, self_ref, counts_ref, c0, c1, c2, c3, w_down, g_out, d_active, cot_half, cot_all
 ):
     at = at_ref[0]
     part, tokens = c0.shape
@@ -419,7 +450,7 @@
         cot_all[pl.ds(pl.multiple_of((at ^ e) * part, 64), part), :] = piece[...]
     for place, side in enumerate((at % 2, 1 - at % 2)):
         now = pl.ds(pl.multiple_of(side * half, half), half)
-        factor = live_row(all_tokens, counts_ref, total_ref, half, side * half)
+        factor = live_row(counts_ref, half, side * half)
 
         def scale(i, _, now=now, factor=factor, place=place):
             rows = rows_at(i)
@@ -502,7 +533,7 @@
 
 
 def middle_gradient_kernel(
-    all_tokens, at_ref, self_ref, counts_ref, chip, received, total_ref, middle, stats, cot_half, norms,
+    at_ref, self_ref, counts_ref, chip, received, middle, stats, cot_half, norms,
     d_middle, g_mid, gains, d_normed, gain_sums, bias_sums,
 ):
     model, half = chip.shape
@@ -521,7 +552,7 @@
         return acc[0] + grad * gain, acc[1] + both * gain
 
     first, second = (column_sum(v) / model for v in each_rows(model, sums, (zero, zero)))
-    factor = self_ref[0] * live_row(all_tokens, counts_ref, total_ref, half, (at_ref[0] % 2) * half)
+    factor = self_ref[0] * live_row(counts_ref, half, (at_ref[0] % 2) * half)
 
     def finish(i, _):
         rows = rows_at(i)
@@ -589,7 +620,7 @@
 
 
 def input_gradient_kernel(
-    at_ref, d_project, w_qkv, x_all, stats, d_middle, norms, gains, mix, send, keep, sums, total, gain_sums, bias_sums
+    width, at_ref, counts_ref, d_project, w_qkv, x_all, stats, d_middle, norms, gains, send, keep, sums, total, gain_sums, bias_sums
 ):
     at = at_ref[0]
     model, half = d_middle.shape
@@ -621,15 +652,15 @@
     sums[2:4] = 0.5 * gains[...]
     sums[4:5, :tokens] = column_sum(first) / model
     sums[5:6, :tokens] = column_sum(second) / model
-    sums[6:7, :128] = mix[...]
+    sums[7:8] = jnp.zeros((1, model), F32) + counts_ref[0].astype(F32) / width
 
 
 def mixed_kernel(
-    all_tokens, self_ref, counts_ref, chip, received, total_ref, running, cotangent, d_mix, mixed, row, table
+    self_ref, counts_ref, chip, received, running, cotangent, d_mix, sums, mixed, all_sums, table
 ):
     layers = d_mix.shape[0]
     part, tokens = chip.shape
-    live = live_row(all_tokens, counts_ref, total_ref, tokens, 0)
+    live = live_row(counts_ref, tokens, 0)
 
     def body(i, acc):
         rows = rows_at(i)
@@ -641,31 +672,43 @@
     table[...] = jnp.zeros_like(table)
     table[:layers] = jnp.sum(d_mix[...], axis=1)
     table[layers : layers + 1] = column_sum(found)
-    row[...] = as_row(table)
-
-
-def ends_kernel(layers, width, at_ref, sums, d_mix, d_self, *ends):
+    all_sums[...] = sums[...]
+    all_sums[6:7, :128] = as_row(table)
+
+
+def ends_kernel(all_tokens, layers, width, at_ref, sums, d_mix, d_self, *ends):
     part = ends[0].shape[1]
-    d_mix[...] = sums[6:7, :layers]
-    d_self[...] = sums[6:7, layers : layers + 1]
+    scale = loss_scale(all_tokens, sums, sums.shape[1])
+    d_mix[...] = sums[6:7, :layers] * scale[:, :layers]
+    d_self[...] = sums[6:7, layers : layers + 1] * scale[:, :1]
     for i, end in enumerate(ends):
-        found = sums[i : i + 1, :part]
+        scaled = sums[i : i + 1] * scale
+        found = scaled[:, :part]
         for w in range(1, width):
-            found = jnp.where(at_ref[0] == w, sums[i : i + 1, w * part : (w + 1) * part], found)
+            found = jnp.where(at_ref[0] == w, scaled[:, w * part : (w + 1) * part], found)
         end[...] = found
 
 
-def d_input_kernel(chip, received, x_in, stats, sums, d_input):
+def d_input_kernel(chip, received, x_in, stats, row_sums, found):
     part, tokens = chip.shape
     mean, scale = stats[0:1], stats[1:2]
-    first, second = sums[4:5, :tokens], sums[5:6, :tokens]
+    first, second = row_sums[4:5, :tokens], row_sums[5:6, :tokens]
 
     def body(i, _):
         rows = rows_at(i)
         xhat = (x_in[rows, :].astype(F32) - mean) * scale
-        d_input[rows, :] = chip[rows, :] + received[rows, :].astype(F32) - scale * (first + xhat * second)
+        found[rows, :] = chip[rows, :] + received[rows, :].astype(F32) - scale * (first + xhat * second)
 
     each_rows(part, body)
+
+
+def scale_kernel(all_tokens, found, sums, d_input):
+    factor = loss_scale(all_tokens, sums, found.shape[1])
+
+    def body(i, _):
+        d_input[rows_at(i), :] = found[rows_at(i), :] * factor
+
+    each_rows(found.shape[0], body)
 
 
 def local(
@@ -695,7 +738,7 @@
     all_tokens = float(tokens * row_devices)
     at = lax.axis_index("width").astype(jnp.int32)[None]
     me = lax.axis_index("rows").astype(jnp.int32)[None]
-    Order.last, Order.cost = None, 10**9
+    Order.last, Order.cost = None, 10**8
     to_width = lambda value, offset: xor_send(value, "width", width, offset)
     to_row = lambda value, offset: xor_send(value, "rows", row_devices, offset)
     w_qkv = w_qkv.reshape(3 * part, model)
@@ -703,53 +746,33 @@
     x_in, cotangent, counts = after((x_in, cotangent, counts), at, me)
 
     x_far, x_near = to_width(x_in, 2), to_width(x_in, 1)
-    cot_now = after(cotangent, x_near)
-    cot_far, cot_near = to_width(cot_now, 2), to_width(cot_now, 1)
-    live_total, norms, cosine, sine = kernel(
-        prepare_kernel,
-        (
-            shape(8, 128),
-            shape(8, -(-part // 128) * 128),
-            shape(HEAD_DIM // 2, tokens),
-            shape(HEAD_DIM // 2, tokens),
-        ),
-        [counts],
-        [
-            after(positions[None, :], x_near),
-            jnp.asarray(rates[:, None], F32),
-            *(v[None, :] for v in (first_norm_gain, first_norm_bias, second_norm_gain, second_norm_bias)),
-        ],
+    norms, cosine, sine = prepare(
+        x_near,
+        positions[None, :],
+        jnp.asarray(rates[:, None], F32),
+        *(v[None, :] for v in (first_norm_gain, first_norm_bias, second_norm_gain, second_norm_bias)),
     )
     strides = [1 << i for i in range(row_devices.bit_length() - 1)]
-
-    def grow_total(value, stride):
-        return add([value, to_row(value, stride)], (0, 8, F32))[0]
-
-    Order.cost = 10**9
     norms_near = join([norms, to_width(norms, 1)])
     norms_far = to_width(norms_near, 2)
-    Order.cost = 10**10
-    live_total = grow_total(live_total, strides[0])
-    x_both = to_width(after(x_far, norms_near), 1)
-
-    Order.cost = 10**8
-    x_all, norms, normed_one, stats_one, qkv = kernel(
+    norms = kernel(norms_kernel, shape(model, 8), [at], [norms_near, norms_far])
+    x_both = to_width(after(x_far, norms), 1)
+    cot_now = after(cotangent, x_far)
+    cot_far, cot_near = to_width(cot_now, 2), to_width(cot_now, 1)
+
+    x_all, normed_one, stats_one, qkv = kernel(
         project_kernel,
         (
             shape(model, tokens, kind=BF16),
-            shape(model, 8),
             shape(model, tokens, kind=BF16),
             shape(2, tokens),
             shape(3 * part, tokens, kind=BF16),
         ),
         [at],
-        [x_in, x_near, x_far, x_both, norms_near, norms_far, cosine, sine, w_qkv],
+        [x_in, x_near, x_far, x_both, norms, cosine, sine, w_qkv, w_out],
         [pltpu.VMEM((3 * part, tokens), F32)],
     )
     Order.cost = 10**9
-    for stride in strides[1:-1]:
-        live_total = grow_total(live_total, stride)
-    cot_both = to_width(cot_far, 1)
     send, keep, x_half, heads_out, probs = kernel(
         attention_kernel,
         (
@@ -765,14 +788,21 @@
     )
     chip, send = add([keep, to_width(send, 1)], (0, model, F32), (0, model, BF16))
     received = to_width(send, 2)
-
-    live_total = grow_total(live_total, strides[-1])
-    running, d_history, d_mix = mix_history(all_tokens, mix_weights, counts, live_total, history, cotangent)
+    cot_both = to_width(after(cot_far, chip), 1)
+
+    running, d_mix = history_call(
+        functools.partial(history_kernel, 32),
+        (shape(part, tokens), shape(layers, STEP // 2, 128)),
+        (False, True),
+        (False, False),
+        [mix_weights, counts],
+        [cotangent, pltpu.with_memory_space_constraint(history, pltpu.HBM)],
+    )
     g_out, d_active, cot_half = kernel(
-        functools.partial(output_gradient_kernel, all_tokens),
+        output_gradient_kernel,
         (shape(model, tokens, kind=BF16), shape(hidden_units, tokens), shape(model, half, kind=BF16)),
         [at, self_weight, counts],
-        [cotangent, cot_near, cot_far, cot_both, live_total, w_down],
+        [cotangent, cot_near, cot_far, cot_both, w_down],
         [pltpu.VMEM((model, tokens), BF16)],
     )
 
@@ -811,10 +841,10 @@
     out_near = to_width(out_send, 1)
 
     d_middle, g_own, gains_two = kernel(
-        functools.partial(middle_gradient_kernel, all_tokens),
+        middle_gradient_kernel,
         (shape(model, half), shape(model, half, kind=BF16), shape(2, model)),
         [at, self_weight, counts],
-        [chip, received, live_total, middle, stats_two, cot_half, norms],
+        [chip, received, middle, stats_two, cot_half, norms],
         [pltpu.VMEM((model, half), F32), pltpu.VMEM((model, 128), F32), pltpu.VMEM((model, 128), F32)],
     )
     g_other = to_width(g_own, 1)
@@ -848,39 +878,32 @@
     first_got = start_stage(first, first_parts, 0)
     second_got = start_stage(second, second_parts, 0)
 
-    Order.cost = 6 * 10**9
-    mixed, mix_row = kernel(
-        functools.partial(mixed_kernel, all_tokens),
-        (shape(part, tokens, kind=BF16), shape(1, 128)),
-        [self_weight, counts],
-        [out_chip, out_far, live_total, running, cotangent, d_mix],
-        [pltpu.VMEM((128, 128), F32)],
-    )
     Order.cost = 10**8
     down_parts = add_stage(down, down_parts, down_got, 1)
     down_got = start_stage(down, down_parts, 2)
-    in_send, in_keep, sums = kernel(
-        input_gradient_kernel,
-        blocks + (shape(8, model),),
-        [at],
-        [d_project, w_qkv, x_all, stats_one, d_middle, norms, gains_two, mix_row],
-        [pltpu.VMEM((model, tokens), F32), pltpu.VMEM((model, 128), F32), pltpu.VMEM((model, 128), F32)],
-    )
-    in_near = to_width(in_send, 1)
-    sums_got = to_width(sums, 1)
     up_parts = add_stage(up, up_parts, up_got, 1)
     up_got = start_stage(up, up_parts, 2)
+    in_send, in_keep, sums = kernel(
+        functools.partial(input_gradient_kernel, width),
+        blocks + (shape(8, model),),
+        [at, counts],
+        [d_project, w_qkv, x_all, stats_one, d_middle, norms, gains_two],
+        [pltpu.VMEM((model, tokens), F32), pltpu.VMEM((model, 128), F32), pltpu.VMEM((model, 128), F32)],
+    )
+    in_near = to_width(in_send, 1)
+    last = len(down.digits) - 1
+    mixed, sums = kernel(
+        mixed_kernel,
+        (shape(part, tokens, kind=BF16), shape(8, model)),
+        [self_weight, counts],
+        [out_chip, out_far, running, cotangent, d_mix, sums],
+        [pltpu.VMEM((128, 128), F32)],
+    )
+    sums_got = to_width(sums, 1)
     first_parts = add_stage(first, first_parts, first_got, 0)
     first_got = start_stage(first, first_parts, 1)
-    Order.cost = 2 * 10**10
     second_parts = add_stage(second, second_parts, second_got, 0)
     second_got = start_stage(second, second_parts, 1)
-    Order.cost = 10**9
-    in_chip, in_send = add([in_keep, in_near], (0, part, F32), (part, 2 * part, BF16))
-    in_far = to_width(in_send, 2)
-    sums = add([sums, sums_got], (0, 8, F32))[0]
-    sums_got = to_width(sums, 2)
-    last = len(down.digits) - 1
     down_value = sum_rest(down, add_stage(down, down_parts, down_got, 2)[0])
     down_pieces = gather_stage(down, down_value, last)
     up_value = sum_rest(up, add_stage(up, up_parts, up_got, 2)[0])
@@ -890,35 +913,55 @@
     second_parts = add_stage(second, second_parts, second_got, 1)
     second_got = start_stage(second, second_parts, 2)
     sums = add([sums, sums_got], (0, 8, F32))[0]
-    sums_got = to_row(sums, strides[0])
-    d_input = kernel(d_input_kernel, shape(part, tokens), [], [in_chip, in_far, x_in, stats_one, sums])
+    sums_got = to_width(sums, 2)
+    first_value = sum_rest(first, add_stage(first, first_parts, first_got, 2)[0])
+    first_pieces = gather_stage(first, first_value, last)
+    Order.cost = 2 * 10**10
+    second_value = sum_rest(second, add_stage(second, second_parts, second_got, 2)[0])
+    second_pieces = gather_stage(second, second_value, last)
+    Order.cost = 10**8
+    in_chip, in_send = add([in_keep, in_near], (0, part, F32), (part, 2 * part, BF16))
+    in_far = to_width(in_send, 2)
+    row_sums = add([sums, sums_got], (0, 8, F32))[0]
+    sums_got = to_row(row_sums, strides[0])
     down_pieces = gather_stage(down, join(down_pieces), last - 1)
     up_pieces = gather_stage(up, join(up_pieces), last - 1)
-    first_value = sum_rest(first, add_stage(first, first_parts, first_got, 2)[0])
-    first_pieces = gather_stage(first, first_value, last)
-    second_value = sum_rest(second, add_stage(second, second_parts, second_got, 2)[0])
-    second_pieces = gather_stage(second, second_value, last)
+    sums = row_sums
     for stride in strides[1:-1]:
         sums = add([sums, sums_got], (0, 8, F32))[0]
         sums_got = to_row(sums, stride)
+    in_total = kernel(d_input_kernel, shape(part, tokens), [], [in_chip, in_far, x_in, stats_one, row_sums])
     first_pieces = gather_stage(first, join(first_pieces), last - 1)
     second_pieces = gather_stage(second, join(second_pieces), last - 1)
+    sums = add([sums, sums_got], (0, 8, F32))[0]
+    sums_got = to_row(sums, strides[-1])
     down_pieces = gather_stage(down, join(down_pieces), 0)
     up_pieces = gather_stage(up, join(up_pieces), 0)
     sums = add([sums, sums_got], (0, 8, F32))[0]
-    sums_got = to_row(sums, strides[-1])
-    first_pieces = gather_stage(first, join(first_pieces), 0)
-    second_pieces = gather_stage(second, join(second_pieces), 0)
-    sums = add([sums, sums_got], (0, 8, F32))[0]
+    d_input = kernel(
+        functools.partial(scale_kernel, all_tokens), shape(part, tokens), [], [in_total, sums]
+    )
+    d_history = history_call(
+        functools.partial(d_history_kernel, all_tokens, 32),
+        (shape(*history.shape, kind=BF16),),
+        (False, False),
+        (True,),
+        [mix_weights, counts],
+        [cotangent, sums],
+    )[0]
     d_mix, d_self, *ends = kernel(
-        functools.partial(ends_kernel, layers, width),
+        functools.partial(ends_kernel, all_tokens, layers, width),
         (shape(1, layers), shape(1, 1)) + (shape(1, part),) * 4,
         [at],
         [sums],
     )
-    d_w_down = place(me, [down], down_pieces, (hidden_units,))[0]
-    d_w_up = place(me, [up], up_pieces, (model,))[0]
-    d_w_qkv, d_w_out = place(me, tail, first_pieces + second_pieces, (3 * part, part))
+    first_pieces = gather_stage(first, join(first_pieces), 0)
+    Order.cost = 2 * 10**10
+    second_pieces = gather_stage(second, join(second_pieces), 0)
+    Order.cost = 10**8
+    d_w_down = place(all_tokens, me, sums, [down], down_pieces, (hidden_units,))[0]
+    d_w_up = place(all_tokens, me, sums, [up], up_pieces, (model,))[0]
+    d_w_qkv, d_w_out = place(all_tokens, me, sums, tail, first_pieces + second_pieces, (3 * part, part))
     return (
         mixed,
         d_input,

time: 157 us -> 150 us (0.955)
  waiting for transfers between devices: 58.5 us -> 40.7 us
  starting transfers between devices: 49.9 us -> 58.9 us
  Pallas kernels: 40.9 us -> 45.5 us
  local copies, waits for them, and re-layouts: 5.08 us -> 1.93 us
    ppermute x50 -> x47, waiting for transfers between devices: 58.5 us -> 40.7 us  [xor_send(): return lax.ppermute(value, axis, [(i, i ^ offset) for i in range(size)])]
    ppermute x50 -> x47, starting transfers between devices: 49.9 us -> 58.9 us  [xor_send(): return lax.ppermute(value, axis, [(i, i ^ offset) for i in range(size)])]
    pallas_call x1 -> x3, Pallas kernels: 5.91 us -> 10.9 us  [the longest x2 9.78 us: history_call(): pl.pallas_call(body, out_shape=outs, in_specs=[pl.BlockSpec(memory_space=...]
    unnamed x30 -> x18, local copies, waits for them, and re-layouts: 5.08 us -> 1.93 us
    pallas_call x52 -> x50, Pallas kernels: 34.9 us -> 34.6 us  [kernel(): pl.pallas_call(body, out_shape=outs, in_specs=[pl.BlockSpec(memory_space=...]
  transfers between devices with their start and end apart: 50 -> 47, of which waited for: 16 -> 19; matrix products, arithmetic and copies ran while one was open for 0% -> 0% of each run, Pallas kernels for 19% -> 23%
where the time goes in v5:
time: 150 us; the launch traced here: 149 us
  starting transfers between devices  58.9 us (39%)
  Pallas kernels  45.5 us (30%)
  waiting for transfers between devices  40.7 us (27%)
  between operations  2.48 us (2%)
  local copies, waits for them, and re-layouts  1.93 us (1%)
    ppermute x47, starting transfers between devices, xor_send(): return lax.ppermute(value, axis, [(i, i ^ offset) for i in range(size)])  58.9 us
    ppermute x47, waiting for transfers between devices, xor_send(): return lax.ppermute(value, axis, [(i, i ^ offset) for i in range(size)])  40.7 us
    pallas_call x50, Pallas kernels, kernel(): pl.pallas_call(body, out_shape=outs, in_specs=[pl.BlockSpec(memory_space=...  34.6 us
    pallas_call x2, Pallas kernels, history_call(): pl.pallas_call(body, out_shape=outs, in_specs=[pl.BlockSpec(memory_space=...  9.78 us
  transfers between devices with their start and end apart: 47, of which 19 were waited for; matrix products, arithmetic and copies ran while one was open for 0% of the time, Pallas kernels for 23%

profile of v5, /device:TPU:0, one launch (start us, length us, event | category | flops | bytes accessed | tf_op | source)
XLA Modules:
  0.0 149.5 jit_solution(10384996571952630447)
XLA Ops:
  1.2 2.6 %collective-permute-start.3 = (bf16[192,512]{1,0:T(8,128)(2,1)}, bf16[192,512]{1,0:T(8,128)(2,1)S(1)}, u32[]{:S(2)}, u32[]{:S(2)}) collective-permute-start(bf16[192,512]{1,0:T(8,128)(2,1)} %x_in), channel_id=1, source_target_pairs={{0,2},{1,3},{2,0},{3,1},{4,6},{5,7},{6,4},{7,5},{8,10},{9,11},{10,... | collective-permute-start | bytes 589832 | tf_op jit(solution)/shard_map/ppermute | solution.py:66
  6.1 1.6 %collective-permute-start.2 = (f32[16,256]{1,0:T(8,128)S(1)}, f32[16,256]{1,0:T(8,128)S(1)}, u32[]{:S(2)}, u32[]{:S(2)}) collective-permute-start(f32[16,256]{1,0:T(8,128)S(1)} %shard_map.256.n01), channel_id=1, source_target_pairs={{0,2},{1,3},{2,0},{3,1},{4,6},{5,7},{6,4},{7,5},{8,10},{9,11},{10,... | collective-permute-start | bytes 49160 | tf_op jit(solution)/shard_map/ppermute | solution.py:66
  7.7 2.2 %collective-permute-done.2.n23 = f32[16,256]{1,0:T(8,128)S(1)} collective-permute-done((f32[16,256]{1,0:T(8,128)S(1)}, f32[16,256]{1,0:T(8,128)S(1)}, u32[]{:S(2)}, u32[]{:S(2)}) %collective-permute-start.2) | collective-permute-done | bytes 16416 | tf_op jit(solution)/shard_map/ppermute | solution.py:66
  10.2 1.8 %collective-permute-start.5 = (bf16[192,512]{1,0:T(8,128)(2,1)}, bf16[192,512]{1,0:T(8,128)(2,1)S(1)}, u32[]{:S(2)}, u32[]{:S(2)}) collective-permute-start(bf16[192,512]{1,0:T(8,128)(2,1)} %cot_ref.1), channel_id=1, source_target_pairs={{0,2},{1,3},{2,0},{3,1},{4,6},{5,7},{6,4},{7,5},{8,10},{9,11},{10,... | collective-permute-start | bytes 589832 | tf_op jit(solution)/shard_map/ppermute | solution.py:66
  13.8 2.2 %shard_map.258 = (bf16[768,512]{1,0:T(8,128)(2,1)S(1)}, bf16[768,512]{1,0:T(8,128)(2,1)S(1)}, f32[2,512]{1,0:T(2,128)S(1)}, bf16[576,512]{1,0:T(8,128)(2,1)S(1)}) custom-call(s32[1]{0:T(128)} %bitcast.at_ref, bf16[192,512]{1,0:T(8,128)(2,1)S(1)} %copy-done.2, bf16[192,512]{1,0:T(8,128)(2,1)S(1)} %collective-permute-done.now.x1, ...), custom_call_target="tpu_custom_call" | custom-call | flops 100000000 | bytes 1024 | tf_op jit(solution)/shard_map/pallas_call | solution.py:31
  16.1 1.6 %collective-permute-done.5.c2 = bf16[192,512]{1,0:T(8,128)(2,1)S(1)} collective-permute-done((bf16[192,512]{1,0:T(8,128)(2,1)}, bf16[192,512]{1,0:T(8,128)(2,1)S(1)}, u32[]{:S(2)}, u32[]{:S(2)}) %collective-permute-start.5) | collective-permute-done | bytes 196640 | tf_op jit(solution)/shard_map/ppermute | solution.py:66
  17.7 4.7 %shard_map.259 = (bf16[768,256]{1,0:T(8,128)(2,1)S(1)}, f32[768,256]{1,0:T(8,128)S(1)}, bf16[768,256]{1,0:T(8,128)(2,1)S(1)}, bf16[192,512]{1,0:T(8,128)(2,1)S(1)}, bf16[3,512,512]{2,1,0:T(8,128)(2,1)S(1)}) custom-call(s32[1]{0:T(128)} %bitcast.at_ref, bf16[576,512]{1,0:T(8,128)(2,1)S(1)} %get-tuple-element.163.qkv, bf16[192,768]{1,0:T(8,128)(2,1)S(1)} %copy-done.4, ...), custom_call_target="tpu_custom_call" | custom-call | flops 1000000000 | bytes 1024 | tf_op jit(solution)/shard_map/pallas_call | solution.py:31
  22.5 1.7 %collective-permute-done.6.refs_1_ = bf16[768,256]{1,0:T(8,128)(2,1)S(1)} collective-permute-done((bf16[768,256]{1,0:T(8,128)(2,1)S(1)}, bf16[768,256]{1,0:T(8,128)(2,1)S(1)}, u32[]{:S(2)}, u32[]{:S(2)}) %collective-permute-start.6) | collective-permute-done | bytes 393248 | tf_op jit(solution)/shard_map/ppermute | solution.py:66
  24.5 1.8 %collective-permute-start.9 = (bf16[768,256]{1,0:T(8,128)(2,1)S(1)}, bf16[768,256]{1,0:T(8,128)(2,1)S(1)}, u32[]{:S(2)}, u32[]{:S(2)}) collective-permute-start(bf16[768,256]{1,0:T(8,128)(2,1)S(1)} %get-tuple-element.175), channel_id=1, source_target_pairs={{0,2},{1,3},{2,0},{3,1},{4,6},{5,7},{6,4},{7,5},{8,10},{9,11},{10,... | collective-permute-start | bytes 1179656 | tf_op jit(solution)/shard_map/ppermute | solution.py:66
  28.1 5.7 %shard_map.261 = (f32[192,512]{1,0:T(8,128)S(1)}, f32[30,8,128]{2,1,0:T(8,128)S(1)}) custom-call(f32[30]{0:T(128)S(1)} %copy-done.6, s32[1]{0:T(128)S(6)} %copy.29.counts_ref, bf16[192,512]{1,0:T(8,128)(2,1)S(1)} %copy-done.1, bf16[30,192,512]{2,1,0:T(8,128)(2,1)} %history_ref.1), custom_call_target="tpu_custom_call" | custom-call | flops 1000000000 | bytes 1024 | tf_op jit(solution)/shard_map/pallas_call | solution.py:303
  35.7 1.5 %shard_map.263 = (f32[768,256]{1,0:T(8,128)S(1)}, f32[2,256]{1,0:T(2,128)S(1)}, bf16[768,256]{1,0:T(8,128)(2,1)S(1)}) custom-call(bf16[768,256]{1,0:T(8,128)(2,1)S(1)} %get-tuple-element.174.x_half, f32[768,256]{1,0:T(8,128)S(1)} %get-tuple-element.168.chip, bf16[768,256]{1,0:T(8,128)(2,1)S(1)} %collective-permute-done.9.received, f32[768,8]{1,0:T(8,128)S(1)} %shard_map.257.norms), custom_call_target="tpu_custom_call" | custom-call | flops 1000000000 | bytes 1024 | tf_op jit(solution)/shard_map/pallas_call | solution.py:31
  37.4 1.7 %collective-permute-done.10.other = bf16[768,256]{1,0:T(8,128)(2,1)S(1)} collective-permute-done((bf16[768,256]{1,0:T(8,128)(2,1)S(1)}, bf16[768,256]{1,0:T(8,128)(2,1)S(1)}, u32[]{:S(2)}, u32[]{:S(2)}) %collective-permute-start.10) | collective-permute-done | bytes 393248 | tf_op jit(solution)/shard_map/ppermute | solution.py:66
  39.1 2.6 %shard_map.264 = (bf16[768,512]{1,0:T(8,128)(2,1)S(1)}, bf16[768,512]{1,0:T(8,128)(2,1)S(1)}, bf16[768,512]{1,0:T(8,128)(2,1)S(1)}, bf16[768,256]{1,0:T(8,128)(2,1)S(1)}, f32[768,256]{1,0:T(8,128)S(1)}) custom-call(bf16[768,256]{1,0:T(8,128)(2,1)S(1)} %get-tuple-element.178.own, bf16[768,256]{1,0:T(8,128)(2,1)S(1)} %collective-permute-done.10.other, ...), custom_call_target="tpu_custom_call" | custom-call | flops 1000000000 | bytes 1024 | tf_op jit(solution)/shard_map/pallas_call | solution.py:31
  43.8 1.8 %collective-permute-start.12 = (bf16[768,256]{1,0:T(8,128)(2,1)S(1)}, bf16[768,256]{1,0:T(8,128)(2,1)S(1)}, u32[]{:S(2)}, u32[]{:S(2)}) collective-permute-start(bf16[768,256]{1,0:T(8,128)(2,1)S(1)} %get-tuple-element.195), channel_id=1, source_target_pairs={{0,2},{1,3},{2,0},{3,1},{4,6},{5,7},{6,4},{7,5},{8,10},{9,11},{10,... | collective-permute-start | bytes 1179656 | tf_op jit(solution)/shard_map/ppermute | solution.py:66
  45.6 1.5 %collective-permute-start.14 = (bf16[384,768]{1,0:T(8,128)(2,1)S(1)}, bf16[384,768]{1,0:T(8,128)(2,1)S(1)}, u32[]{:S(2)}, u32[]{:S(2)}) collective-permute-start(bf16[384,768]{1,0:T(8,128)(2,1)S(1)} %get-tuple-element.203), channel_id=1, source_target_pairs={{0,4},{4,0},{8,12},{12,8},{16,20},{20,16},{24,28},{28,24},{1,5},{5... | collective-permute-start | bytes 1769480 | tf_op jit(solution)/shard_map/ppermute | solution.py:66
  48.0 1.6 %collective-permute-start.15 = (bf16[384,768]{1,0:T(8,128)(2,1)S(1)}, bf16[384,768]{1,0:T(8,128)(2,1)S(1)}, u32[]{:S(2)}, u32[]{:S(2)}) collective-permute-start(bf16[384,768]{1,0:T(8,128)(2,1)S(1)} %get-tuple-element.206), channel_id=1, source_target_pairs={{0,8},{4,12},{8,0},{12,4},{16,24},{20,28},{24,16},{28,20},{1,9},{5... | collective-permute-start | bytes 1769480 | tf_op jit(solution)/shard_map/ppermute | solution.py:66
  50.6 4.4 %collective-permute-done.12.received = bf16[768,256]{1,0:T(8,128)(2,1)S(1)} collective-permute-done((bf16[768,256]{1,0:T(8,128)(2,1)S(1)}, bf16[768,256]{1,0:T(8,128)(2,1)S(1)}, u32[]{:S(2)}, u32[]{:S(2)}) %collective-permute-start.12) | collective-permute-done | bytes 393248 | tf_op jit(solution)/shard_map/ppermute | solution.py:66
  55.1 2.3 %shard_map.269 = (f32[768,256]{1,0:T(8,128)S(1)}, bf16[768,256]{1,0:T(8,128)(2,1)S(1)}, f32[2,768]{1,0:T(2,128)S(1)}) custom-call(s32[1]{0:T(128)} %bitcast.at_ref, f32[1]{0:T(128)S(6)} %copy.30.self_ref, s32[1]{0:T(128)S(6)} %copy.29.counts_ref, f32[768,256]{1,0:T(8,128)S(1)} %get-tuple-element.194.chip, ...), custom_call_target="tpu_custom_call" | custom-call | flops 1000000000 | bytes 1024 | tf_op jit(solution)/shard_map/pallas_call | solution.py:31
  57.6 3.1 %collective-permute-done.14.refs_1_ = bf16[384,768]{1,0:T(8,128)(2,1)S(1)} collective-permute-done((bf16[384,768]{1,0:T(8,128)(2,1)S(1)}, bf16[384,768]{1,0:T(8,128)(2,1)S(1)}, u32[]{:S(2)}, u32[]{:S(2)}) %collective-permute-start.14) | collective-permute-done | bytes 589856 | tf_op jit(solution)/shard_map/ppermute | solution.py:66
  60.9 1.6 %collective-permute-start.17 = (bf16[192,768]{1,0:T(8,128)(2,1)S(1)}, bf16[192,768]{1,0:T(8,128)(2,1)S(1)}, u32[]{:S(2)}, u32[]{:S(2)}) collective-permute-start(bf16[192,768]{1,0:T(8,128)(2,1)S(1)} %get-tuple-element.217), channel_id=1, source_target_pairs={{0,8},{4,12},{8,0},{12,4},{16,24},{20,28},{24,16},{28,20},{1,9},{5... | collective-permute-start | bytes 884744 | tf_op jit(solution)/shard_map/ppermute | solution.py:66
  64.3 3.6 %shard_map.273 = (bf16[576,512]{1,0:T(8,128)(2,1)S(1)}, bf16[768,512]{1,0:T(8,128)(2,1)S(1)}) custom-call(s32[1]{0:T(128)} %bitcast.at_ref, bf16[768,256]{1,0:T(8,128)(2,1)S(1)} %get-tuple-element.208.own, bf16[768,256]{1,0:T(8,128)(2,1)S(1)} %collective-permute-done.16.other, bf16[192,768]{1,0:T(8,128)(2,1)S(1)} %copy-done.5, ...), custom_call_target="tpu_custom_call" | custom-call | flops 1000000000 | bytes 1024 | tf_op jit(solution)/shard_map/pallas_call | solution.py:31
  70.0 1.6 %collective-permute-start.21 = (bf16[192,768]{1,0:T(8,128)(2,1)S(1)}, bf16[192,768]{1,0:T(8,128)(2,1)S(1)}, u32[]{:S(2)}, u32[]{:S(2)}) collective-permute-start(bf16[192,768]{1,0:T(8,128)(2,1)S(1)} %get-tuple-element.237), channel_id=1, source_target_pairs={{0,8},{4,12},{8,0},{12,4},{16,24},{20,28},{24,16},{28,20},{1,9},{5... | collective-permute-start | bytes 884744 | tf_op jit(solution)/shard_map/ppermute | solution.py:66
  72.2 2.6 %collective-permute-start.22 = (bf16[96,768]{1,0:T(8,128)(2,1)S(1)}, bf16[96,768]{1,0:T(8,128)(2,1)S(1)}, u32[]{:S(2)}, u32[]{:S(2)}) collective-permute-start(bf16[96,768]{1,0:T(8,128)(2,1)S(1)} %get-tuple-element.240), channel_id=1, source_target_pairs={{0,16},{4,20},{8,24},{12,28},{16,0},{20,4},{24,8},{28,12},{1,17},{... | collective-permute-start | bytes 442376 | tf_op jit(solution)/shard_map/ppermute | solution.py:66
  74.9 2.6 %shard_map.277 = (bf16[384,512]{1,0:T(8,128)(2,1)S(1)}, f32[384,512]{1,0:T(8,128)S(1)}, f32[8,768]{1,0:T(8,128)S(1)}) custom-call(s32[1]{0:T(128)} %bitcast.at_ref, s32[1]{0:T(128)S(6)} %copy.29.counts_ref, bf16[576,512]{1,0:T(8,128)(2,1)S(1)} %get-tuple-element.222.refs_0_.d_project, bf16[576,768]{1,0:T(8,128)(2,1)S(1)} %bitcast.16, ...), custom_call_target="tpu_custom_call" | custom-call | flops 100000000 | bytes 1024 | tf_op jit(solution)/shard_map/pallas_call | solution.py:31
  78.4 2.3 %collective-permute-start.23 = (bf16[96,768]{1,0:T(8,128)(2,1)S(1)}, bf16[96,768]{1,0:T(8,128)(2,1)S(1)}, u32[]{:S(2)}, u32[]{:S(2)}) collective-permute-start(bf16[96,768]{1,0:T(8,128)(2,1)S(1)} %get-tuple-element.242), channel_id=1, source_target_pairs={{0,16},{4,20},{8,24},{12,28},{16,0},{20,4},{24,8},{28,12},{1,17},{... | collective-permute-start | bytes 442376 | tf_op jit(solution)/shard_map/ppermute | solution.py:66
  81.6 2.0 %collective-permute-start.25 = (bf16[96,768]{1,0:T(8,128)(2,1)S(1)}, bf16[96,768]{1,0:T(8,128)(2,1)S(1)}, u32[]{:S(2)}, u32[]{:S(2)}) collective-permute-start(bf16[96,768]{1,0:T(8,128)(2,1)S(1)} %get-tuple-element.247), channel_id=1, source_target_pairs={{0,4},{4,0},{8,12},{12,8},{16,20},{20,16},{24,28},{28,24},{1,5},{5... | collective-permute-start | bytes 442376 | tf_op jit(solution)/shard_map/ppermute | solution.py:66
  83.6 3.7 %collective-permute-done.23.refs_1_ = bf16[96,768]{1,0:T(8,128)(2,1)S(1)} collective-permute-done((bf16[96,768]{1,0:T(8,128)(2,1)S(1)}, bf16[96,768]{1,0:T(8,128)(2,1)S(1)}, u32[]{:S(2)}, u32[]{:S(2)}) %collective-permute-start.23) | collective-permute-done | bytes 147488 | tf_op jit(solution)/shard_map/ppermute | solution.py:66
  87.5 1.5 collective-permute-start.27
  89.1 1.6 %collective-permute-start.28 = (bf16[48,768]{1,0:T(8,128)(2,1)S(1)}, bf16[48,768]{1,0:T(8,128)(2,1)S(1)}, u32[]{:S(2)}, u32[]{:S(2)}) collective-permute-start(bf16[48,768]{1,0:T(8,128)(2,1)S(1)} %get-tuple-element.254), channel_id=1, source_target_pairs={{0,16},{4,20},{8,24},{12,28},{16,0},{20,4},{24,8},{28,12},{1,17},{... | collective-permute-start | bytes 221192 | tf_op jit(solution)/shard_map/ppermute | solution.py:66
  91.1 1.4 collective-permute-start.32
  92.6 1.5 %collective-permute-start.31 = (bf16[96,768]{1,0:T(8,128)(2,1)S(1)}, bf16[96,768]{1,0:T(8,128)(2,1)S(1)}, u32[]{:S(2)}, u32[]{:S(2)}) collective-permute-start(bf16[96,768]{1,0:T(8,128)(2,1)S(1)} %shard_map.281.refs_0_), channel_id=1, source_target_pairs={{0,16},{4,20},{8,24},{12,28},{16,0},{20,4},{24,8},{28,12},{1,17},{... | collective-permute-start | bytes 442376 | tf_op jit(solution)/shard_map/ppermute | solution.py:66
  96.5 7.4 %collective-permute-start.34 = (bf16[192,512]{1,0:T(8,128)(2,1)S(1)}, bf16[192,512]{1,0:T(8,128)(2,1)S(1)}, u32[]{:S(2)}, u32[]{:S(2)}) collective-permute-start(bf16[192,512]{1,0:T(8,128)(2,1)S(1)} %get-tuple-element.262), channel_id=1, source_target_pairs={{0,2},{1,3},{2,0},{3,1},{4,6},{5,7},{6,4},{7,5},{8,10},{9,11},{10,... | collective-permute-start | bytes 589832 | tf_op jit(solution)/shard_map/ppermute | solution.py:66
  103.9 4.6 %collective-permute-done.31.refs_1_ = bf16[96,768]{1,0:T(8,128)(2,1)S(1)} collective-permute-done((bf16[96,768]{1,0:T(8,128)(2,1)S(1)}, bf16[96,768]{1,0:T(8,128)(2,1)S(1)}, u32[]{:S(2)}, u32[]{:S(2)}) %collective-permute-start.31) | collective-permute-done | bytes 147488 | tf_op jit(solution)/shard_map/ppermute | solution.py:66
  109.4 1.4 collective-permute-start.33
  110.8 2.4 %collective-permute-start.35 = (bf16[48,768]{1,0:T(8,128)(2,1)S(1)}, bf16[48,768]{1,0:T(8,128)(2,1)S(1)}, u32[]{:S(2)}, u32[]{:S(2)}) collective-permute-start(bf16[48,768]{1,0:T(8,128)(2,1)S(1)} %shard_map.286.refs_0_), channel_id=1, source_target_pairs={{0,16},{4,20},{8,24},{12,28},{16,0},{20,4},{24,8},{28,12},{1,17},{... | collective-permute-start | bytes 221192 | tf_op jit(solution)/shard_map/ppermute | solution.py:66
  113.2 4.7 %collective-permute-done.33.refs_1_ = f32[8,768]{1,0:T(8,128)S(1)} collective-permute-done((f32[8,768]{1,0:T(8,128)S(1)}, f32[8,768]{1,0:T(8,128)S(1)}, u32[]{:S(2)}, u32[]{:S(2)}) %collective-permute-start.33) | collective-permute-done | bytes 24608 | tf_op jit(solution)/shard_map/ppermute | solution.py:66
  117.9 1.7 %collective-permute-start.36 = (bf16[48,768]{1,0:T(8,128)(2,1)S(1)}, bf16[48,768]{1,0:T(8,128)(2,1)S(1)}, u32[]{:S(2)}, u32[]{:S(2)}) collective-permute-start(bf16[48,768]{1,0:T(8,128)(2,1)S(1)} %shard_map.287.refs_0_), channel_id=1, source_target_pairs={{0,16},{4,20},{8,24},{12,28},{16,0},{20,4},{24,8},{28,12},{1,17},{... | collective-permute-start | bytes 221192 | tf_op jit(solution)/shard_map/ppermute | solution.py:66
  120.2 3.0 %collective-permute-done.36.refs_1_ = bf16[48,768]{1,0:T(8,128)(2,1)S(1)} collective-permute-done((bf16[48,768]{1,0:T(8,128)(2,1)S(1)}, bf16[48,768]{1,0:T(8,128)(2,1)S(1)}, u32[]{:S(2)}, u32[]{:S(2)}) %collective-permute-start.36) | collective-permute-done | bytes 73760 | tf_op jit(solution)/shard_map/ppermute | solution.py:66
  123.9 1.6 %collective-permute-start.37 = (f32[8,768]{1,0:T(8,128)S(1)}, f32[8,768]{1,0:T(8,128)S(1)}, u32[]{:S(2)}, u32[]{:S(2)}) collective-permute-start(f32[8,768]{1,0:T(8,128)S(1)} %shard_map.292.refs_0_), channel_id=1, source_target_pairs={{0,8},{4,12},{8,0},{12,4},{16,24},{20,28},{24,16},{28,20},{1,9},{5... | collective-permute-start | bytes 73736 | tf_op jit(solution)/shard_map/ppermute | solution.py:66
  125.5 2.2 %collective-permute-done.37.refs_1_ = f32[8,768]{1,0:T(8,128)S(1)} collective-permute-done((f32[8,768]{1,0:T(8,128)S(1)}, f32[8,768]{1,0:T(8,128)S(1)}, u32[]{:S(2)}, u32[]{:S(2)}) %collective-permute-start.37) | collective-permute-done | bytes 24608 | tf_op jit(solution)/shard_map/ppermute | solution.py:66
  127.8 1.7 %collective-permute-start.40 = (f32[8,768]{1,0:T(8,128)S(1)}, f32[8,768]{1,0:T(8,128)S(1)}, u32[]{:S(2)}, u32[]{:S(2)}) collective-permute-start(f32[8,768]{1,0:T(8,128)S(1)} %shard_map.296.refs_0_), channel_id=1, source_target_pairs={{0,16},{4,20},{8,24},{12,28},{16,0},{20,4},{24,8},{28,12},{1,17},{... | collective-permute-start | bytes 73736 | tf_op jit(solution)/shard_map/ppermute | solution.py:66
  133.5 4.1 %shard_map.301 = bf16[30,192,512]{2,1,0:T(8,128)(2,1)} custom-call(f32[30]{0:T(128)S(1)} %copy-done.6, s32[1]{0:T(128)S(6)} %copy.29.counts_ref, bf16[192,512]{1,0:T(8,128)(2,1)S(1)} %copy-done.1, f32[8,768]{1,0:T(8,128)S(1)} %shard_map.299.sums), custom_call_target="tpu_custom_call" | custom-call | flops 100000000 | bytes 1024 | tf_op jit(solution)/shard_map/pallas_call | solution.py:303
  138.3 2.1 %collective-permute-start.46 = (bf16[192,768]{1,0:T(8,128)(2,1)S(1)}, bf16[192,768]{1,0:T(8,128)(2,1)S(1)}, u32[]{:S(2)}, u32[]{:S(2)}) collective-permute-start(bf16[192,768]{1,0:T(8,128)(2,1)S(1)} %shard_map.304.refs_2_), channel_id=1, source_target_pairs={{0,8},{4,12},{8,0},{12,4},{16,24},{20,28},{24,16},{28,20},{1,9},{5... | collective-permute-start | bytes 884744 | tf_op jit(solution)/shard_map/ppermute | solution.py:66
  140.4 1.4 collective-permute-start.45
  141.9 2.4 %collective-permute-done.43.refs_1_ = bf16[384,768]{1,0:T(8,128)(2,1)S(1)} collective-permute-done((bf16[384,768]{1,0:T(8,128)(2,1)S(1)}, bf16[384,768]{1,0:T(8,128)(2,1)S(1)}, u32[]{:S(2)}, u32[]{:S(2)}) %collective-permute-start.43) | collective-permute-done | bytes 589856 | tf_op jit(solution)/shard_map/ppermute | solution.py:66
  144.3 1.6 %shard_map.305 = f32[768,768]{1,0:T(8,128)} custom-call(s32[1]{0:T(128)} %bitcast.1.me_ref, f32[8,768]{1,0:T(8,128)S(1)} %shard_map.299.sums, bf16[384,768]{1,0:T(8,128)(2,1)S(1)} %shard_map.297.refs_0_, bf16[384,768]{1,0:T(8,128)(2,1)S(1)} %collective-permute-done.43.refs_1_), custom_call_target="tpu_custom_call" | custom-call | flops 100000000 | bytes 1024 | tf_op jit(solution)/shard_map/pallas_call | solution.py:31
  145.9 1.6 %shard_map.306 = f32[768,768]{1,0:T(8,128)} custom-call(s32[1]{0:T(128)} %bitcast.1.me_ref, f32[8,768]{1,0:T(8,128)S(1)} %shard_map.299.sums, bf16[384,768]{1,0:T(8,128)(2,1)S(1)} %shard_map.298.refs_0_, bf16[384,768]{1,0:T(8,128)(2,1)S(1)} %collective-permute-done.44.refs_1_), custom_call_target="tpu_custom_call" | custom-call | flops 100000000 | bytes 1024 | tf_op jit(solution)/shard_map/pallas_call | solution.py:31
  147.6 1.9 %shard_map.307 = (f32[576,768]{1,0:T(8,128)}, f32[192,768]{1,0:T(8,128)}) custom-call(s32[1]{0:T(128)} %bitcast.1.me_ref, f32[8,768]{1,0:T(8,128)S(1)} %shard_map.299.sums, bf16[192,768]{1,0:T(8,128)(2,1)S(1)} %shard_map.303.refs_0_, bf16[192,768]{1,0:T(8,128)(2,1)S(1)} %collective-permute-done.45.refs_1_, bf16[192,768]{1,0:T(8,128)(2,1)S(1)} %shard_map.304.refs_2_, ...), custom_call_target="tpu_custom_call" | custom-call | flops 100000000 | bytes 1024 | tf_op jit(solution)/shard_map/pallas_call | solution.py:31
  (117 shorter events, 28.4 us)
Async XLA Ops:
  0.7 3.1 %collective-permute-start = (bf16[192,512]{1,0:T(8,128)(2,1)}, bf16[192,512]{1,0:T(8,128)(2,1)S(1)}, u32[]{:S(2)}, u32[]{:S(2)}) collective-permute-start(bf16[192,512]{1,0:T(8,128)(2,1)} %x_in), channel_id=1, source_target_pairs={{0,1},{1,0},{2,3},{3,2},{4,5},{5,4},{6,7},{7,6},{8,9},{9,8},{10,11... | collective-permute-start | bytes 589832 | tf_op jit(solution)/shard_map/ppermute | solution.py:66
  1.2 8.9 %collective-permute-start.3 = (bf16[192,512]{1,0:T(8,128)(2,1)}, bf16[192,512]{1,0:T(8,128)(2,1)S(1)}, u32[]{:S(2)}, u32[]{:S(2)}) collective-permute-start(bf16[192,512]{1,0:T(8,128)(2,1)} %x_in), channel_id=1, source_target_pairs={{0,2},{1,3},{2,0},{3,1},{4,6},{5,7},{6,4},{7,5},{8,10},{9,11},{10,... | collective-permute-start | bytes 589832 | tf_op jit(solution)/shard_map/ppermute | solution.py:66
  4.9 1.2 collective-permute-start.1
  6.1 3.7 %collective-permute-start.2 = (f32[16,256]{1,0:T(8,128)S(1)}, f32[16,256]{1,0:T(8,128)S(1)}, u32[]{:S(2)}, u32[]{:S(2)}) collective-permute-start(f32[16,256]{1,0:T(8,128)S(1)} %shard_map.256.n01), channel_id=1, source_target_pairs={{0,2},{1,3},{2,0},{3,1},{4,6},{5,7},{6,4},{7,5},{8,10},{9,11},{10,... | collective-permute-start | bytes 49160 | tf_op jit(solution)/shard_map/ppermute | solution.py:66
  10.1 1.8 %collective-permute-start.4 = (bf16[192,512]{1,0:T(8,128)(2,1)S(1)}, bf16[192,512]{1,0:T(8,128)(2,1)S(1)}, u32[]{:S(2)}, u32[]{:S(2)}) collective-permute-start(bf16[192,512]{1,0:T(8,128)(2,1)S(1)} %collective-permute-done.3.x2), channel_id=1, source_target_pairs={{0,1},{1,0},{2,3},{3,2},{4,5},{5,4},{6,7},{7,6},{8,9},{9,8},{10,11... | collective-permute-start | bytes 589832 | tf_op jit(solution)/shard_map/ppermute | solution.py:66
  10.2 7.5 %collective-permute-start.5 = (bf16[192,512]{1,0:T(8,128)(2,1)}, bf16[192,512]{1,0:T(8,128)(2,1)S(1)}, u32[]{:S(2)}, u32[]{:S(2)}) collective-permute-start(bf16[192,512]{1,0:T(8,128)(2,1)} %cot_ref.1), channel_id=1, source_target_pairs={{0,2},{1,3},{2,0},{3,1},{4,6},{5,7},{6,4},{7,5},{8,10},{9,11},{10,... | collective-permute-start | bytes 589832 | tf_op jit(solution)/shard_map/ppermute | solution.py:66
  22.4 1.8 %collective-permute-start.6 = (bf16[768,256]{1,0:T(8,128)(2,1)S(1)}, bf16[768,256]{1,0:T(8,128)(2,1)S(1)}, u32[]{:S(2)}, u32[]{:S(2)}) collective-permute-start(bf16[768,256]{1,0:T(8,128)(2,1)S(1)} %get-tuple-element.166), channel_id=1, source_target_pairs={{0,1},{1,0},{2,3},{3,2},{4,5},{5,4},{6,7},{7,6},{8,9},{9,8},{10,11... | collective-permute-start | bytes 1179656 | tf_op jit(solution)/shard_map/ppermute | solution.py:66
  24.5 11.2 %collective-permute-start.9 = (bf16[768,256]{1,0:T(8,128)(2,1)S(1)}, bf16[768,256]{1,0:T(8,128)(2,1)S(1)}, u32[]{:S(2)}, u32[]{:S(2)}) collective-permute-start(bf16[768,256]{1,0:T(8,128)(2,1)S(1)} %get-tuple-element.175), channel_id=1, source_target_pairs={{0,2},{1,3},{2,0},{3,1},{4,6},{5,7},{6,4},{7,5},{8,10},{9,11},{10,... | collective-permute-start | bytes 1179656 | tf_op jit(solution)/shard_map/ppermute | solution.py:66
  26.3 7.5 %collective-permute-start.7 = (bf16[192,512]{1,0:T(8,128)(2,1)S(1)}, bf16[192,512]{1,0:T(8,128)(2,1)S(1)}, u32[]{:S(2)}, u32[]{:S(2)}) collective-permute-start(bf16[192,512]{1,0:T(8,128)(2,1)S(1)} %copy-done.1), channel_id=1, source_target_pairs={{0,1},{1,0},{2,3},{3,2},{4,5},{5,4},{6,7},{7,6},{8,9},{9,8},{10,11... | collective-permute-start | bytes 589832 | tf_op jit(solution)/shard_map/ppermute | solution.py:66
  26.3 7.5 %collective-permute-start.8 = (bf16[192,512]{1,0:T(8,128)(2,1)S(1)}, bf16[192,512]{1,0:T(8,128)(2,1)S(1)}, u32[]{:S(2)}, u32[]{:S(2)}) collective-permute-start(bf16[192,512]{1,0:T(8,128)(2,1)S(1)} %collective-permute-done.5.c2), channel_id=1, source_target_pairs={{0,1},{1,0},{2,3},{3,2},{4,5},{5,4},{6,7},{7,6},{8,9},{9,8},{10,11... | collective-permute-start | bytes 589832 | tf_op jit(solution)/shard_map/ppermute | solution.py:66
  37.3 1.8 %collective-permute-start.10 = (bf16[768,256]{1,0:T(8,128)(2,1)S(1)}, bf16[768,256]{1,0:T(8,128)(2,1)S(1)}, u32[]{:S(2)}, u32[]{:S(2)}) collective-permute-start(bf16[768,256]{1,0:T(8,128)(2,1)S(1)} %get-tuple-element.178.own), channel_id=1, source_target_pairs={{0,1},{1,0},{2,3},{3,2},{4,5},{5,4},{6,7},{7,6},{8,9},{9,8},{10,11... | collective-permute-start | bytes 1179656 | tf_op jit(solution)/shard_map/ppermute | solution.py:66
  41.7 1.8 %collective-permute-start.11 = (bf16[768,256]{1,0:T(8,128)(2,1)S(1)}, bf16[768,256]{1,0:T(8,128)(2,1)S(1)}, u32[]{:S(2)}, u32[]{:S(2)}) collective-permute-start(bf16[768,256]{1,0:T(8,128)(2,1)S(1)} %get-tuple-element.186), channel_id=1, source_target_pairs={{0,1},{1,0},{2,3},{3,2},{4,5},{5,4},{6,7},{7,6},{8,9},{9,8},{10,11... | collective-permute-start | bytes 1179656 | tf_op jit(solution)/shard_map/ppermute | solution.py:66
  43.8 11.2 %collective-permute-start.12 = (bf16[768,256]{1,0:T(8,128)(2,1)S(1)}, bf16[768,256]{1,0:T(8,128)(2,1)S(1)}, u32[]{:S(2)}, u32[]{:S(2)}) collective-permute-start(bf16[768,256]{1,0:T(8,128)(2,1)S(1)} %get-tuple-element.195), channel_id=1, source_target_pairs={{0,2},{1,3},{2,0},{3,1},{4,6},{5,7},{6,4},{7,5},{8,10},{9,11},{10,... | collective-permute-start | bytes 1179656 | tf_op jit(solution)/shard_map/ppermute | solution.py:66
  45.6 15.1 %collective-permute-start.14 = (bf16[384,768]{1,0:T(8,128)(2,1)S(1)}, bf16[384,768]{1,0:T(8,128)(2,1)S(1)}, u32[]{:S(2)}, u32[]{:S(2)}) collective-permute-start(bf16[384,768]{1,0:T(8,128)(2,1)S(1)} %get-tuple-element.203), channel_id=1, source_target_pairs={{0,4},{4,0},{8,12},{12,8},{16,20},{20,16},{24,28},{28,24},{1,5},{5... | collective-permute-start | bytes 1769480 | tf_op jit(solution)/shard_map/ppermute | solution.py:66
  48.0 15.1 %collective-permute-start.15 = (bf16[384,768]{1,0:T(8,128)(2,1)S(1)}, bf16[384,768]{1,0:T(8,128)(2,1)S(1)}, u32[]{:S(2)}, u32[]{:S(2)}) collective-permute-start(bf16[384,768]{1,0:T(8,128)(2,1)S(1)} %get-tuple-element.206), channel_id=1, source_target_pairs={{0,8},{4,12},{8,0},{12,4},{16,24},{20,28},{24,16},{28,20},{1,9},{5... | collective-permute-start | bytes 1769480 | tf_op jit(solution)/shard_map/ppermute | solution.py:66
  50.5 6.9 %collective-permute-start.13 = (bf16[384,512]{1,0:T(8,128)(2,1)S(1)}, bf16[384,512]{1,0:T(8,128)(2,1)S(1)}, u32[]{:S(2)}, u32[]{:S(2)}) collective-permute-start(bf16[384,512]{1,0:T(8,128)(2,1)S(1)} %get-tuple-element.193), channel_id=1, source_target_pairs={{0,1},{1,0},{2,3},{3,2},{4,5},{5,4},{6,7},{7,6},{8,9},{9,8},{10,11... | collective-permute-start | bytes 1179656 | tf_op jit(solution)/shard_map/ppermute | solution.py:66
  57.3 6.9 %collective-permute-start.16 = (bf16[768,256]{1,0:T(8,128)(2,1)S(1)}, bf16[768,256]{1,0:T(8,128)(2,1)S(1)}, u32[]{:S(2)}, u32[]{:S(2)}) collective-permute-start(bf16[768,256]{1,0:T(8,128)(2,1)S(1)} %get-tuple-element.208.own), channel_id=1, source_target_pairs={{0,1},{1,0},{2,3},{3,2},{4,5},{5,4},{6,7},{7,6},{8,9},{9,8},{10,11... | collective-permute-start | bytes 1179656 | tf_op jit(solution)/shard_map/ppermute | solution.py:66
  60.9 11.2 %collective-permute-start.17 = (bf16[192,768]{1,0:T(8,128)(2,1)S(1)}, bf16[192,768]{1,0:T(8,128)(2,1)S(1)}, u32[]{:S(2)}, u32[]{:S(2)}) collective-permute-start(bf16[192,768]{1,0:T(8,128)(2,1)S(1)} %get-tuple-element.217), channel_id=1, source_target_pairs={{0,8},{4,12},{8,0},{12,4},{16,24},{20,28},{24,16},{28,20},{1,9},{5... | collective-permute-start | bytes 884744 | tf_op jit(solution)/shard_map/ppermute | solution.py:66
  63.3 11.6 %collective-permute-start.18 = (bf16[192,768]{1,0:T(8,128)(2,1)S(1)}, bf16[192,768]{1,0:T(8,128)(2,1)S(1)}, u32[]{:S(2)}, u32[]{:S(2)}) collective-permute-start(bf16[192,768]{1,0:T(8,128)(2,1)S(1)} %get-tuple-element.220), channel_id=1, source_target_pairs={{0,4},{4,0},{8,12},{12,8},{16,20},{20,16},{24,28},{28,24},{1,5},{5... | collective-permute-start | bytes 884744 | tf_op jit(solution)/shard_map/ppermute | solution.py:66
  68.8 11.8 %collective-permute-start.20 = (bf16[192,768]{1,0:T(8,128)(2,1)S(1)}, bf16[192,768]{1,0:T(8,128)(2,1)S(1)}, u32[]{:S(2)}, u32[]{:S(2)}) collective-permute-start(bf16[192,768]{1,0:T(8,128)(2,1)S(1)} %get-tuple-element.234), channel_id=1, source_target_pairs={{0,4},{4,0},{8,12},{12,8},{16,20},{20,16},{24,28},{28,24},{1,5},{5... | collective-permute-start | bytes 884744 | tf_op jit(solution)/shard_map/ppermute | solution.py:66
  70.0 11.5 %collective-permute-start.21 = (bf16[192,768]{1,0:T(8,128)(2,1)S(1)}, bf16[192,768]{1,0:T(8,128)(2,1)S(1)}, u32[]{:S(2)}, u32[]{:S(2)}) collective-permute-start(bf16[192,768]{1,0:T(8,128)(2,1)S(1)} %get-tuple-element.237), channel_id=1, source_target_pairs={{0,8},{4,12},{8,0},{12,4},{16,24},{20,28},{24,16},{28,20},{1,9},{5... | collective-permute-start | bytes 884744 | tf_op jit(solution)/shard_map/ppermute | solution.py:66
  71.6 6.0 %collective-permute-start.19 = (bf16[192,512]{1,0:T(8,128)(2,1)S(1)}, bf16[192,512]{1,0:T(8,128)(2,1)S(1)}, u32[]{:S(2)}, u32[]{:S(2)}) collective-permute-start(bf16[192,512]{1,0:T(8,128)(2,1)S(1)} %get-tuple-element.227), channel_id=1, source_target_pairs={{0,2},{1,3},{2,0},{3,1},{4,6},{5,7},{6,4},{7,5},{8,10},{9,11},{10,... | collective-permute-start | bytes 589832 | tf_op jit(solution)/shard_map/ppermute | solution.py:66
  72.2 11.4 %collective-permute-start.22 = (bf16[96,768]{1,0:T(8,128)(2,1)S(1)}, bf16[96,768]{1,0:T(8,128)(2,1)S(1)}, u32[]{:S(2)}, u32[]{:S(2)}) collective-permute-start(bf16[96,768]{1,0:T(8,128)(2,1)S(1)} %get-tuple-element.240), channel_id=1, source_target_pairs={{0,16},{4,20},{8,24},{12,28},{16,0},{20,4},{24,8},{28,12},{1,17},{... | collective-permute-start | bytes 442376 | tf_op jit(solution)/shard_map/ppermute | solution.py:66
  78.4 9.0 %collective-permute-start.23 = (bf16[96,768]{1,0:T(8,128)(2,1)S(1)}, bf16[96,768]{1,0:T(8,128)(2,1)S(1)}, u32[]{:S(2)}, u32[]{:S(2)}) collective-permute-start(bf16[96,768]{1,0:T(8,128)(2,1)S(1)} %get-tuple-element.242), channel_id=1, source_target_pairs={{0,16},{4,20},{8,24},{12,28},{16,0},{20,4},{24,8},{28,12},{1,17},{... | collective-permute-start | bytes 442376 | tf_op jit(solution)/shard_map/ppermute | solution.py:66
  80.9 6.5 %collective-permute-start.24 = (bf16[96,768]{1,0:T(8,128)(2,1)S(1)}, bf16[96,768]{1,0:T(8,128)(2,1)S(1)}, u32[]{:S(2)}, u32[]{:S(2)}) collective-permute-start(bf16[96,768]{1,0:T(8,128)(2,1)S(1)} %get-tuple-element.244), channel_id=1, source_target_pairs={{0,8},{4,12},{8,0},{12,4},{16,24},{20,28},{24,16},{28,20},{1,9},{5... | collective-permute-start | bytes 442376 | tf_op jit(solution)/shard_map/ppermute | solution.py:66
  81.6 7.4 %collective-permute-start.25 = (bf16[96,768]{1,0:T(8,128)(2,1)S(1)}, bf16[96,768]{1,0:T(8,128)(2,1)S(1)}, u32[]{:S(2)}, u32[]{:S(2)}) collective-permute-start(bf16[96,768]{1,0:T(8,128)(2,1)S(1)} %get-tuple-element.247), channel_id=1, source_target_pairs={{0,4},{4,0},{8,12},{12,8},{16,20},{20,16},{24,28},{28,24},{1,5},{5... | collective-permute-start | bytes 442376 | tf_op jit(solution)/shard_map/ppermute | solution.py:66
  87.5 6.8 %collective-permute-start.27 = (bf16[48,768]{1,0:T(8,128)(2,1)S(1)}, bf16[48,768]{1,0:T(8,128)(2,1)S(1)}, u32[]{:S(2)}, u32[]{:S(2)}) collective-permute-start(bf16[48,768]{1,0:T(8,128)(2,1)S(1)} %get-tuple-element.252), channel_id=1, source_target_pairs={{0,16},{4,20},{8,24},{12,28},{16,0},{20,4},{24,8},{28,12},{1,17},{... | collective-permute-start | bytes 221192 | tf_op jit(solution)/shard_map/ppermute | solution.py:66
  89.1 7.3 %collective-permute-start.28 = (bf16[48,768]{1,0:T(8,128)(2,1)S(1)}, bf16[48,768]{1,0:T(8,128)(2,1)S(1)}, u32[]{:S(2)}, u32[]{:S(2)}) collective-permute-start(bf16[48,768]{1,0:T(8,128)(2,1)S(1)} %get-tuple-element.254), channel_id=1, source_target_pairs={{0,16},{4,20},{8,24},{12,28},{16,0},{20,4},{24,8},{28,12},{1,17},{... | collective-permute-start | bytes 221192 | tf_op jit(solution)/shard_map/ppermute | solution.py:66
  90.6 1.9 %collective-permute-start.26 = (f32[8,768]{1,0:T(8,128)S(1)}, f32[8,768]{1,0:T(8,128)S(1)}, u32[]{:S(2)}, u32[]{:S(2)}) collective-permute-start(f32[8,768]{1,0:T(8,128)S(1)} %get-tuple-element.250.refs_0_), channel_id=1, source_target_pairs={{0,1},{1,0},{2,3},{3,2},{4,5},{5,4},{6,7},{7,6},{8,9},{9,8},{10,11... | collective-permute-start | bytes 73736 | tf_op jit(solution)/shard_map/ppermute | solution.py:66
  90.6 5.7 %collective-permute-start.29 = (bf16[384,512]{1,0:T(8,128)(2,1)S(1)}, bf16[384,512]{1,0:T(8,128)(2,1)S(1)}, u32[]{:S(2)}, u32[]{:S(2)}) collective-permute-start(bf16[384,512]{1,0:T(8,128)(2,1)S(1)} %get-tuple-element.225), channel_id=1, source_target_pairs={{0,1},{1,0},{2,3},{3,2},{4,5},{5,4},{6,7},{7,6},{8,9},{9,8},{10,11... | collective-permute-start | bytes 1179656 | tf_op jit(solution)/shard_map/ppermute | solution.py:66
  91.1 17.5 %collective-permute-start.32 = (bf16[96,768]{1,0:T(8,128)(2,1)S(1)}, bf16[96,768]{1,0:T(8,128)(2,1)S(1)}, u32[]{:S(2)}, u32[]{:S(2)}) collective-permute-start(bf16[96,768]{1,0:T(8,128)(2,1)S(1)} %shard_map.282.refs_0_), channel_id=1, source_target_pairs={{0,16},{4,20},{8,24},{12,28},{16,0},{20,4},{24,8},{28,12},{1,17},{... | collective-permute-start | bytes 442376 | tf_op jit(solution)/shard_map/ppermute | solution.py:66
  92.6 16.0 %collective-permute-start.31 = (bf16[96,768]{1,0:T(8,128)(2,1)S(1)}, bf16[96,768]{1,0:T(8,128)(2,1)S(1)}, u32[]{:S(2)}, u32[]{:S(2)}) collective-permute-start(bf16[96,768]{1,0:T(8,128)(2,1)S(1)} %shard_map.281.refs_0_), channel_id=1, source_target_pairs={{0,16},{4,20},{8,24},{12,28},{16,0},{20,4},{24,8},{28,12},{1,17},{... | collective-permute-start | bytes 442376 | tf_op jit(solution)/shard_map/ppermute | solution.py:66
  94.3 9.6 %collective-permute-start.30 = (f32[8,768]{1,0:T(8,128)S(1)}, f32[8,768]{1,0:T(8,128)S(1)}, u32[]{:S(2)}, u32[]{:S(2)}) collective-permute-start(f32[8,768]{1,0:T(8,128)S(1)} %shard_map.285.refs_0_), channel_id=1, source_target_pairs={{0,2},{1,3},{2,0},{3,1},{4,6},{5,7},{6,4},{7,5},{8,10},{9,11},{10,... | collective-permute-start | bytes 73736 | tf_op jit(solution)/shard_map/ppermute | solution.py:66
  96.3 23.3 %copy-start.3 = (bf16[192,512]{1,0:T(8,128)(2,1)S(1)}, bf16[192,512]{1,0:T(8,128)(2,1)}, u32[]{:S(2)}) copy-start(bf16[192,512]{1,0:T(8,128)(2,1)} %x_in) | copy-start | bytes 589828
  96.5 23.1 %collective-permute-start.34 = (bf16[192,512]{1,0:T(8,128)(2,1)S(1)}, bf16[192,512]{1,0:T(8,128)(2,1)S(1)}, u32[]{:S(2)}, u32[]{:S(2)}) collective-permute-start(bf16[192,512]{1,0:T(8,128)(2,1)S(1)} %get-tuple-element.262), channel_id=1, source_target_pairs={{0,2},{1,3},{2,0},{3,1},{4,6},{5,7},{6,4},{7,5},{8,10},{9,11},{10,... | collective-permute-start | bytes 589832 | tf_op jit(solution)/shard_map/ppermute | solution.py:66
  108.6 20.9 %collective-permute-start.38 = (bf16[192,768]{1,0:T(8,128)(2,1)S(1)}, bf16[192,768]{1,0:T(8,128)(2,1)S(1)}, u32[]{:S(2)}, u32[]{:S(2)}) collective-permute-start(bf16[192,768]{1,0:T(8,128)(2,1)S(1)} %shard_map.290.refs_0_), channel_id=1, source_target_pairs={{0,8},{4,12},{8,0},{12,4},{16,24},{20,28},{24,16},{28,20},{1,9},{5... | collective-permute-start | bytes 884744 | tf_op jit(solution)/shard_map/ppermute | solution.py:66
  108.7 20.8 %collective-permute-start.39 = (bf16[192,768]{1,0:T(8,128)(2,1)S(1)}, bf16[192,768]{1,0:T(8,128)(2,1)S(1)}, u32[]{:S(2)}, u32[]{:S(2)}) collective-permute-start(bf16[192,768]{1,0:T(8,128)(2,1)S(1)} %shard_map.291.refs_0_), channel_id=1, source_target_pairs={{0,4},{4,0},{8,12},{12,8},{16,20},{20,16},{24,28},{28,24},{1,5},{5... | collective-permute-start | bytes 884744 | tf_op jit(solution)/shard_map/ppermute | solution.py:66
  109.4 8.5 %collective-permute-start.33 = (f32[8,768]{1,0:T(8,128)S(1)}, f32[8,768]{1,0:T(8,128)S(1)}, u32[]{:S(2)}, u32[]{:S(2)}) collective-permute-start(f32[8,768]{1,0:T(8,128)S(1)} %shard_map.289.refs_0_.row_sums), channel_id=1, source_target_pairs={{0,4},{4,0},{8,12},{12,8},{16,20},{20,16},{24,28},{28,24},{1,5},{5... | collective-permute-start | bytes 73736 | tf_op jit(solution)/shard_map/ppermute | solution.py:66
  110.8 9.0 %collective-permute-start.35 = (bf16[48,768]{1,0:T(8,128)(2,1)S(1)}, bf16[48,768]{1,0:T(8,128)(2,1)S(1)}, u32[]{:S(2)}, u32[]{:S(2)}) collective-permute-start(bf16[48,768]{1,0:T(8,128)(2,1)S(1)} %shard_map.286.refs_0_), channel_id=1, source_target_pairs={{0,16},{4,20},{8,24},{12,28},{16,0},{20,4},{24,8},{28,12},{1,17},{... | collective-permute-start | bytes 221192 | tf_op jit(solution)/shard_map/ppermute | solution.py:66
  117.9 5.4 %collective-permute-start.36 = (bf16[48,768]{1,0:T(8,128)(2,1)S(1)}, bf16[48,768]{1,0:T(8,128)(2,1)S(1)}, u32[]{:S(2)}, u32[]{:S(2)}) collective-permute-start(bf16[48,768]{1,0:T(8,128)(2,1)S(1)} %shard_map.287.refs_0_), channel_id=1, source_target_pairs={{0,16},{4,20},{8,24},{12,28},{16,0},{20,4},{24,8},{28,12},{1,17},{... | collective-permute-start | bytes 221192 | tf_op jit(solution)/shard_map/ppermute | solution.py:66
  119.8 18.4 %collective-permute-start.41 = (bf16[96,768]{1,0:T(8,128)(2,1)S(1)}, bf16[96,768]{1,0:T(8,128)(2,1)S(1)}, u32[]{:S(2)}, u32[]{:S(2)}) collective-permute-start(bf16[96,768]{1,0:T(8,128)(2,1)S(1)} %shard_map.294.refs_0_), channel_id=1, source_target_pairs={{0,8},{4,12},{8,0},{12,4},{16,24},{20,28},{24,16},{28,20},{1,9},{5... | collective-permute-start | bytes 442376 | tf_op jit(solution)/shard_map/ppermute | solution.py:66
  123.3 15.0 %collective-permute-start.42 = (bf16[96,768]{1,0:T(8,128)(2,1)S(1)}, bf16[96,768]{1,0:T(8,128)(2,1)S(1)}, u32[]{:S(2)}, u32[]{:S(2)}) collective-permute-start(bf16[96,768]{1,0:T(8,128)(2,1)S(1)} %shard_map.295.refs_0_), channel_id=1, source_target_pairs={{0,4},{4,0},{8,12},{12,8},{16,20},{20,16},{24,28},{28,24},{1,5},{5... | collective-permute-start | bytes 442376 | tf_op jit(solution)/shard_map/ppermute | solution.py:66
  123.9 3.8 %collective-permute-start.37 = (f32[8,768]{1,0:T(8,128)S(1)}, f32[8,768]{1,0:T(8,128)S(1)}, u32[]{:S(2)}, u32[]{:S(2)}) collective-permute-start(f32[8,768]{1,0:T(8,128)S(1)} %shard_map.292.refs_0_), channel_id=1, source_target_pairs={{0,8},{4,12},{8,0},{12,4},{16,24},{20,28},{24,16},{28,20},{1,9},{5... | collective-permute-start | bytes 73736 | tf_op jit(solution)/shard_map/ppermute | solution.py:66
  127.8 4.8 %collective-permute-start.40 = (f32[8,768]{1,0:T(8,128)S(1)}, f32[8,768]{1,0:T(8,128)S(1)}, u32[]{:S(2)}, u32[]{:S(2)}) collective-permute-start(f32[8,768]{1,0:T(8,128)S(1)} %shard_map.296.refs_0_), channel_id=1, source_target_pairs={{0,16},{4,20},{8,24},{12,28},{16,0},{20,4},{24,8},{28,12},{1,17},{... | collective-permute-start | bytes 73736 | tf_op jit(solution)/shard_map/ppermute | solution.py:66
  129.6 16.3 %collective-permute-start.44 = (bf16[384,768]{1,0:T(8,128)(2,1)S(1)}, bf16[384,768]{1,0:T(8,128)(2,1)S(1)}, u32[]{:S(2)}, u32[]{:S(2)}) collective-permute-start(bf16[384,768]{1,0:T(8,128)(2,1)S(1)} %shard_map.298.refs_0_), channel_id=1, source_target_pairs={{0,8},{4,12},{8,0},{12,4},{16,24},{20,28},{24,16},{28,20},{1,9},{5... | collective-permute-start | bytes 1769480 | tf_op jit(solution)/shard_map/ppermute | solution.py:66
  130.3 14.0 %collective-permute-start.43 = (bf16[384,768]{1,0:T(8,128)(2,1)S(1)}, bf16[384,768]{1,0:T(8,128)(2,1)S(1)}, u32[]{:S(2)}, u32[]{:S(2)}) collective-permute-start(bf16[384,768]{1,0:T(8,128)(2,1)S(1)} %shard_map.297.refs_0_), channel_id=1, source_target_pairs={{0,4},{4,0},{8,12},{12,8},{16,20},{20,16},{24,28},{28,24},{1,5},{5... | collective-permute-start | bytes 1769480 | tf_op jit(solution)/shard_map/ppermute | solution.py:66
  138.3 9.2 %collective-permute-start.46 = (bf16[192,768]{1,0:T(8,128)(2,1)S(1)}, bf16[192,768]{1,0:T(8,128)(2,1)S(1)}, u32[]{:S(2)}, u32[]{:S(2)}) collective-permute-start(bf16[192,768]{1,0:T(8,128)(2,1)S(1)} %shard_map.304.refs_2_), channel_id=1, source_target_pairs={{0,8},{4,12},{8,0},{12,4},{16,24},{20,28},{24,16},{28,20},{1,9},{5... | collective-permute-start | bytes 884744 | tf_op jit(solution)/shard_map/ppermute | solution.py:66
  140.4 7.1 %collective-permute-start.45 = (bf16[192,768]{1,0:T(8,128)(2,1)S(1)}, bf16[192,768]{1,0:T(8,128)(2,1)S(1)}, u32[]{:S(2)}, u32[]{:S(2)}) collective-permute-start(bf16[192,768]{1,0:T(8,128)(2,1)S(1)} %shard_map.303.refs_0_), channel_id=1, source_target_pairs={{0,4},{4,0},{8,12},{12,8},{16,20},{20,16},{24,28},{28,24},{1,5},{5... | collective-permute-start | bytes 884744 | tf_op jit(solution)/shard_map/ppermute | solution.py:66
  (8 other events, 35.7 us)

commit v6 on v5

--- a/solution.py
+++ b/solution.py
@@ -24,15 +24,17 @@
     cost = 10**9
 
 
-def kernel(body, outs, scalars, arrays, scratch=(), limit=12):
+def kernel(body, outs, scalars, arrays, scratch=(), limit=12, streamed=()):
     arrays = list(arrays)
     if Order.last is not None:
         arrays[0] = after(arrays[0], Order.last)
+    spaces = [pltpu.VMEM] * len(arrays) + [pltpu.HBM] * len(streamed)
+    arrays += [pltpu.with_memory_space_constraint(v, pltpu.HBM) for v in streamed]
     found = pl.pallas_call(
         body,
         out_shape=outs,
         in_specs=[pl.BlockSpec(memory_space=pltpu.SMEM)] * len(scalars)
-        + [pl.BlockSpec(memory_space=pltpu.VMEM)] * len(arrays),
+        + [pl.BlockSpec(memory_space=space) for space in spaces],
         out_specs=jax.tree.map(lambda _: pl.BlockSpec(memory_space=pltpu.VMEM), outs),
         scratch_shapes=list(scratch),
         compiler_params=pltpu.CompilerParams(vmem_limit_bytes=limit * 1024 * 1024),
@@ -323,7 +325,8 @@
     return mean, lax.rsqrt(column_sum(each_rows(count, squares, zero)) / count + EPSILON)
 
 
-def prepare_kernel(now, *refs):
+def prepare_kernel(held, *refs):
+    refs = refs[held:]
     sources, (norms, cosine, sine), places, sem = refs[:6], refs[6:9], refs[9:15], refs[15]
     copies = [pltpu.make_async_copy(*pair, sem.at[i]) for i, pair in enumerate(zip(sources, places))]
     for copy in copies:
@@ -339,19 +342,19 @@
     sine[...] = jnp.sin(angles)
 
 
-def prepare(now, *sources):
+def prepare(held, *sources):
     tokens, part = sources[0].shape[1], sources[2].shape[1]
     rates = sources[1].shape[0]
     vmem = pl.BlockSpec(memory_space=pltpu.VMEM)
     found = pl.pallas_call(
-        prepare_kernel,
+        functools.partial(prepare_kernel, len(held)),
         out_shape=(shape(8, -(-part // 128) * 128), shape(rates, tokens), shape(rates, tokens)),
-        in_specs=[vmem] + [pl.BlockSpec(memory_space=pltpu.HBM)] * len(sources),
+        in_specs=[vmem] * len(held) + [pl.BlockSpec(memory_space=pltpu.HBM)] * len(sources),
         out_specs=(vmem,) * 3,
         scratch_shapes=[pltpu.VMEM(v.shape, v.dtype) for v in sources] + [pltpu.SemaphoreType.DMA((len(sources),))],
         compiler_params=pltpu.CompilerParams(vmem_limit_bytes=4 * 1024 * 1024),
         cost_estimate=pl.CostEstimate(flops=Order.cost, bytes_accessed=1024, transcendentals=0),
-    )(now, *(pltpu.with_memory_space_constraint(v, pltpu.HBM) for v in sources))
+    )(*held, *(pltpu.with_memory_space_constraint(v, pltpu.HBM) for v in sources))
     Order.last = found[0]
     return found
 
@@ -365,13 +368,17 @@
 
 
 def project_kernel(
-    at_ref, x0, x1, x2, x3, norms, cosine, sine, w_qkv, w_out, x_all, normed, stats, qkv, project
+    at_ref, x1, x2, x3, norms, cosine, sine, w_qkv, x0, x_all, normed, stats, qkv, project, own, sem
 ):
     at = at_ref[0]
-    part, tokens = x0.shape
+    part, tokens = x1.shape
     model = w_qkv.shape[1]
-    for e, piece in enumerate((x0, x1, x2, x3)):
+    copy = pltpu.make_async_copy(x0, own, sem)
+    copy.start()
+    for e, piece in ((1, x1), (2, x2), (3, x3)):
         x_all[pl.ds(pl.multiple_of((at ^ e) * part, 64), part), :] = piece[...]
+    copy.wait()
+    x_all[pl.ds(pl.multiple_of(at * part, 64), part), :] = own[...]
     mean, scale = spread_of(lambda i: x_all[rows_at(i), :].astype(F32), model, tokens)
     stats[0:1] = mean
     stats[1:2] = scale
@@ -393,8 +400,10 @@
     qkv[2 * part :] = project[2 * part :].astype(BF16)
 
 
-def attention_kernel(at_ref, qkv, w_out, x_all, send, keep, x_half, heads_out, probs, scores):
+def attention_kernel(at_ref, qkv, x_all, w_out_hbm, send, keep, x_half, heads_out, probs, scores, w_out, sem):
     at = at_ref[0]
+    copy = pltpu.make_async_copy(w_out_hbm, w_out, sem)
+    copy.start()
     part, tokens = heads_out.shape
     half = tokens // 2
     for h in range(part // HEAD_DIM):
@@ -435,6 +444,7 @@
             heads_out[head, now] = dot(value, probs[h, :count, now], 1, 0).astype(BF16)
     own = pl.multiple_of((at % 2) * half, half)
     other = pl.multiple_of((1 - at % 2) * half, half)
+    copy.wait()
     send[...] = dot(w_out[...], heads_out[:, pl.ds(other, half)], 0, 0).astype(BF16)
     keep[...] = dot(w_out[...], heads_out[:, pl.ds(own, half)], 0, 0)
     x_half[...] = x_all[:, pl.ds(own, half)]
@@ -506,22 +516,20 @@
     keep[...] = dot(w_up[...], d_hidden[:, :half], 1, 0)
 
 
-def store_blocks(at, total, part, send, keep):
-    for place in range(2):
-        for low, out in ((1, send), (0, keep)):
-            rows = pl.ds(pl.multiple_of((at ^ (2 * place + low)) * part, 64), part)
-            out[place * part : (place + 1) * part] = total[rows, :].astype(out.dtype)
-
-
-def output_kernel(at_ref, active, w_down, middle, send, keep, total):
+def store_blocks(at, total, part, near, *outs):
+    for e, out in zip(near, outs):
+        out[...] = total[pl.ds(pl.multiple_of((at ^ e) * part, 64), part), :].astype(out.dtype)
+
+
+def output_kernel(at_ref, active, w_down, middle, send, send_far, keep, keep_far, total):
     at = at_ref[0]
     model, half = middle.shape
-    part = send.shape[0] // 2
+    part = send.shape[0]
     own = pl.ds(pl.multiple_of((at % 2) * half, half), half)
     other = pl.ds(pl.multiple_of((1 - at % 2) * half, half), half)
     total[:, own] = dot(w_down[...], active[:, :half], 0, 0) + 0.5 * middle[...]
     total[:, other] = dot(w_down[...], active[:, half:], 0, 0)
-    store_blocks(at, total, part, send, keep)
+    store_blocks(at, total, part, (1, 3, 0, 2), send, send_far, keep, keep_far)
 
 
 def fold_lanes(value):
@@ -620,12 +628,13 @@
 
 
 def input_gradient_kernel(
-    width, at_ref, counts_ref, d_project, w_qkv, x_all, stats, d_middle, norms, gains, send, keep, sums, total, gain_sums, bias_sums
+    width, at_ref, counts_ref, d_project, w_qkv, x_all, stats, d_middle, norms, gains,
+    send, send_far, keep, keep_far, sums, total, gain_sums, bias_sums,
 ):
     at = at_ref[0]
     model, half = d_middle.shape
     tokens = x_all.shape[1]
-    part = send.shape[0] // 2
+    part = send.shape[0]
     total[...] = dot(w_qkv[...], d_project[...], 0, 0)
     mean, scale = stats[0:1], stats[1:2]
     zero = jnp.zeros((STEP, tokens), F32)
@@ -645,7 +654,7 @@
         return acc[0] + lifted, acc[1] + both * gain
 
     first, second = each_rows(model, body, (zero, zero))
-    store_blocks(at, total, part, send, keep)
+    store_blocks(at, total, part, (1, 3, 0, 2), send, send_far, keep, keep_far)
     sums[...] = jnp.zeros_like(sums)
     sums[0:1] = as_row(gain_sums)
     sums[1:2] = as_row(bias_sums)
@@ -656,15 +665,15 @@
 
 
 def mixed_kernel(
-    self_ref, counts_ref, chip, received, running, cotangent, d_mix, sums, mixed, all_sums, table
+    self_ref, counts_ref, own, near, far, running, cotangent, d_mix, sums, mixed, all_sums, table
 ):
     layers = d_mix.shape[0]
-    part, tokens = chip.shape
+    part, tokens = own.shape
     live = live_row(counts_ref, tokens, 0)
 
     def body(i, acc):
         rows = rows_at(i)
-        output = chip[rows, :] + received[rows, :].astype(F32)
+        output = own[rows, :] + near[rows, :].astype(F32) + far[rows, :].astype(F32)
         mixed[rows, :] = (self_ref[0] * output + running[rows, :]).astype(BF16)
         return acc + fold_lanes(cotangent[rows, :].astype(F32) * live * output)
 
@@ -689,15 +698,16 @@
         end[...] = found
 
 
-def d_input_kernel(chip, received, x_in, stats, row_sums, found):
-    part, tokens = chip.shape
+def d_input_kernel(own, near, far, x_in, stats, row_sums, found):
+    part, tokens = own.shape
     mean, scale = stats[0:1], stats[1:2]
     first, second = row_sums[4:5, :tokens], row_sums[5:6, :tokens]
 
     def body(i, _):
         rows = rows_at(i)
         xhat = (x_in[rows, :].astype(F32) - mean) * scale
-        found[rows, :] = chip[rows, :] + received[rows, :].astype(F32) - scale * (first + xhat * second)
+        total = own[rows, :] + near[rows, :].astype(F32) + far[rows, :].astype(F32)
+        found[rows, :] = total - scale * (first + xhat * second)
 
     each_rows(part, body)
 
@@ -747,7 +757,7 @@
 
     x_far, x_near = to_width(x_in, 2), to_width(x_in, 1)
     norms, cosine, sine = prepare(
-        x_near,
+        [x_near],
         positions[None, :],
         jnp.asarray(rates[:, None], F32),
         *(v[None, :] for v in (first_norm_gain, first_norm_bias, second_norm_gain, second_norm_bias)),
@@ -757,7 +767,7 @@
     norms_far = to_width(norms_near, 2)
     norms = kernel(norms_kernel, shape(model, 8), [at], [norms_near, norms_far])
     x_both = to_width(after(x_far, norms), 1)
-    cot_now = after(cotangent, x_far)
+    cot_now = after(cotangent, norms_near)
     cot_far, cot_near = to_width(cot_now, 2), to_width(cot_now, 1)
 
     x_all, normed_one, stats_one, qkv = kernel(
@@ -769,8 +779,9 @@
             shape(3 * part, tokens, kind=BF16),
         ),
         [at],
-        [x_in, x_near, x_far, x_both, norms, cosine, sine, w_qkv, w_out],
-        [pltpu.VMEM((3 * part, tokens), F32)],
+        [x_near, x_far, x_both, norms, cosine, sine, w_qkv],
+        [pltpu.VMEM((3 * part, tokens), F32), pltpu.VMEM((part, tokens), BF16), pltpu.SemaphoreType.DMA],
+        streamed=[x_in],
     )
     Order.cost = 10**9
     send, keep, x_half, heads_out, probs = kernel(
@@ -783,8 +794,9 @@
             shape(part // HEAD_DIM, tokens, tokens, kind=BF16),
         ),
         [at],
-        [after(qkv, cot_far), w_out, x_all],
-        [pltpu.VMEM((tokens, half), F32)],
+        [after(qkv, cot_far), x_all],
+        [pltpu.VMEM((tokens, half), F32), pltpu.VMEM((part, model), BF16), pltpu.SemaphoreType.DMA],
+        streamed=[w_out],
     )
     chip, send = add([keep, to_width(send, 1)], (0, model, F32), (0, model, BF16))
     received = to_width(send, 2)
@@ -834,11 +846,11 @@
     received = to_width(send, 2)
     up_parts = weight_gradient(me, [up], normed_two, d_hidden)[0]
     up_got = start_stage(up, up_parts, 0)
-    blocks = (shape(2 * part, tokens, kind=BF16), shape(2 * part, tokens))
-    out_send, out_keep = kernel(
+    blocks = (shape(part, tokens, kind=BF16),) * 2 + (shape(part, tokens),) * 2
+    out_send, out_send_far, out_keep, out_keep_far = kernel(
         output_kernel, blocks, [at], [active, w_down, middle], [pltpu.VMEM((model, tokens), F32)]
     )
-    out_near = to_width(out_send, 1)
+    out_got = to_width(out_send, 1), to_width(out_send_far, 1)
 
     d_middle, g_own, gains_two = kernel(
         middle_gradient_kernel,
@@ -848,7 +860,7 @@
         [pltpu.VMEM((model, half), F32), pltpu.VMEM((model, 128), F32), pltpu.VMEM((model, 128), F32)],
     )
     g_other = to_width(g_own, 1)
-    out_chip, out_send = add([out_keep, out_near], (0, part, F32), (part, 2 * part, BF16))
+    out_send = add([out_keep_far, out_got[1]], (0, part, BF16))[0]
     out_far = to_width(out_send, 2)
     down_parts = add_stage(down, down_parts, down_got, 0)
     down_got = start_stage(down, down_parts, 1)
@@ -883,20 +895,20 @@
     down_got = start_stage(down, down_parts, 2)
     up_parts = add_stage(up, up_parts, up_got, 1)
     up_got = start_stage(up, up_parts, 2)
-    in_send, in_keep, sums = kernel(
+    in_send, in_send_far, in_keep, in_keep_far, sums = kernel(
         functools.partial(input_gradient_kernel, width),
         blocks + (shape(8, model),),
         [at, counts],
         [d_project, w_qkv, x_all, stats_one, d_middle, norms, gains_two],
         [pltpu.VMEM((model, tokens), F32), pltpu.VMEM((model, 128), F32), pltpu.VMEM((model, 128), F32)],
     )
-    in_near = to_width(in_send, 1)
+    in_got = to_width(in_send, 1), to_width(in_send_far, 1)
     last = len(down.digits) - 1
     mixed, sums = kernel(
         mixed_kernel,
         (shape(part, tokens, kind=BF16), shape(8, model)),
         [self_weight, counts],
-        [out_chip, out_far, running, cotangent, d_mix, sums],
+        [out_keep, out_got[0], out_far, running, cotangent, d_mix, sums],
         [pltpu.VMEM((128, 128), F32)],
     )
     sums_got = to_width(sums, 1)
@@ -914,29 +926,27 @@
     second_got = start_stage(second, second_parts, 2)
     sums = add([sums, sums_got], (0, 8, F32))[0]
     sums_got = to_width(sums, 2)
-    first_value = sum_rest(first, add_stage(first, first_parts, first_got, 2)[0])
-    first_pieces = gather_stage(first, first_value, last)
-    Order.cost = 2 * 10**10
-    second_value = sum_rest(second, add_stage(second, second_parts, second_got, 2)[0])
-    second_pieces = gather_stage(second, second_value, last)
-    Order.cost = 10**8
-    in_chip, in_send = add([in_keep, in_near], (0, part, F32), (part, 2 * part, BF16))
-    in_far = to_width(in_send, 2)
     row_sums = add([sums, sums_got], (0, 8, F32))[0]
     sums_got = to_row(row_sums, strides[0])
     down_pieces = gather_stage(down, join(down_pieces), last - 1)
     up_pieces = gather_stage(up, join(up_pieces), last - 1)
+    in_send = add([in_keep_far, in_got[1]], (0, part, BF16))[0]
+    in_far = to_width(in_send, 2)
     sums = row_sums
     for stride in strides[1:-1]:
         sums = add([sums, sums_got], (0, 8, F32))[0]
         sums_got = to_row(sums, stride)
-    in_total = kernel(d_input_kernel, shape(part, tokens), [], [in_chip, in_far, x_in, stats_one, row_sums])
+    first_value = sum_rest(first, add_stage(first, first_parts, first_got, 2)[0])
+    first_pieces = gather_stage(first, first_value, last)
+    second_value = sum_rest(second, add_stage(second, second_parts, second_got, 2)[0])
+    second_pieces = gather_stage(second, second_value, last)
+    sums = add([sums, sums_got], (0, 8, F32))[0]
+    sums_got = to_row(sums, strides[-1])
+    in_total = kernel(d_input_kernel, shape(part, tokens), [], [in_keep, in_got[0], in_far, x_in, stats_one, row_sums])
+    down_pieces = gather_stage(down, join(down_pieces), 0)
+    up_pieces = gather_stage(up, join(up_pieces), 0)
     first_pieces = gather_stage(first, join(first_pieces), last - 1)
     second_pieces = gather_stage(second, join(second_pieces), last - 1)
-    sums = add([sums, sums_got], (0, 8, F32))[0]
-    sums_got = to_row(sums, strides[-1])
-    down_pieces = gather_stage(down, join(down_pieces), 0)
-    up_pieces = gather_stage(up, join(up_pieces), 0)
     sums = add([sums, sums_got], (0, 8, F32))[0]
     d_input = kernel(
         functools.partial(scale_kernel, all_tokens), shape(part, tokens), [], [in_total, sums]

time: 150 us -> 150 us (level)
  waiting for transfers between devices: 40.7 us -> 52.5 us
  starting transfers between devices: 58.9 us -> 48.7 us
  local copies, waits for them, and re-layouts: 1.93 us -> 0.04 us
    ppermute x47 -> x49, waiting for transfers between devices: 40.7 us -> 52.5 us  [xor_send(): return lax.ppermute(value, axis, [(i, i ^ offset) for i in range(size)])]
    ppermute x47 -> x49, starting transfers between devices: 58.9 us -> 48.7 us  [xor_send(): return lax.ppermute(value, axis, [(i, i ^ offset) for i in range(size)])]
    unnamed x18 -> x14, local copies, waits for them, and re-layouts: 1.93 us -> 0.04 us
  transfers between devices with their start and end apart: 47 -> 49, of which waited for: 19 -> 23; matrix products, arithmetic and copies ran while one was open for 0% -> 0% of each run, Pallas kernels for 23% -> 23%
where the time goes in v6:
time: 150 us
  waiting for transfers between devices  52.5 us (35%)
  starting transfers between devices  48.7 us (32%)
  Pallas kernels  46.4 us (31%)
  between operations  2.52 us (2%)
    ppermute x49, waiting for transfers between devices, xor_send(): return lax.ppermute(value, axis, [(i, i ^ offset) for i in range(size)])  52.5 us
    ppermute x49, starting transfers between devices, xor_send(): return lax.ppermute(value, axis, [(i, i ^ offset) for i in range(size)])  48.7 us
    pallas_call x50, Pallas kernels, kernel(): pl.pallas_call(body, out_shape=outs, in_specs=[pl.BlockSpec(memory_space=...  35.5 us
    pallas_call x2, Pallas kernels, history_call(): pl.pallas_call(body, out_shape=outs, in_specs=[pl.BlockSpec(memory_space=...  9.78 us
  transfers between devices with their start and end apart: 49, of which 23 were waited for; matrix products, arithmetic and copies ran while one was open for 0% of the time, Pallas kernels for 23%

profile of v6, /device:TPU:0, one launch (start us, length us, event | category | flops | bytes accessed | tf_op | source)
XLA Modules:
  0.0 150.2 jit_solution(3656429095959936488)
XLA Ops:
  1.2 2.6 %collective-permute-start.3 = (bf16[192,512]{1,0:T(8,128)(2,1)}, bf16[192,512]{1,0:T(8,128)(2,1)S(1)}, u32[]{:S(2)}, u32[]{:S(2)}) collective-permute-start(bf16[192,512]{1,0:T(8,128)(2,1)} %x_in), channel_id=1, source_target_pairs={{0,2},{1,3},{2,0},{3,1},{4,6},{5,7},{6,4},{7,5},{8,10},{9,11},{10,... | collective-permute-start | bytes 589832 | tf_op jit(solution)/shard_map/ppermute | solution.py:68
  6.1 1.6 %collective-permute-start.2 = (f32[16,256]{1,0:T(8,128)S(1)}, f32[16,256]{1,0:T(8,128)S(1)}, u32[]{:S(2)}, u32[]{:S(2)}) collective-permute-start(f32[16,256]{1,0:T(8,128)S(1)} %shard_map.256.n01), channel_id=1, source_target_pairs={{0,2},{1,3},{2,0},{3,1},{4,6},{5,7},{6,4},{7,5},{8,10},{9,11},{10,... | collective-permute-start | bytes 49160 | tf_op jit(solution)/shard_map/ppermute | solution.py:68
  7.7 2.2 %collective-permute-done.2.n23 = f32[16,256]{1,0:T(8,128)S(1)} collective-permute-done((f32[16,256]{1,0:T(8,128)S(1)}, f32[16,256]{1,0:T(8,128)S(1)}, u32[]{:S(2)}, u32[]{:S(2)}) %collective-permute-start.2) | collective-permute-done | bytes 16416 | tf_op jit(solution)/shard_map/ppermute | solution.py:68
  10.2 1.8 %collective-permute-start.5 = (bf16[192,512]{1,0:T(8,128)(2,1)}, bf16[192,512]{1,0:T(8,128)(2,1)S(1)}, u32[]{:S(2)}, u32[]{:S(2)}) collective-permute-start(bf16[192,512]{1,0:T(8,128)(2,1)} %cot_ref.1), channel_id=1, source_target_pairs={{0,2},{1,3},{2,0},{3,1},{4,6},{5,7},{6,4},{7,5},{8,10},{9,11},{10,... | collective-permute-start | bytes 589832 | tf_op jit(solution)/shard_map/ppermute | solution.py:68
  12.0 3.1 %shard_map.258 = (bf16[768,512]{1,0:T(8,128)(2,1)S(1)}, bf16[768,512]{1,0:T(8,128)(2,1)S(1)}, f32[2,512]{1,0:T(2,128)S(1)}, bf16[576,512]{1,0:T(8,128)(2,1)S(1)}) custom-call(s32[1]{0:T(128)} %bitcast.at_ref, bf16[192,512]{1,0:T(8,128)(2,1)S(1)} %collective-permute-done.refs_0_.x1, bf16[192,512]{1,0:T(8,128)(2,1)S(1)} %collective-permute-done.3.x2, ...), custom_call_target="tpu_custom_call" | custom-call | flops 100000000 | bytes 1024 | tf_op jit(solution)/shard_map/pallas_call | solution.py:33
  15.1 2.6 %collective-permute-done.5.c2 = bf16[192,512]{1,0:T(8,128)(2,1)S(1)} collective-permute-done((bf16[192,512]{1,0:T(8,128)(2,1)}, bf16[192,512]{1,0:T(8,128)(2,1)S(1)}, u32[]{:S(2)}, u32[]{:S(2)}) %collective-permute-start.5) | collective-permute-done | bytes 196640 | tf_op jit(solution)/shard_map/ppermute | solution.py:68
  17.7 4.8 %shard_map.259 = (bf16[768,256]{1,0:T(8,128)(2,1)S(1)}, f32[768,256]{1,0:T(8,128)S(1)}, bf16[768,256]{1,0:T(8,128)(2,1)S(1)}, bf16[192,512]{1,0:T(8,128)(2,1)S(1)}, bf16[3,512,512]{2,1,0:T(8,128)(2,1)S(1)}) custom-call(s32[1]{0:T(128)} %bitcast.at_ref, bf16[576,512]{1,0:T(8,128)(2,1)S(1)} %get-tuple-element.163.qkv, ...), custom_call_target="tpu_custom_call" | custom-call | flops 1000000000 | bytes 1024 | tf_op jit(solution)/shard_map/pallas_call | solution.py:33
  22.6 1.7 %collective-permute-done.6.refs_1_ = bf16[768,256]{1,0:T(8,128)(2,1)S(1)} collective-permute-done((bf16[768,256]{1,0:T(8,128)(2,1)S(1)}, bf16[768,256]{1,0:T(8,128)(2,1)S(1)}, u32[]{:S(2)}, u32[]{:S(2)}) %collective-permute-start.6) | collective-permute-done | bytes 393248 | tf_op jit(solution)/shard_map/ppermute | solution.py:68
  24.6 1.8 %collective-permute-start.9 = (bf16[768,256]{1,0:T(8,128)(2,1)S(1)}, bf16[768,256]{1,0:T(8,128)(2,1)S(1)}, u32[]{:S(2)}, u32[]{:S(2)}) collective-permute-start(bf16[768,256]{1,0:T(8,128)(2,1)S(1)} %get-tuple-element.175), channel_id=1, source_target_pairs={{0,2},{1,3},{2,0},{3,1},{4,6},{5,7},{6,4},{7,5},{8,10},{9,11},{10,... | collective-permute-start | bytes 1179656 | tf_op jit(solution)/shard_map/ppermute | solution.py:68
  28.2 5.7 %shard_map.261 = (f32[192,512]{1,0:T(8,128)S(1)}, f32[30,8,128]{2,1,0:T(8,128)S(1)}) custom-call(f32[30]{0:T(128)S(1)} %copy-done.3, s32[1]{0:T(128)S(6)} %copy.29.counts_ref, bf16[192,512]{1,0:T(8,128)(2,1)S(1)} %copy-done.1, bf16[30,192,512]{2,1,0:T(8,128)(2,1)} %history_ref.1), custom_call_target="tpu_custom_call" | custom-call | flops 1000000000 | bytes 1024 | tf_op jit(solution)/shard_map/pallas_call | solution.py:305
  33.9 1.2 shard_map.262
  35.8 1.5 %shard_map.263 = (f32[768,256]{1,0:T(8,128)S(1)}, f32[2,256]{1,0:T(2,128)S(1)}, bf16[768,256]{1,0:T(8,128)(2,1)S(1)}) custom-call(bf16[768,256]{1,0:T(8,128)(2,1)S(1)} %get-tuple-element.174.x_half, f32[768,256]{1,0:T(8,128)S(1)} %get-tuple-element.168.chip, bf16[768,256]{1,0:T(8,128)(2,1)S(1)} %collective-permute-done.9.received, f32[768,8]{1,0:T(8,128)S(1)} %shard_map.257.norms), custom_call_target="tpu_custom_call" | custom-call | flops 1000000000 | bytes 1024 | tf_op jit(solution)/shard_map/pallas_call | solution.py:33
  37.4 1.7 %collective-permute-done.10.other = bf16[768,256]{1,0:T(8,128)(2,1)S(1)} collective-permute-done((bf16[768,256]{1,0:T(8,128)(2,1)S(1)}, bf16[768,256]{1,0:T(8,128)(2,1)S(1)}, u32[]{:S(2)}, u32[]{:S(2)}) %collective-permute-start.10) | collective-permute-done | bytes 393248 | tf_op jit(solution)/shard_map/ppermute | solution.py:68
  39.1 2.6 %shard_map.264 = (bf16[768,512]{1,0:T(8,128)(2,1)S(1)}, bf16[768,512]{1,0:T(8,128)(2,1)S(1)}, bf16[768,512]{1,0:T(8,128)(2,1)S(1)}, bf16[768,256]{1,0:T(8,128)(2,1)S(1)}, f32[768,256]{1,0:T(8,128)S(1)}) custom-call(bf16[768,256]{1,0:T(8,128)(2,1)S(1)} %get-tuple-element.178.own, bf16[768,256]{1,0:T(8,128)(2,1)S(1)} %collective-permute-done.10.other, ...), custom_call_target="tpu_custom_call" | custom-call | flops 1000000000 | bytes 1024 | tf_op jit(solution)/shard_map/pallas_call | solution.py:33
  43.9 1.8 %collective-permute-start.12 = (bf16[768,256]{1,0:T(8,128)(2,1)S(1)}, bf16[768,256]{1,0:T(8,128)(2,1)S(1)}, u32[]{:S(2)}, u32[]{:S(2)}) collective-permute-start(bf16[768,256]{1,0:T(8,128)(2,1)S(1)} %get-tuple-element.195), channel_id=1, source_target_pairs={{0,2},{1,3},{2,0},{3,1},{4,6},{5,7},{6,4},{7,5},{8,10},{9,11},{10,... | collective-permute-start | bytes 1179656 | tf_op jit(solution)/shard_map/ppermute | solution.py:68
  45.7 1.5 collective-permute-start.14
  48.0 1.6 %collective-permute-start.15 = (bf16[384,768]{1,0:T(8,128)(2,1)S(1)}, bf16[384,768]{1,0:T(8,128)(2,1)S(1)}, u32[]{:S(2)}, u32[]{:S(2)}) collective-permute-start(bf16[384,768]{1,0:T(8,128)(2,1)S(1)} %get-tuple-element.207), channel_id=1, source_target_pairs={{0,8},{4,12},{8,0},{12,4},{16,24},{20,28},{24,16},{28,20},{1,9},{5... | collective-permute-start | bytes 1769480 | tf_op jit(solution)/shard_map/ppermute | solution.py:68
  50.7 4.4 %collective-permute-done.12.received = bf16[768,256]{1,0:T(8,128)(2,1)S(1)} collective-permute-done((bf16[768,256]{1,0:T(8,128)(2,1)S(1)}, bf16[768,256]{1,0:T(8,128)(2,1)S(1)}, u32[]{:S(2)}, u32[]{:S(2)}) %collective-permute-start.12) | collective-permute-done | bytes 393248 | tf_op jit(solution)/shard_map/ppermute | solution.py:68
  55.1 2.3 %shard_map.269 = (f32[768,256]{1,0:T(8,128)S(1)}, bf16[768,256]{1,0:T(8,128)(2,1)S(1)}, f32[2,768]{1,0:T(2,128)S(1)}) custom-call(s32[1]{0:T(128)} %bitcast.at_ref, f32[1]{0:T(128)S(6)} %copy.30.self_ref, s32[1]{0:T(128)S(6)} %copy.29.counts_ref, f32[768,256]{1,0:T(8,128)S(1)} %get-tuple-element.194.chip, ...), custom_call_target="tpu_custom_call" | custom-call | flops 1000000000 | bytes 1024 | tf_op jit(solution)/shard_map/pallas_call | solution.py:33
  57.6 3.2 %collective-permute-done.14.refs_1_ = bf16[384,768]{1,0:T(8,128)(2,1)S(1)} collective-permute-done((bf16[384,768]{1,0:T(8,128)(2,1)S(1)}, bf16[384,768]{1,0:T(8,128)(2,1)S(1)}, u32[]{:S(2)}, u32[]{:S(2)}) %collective-permute-start.14) | collective-permute-done | bytes 589856 | tf_op jit(solution)/shard_map/ppermute | solution.py:68
  60.9 1.6 %collective-permute-start.17 = (bf16[192,768]{1,0:T(8,128)(2,1)S(1)}, bf16[192,768]{1,0:T(8,128)(2,1)S(1)}, u32[]{:S(2)}, u32[]{:S(2)}) collective-permute-start(bf16[192,768]{1,0:T(8,128)(2,1)S(1)} %get-tuple-element.218), channel_id=1, source_target_pairs={{0,8},{4,12},{8,0},{12,4},{16,24},{20,28},{24,16},{28,20},{1,9},{5... | collective-permute-start | bytes 884744 | tf_op jit(solution)/shard_map/ppermute | solution.py:68
  64.3 3.6 %shard_map.273 = (bf16[576,512]{1,0:T(8,128)(2,1)S(1)}, bf16[768,512]{1,0:T(8,128)(2,1)S(1)}) custom-call(s32[1]{0:T(128)} %bitcast.at_ref, bf16[768,256]{1,0:T(8,128)(2,1)S(1)} %get-tuple-element.209.own, bf16[768,256]{1,0:T(8,128)(2,1)S(1)} %collective-permute-done.16.other, bf16[192,768]{1,0:T(8,128)(2,1)S(1)} %copy-done.6, ...), custom_call_target="tpu_custom_call" | custom-call | flops 1000000000 | bytes 1024 | tf_op jit(solution)/shard_map/pallas_call | solution.py:33
  68.9 1.2 collective-permute-start.21
  70.1 1.6 %collective-permute-start.22 = (bf16[192,768]{1,0:T(8,128)(2,1)S(1)}, bf16[192,768]{1,0:T(8,128)(2,1)S(1)}, u32[]{:S(2)}, u32[]{:S(2)}) collective-permute-start(bf16[192,768]{1,0:T(8,128)(2,1)S(1)} %get-tuple-element.238), channel_id=1, source_target_pairs={{0,8},{4,12},{8,0},{12,4},{16,24},{20,28},{24,16},{28,20},{1,9},{5... | collective-permute-start | bytes 884744 | tf_op jit(solution)/shard_map/ppermute | solution.py:68
  72.3 2.7 %collective-permute-start.23 = (bf16[96,768]{1,0:T(8,128)(2,1)S(1)}, bf16[96,768]{1,0:T(8,128)(2,1)S(1)}, u32[]{:S(2)}, u32[]{:S(2)}) collective-permute-start(bf16[96,768]{1,0:T(8,128)(2,1)S(1)} %get-tuple-element.241), channel_id=1, source_target_pairs={{0,16},{4,20},{8,24},{12,28},{16,0},{20,4},{24,8},{28,12},{1,17},{... | collective-permute-start | bytes 442376 | tf_op jit(solution)/shard_map/ppermute | solution.py:68
  75.7 2.6 %shard_map.277 = (bf16[192,512]{1,0:T(8,128)(2,1)S(1)}, bf16[192,512]{1,0:T(8,128)(2,1)S(1)}, f32[192,512]{1,0:T(8,128)S(1)}, f32[192,512]{1,0:T(8,128)S(1)}, f32[8,768]{1,0:T(8,128)S(1)}) custom-call(s32[1]{0:T(128)} %bitcast.at_ref, s32[1]{0:T(128)S(6)} %copy.29.counts_ref, bf16[576,512]{1,0:T(8,128)(2,1)S(1)} %get-tuple-element.223.refs_0_.d_project, ...), custom_call_target="tpu_custom_call" | custom-call | flops 100000000 | bytes 1024 | tf_op jit(solution)/shard_map/pallas_call | solution.py:33
  81.7 4.1 %collective-permute-done.23.refs_1_ = bf16[96,768]{1,0:T(8,128)(2,1)S(1)} collective-permute-done((bf16[96,768]{1,0:T(8,128)(2,1)S(1)}, bf16[96,768]{1,0:T(8,128)(2,1)S(1)}, u32[]{:S(2)}, u32[]{:S(2)}) %collective-permute-start.23) | collective-permute-done | bytes 147488 | tf_op jit(solution)/shard_map/ppermute | solution.py:68
  85.9 4.7 %collective-permute-done.24.refs_1_ = bf16[96,768]{1,0:T(8,128)(2,1)S(1)} collective-permute-done((bf16[96,768]{1,0:T(8,128)(2,1)S(1)}, bf16[96,768]{1,0:T(8,128)(2,1)S(1)}, u32[]{:S(2)}, u32[]{:S(2)}) %collective-permute-start.24) | collective-permute-done | bytes 147488 | tf_op jit(solution)/shard_map/ppermute | solution.py:68
  92.3 1.3 collective-permute-start.28
  93.6 2.6 %collective-permute-done.28.refs_1_ = f32[8,768]{1,0:T(8,128)S(1)} collective-permute-done((f32[8,768]{1,0:T(8,128)S(1)}, f32[8,768]{1,0:T(8,128)S(1)}, u32[]{:S(2)}, u32[]{:S(2)}) %collective-permute-start.28) | collective-permute-done | bytes 24608 | tf_op jit(solution)/shard_map/ppermute | solution.py:68
  97.0 8.1 %collective-permute-start.38 = (bf16[192,768]{1,0:T(8,128)(2,1)S(1)}, bf16[192,768]{1,0:T(8,128)(2,1)S(1)}, u32[]{:S(2)}, u32[]{:S(2)}) collective-permute-start(bf16[192,768]{1,0:T(8,128)(2,1)S(1)} %shard_map.287.refs_0_), channel_id=1, source_target_pairs={{0,8},{4,12},{8,0},{12,4},{16,24},{20,28},{24,16},{28,20},{1,9},{5... | collective-permute-start | bytes 884744 | tf_op jit(solution)/shard_map/ppermute | solution.py:68
  105.2 1.5 collective-permute-start.37
  106.7 1.4 collective-permute-start.32
  108.2 5.2 %collective-permute-done.32.refs_1_ = f32[8,768]{1,0:T(8,128)S(1)} collective-permute-done((f32[8,768]{1,0:T(8,128)S(1)}, f32[8,768]{1,0:T(8,128)S(1)}, u32[]{:S(2)}, u32[]{:S(2)}) %collective-permute-start.32) | collective-permute-done | bytes 24608 | tf_op jit(solution)/shard_map/ppermute | solution.py:68
  114.2 5.5 %collective-permute-done.34.refs_1_ = bf16[48,768]{1,0:T(8,128)(2,1)S(1)} collective-permute-done((bf16[48,768]{1,0:T(8,128)(2,1)S(1)}, bf16[48,768]{1,0:T(8,128)(2,1)S(1)}, u32[]{:S(2)}, u32[]{:S(2)}) %collective-permute-start.34) | collective-permute-done | bytes 73760 | tf_op jit(solution)/shard_map/ppermute | solution.py:68
  119.7 3.0 %collective-permute-start.41 = (bf16[48,768]{1,0:T(8,128)(2,1)S(1)}, bf16[48,768]{1,0:T(8,128)(2,1)S(1)}, u32[]{:S(2)}, u32[]{:S(2)}) collective-permute-start(bf16[48,768]{1,0:T(8,128)(2,1)S(1)} %shard_map.292.refs_0_), channel_id=1, source_target_pairs={{0,16},{4,20},{8,24},{12,28},{16,0},{20,4},{24,8},{28,12},{1,17},{... | collective-permute-start | bytes 221192 | tf_op jit(solution)/shard_map/ppermute | solution.py:68
  123.1 2.7 %collective-permute-done.40.refs_1_ = bf16[48,768]{1,0:T(8,128)(2,1)S(1)} collective-permute-done((bf16[48,768]{1,0:T(8,128)(2,1)S(1)}, bf16[48,768]{1,0:T(8,128)(2,1)S(1)}, u32[]{:S(2)}, u32[]{:S(2)}) %collective-permute-start.40) | collective-permute-done | bytes 73760 | tf_op jit(solution)/shard_map/ppermute | solution.py:68
  125.8 1.3 collective-permute-done.41.refs_1_
  127.2 1.7 %collective-permute-start.42 = (f32[8,768]{1,0:T(8,128)S(1)}, f32[8,768]{1,0:T(8,128)S(1)}, u32[]{:S(2)}, u32[]{:S(2)}) collective-permute-start(f32[8,768]{1,0:T(8,128)S(1)} %shard_map.293.refs_0_), channel_id=1, source_target_pairs={{0,16},{4,20},{8,24},{12,28},{16,0},{20,4},{24,8},{28,12},{1,17},{... | collective-permute-start | bytes 73736 | tf_op jit(solution)/shard_map/ppermute | solution.py:68
  128.9 1.9 %collective-permute-start.45 = (bf16[384,768]{1,0:T(8,128)(2,1)S(1)}, bf16[384,768]{1,0:T(8,128)(2,1)S(1)}, u32[]{:S(2)}, u32[]{:S(2)}) collective-permute-start(bf16[384,768]{1,0:T(8,128)(2,1)S(1)} %shard_map.295.refs_0_), channel_id=1, source_target_pairs={{0,4},{4,0},{8,12},{12,8},{16,20},{20,16},{24,28},{28,24},{1,5},{5... | collective-permute-start | bytes 1769480 | tf_op jit(solution)/shard_map/ppermute | solution.py:68
  130.9 1.3 collective-permute-done.42.refs_1_
  133.0 4.1 %shard_map.301 = bf16[30,192,512]{2,1,0:T(8,128)(2,1)} custom-call(f32[30]{0:T(128)S(1)} %copy-done.3, s32[1]{0:T(128)S(6)} %copy.29.counts_ref, bf16[192,512]{1,0:T(8,128)(2,1)S(1)} %copy-done.1, f32[8,768]{1,0:T(8,128)S(1)} %shard_map.299.sums), custom_call_target="tpu_custom_call" | custom-call | flops 100000000 | bytes 1024 | tf_op jit(solution)/shard_map/pallas_call | solution.py:305
  138.9 1.9 %collective-permute-start.47 = (bf16[192,768]{1,0:T(8,128)(2,1)S(1)}, bf16[192,768]{1,0:T(8,128)(2,1)S(1)}, u32[]{:S(2)}, u32[]{:S(2)}) collective-permute-start(bf16[192,768]{1,0:T(8,128)(2,1)S(1)} %shard_map.303.refs_0_), channel_id=1, source_target_pairs={{0,4},{4,0},{8,12},{12,8},{16,20},{20,16},{24,28},{28,24},{1,5},{5... | collective-permute-start | bytes 884744 | tf_op jit(solution)/shard_map/ppermute | solution.py:68
  140.8 3.0 %collective-permute-done.45.refs_1_ = bf16[384,768]{1,0:T(8,128)(2,1)S(1)} collective-permute-done((bf16[384,768]{1,0:T(8,128)(2,1)S(1)}, bf16[384,768]{1,0:T(8,128)(2,1)S(1)}, u32[]{:S(2)}, u32[]{:S(2)}) %collective-permute-start.45) | collective-permute-done | bytes 589856 | tf_op jit(solution)/shard_map/ppermute | solution.py:68
  143.8 1.6 %shard_map.305 = f32[768,768]{1,0:T(8,128)} custom-call(s32[1]{0:T(128)} %bitcast.1.me_ref, f32[8,768]{1,0:T(8,128)S(1)} %shard_map.299.sums, bf16[384,768]{1,0:T(8,128)(2,1)S(1)} %shard_map.295.refs_0_, bf16[384,768]{1,0:T(8,128)(2,1)S(1)} %collective-permute-done.45.refs_1_), custom_call_target="tpu_custom_call" | custom-call | flops 100000000 | bytes 1024 | tf_op jit(solution)/shard_map/pallas_call | solution.py:33
  145.4 1.6 %shard_map.306 = f32[768,768]{1,0:T(8,128)} custom-call(s32[1]{0:T(128)} %bitcast.1.me_ref, f32[8,768]{1,0:T(8,128)S(1)} %shard_map.299.sums, bf16[384,768]{1,0:T(8,128)(2,1)S(1)} %shard_map.296.refs_0_, bf16[384,768]{1,0:T(8,128)(2,1)S(1)} %collective-permute-done.46.refs_1_), custom_call_target="tpu_custom_call" | custom-call | flops 100000000 | bytes 1024 | tf_op jit(solution)/shard_map/pallas_call | solution.py:33
  147.1 1.2 collective-permute-done.48.refs_3_
  148.3 1.9 %shard_map.307 = (f32[576,768]{1,0:T(8,128)}, f32[192,768]{1,0:T(8,128)}) custom-call(s32[1]{0:T(128)} %bitcast.1.me_ref, f32[8,768]{1,0:T(8,128)S(1)} %shard_map.299.sums, bf16[192,768]{1,0:T(8,128)(2,1)S(1)} %shard_map.303.refs_0_, bf16[192,768]{1,0:T(8,128)(2,1)S(1)} %collective-permute-done.47.refs_1_, bf16[192,768]{1,0:T(8,128)(2,1)S(1)} %shard_map.304.refs_2_, ...), custom_call_target="tpu_custom_call" | custom-call | flops 100000000 | bytes 1024 | tf_op jit(solution)/shard_map/pallas_call | solution.py:33
  (117 shorter events, 23.1 us)
Async XLA Ops:
  0.7 3.1 %collective-permute-start = (bf16[192,512]{1,0:T(8,128)(2,1)}, bf16[192,512]{1,0:T(8,128)(2,1)S(1)}, u32[]{:S(2)}, u32[]{:S(2)}) collective-permute-start(bf16[192,512]{1,0:T(8,128)(2,1)} %x_in), channel_id=1, source_target_pairs={{0,1},{1,0},{2,3},{3,2},{4,5},{5,4},{6,7},{7,6},{8,9},{9,8},{10,11... | collective-permute-start | bytes 589832 | tf_op jit(solution)/shard_map/ppermute | solution.py:68
  1.2 8.9 %collective-permute-start.3 = (bf16[192,512]{1,0:T(8,128)(2,1)}, bf16[192,512]{1,0:T(8,128)(2,1)S(1)}, u32[]{:S(2)}, u32[]{:S(2)}) collective-permute-start(bf16[192,512]{1,0:T(8,128)(2,1)} %x_in), channel_id=1, source_target_pairs={{0,2},{1,3},{2,0},{3,1},{4,6},{5,7},{6,4},{7,5},{8,10},{9,11},{10,... | collective-permute-start | bytes 589832 | tf_op jit(solution)/shard_map/ppermute | solution.py:68
  6.1 3.7 %collective-permute-start.2 = (f32[16,256]{1,0:T(8,128)S(1)}, f32[16,256]{1,0:T(8,128)S(1)}, u32[]{:S(2)}, u32[]{:S(2)}) collective-permute-start(f32[16,256]{1,0:T(8,128)S(1)} %shard_map.256.n01), channel_id=1, source_target_pairs={{0,2},{1,3},{2,0},{3,1},{4,6},{5,7},{6,4},{7,5},{8,10},{9,11},{10,... | collective-permute-start | bytes 49160 | tf_op jit(solution)/shard_map/ppermute | solution.py:68
  10.1 1.8 %collective-permute-start.4 = (bf16[192,512]{1,0:T(8,128)(2,1)S(1)}, bf16[192,512]{1,0:T(8,128)(2,1)S(1)}, u32[]{:S(2)}, u32[]{:S(2)}) collective-permute-start(bf16[192,512]{1,0:T(8,128)(2,1)S(1)} %collective-permute-done.3.x2), channel_id=1, source_target_pairs={{0,1},{1,0},{2,3},{3,2},{4,5},{5,4},{6,7},{7,6},{8,9},{9,8},{10,11... | collective-permute-start | bytes 589832 | tf_op jit(solution)/shard_map/ppermute | solution.py:68
  10.2 7.5 %collective-permute-start.5 = (bf16[192,512]{1,0:T(8,128)(2,1)}, bf16[192,512]{1,0:T(8,128)(2,1)S(1)}, u32[]{:S(2)}, u32[]{:S(2)}) collective-permute-start(bf16[192,512]{1,0:T(8,128)(2,1)} %cot_ref.1), channel_id=1, source_target_pairs={{0,2},{1,3},{2,0},{3,1},{4,6},{5,7},{6,4},{7,5},{8,10},{9,11},{10,... | collective-permute-start | bytes 589832 | tf_op jit(solution)/shard_map/ppermute | solution.py:68
  22.5 1.8 %collective-permute-start.6 = (bf16[768,256]{1,0:T(8,128)(2,1)S(1)}, bf16[768,256]{1,0:T(8,128)(2,1)S(1)}, u32[]{:S(2)}, u32[]{:S(2)}) collective-permute-start(bf16[768,256]{1,0:T(8,128)(2,1)S(1)} %get-tuple-element.166), channel_id=1, source_target_pairs={{0,1},{1,0},{2,3},{3,2},{4,5},{5,4},{6,7},{7,6},{8,9},{9,8},{10,11... | collective-permute-start | bytes 1179656 | tf_op jit(solution)/shard_map/ppermute | solution.py:68
  24.6 11.2 %collective-permute-start.9 = (bf16[768,256]{1,0:T(8,128)(2,1)S(1)}, bf16[768,256]{1,0:T(8,128)(2,1)S(1)}, u32[]{:S(2)}, u32[]{:S(2)}) collective-permute-start(bf16[768,256]{1,0:T(8,128)(2,1)S(1)} %get-tuple-element.175), channel_id=1, source_target_pairs={{0,2},{1,3},{2,0},{3,1},{4,6},{5,7},{6,4},{7,5},{8,10},{9,11},{10,... | collective-permute-start | bytes 1179656 | tf_op jit(solution)/shard_map/ppermute | solution.py:68
  26.3 7.5 %collective-permute-start.7 = (bf16[192,512]{1,0:T(8,128)(2,1)S(1)}, bf16[192,512]{1,0:T(8,128)(2,1)S(1)}, u32[]{:S(2)}, u32[]{:S(2)}) collective-permute-start(bf16[192,512]{1,0:T(8,128)(2,1)S(1)} %copy-done.1), channel_id=1, source_target_pairs={{0,1},{1,0},{2,3},{3,2},{4,5},{5,4},{6,7},{7,6},{8,9},{9,8},{10,11... | collective-permute-start | bytes 589832 | tf_op jit(solution)/shard_map/ppermute | solution.py:68
  26.4 7.5 %collective-permute-start.8 = (bf16[192,512]{1,0:T(8,128)(2,1)S(1)}, bf16[192,512]{1,0:T(8,128)(2,1)S(1)}, u32[]{:S(2)}, u32[]{:S(2)}) collective-permute-start(bf16[192,512]{1,0:T(8,128)(2,1)S(1)} %collective-permute-done.5.c2), channel_id=1, source_target_pairs={{0,1},{1,0},{2,3},{3,2},{4,5},{5,4},{6,7},{7,6},{8,9},{9,8},{10,11... | collective-permute-start | bytes 589832 | tf_op jit(solution)/shard_map/ppermute | solution.py:68
  37.4 1.8 %collective-permute-start.10 = (bf16[768,256]{1,0:T(8,128)(2,1)S(1)}, bf16[768,256]{1,0:T(8,128)(2,1)S(1)}, u32[]{:S(2)}, u32[]{:S(2)}) collective-permute-start(bf16[768,256]{1,0:T(8,128)(2,1)S(1)} %get-tuple-element.178.own), channel_id=1, source_target_pairs={{0,1},{1,0},{2,3},{3,2},{4,5},{5,4},{6,7},{7,6},{8,9},{9,8},{10,11... | collective-permute-start | bytes 1179656 | tf_op jit(solution)/shard_map/ppermute | solution.py:68
  41.8 1.8 %collective-permute-start.11 = (bf16[768,256]{1,0:T(8,128)(2,1)S(1)}, bf16[768,256]{1,0:T(8,128)(2,1)S(1)}, u32[]{:S(2)}, u32[]{:S(2)}) collective-permute-start(bf16[768,256]{1,0:T(8,128)(2,1)S(1)} %get-tuple-element.186), channel_id=1, source_target_pairs={{0,1},{1,0},{2,3},{3,2},{4,5},{5,4},{6,7},{7,6},{8,9},{9,8},{10,11... | collective-permute-start | bytes 1179656 | tf_op jit(solution)/shard_map/ppermute | solution.py:68
  43.9 11.2 %collective-permute-start.12 = (bf16[768,256]{1,0:T(8,128)(2,1)S(1)}, bf16[768,256]{1,0:T(8,128)(2,1)S(1)}, u32[]{:S(2)}, u32[]{:S(2)}) collective-permute-start(bf16[768,256]{1,0:T(8,128)(2,1)S(1)} %get-tuple-element.195), channel_id=1, source_target_pairs={{0,2},{1,3},{2,0},{3,1},{4,6},{5,7},{6,4},{7,5},{8,10},{9,11},{10,... | collective-permute-start | bytes 1179656 | tf_op jit(solution)/shard_map/ppermute | solution.py:68
  45.7 15.1 %collective-permute-start.14 = (bf16[384,768]{1,0:T(8,128)(2,1)S(1)}, bf16[384,768]{1,0:T(8,128)(2,1)S(1)}, u32[]{:S(2)}, u32[]{:S(2)}) collective-permute-start(bf16[384,768]{1,0:T(8,128)(2,1)S(1)} %get-tuple-element.204), channel_id=1, source_target_pairs={{0,4},{4,0},{8,12},{12,8},{16,20},{20,16},{24,28},{28,24},{1,5},{5... | collective-permute-start | bytes 1769480 | tf_op jit(solution)/shard_map/ppermute | solution.py:68
  48.0 15.1 %collective-permute-start.15 = (bf16[384,768]{1,0:T(8,128)(2,1)S(1)}, bf16[384,768]{1,0:T(8,128)(2,1)S(1)}, u32[]{:S(2)}, u32[]{:S(2)}) collective-permute-start(bf16[384,768]{1,0:T(8,128)(2,1)S(1)} %get-tuple-element.207), channel_id=1, source_target_pairs={{0,8},{4,12},{8,0},{12,4},{16,24},{20,28},{24,16},{28,20},{1,9},{5... | collective-permute-start | bytes 1769480 | tf_op jit(solution)/shard_map/ppermute | solution.py:68
  50.6 6.9 %collective-permute-start.13 = (bf16[192,512]{1,0:T(8,128)(2,1)S(1)}, bf16[192,512]{1,0:T(8,128)(2,1)S(1)}, u32[]{:S(2)}, u32[]{:S(2)}) collective-permute-start(bf16[192,512]{1,0:T(8,128)(2,1)S(1)} %get-tuple-element.202), channel_id=1, source_target_pairs={{0,1},{1,0},{2,3},{3,2},{4,5},{5,4},{6,7},{7,6},{8,9},{9,8},{10,11... | collective-permute-start | bytes 589832 | tf_op jit(solution)/shard_map/ppermute | solution.py:68
  57.4 6.9 %collective-permute-start.16 = (bf16[768,256]{1,0:T(8,128)(2,1)S(1)}, bf16[768,256]{1,0:T(8,128)(2,1)S(1)}, u32[]{:S(2)}, u32[]{:S(2)}) collective-permute-start(bf16[768,256]{1,0:T(8,128)(2,1)S(1)} %get-tuple-element.209.own), channel_id=1, source_target_pairs={{0,1},{1,0},{2,3},{3,2},{4,5},{5,4},{6,7},{7,6},{8,9},{9,8},{10,11... | collective-permute-start | bytes 1179656 | tf_op jit(solution)/shard_map/ppermute | solution.py:68
  60.9 10.7 %collective-permute-start.17 = (bf16[192,768]{1,0:T(8,128)(2,1)S(1)}, bf16[192,768]{1,0:T(8,128)(2,1)S(1)}, u32[]{:S(2)}, u32[]{:S(2)}) collective-permute-start(bf16[192,768]{1,0:T(8,128)(2,1)S(1)} %get-tuple-element.218), channel_id=1, source_target_pairs={{0,8},{4,12},{8,0},{12,4},{16,24},{20,28},{24,16},{28,20},{1,9},{5... | collective-permute-start | bytes 884744 | tf_op jit(solution)/shard_map/ppermute | solution.py:68
  63.4 8.9 %collective-permute-start.18 = (bf16[192,768]{1,0:T(8,128)(2,1)S(1)}, bf16[192,768]{1,0:T(8,128)(2,1)S(1)}, u32[]{:S(2)}, u32[]{:S(2)}) collective-permute-start(bf16[192,768]{1,0:T(8,128)(2,1)S(1)} %get-tuple-element.221), channel_id=1, source_target_pairs={{0,4},{4,0},{8,12},{12,8},{16,20},{20,16},{24,28},{28,24},{1,5},{5... | collective-permute-start | bytes 884744 | tf_op jit(solution)/shard_map/ppermute | solution.py:68
  68.9 10.9 %collective-permute-start.21 = (bf16[192,768]{1,0:T(8,128)(2,1)S(1)}, bf16[192,768]{1,0:T(8,128)(2,1)S(1)}, u32[]{:S(2)}, u32[]{:S(2)}) collective-permute-start(bf16[192,768]{1,0:T(8,128)(2,1)S(1)} %get-tuple-element.235), channel_id=1, source_target_pairs={{0,4},{4,0},{8,12},{12,8},{16,20},{20,16},{24,28},{28,24},{1,5},{5... | collective-permute-start | bytes 884744 | tf_op jit(solution)/shard_map/ppermute | solution.py:68
  70.1 10.5 %collective-permute-start.22 = (bf16[192,768]{1,0:T(8,128)(2,1)S(1)}, bf16[192,768]{1,0:T(8,128)(2,1)S(1)}, u32[]{:S(2)}, u32[]{:S(2)}) collective-permute-start(bf16[192,768]{1,0:T(8,128)(2,1)S(1)} %get-tuple-element.238), channel_id=1, source_target_pairs={{0,8},{4,12},{8,0},{12,4},{16,24},{20,28},{24,16},{28,20},{1,9},{5... | collective-permute-start | bytes 884744 | tf_op jit(solution)/shard_map/ppermute | solution.py:68
  71.7 3.4 %collective-permute-start.19 = (bf16[192,512]{1,0:T(8,128)(2,1)S(1)}, bf16[192,512]{1,0:T(8,128)(2,1)S(1)}, u32[]{:S(2)}, u32[]{:S(2)}) collective-permute-start(bf16[192,512]{1,0:T(8,128)(2,1)S(1)} %get-tuple-element.193), channel_id=1, source_target_pairs={{0,1},{1,0},{2,3},{3,2},{4,5},{5,4},{6,7},{7,6},{8,9},{9,8},{10,11... | collective-permute-start | bytes 589832 | tf_op jit(solution)/shard_map/ppermute | solution.py:68
  71.7 7.3 %collective-permute-start.20 = (bf16[192,512]{1,0:T(8,128)(2,1)S(1)}, bf16[192,512]{1,0:T(8,128)(2,1)S(1)}, u32[]{:S(2)}, u32[]{:S(2)}) collective-permute-start(bf16[192,512]{1,0:T(8,128)(2,1)S(1)} %shard_map.270), channel_id=1, source_target_pairs={{0,2},{1,3},{2,0},{3,1},{4,6},{5,7},{6,4},{7,5},{8,10},{9,11},{10,... | collective-permute-start | bytes 589832 | tf_op jit(solution)/shard_map/ppermute | solution.py:68
  72.3 13.5 %collective-permute-start.23 = (bf16[96,768]{1,0:T(8,128)(2,1)S(1)}, bf16[96,768]{1,0:T(8,128)(2,1)S(1)}, u32[]{:S(2)}, u32[]{:S(2)}) collective-permute-start(bf16[96,768]{1,0:T(8,128)(2,1)S(1)} %get-tuple-element.241), channel_id=1, source_target_pairs={{0,16},{4,20},{8,24},{12,28},{16,0},{20,4},{24,8},{28,12},{1,17},{... | collective-permute-start | bytes 442376 | tf_op jit(solution)/shard_map/ppermute | solution.py:68
  75.0 15.6 %collective-permute-start.24 = (bf16[96,768]{1,0:T(8,128)(2,1)S(1)}, bf16[96,768]{1,0:T(8,128)(2,1)S(1)}, u32[]{:S(2)}, u32[]{:S(2)}) collective-permute-start(bf16[96,768]{1,0:T(8,128)(2,1)S(1)} %get-tuple-element.243), channel_id=1, source_target_pairs={{0,16},{4,20},{8,24},{12,28},{16,0},{20,4},{24,8},{28,12},{1,17},{... | collective-permute-start | bytes 442376 | tf_op jit(solution)/shard_map/ppermute | solution.py:68
  80.1 10.8 %collective-permute-start.25 = (bf16[96,768]{1,0:T(8,128)(2,1)S(1)}, bf16[96,768]{1,0:T(8,128)(2,1)S(1)}, u32[]{:S(2)}, u32[]{:S(2)}) collective-permute-start(bf16[96,768]{1,0:T(8,128)(2,1)S(1)} %get-tuple-element.245), channel_id=1, source_target_pairs={{0,8},{4,12},{8,0},{12,4},{16,24},{20,28},{24,16},{28,20},{1,9},{5... | collective-permute-start | bytes 442376 | tf_op jit(solution)/shard_map/ppermute | solution.py:68
  80.7 10.7 %collective-permute-start.26 = (bf16[96,768]{1,0:T(8,128)(2,1)S(1)}, bf16[96,768]{1,0:T(8,128)(2,1)S(1)}, u32[]{:S(2)}, u32[]{:S(2)}) collective-permute-start(bf16[96,768]{1,0:T(8,128)(2,1)S(1)} %get-tuple-element.248), channel_id=1, source_target_pairs={{0,4},{4,0},{8,12},{12,8},{16,20},{20,16},{24,28},{28,24},{1,5},{5... | collective-permute-start | bytes 442376 | tf_op jit(solution)/shard_map/ppermute | solution.py:68
  85.9 11.1 %collective-permute-start.29 = (bf16[96,768]{1,0:T(8,128)(2,1)S(1)}, bf16[96,768]{1,0:T(8,128)(2,1)S(1)}, u32[]{:S(2)}, u32[]{:S(2)}) collective-permute-start(bf16[96,768]{1,0:T(8,128)(2,1)S(1)} %shard_map.281.refs_0_), channel_id=1, source_target_pairs={{0,16},{4,20},{8,24},{12,28},{16,0},{20,4},{24,8},{28,12},{1,17},{... | collective-permute-start | bytes 442376 | tf_op jit(solution)/shard_map/ppermute | solution.py:68
  90.7 14.4 %collective-permute-start.30 = (bf16[96,768]{1,0:T(8,128)(2,1)S(1)}, bf16[96,768]{1,0:T(8,128)(2,1)S(1)}, u32[]{:S(2)}, u32[]{:S(2)}) collective-permute-start(bf16[96,768]{1,0:T(8,128)(2,1)S(1)} %shard_map.282.refs_0_), channel_id=1, source_target_pairs={{0,16},{4,20},{8,24},{12,28},{16,0},{20,4},{24,8},{28,12},{1,17},{... | collective-permute-start | bytes 442376 | tf_op jit(solution)/shard_map/ppermute | solution.py:68
  90.8 14.4 %collective-permute-start.31 = (bf16[192,512]{1,0:T(8,128)(2,1)S(1)}, bf16[192,512]{1,0:T(8,128)(2,1)S(1)}, u32[]{:S(2)}, u32[]{:S(2)}) collective-permute-start(bf16[192,512]{1,0:T(8,128)(2,1)S(1)} %get-tuple-element.256), channel_id=1, source_target_pairs={{0,1},{1,0},{2,3},{3,2},{4,5},{5,4},{6,7},{7,6},{8,9},{9,8},{10,11... | collective-permute-start | bytes 589832 | tf_op jit(solution)/shard_map/ppermute | solution.py:68
  90.9 1.5 collective-permute-start.27
  91.4 16.7 %collective-permute-start.36 = (bf16[192,512]{1,0:T(8,128)(2,1)S(1)}, bf16[192,512]{1,0:T(8,128)(2,1)S(1)}, u32[]{:S(2)}, u32[]{:S(2)}) collective-permute-start(bf16[192,512]{1,0:T(8,128)(2,1)S(1)} %get-tuple-element.226), channel_id=1, source_target_pairs={{0,1},{1,0},{2,3},{3,2},{4,5},{5,4},{6,7},{7,6},{8,9},{9,8},{10,11... | collective-permute-start | bytes 589832 | tf_op jit(solution)/shard_map/ppermute | solution.py:68
  92.3 3.8 %collective-permute-start.28 = (f32[8,768]{1,0:T(8,128)S(1)}, f32[8,768]{1,0:T(8,128)S(1)}, u32[]{:S(2)}, u32[]{:S(2)}) collective-permute-start(f32[8,768]{1,0:T(8,128)S(1)} %shard_map.285.refs_0_), channel_id=1, source_target_pairs={{0,2},{1,3},{2,0},{3,1},{4,6},{5,7},{6,4},{7,5},{8,10},{9,11},{10,... | collective-permute-start | bytes 73736 | tf_op jit(solution)/shard_map/ppermute | solution.py:68
  97.0 26.0 %collective-permute-start.38 = (bf16[192,768]{1,0:T(8,128)(2,1)S(1)}, bf16[192,768]{1,0:T(8,128)(2,1)S(1)}, u32[]{:S(2)}, u32[]{:S(2)}) collective-permute-start(bf16[192,768]{1,0:T(8,128)(2,1)S(1)} %shard_map.287.refs_0_), channel_id=1, source_target_pairs={{0,8},{4,12},{8,0},{12,4},{16,24},{20,28},{24,16},{28,20},{1,9},{5... | collective-permute-start | bytes 884744 | tf_op jit(solution)/shard_map/ppermute | solution.py:68
  105.1 17.9 %collective-permute-start.39 = (bf16[192,768]{1,0:T(8,128)(2,1)S(1)}, bf16[192,768]{1,0:T(8,128)(2,1)S(1)}, u32[]{:S(2)}, u32[]{:S(2)}) collective-permute-start(bf16[192,768]{1,0:T(8,128)(2,1)S(1)} %shard_map.288.refs_0_), channel_id=1, source_target_pairs={{0,4},{4,0},{8,12},{12,8},{16,20},{20,16},{24,28},{28,24},{1,5},{5... | collective-permute-start | bytes 884744 | tf_op jit(solution)/shard_map/ppermute | solution.py:68
  105.2 17.5 %collective-permute-start.37 = (bf16[192,512]{1,0:T(8,128)(2,1)S(1)}, bf16[192,512]{1,0:T(8,128)(2,1)S(1)}, u32[]{:S(2)}, u32[]{:S(2)}) collective-permute-start(bf16[192,512]{1,0:T(8,128)(2,1)S(1)} %shard_map.289), channel_id=1, source_target_pairs={{0,2},{1,3},{2,0},{3,1},{4,6},{5,7},{6,4},{7,5},{8,10},{9,11},{10,... | collective-permute-start | bytes 589832 | tf_op jit(solution)/shard_map/ppermute | solution.py:68
  106.7 6.7 %collective-permute-start.32 = (f32[8,768]{1,0:T(8,128)S(1)}, f32[8,768]{1,0:T(8,128)S(1)}, u32[]{:S(2)}, u32[]{:S(2)}) collective-permute-start(f32[8,768]{1,0:T(8,128)S(1)} %shard_map.286.refs_0_.row_sums), channel_id=1, source_target_pairs={{0,4},{4,0},{8,12},{12,8},{16,20},{20,16},{24,28},{28,24},{1,5},{5... | collective-permute-start | bytes 73736 | tf_op jit(solution)/shard_map/ppermute | solution.py:68
  108.1 5.6 %collective-permute-start.33 = (bf16[48,768]{1,0:T(8,128)(2,1)S(1)}, bf16[48,768]{1,0:T(8,128)(2,1)S(1)}, u32[]{:S(2)}, u32[]{:S(2)}) collective-permute-start(bf16[48,768]{1,0:T(8,128)(2,1)S(1)} %get-tuple-element.259), channel_id=1, source_target_pairs={{0,16},{4,20},{8,24},{12,28},{16,0},{20,4},{24,8},{28,12},{1,17},{... | collective-permute-start | bytes 221192 | tf_op jit(solution)/shard_map/ppermute | solution.py:68
  113.4 6.3 %collective-permute-start.34 = (bf16[48,768]{1,0:T(8,128)(2,1)S(1)}, bf16[48,768]{1,0:T(8,128)(2,1)S(1)}, u32[]{:S(2)}, u32[]{:S(2)}) collective-permute-start(bf16[48,768]{1,0:T(8,128)(2,1)S(1)} %get-tuple-element.261), channel_id=1, source_target_pairs={{0,16},{4,20},{8,24},{12,28},{16,0},{20,4},{24,8},{28,12},{1,17},{... | collective-permute-start | bytes 221192 | tf_op jit(solution)/shard_map/ppermute | solution.py:68
  113.8 5.9 %collective-permute-start.35 = (f32[8,768]{1,0:T(8,128)S(1)}, f32[8,768]{1,0:T(8,128)S(1)}, u32[]{:S(2)}, u32[]{:S(2)}) collective-permute-start(f32[8,768]{1,0:T(8,128)S(1)} %shard_map.290.refs_0_), channel_id=1, source_target_pairs={{0,8},{4,12},{8,0},{12,4},{16,24},{20,28},{24,16},{28,20},{1,9},{5... | collective-permute-start | bytes 73736 | tf_op jit(solution)/shard_map/ppermute | solution.py:68
  119.7 6.0 %collective-permute-start.40 = (bf16[48,768]{1,0:T(8,128)(2,1)S(1)}, bf16[48,768]{1,0:T(8,128)(2,1)S(1)}, u32[]{:S(2)}, u32[]{:S(2)}) collective-permute-start(bf16[48,768]{1,0:T(8,128)(2,1)S(1)} %shard_map.291.refs_0_), channel_id=1, source_target_pairs={{0,16},{4,20},{8,24},{12,28},{16,0},{20,4},{24,8},{28,12},{1,17},{... | collective-permute-start | bytes 221192 | tf_op jit(solution)/shard_map/ppermute | solution.py:68
  119.7 7.4 %collective-permute-start.41 = (bf16[48,768]{1,0:T(8,128)(2,1)S(1)}, bf16[48,768]{1,0:T(8,128)(2,1)S(1)}, u32[]{:S(2)}, u32[]{:S(2)}) collective-permute-start(bf16[48,768]{1,0:T(8,128)(2,1)S(1)} %shard_map.292.refs_0_), channel_id=1, source_target_pairs={{0,16},{4,20},{8,24},{12,28},{16,0},{20,4},{24,8},{28,12},{1,17},{... | collective-permute-start | bytes 221192 | tf_op jit(solution)/shard_map/ppermute | solution.py:68
  125.7 12.1 %collective-permute-start.43 = (bf16[96,768]{1,0:T(8,128)(2,1)S(1)}, bf16[96,768]{1,0:T(8,128)(2,1)S(1)}, u32[]{:S(2)}, u32[]{:S(2)}) collective-permute-start(bf16[96,768]{1,0:T(8,128)(2,1)S(1)} %shard_map.297.refs_0_), channel_id=1, source_target_pairs={{0,8},{4,12},{8,0},{12,4},{16,24},{20,28},{24,16},{28,20},{1,9},{5... | collective-permute-start | bytes 442376 | tf_op jit(solution)/shard_map/ppermute | solution.py:68
  127.2 10.7 %collective-permute-start.44 = (bf16[96,768]{1,0:T(8,128)(2,1)S(1)}, bf16[96,768]{1,0:T(8,128)(2,1)S(1)}, u32[]{:S(2)}, u32[]{:S(2)}) collective-permute-start(bf16[96,768]{1,0:T(8,128)(2,1)S(1)} %shard_map.298.refs_0_), channel_id=1, source_target_pairs={{0,4},{4,0},{8,12},{12,8},{16,20},{20,16},{24,28},{28,24},{1,5},{5... | collective-permute-start | bytes 442376 | tf_op jit(solution)/shard_map/ppermute | solution.py:68
  127.2 4.9 %collective-permute-start.42 = (f32[8,768]{1,0:T(8,128)S(1)}, f32[8,768]{1,0:T(8,128)S(1)}, u32[]{:S(2)}, u32[]{:S(2)}) collective-permute-start(f32[8,768]{1,0:T(8,128)S(1)} %shard_map.293.refs_0_), channel_id=1, source_target_pairs={{0,16},{4,20},{8,24},{12,28},{16,0},{20,4},{24,8},{28,12},{1,17},{... | collective-permute-start | bytes 73736 | tf_op jit(solution)/shard_map/ppermute | solution.py:68
  128.9 16.5 %collective-permute-start.46 = (bf16[384,768]{1,0:T(8,128)(2,1)S(1)}, bf16[384,768]{1,0:T(8,128)(2,1)S(1)}, u32[]{:S(2)}, u32[]{:S(2)}) collective-permute-start(bf16[384,768]{1,0:T(8,128)(2,1)S(1)} %shard_map.296.refs_0_), channel_id=1, source_target_pairs={{0,8},{4,12},{8,0},{12,4},{16,24},{20,28},{24,16},{28,20},{1,9},{5... | collective-permute-start | bytes 1769480 | tf_op jit(solution)/shard_map/ppermute | solution.py:68
  128.9 14.9 %collective-permute-start.45 = (bf16[384,768]{1,0:T(8,128)(2,1)S(1)}, bf16[384,768]{1,0:T(8,128)(2,1)S(1)}, u32[]{:S(2)}, u32[]{:S(2)}) collective-permute-start(bf16[384,768]{1,0:T(8,128)(2,1)S(1)} %shard_map.295.refs_0_), channel_id=1, source_target_pairs={{0,4},{4,0},{8,12},{12,8},{16,20},{20,16},{24,28},{28,24},{1,5},{5... | collective-permute-start | bytes 1769480 | tf_op jit(solution)/shard_map/ppermute | solution.py:68
  137.9 10.4 %collective-permute-start.48 = (bf16[192,768]{1,0:T(8,128)(2,1)S(1)}, bf16[192,768]{1,0:T(8,128)(2,1)S(1)}, u32[]{:S(2)}, u32[]{:S(2)}) collective-permute-start(bf16[192,768]{1,0:T(8,128)(2,1)S(1)} %shard_map.304.refs_2_), channel_id=1, source_target_pairs={{0,8},{4,12},{8,0},{12,4},{16,24},{20,28},{24,16},{28,20},{1,9},{5... | collective-permute-start | bytes 884744 | tf_op jit(solution)/shard_map/ppermute | solution.py:68
  138.9 9.4 %collective-permute-start.47 = (bf16[192,768]{1,0:T(8,128)(2,1)S(1)}, bf16[192,768]{1,0:T(8,128)(2,1)S(1)}, u32[]{:S(2)}, u32[]{:S(2)}) collective-permute-start(bf16[192,768]{1,0:T(8,128)(2,1)S(1)} %shard_map.303.refs_0_), channel_id=1, source_target_pairs={{0,4},{4,0},{8,12},{12,8},{16,20},{20,16},{24,28},{28,24},{1,5},{5... | collective-permute-start | bytes 884744 | tf_op jit(solution)/shard_map/ppermute | solution.py:68
  (8 other events, 61.7 us)

commit v7 on v6

--- a/solution.py
+++ b/solution.py
@@ -15,13 +15,73 @@
 STEP = 16
 
 
+SCHEDULE = (
+    ("down", 10),
+    ("chip", 8),
+    ("up", 10),
+    ("out", 100),
+    ("middle", 10),
+    ("out_sum", 10),
+    ("down1", 10),
+    ("up1", 100),
+    ("attention", 8),
+    ("tail", 4),
+    ("down2", 100),
+    ("up2", 0.3),
+    ("input", 1),
+    ("mix", 8),
+    ("first1", 1),
+    ("second1", 1),
+    ("up3", 100),
+    ("down3", 1),
+    ("first2", 2),
+    ("sums1", 4),
+    ("sums2", 1),
+    ("input_sum", 1),
+    ("second2", 1),
+    ("sums3", 1),
+    ("up4", 2),
+    ("sums4", 1),
+    ("down4", 4),
+    ("first3", 40),
+    ("input_total", 1),
+    ("second3", 2),
+    ("down5", 1),
+    ("first4", 200),
+    ("up5", 0.3),
+    ("second4", 16),
+    ("sums5", 1),
+    ("scale", 0.1),
+    ("first5", 40),
+    ("ends", 1),
+    ("history", 1),
+    ("place_down", 1),
+    ("second5", 200),
+    ("place_up", 4),
+    ("place_tail", 1),
+)
+
+FRONT = (1, 1, 1, 1, 1, 1, 10, 10, 10, 10, 10)
+
+
 def shape(*dims, kind=F32):
     return jax.ShapeDtypeStruct(dims, kind)
 
 
+class Values:
+    pass
+
+
 class Order:
     last = None
-    cost = 10**9
+    cost = 0
+    front = ()
+
+    @classmethod
+    def estimate(cls):
+        if cls.front:
+            cls.cost, *cls.front = cls.front
+        return pl.CostEstimate(flops=int(cls.cost * 10**8), bytes_accessed=1024, transcendentals=0)
 
 
 def kernel(body, outs, scalars, arrays, scratch=(), limit=12, streamed=()):
@@ -38,7 +98,7 @@
         out_specs=jax.tree.map(lambda _: pl.BlockSpec(memory_space=pltpu.VMEM), outs),
         scratch_shapes=list(scratch),
         compiler_params=pltpu.CompilerParams(vmem_limit_bytes=limit * 1024 * 1024),
-        cost_estimate=pl.CostEstimate(flops=Order.cost, bytes_accessed=1024, transcendentals=0),
+        cost_estimate=Order.estimate(),
     )(*scalars, *arrays)
     Order.last = jax.tree.leaves(found)[0]
     return found
@@ -219,26 +279,26 @@
 
 
 def place_kernel(all_tokens, streams, bounds, me_ref, sums, *refs):
-    pieces, outs = list(refs[: -len(bounds)]), refs[-len(bounds) :]
-    scale = loss_scale(all_tokens, sums, outs[0].shape[1])
+    outs, found, sems = refs[-len(bounds) - 2 : -2], refs[-2], refs[-1]
+    pieces = list(refs[: -len(bounds) - 2])
+    scale = loss_scale(all_tokens, sums, found.shape[1])
+    copies, start = [], 0
     for stream in streams:
         for offsets in stream.parts():
-            piece = pieces.pop(0)
+            piece, size = pieces.pop(0), stream.chunk
             for place, offset in enumerate(offsets):
-                chunk = (me_ref[0] % stream.count) ^ offset
-                row = stream.first + chunk * stream.chunk
+                row = stream.first + ((me_ref[0] % stream.count) ^ offset) * size
+                here = slice(start, start + size)
+                found[here] = piece[place * size : (place + 1) * size].astype(F32) * scale
                 for (first, last), out in zip(bounds, outs):
-
-                    def store(out=out, first=first, piece=piece, place=place, row=row, size=stream.chunk):
-                        at = pl.multiple_of(row - first, 16)
-                        out[pl.ds(at, size), :] = (
-                            piece[place * size : (place + 1) * size].astype(F32) * scale
-                        )
-
-                    if len(bounds) == 1:
-                        store()
-                    else:
-                        pl.when((row >= first) & (row < last))(store)
+                    at = pl.ds(pl.multiple_of(jnp.clip(row - first, 0, last - first - size), 16), size)
+                    copy = pltpu.make_async_copy(found.at[here], out.at[at, :], sems.at[len(copies)])
+                    inside = None if len(bounds) == 1 else (row >= first) & (row < last)
+                    copies.append((copy, inside))
+                    copy.start() if inside is None else pl.when(inside)(copy.start)
+                start += size
+    for copy, inside in copies:
+        copy.wait() if inside is None else pl.when(inside)(copy.wait)
 
 
 def place(all_tokens, me, sums, streams, pieces, sizes):
@@ -247,8 +307,19 @@
     for size in sizes:
         bounds.append((start, start + size))
         start += size
-    outs = tuple(shape(size, columns) for size in sizes)
-    return kernel(functools.partial(place_kernel, all_tokens, streams, bounds), outs, [me], [sums, *pieces])
+    count = len(sizes) * sum(stream.count for stream in streams)
+    vmem, hbm = pl.BlockSpec(memory_space=pltpu.VMEM), pl.BlockSpec(memory_space=pltpu.HBM)
+    found = pl.pallas_call(
+        functools.partial(place_kernel, all_tokens, streams, bounds),
+        out_shape=tuple(shape(size, columns) for size in sizes),
+        in_specs=[pl.BlockSpec(memory_space=pltpu.SMEM)] + [vmem] * (1 + len(pieces)),
+        out_specs=(hbm,) * len(sizes),
+        scratch_shapes=[pltpu.VMEM((start, columns), F32), pltpu.SemaphoreType.DMA((count,))],
+        compiler_params=pltpu.CompilerParams(vmem_limit_bytes=12 * 1024 * 1024),
+        cost_estimate=Order.estimate(),
+    )(me, after(sums, Order.last), *pieces)
+    Order.last = found[0]
+    return found
 
 
 def live_row(counts_ref, width, first):
@@ -308,15 +379,17 @@
         in_specs=[pl.BlockSpec(memory_space=pltpu.SMEM)] * len(scalars) + [hbm if h else vmem for h in in_hbm],
         out_specs=tuple(hbm if h else vmem for h in out_hbm),
         compiler_params=pltpu.CompilerParams(vmem_limit_bytes=12 * 1024 * 1024),
-        cost_estimate=pl.CostEstimate(flops=Order.cost, bytes_accessed=1024, transcendentals=0),
+        cost_estimate=Order.estimate(),
     )(*scalars, *arrays)
     Order.last = found[0]
     return found
 
 
-def spread_of(load, count, width):
+def spread_of(load, count, width, total=None):
     zero = jnp.zeros((STEP, width), F32)
-    mean = column_sum(each_rows(count, lambda i, acc: acc + load(i), zero)) / count
+    if total is None:
+        total = each_rows(count, lambda i, acc: acc + load(i), zero)
+    mean = column_sum(total) / count
 
     def squares(i, acc):
         centred = load(i) - mean
@@ -327,9 +400,10 @@
 
 def prepare_kernel(held, *refs):
     refs = refs[held:]
-    sources, (norms, cosine, sine), places, sem = refs[:6], refs[6:9], refs[9:15], refs[15]
+    sources, x_in, (own, norms, cosine, sine), places, sem = refs[:6], refs[6], refs[7:11], refs[11:17], refs[17]
     copies = [pltpu.make_async_copy(*pair, sem.at[i]) for i, pair in enumerate(zip(sources, places))]
-    for copy in copies:
+    whole = pltpu.make_async_copy(x_in, own, sem.at[6])
+    for copy in [*copies, whole]:
         copy.start()
     norms[...] = jnp.zeros_like(norms)
     for copy in copies:
@@ -340,21 +414,27 @@
     angles = positions[...].astype(F32) * rates[...]
     cosine[...] = jnp.cos(angles)
     sine[...] = jnp.sin(angles)
-
-
-def prepare(held, *sources):
+    whole.wait()
+
+
+def prepare(held, x_in, *sources):
     tokens, part = sources[0].shape[1], sources[2].shape[1]
     rates = sources[1].shape[0]
     vmem = pl.BlockSpec(memory_space=pltpu.VMEM)
     found = pl.pallas_call(
         functools.partial(prepare_kernel, len(held)),
-        out_shape=(shape(8, -(-part // 128) * 128), shape(rates, tokens), shape(rates, tokens)),
-        in_specs=[vmem] * len(held) + [pl.BlockSpec(memory_space=pltpu.HBM)] * len(sources),
-        out_specs=(vmem,) * 3,
-        scratch_shapes=[pltpu.VMEM(v.shape, v.dtype) for v in sources] + [pltpu.SemaphoreType.DMA((len(sources),))],
+        out_shape=(
+            shape(part, tokens, kind=BF16),
+            shape(8, -(-part // 128) * 128),
+            shape(rates, tokens),
+            shape(rates, tokens),
+        ),
+        in_specs=[vmem] * len(held) + [pl.BlockSpec(memory_space=pltpu.HBM)] * (len(sources) + 1),
+        out_specs=(vmem,) * 4,
+        scratch_shapes=[pltpu.VMEM(v.shape, v.dtype) for v in sources] + [pltpu.SemaphoreType.DMA((len(sources) + 1,))],
         compiler_params=pltpu.CompilerParams(vmem_limit_bytes=4 * 1024 * 1024),
-        cost_estimate=pl.CostEstimate(flops=Order.cost, bytes_accessed=1024, transcendentals=0),
-    )(*held, *(pltpu.with_memory_space_constraint(v, pltpu.HBM) for v in sources))
+        cost_estimate=Order.estimate(),
+    )(*held, *(pltpu.with_memory_space_constraint(v, pltpu.HBM) for v in (*sources, x_in)))
     Order.last = found[0]
     return found
 
@@ -368,17 +448,13 @@
 
 
 def project_kernel(
-    at_ref, x1, x2, x3, norms, cosine, sine, w_qkv, x0, x_all, normed, stats, qkv, project, own, sem
+    at_ref, x0, x1, x2, x3, norms, cosine, sine, w_qkv, x_all, normed, stats, qkv, project
 ):
     at = at_ref[0]
-    part, tokens = x1.shape
+    part, tokens = x0.shape
     model = w_qkv.shape[1]
-    copy = pltpu.make_async_copy(x0, own, sem)
-    copy.start()
-    for e, piece in ((1, x1), (2, x2), (3, x3)):
+    for e, piece in enumerate((x0, x1, x2, x3)):
         x_all[pl.ds(pl.multiple_of((at ^ e) * part, 64), part), :] = piece[...]
-    copy.wait()
-    x_all[pl.ds(pl.multiple_of(at * part, 64), part), :] = own[...]
     mean, scale = spread_of(lambda i: x_all[rows_at(i), :].astype(F32), model, tokens)
     stats[0:1] = mean
     stats[1:2] = scale
@@ -400,10 +476,10 @@
     qkv[2 * part :] = project[2 * part :].astype(BF16)
 
 
-def attention_kernel(at_ref, qkv, x_all, w_out_hbm, send, keep, x_half, heads_out, probs, scores, w_out, sem):
+def attention_kernel(
+    at_ref, qkv, x_all, heads_send, heads_own, x_half, heads_out, probs, scores
+):
     at = at_ref[0]
-    copy = pltpu.make_async_copy(w_out_hbm, w_out, sem)
-    copy.start()
     part, tokens = heads_out.shape
     half = tokens // 2
     for h in range(part // HEAD_DIM):
@@ -416,42 +492,41 @@
             value = qkv[2 * part + h * HEAD_DIM : 2 * part + (h + 1) * HEAD_DIM, :count]
             scores[:count] = dot(key, query, 0, 0)
 
-            def masked_top(i, acc):
+            def masked(i):
+                behind = lax.broadcasted_iota(jnp.int32, (STEP, half), 0) + (i * STEP - t * half)
+                ahead = lax.broadcasted_iota(jnp.int32, (STEP, half), 1)
+                return jnp.where(behind <= ahead, scores[rows_at(i), :], -1e30)
+
+            def raised(found, i, acc):
+                found = jnp.exp(found - top)
+                scores[rows_at(i), :] = found
+                return acc + found
+
+            def settle(i, _):
                 rows = rows_at(i)
-                behind = lax.broadcasted_iota(jnp.int32, (STEP, half), 0) + (i * STEP - t * half)
-                found = jnp.where(behind <= lax.broadcasted_iota(jnp.int32, (STEP, half), 1), scores[rows, :], -1e30)
-                scores[rows, :] = found
-                return jnp.maximum(acc, found)
+                probs[h, rows, now] = (scores[rows, :] * divisor).astype(BF16)
 
             top = each_rows(
                 t * half, lambda i, acc: jnp.maximum(acc, scores[rows_at(i), :]), jnp.full((STEP, half), -1e30, F32)
             )
-            top = jnp.max(each_rows(count, masked_top, top, first=t * half), axis=0, keepdims=True)
-
-            def raise_rows(i, acc):
-                rows = rows_at(i)
-                found = jnp.exp(scores[rows, :] - top)
-                scores[rows, :] = found
-                return acc + found
-
-            total = 1.0 / column_sum(each_rows(count, raise_rows, jnp.zeros((STEP, half), F32)))
-
-            def settle(i, _):
-                rows = rows_at(i)
-                probs[h, rows, now] = (scores[rows, :] * total).astype(BF16)
-
+            top = each_rows(count, lambda i, acc: jnp.maximum(acc, masked(i)), top, first=t * half)
+            top = jnp.max(top, axis=0, keepdims=True)
+            total = each_rows(
+                t * half, lambda i, acc: raised(scores[rows_at(i), :], i, acc), jnp.zeros((STEP, half), F32)
+            )
+            total = each_rows(count, lambda i, acc: raised(masked(i), i, acc), total, first=t * half)
+            divisor = 1.0 / column_sum(total)
             each_rows(count, settle)
             heads_out[head, now] = dot(value, probs[h, :count, now], 1, 0).astype(BF16)
     own = pl.multiple_of((at % 2) * half, half)
     other = pl.multiple_of((1 - at % 2) * half, half)
-    copy.wait()
-    send[...] = dot(w_out[...], heads_out[:, pl.ds(other, half)], 0, 0).astype(BF16)
-    keep[...] = dot(w_out[...], heads_out[:, pl.ds(own, half)], 0, 0)
+    heads_send[...] = heads_out[:, pl.ds(other, half)]
+    heads_own[...] = heads_out[:, pl.ds(own, half)]
     x_half[...] = x_all[:, pl.ds(own, half)]
 
 
 def output_gradient_kernel(
-    at_ref, self_ref, counts_ref, c0, c1, c2, c3, w_down, g_out, d_active, cot_half, cot_all
+    at_ref, self_ref, counts_ref, c0, c1, c2, c3, w_down, g_out, d_active, cot_all
 ):
     at = at_ref[0]
     part, tokens = c0.shape
@@ -466,22 +541,33 @@
             rows = rows_at(i)
             grad = cot_all[rows, now].astype(F32) * factor
             g_out[rows, place * half : (place + 1) * half] = (self_ref[0] * grad).astype(BF16)
-            if place == 0:
-                cot_half[rows, :] = cot_all[rows, now]
 
         each_rows(cot_all.shape[0], scale)
     d_active[...] = dot(w_down[...], g_out[...], 1, 0)
 
 
-def middle_kernel(x_half, chip, received, norms, middle, stats, normed):
-    model, half = chip.shape
-
-    def add(i, _):
+def rows_kernel(at_ref, *refs):
+    out = refs[-1]
+    for e, piece in enumerate(refs[:-1]):
+        rows = piece.shape[0]
+        out[pl.ds(pl.multiple_of((at_ref[0] ^ e) * rows, 64), rows), :] = piece[...]
+
+
+def middle_kernel(at_ref, pair, pair_far, w_all, x_half, norms, middle, stats, normed, heads):
+    model, half = x_half.shape
+    part = pair.shape[0] // 2
+    for e, piece in enumerate((pair[:part], pair[part:], pair_far[:part], pair_far[part:])):
+        heads[pl.ds(pl.multiple_of((at_ref[0] ^ e) * part, 64), part), :] = piece
+    middle[...] = dot(w_all[...], heads[...], 0, 0)
+
+    def add(i, acc):
         rows = rows_at(i)
-        middle[rows, :] = x_half[rows, :].astype(F32) + chip[rows, :] + received[rows, :].astype(F32)
-
-    each_rows(model, add)
-    mean, scale = spread_of(lambda i: middle[rows_at(i), :], model, half)
+        found = x_half[rows, :].astype(F32) + middle[rows, :]
+        middle[rows, :] = found
+        return acc + found
+
+    total = each_rows(model, add, jnp.zeros((STEP, half), F32))
+    mean, scale = spread_of(lambda i: middle[rows_at(i), :], model, half, total)
     stats[0:1] = mean
     stats[1:2] = scale
 
@@ -521,7 +607,7 @@
         out[...] = total[pl.ds(pl.multiple_of((at ^ e) * part, 64), part), :].astype(out.dtype)
 
 
-def output_kernel(at_ref, active, w_down, middle, send, send_far, keep, keep_far, total):
+def output_kernel(at_ref, counts_ref, active, w_down, middle, cot_all, send, send_far, keep, keep_far, product, total):
     at = at_ref[0]
     model, half = middle.shape
     part = send.shape[0]
@@ -529,6 +615,13 @@
     other = pl.ds(pl.multiple_of((1 - at % 2) * half, half), half)
     total[:, own] = dot(w_down[...], active[:, :half], 0, 0) + 0.5 * middle[...]
     total[:, other] = dot(w_down[...], active[:, half:], 0, 0)
+    live = live_row(counts_ref, 2 * half, 0)
+
+    def weigh(i, acc):
+        rows = rows_at(i)
+        return acc + fold_lanes(total[rows, :] * (cot_all[rows, :].astype(F32) * live))
+
+    product[...] = each_rows(model, weigh, jnp.zeros((STEP, 128), F32))
     store_blocks(at, total, part, (1, 3, 0, 2), send, send_far, keep, keep_far)
 
 
@@ -541,7 +634,7 @@
 
 
 def middle_gradient_kernel(
-    at_ref, self_ref, counts_ref, chip, received, middle, stats, cot_half, norms,
+    at_ref, self_ref, counts_ref, chip, received, middle, stats, cot_all, norms,
     d_middle, g_mid, gains, d_normed, gain_sums, bias_sums,
 ):
     model, half = chip.shape
@@ -560,12 +653,14 @@
         return acc[0] + grad * gain, acc[1] + both * gain
 
     first, second = (column_sum(v) / model for v in each_rows(model, sums, (zero, zero)))
-    factor = self_ref[0] * live_row(counts_ref, half, (at_ref[0] % 2) * half)
+    side = (at_ref[0] % 2) * half
+    factor = self_ref[0] * live_row(counts_ref, half, side)
+    own = pl.ds(pl.multiple_of(side, half), half)
 
     def finish(i, _):
         rows = rows_at(i)
         xhat = (middle[rows, :] - mean) * scale
-        found = cot_half[rows, :].astype(F32) * factor + scale * (
+        found = cot_all[rows, own].astype(F32) * factor + scale * (
             d_normed[rows, :] * norms[rows, 2:3] - first - xhat * second
         )
         d_middle[rows, :] = found
@@ -664,23 +759,18 @@
     sums[7:8] = jnp.zeros((1, model), F32) + counts_ref[0].astype(F32) / width
 
 
-def mixed_kernel(
-    self_ref, counts_ref, own, near, far, running, cotangent, d_mix, sums, mixed, all_sums, table
-):
+def mixed_kernel(self_ref, own, near, far, running, d_mix, product, sums, mixed, all_sums, table):
     layers = d_mix.shape[0]
-    part, tokens = own.shape
-    live = live_row(counts_ref, tokens, 0)
-
-    def body(i, acc):
+
+    def body(i, _):
         rows = rows_at(i)
         output = own[rows, :] + near[rows, :].astype(F32) + far[rows, :].astype(F32)
         mixed[rows, :] = (self_ref[0] * output + running[rows, :]).astype(BF16)
-        return acc + fold_lanes(cotangent[rows, :].astype(F32) * live * output)
-
-    found = each_rows(part, body, jnp.zeros((STEP, 128), F32))
+
+    each_rows(own.shape[0], body)
     table[...] = jnp.zeros_like(table)
     table[:layers] = jnp.sum(d_mix[...], axis=1)
-    table[layers : layers + 1] = column_sum(found)
+    table[layers : layers + 1] = column_sum(product[...])
     all_sums[...] = sums[...]
     all_sums[6:7, :128] = as_row(table)
 
@@ -748,7 +838,7 @@
     all_tokens = float(tokens * row_devices)
     at = lax.axis_index("width").astype(jnp.int32)[None]
     me = lax.axis_index("rows").astype(jnp.int32)[None]
-    Order.last, Order.cost = None, 10**8
+    Order.last, Order.front = None, FRONT
     to_width = lambda value, offset: xor_send(value, "width", width, offset)
     to_row = lambda value, offset: xor_send(value, "rows", row_devices, offset)
     w_qkv = w_qkv.reshape(3 * part, model)
@@ -756,19 +846,20 @@
     x_in, cotangent, counts = after((x_in, cotangent, counts), at, me)
 
     x_far, x_near = to_width(x_in, 2), to_width(x_in, 1)
-    norms, cosine, sine = prepare(
+    x_own, norms, cosine, sine = prepare(
         [x_near],
+        x_in,
         positions[None, :],
         jnp.asarray(rates[:, None], F32),
         *(v[None, :] for v in (first_norm_gain, first_norm_bias, second_norm_gain, second_norm_bias)),
     )
-    strides = [1 << i for i in range(row_devices.bit_length() - 1)]
     norms_near = join([norms, to_width(norms, 1)])
     norms_far = to_width(norms_near, 2)
     norms = kernel(norms_kernel, shape(model, 8), [at], [norms_near, norms_far])
     x_both = to_width(after(x_far, norms), 1)
-    cot_now = after(cotangent, norms_near)
+    cot_now, w_now = after((cotangent, w_out), norms_near)
     cot_far, cot_near = to_width(cot_now, 2), to_width(cot_now, 1)
+    w_far, w_near = to_width(w_now, 2), to_width(w_now, 1)
 
     x_all, normed_one, stats_one, qkv = kernel(
         project_kernel,
@@ -779,28 +870,26 @@
             shape(3 * part, tokens, kind=BF16),
         ),
         [at],
-        [x_near, x_far, x_both, norms, cosine, sine, w_qkv],
-        [pltpu.VMEM((3 * part, tokens), F32), pltpu.VMEM((part, tokens), BF16), pltpu.SemaphoreType.DMA],
-        streamed=[x_in],
+        [x_own, x_near, x_far, x_both, norms, cosine, sine, w_qkv],
+        [pltpu.VMEM((3 * part, tokens), F32)],
     )
-    Order.cost = 10**9
-    send, keep, x_half, heads_out, probs = kernel(
+    heads_send, heads_own, x_half, heads_out, probs = kernel(
         attention_kernel,
         (
-            shape(model, half, kind=BF16),
-            shape(model, half),
+            shape(part, half, kind=BF16),
+            shape(part, half, kind=BF16),
             shape(model, half, kind=BF16),
             shape(part, tokens, kind=BF16),
             shape(part // HEAD_DIM, tokens, tokens, kind=BF16),
         ),
         [at],
-        [after(qkv, cot_far), x_all],
-        [pltpu.VMEM((tokens, half), F32), pltpu.VMEM((part, model), BF16), pltpu.SemaphoreType.DMA],
-        streamed=[w_out],
+        [qkv, x_all],
+        [pltpu.VMEM((tokens, half), F32)],
     )
-    chip, send = add([keep, to_width(send, 1)], (0, model, F32), (0, model, BF16))
-    received = to_width(send, 2)
-    cot_both = to_width(after(cot_far, chip), 1)
+    pair = join([after(heads_own, cot_far, w_far), to_width(heads_send, 1)])
+    pair_far = to_width(pair, 2)
+    cot_both = to_width(after(cot_far, pair), 1)
+    w_both = to_width(after(w_far, pair), 1)
 
     running, d_mix = history_call(
         functools.partial(history_kernel, 32),
@@ -810,19 +899,20 @@
         [mix_weights, counts],
         [cotangent, pltpu.with_memory_space_constraint(history, pltpu.HBM)],
     )
-    g_out, d_active, cot_half = kernel(
+    g_out, d_active, cot_all = kernel(
         output_gradient_kernel,
-        (shape(model, tokens, kind=BF16), shape(hidden_units, tokens), shape(model, half, kind=BF16)),
+        (shape(model, tokens, kind=BF16), shape(hidden_units, tokens), shape(model, tokens, kind=BF16)),
         [at, self_weight, counts],
         [cotangent, cot_near, cot_far, cot_both, w_down],
-        [pltpu.VMEM((model, tokens), BF16)],
     )
 
+    w_all = kernel(rows_kernel, shape(model, model, kind=BF16), [at], [w_out, w_near, w_far, w_both])
     middle, stats_two, normed_own = kernel(
         middle_kernel,
         (shape(model, half), shape(2, half), shape(model, half, kind=BF16)),
-        [],
-        [x_half, chip, received, norms],
+        [at],
+        [pair, pair_far, w_all, x_half, norms],
+        [pltpu.VMEM((model, half), BF16)],
     )
     normed_two, active, d_hidden, send, keep = kernel(
         feed_forward_kernel,
@@ -838,154 +928,255 @@
         [pltpu.VMEM((hidden_units, tokens), F32)],
     )
 
+    v = Values()
+    v.send, v.keep = send, keep
     down = Stream(row_devices, 0, hidden_units, "halving")
     up = Stream(row_devices, 0, model, "crossed")
-    down_parts = weight_gradient(me, [down], active, g_out)[0]
-    down_got = start_stage(down, down_parts, 0)
-    chip, send = add([keep, to_width(send, 1)], (0, model, F32), (0, model, BF16))
-    received = to_width(send, 2)
-    up_parts = weight_gradient(me, [up], normed_two, d_hidden)[0]
-    up_got = start_stage(up, up_parts, 0)
+    first = Stream(row_devices, 0, 2 * part, "halving")
+    second = Stream(row_devices, 2 * part, 2 * part, "crossed")
+    strides = [1 << i for i in range(row_devices.bit_length() - 1)]
     blocks = (shape(part, tokens, kind=BF16),) * 2 + (shape(part, tokens),) * 2
-    out_send, out_send_far, out_keep, out_keep_far = kernel(
-        output_kernel, blocks, [at], [active, w_down, middle], [pltpu.VMEM((model, tokens), F32)]
+    last = len(down.digits) - 1
+
+    def scatter(stream, stage):
+        stream.held = add_stage(stream, stream.held, stream.got, stage)
+        stream.got = start_stage(stream, stream.held, stage + 1)
+
+    def turn(stream):
+        value = sum_rest(stream, add_stage(stream, stream.held, stream.got, last)[0])
+        stream.pieces = gather_stage(stream, value, last)
+
+    def gather(stream, stage):
+        stream.pieces = gather_stage(stream, join(stream.pieces), stage)
+
+    def steps_of(stream):
+        return (
+            *(functools.partial(scatter, stream, stage) for stage in range(last)),
+            functools.partial(turn, stream),
+            *(functools.partial(gather, stream, stage) for stage in range(last - 1, -1, -1)),
+        )
+
+    def begin(streams, found):
+        for stream, parts in zip(streams, found):
+            stream.held, stream.got = parts, start_stage(stream, parts, 0)
+
+    def down_product():
+        begin([down], weight_gradient(me, [down], active, g_out))
+
+    def up_product():
+        begin([up], weight_gradient(me, [up], normed_two, d_hidden))
+
+    def tail_product():
+        found = weight_gradient(me, [first, second], v.d_project, normed_one, heads_out, v.g_mid)
+        begin([first, second], found)
+
+    def middle_sum():
+        v.chip, sent = add([v.keep, to_width(v.send, 1)], (0, model, F32), (0, model, BF16))
+        v.received = to_width(sent, 2)
+
+    def output_product():
+        near, far, v.out, v.out_far, v.product = kernel(
+            output_kernel,
+            blocks + (shape(STEP, 128),),
+            [at, counts],
+            [active, w_down, middle, cot_all],
+            [pltpu.VMEM((model, tokens), F32)],
+        )
+        v.out_got = to_width(near, 1), to_width(far, 1)
+
+    def output_sum():
+        v.out_last = to_width(add([v.out_far, v.out_got[1]], (0, part, BF16))[0], 2)
+
+    def middle_gradient():
+        v.d_middle, v.g_own, v.gains = kernel(
+            middle_gradient_kernel,
+            (shape(model, half), shape(model, half, kind=BF16), shape(2, model)),
+            [at, self_weight, counts],
+            [v.chip, v.received, middle, stats_two, cot_all, norms],
+            [pltpu.VMEM((model, half), F32), pltpu.VMEM((model, 128), F32), pltpu.VMEM((model, 128), F32)],
+        )
+        v.g_other = to_width(v.g_own, 1)
+
+    def attention_gradient():
+        v.d_project, v.g_mid = kernel(
+            attention_gradient_kernel,
+            (shape(3 * part, tokens, kind=BF16), shape(model, tokens, kind=BF16)),
+            [at],
+            [v.g_own, v.g_other, w_out, qkv, probs, cosine, sine],
+            [
+                pltpu.VMEM((part, tokens), BF16),
+                pltpu.VMEM((tokens, half), BF16),
+                pltpu.VMEM((tokens, half), F32),
+                pltpu.VMEM((HEAD_DIM, tokens), F32),
+                pltpu.VMEM((HEAD_DIM, tokens), F32),
+                pltpu.VMEM((HEAD_DIM, tokens), F32),
+            ],
+        )
+
+    def input_gradient():
+        near, far, v.own_in, v.in_far, v.sums = kernel(
+            functools.partial(input_gradient_kernel, width),
+            blocks + (shape(8, model),),
+            [at, counts],
+            [v.d_project, w_qkv, x_all, stats_one, v.d_middle, norms, v.gains],
+            [pltpu.VMEM((model, tokens), F32), pltpu.VMEM((model, 128), F32), pltpu.VMEM((model, 128), F32)],
+        )
+        v.in_got = to_width(near, 1), to_width(far, 1)
+
+    def input_sum():
+        v.in_last = to_width(add([v.in_far, v.in_got[1]], (0, part, BF16))[0], 2)
+
+    def input_total():
+        v.in_total = kernel(
+            d_input_kernel,
+            shape(part, tokens),
+            [],
+            [v.own_in, v.in_got[0], v.in_last, x_own, stats_one, v.row_sums],
+        )
+
+    def mix():
+        v.mixed, v.sums = kernel(
+            mixed_kernel,
+            (shape(part, tokens, kind=BF16), shape(8, model)),
+            [self_weight],
+            [
+                v.out,
+                v.out_got[0],
+                v.out_last,
+                running,
+                d_mix,
+                v.product,
+                v.sums,
+            ],
+            [pltpu.VMEM((128, 128), F32)],
+        )
+        v.sums_got = to_width(v.sums, 1)
+
+    def sums_step(*sends):
+        for send_on in sends:
+            v.sums = add([v.sums, v.sums_got], (0, 8, F32))[0]
+            v.sums_got = send_on(v.sums)
+
+    def sums_1():
+        sums_step(lambda value: to_width(value, 2))
+
+    def sums_2():
+        sums_step(row_send(strides[0]))
+        v.row_sums = v.sums
+
+    def sums_3():
+        sums_step(row_send(strides[1]))
+
+    def sums_4():
+        sums_step(*(row_send(stride) for stride in strides[2:]))
+
+    def last_sums():
+        v.sums = add([v.sums, v.sums_got], (0, 8, F32))[0]
+
+    def scale_input():
+        v.d_input = kernel(
+            functools.partial(scale_kernel, all_tokens), shape(part, tokens), [], [v.in_total, v.sums]
+        )
+
+    def history_gradient():
+        v.d_history = history_call(
+            functools.partial(d_history_kernel, all_tokens, 32),
+            (shape(*history.shape, kind=BF16),),
+            (False, False),
+            (True,),
+            [mix_weights, counts],
+            [cotangent, v.sums],
+        )[0]
+
+    def ends():
+        v.ends = kernel(
+            functools.partial(ends_kernel, all_tokens, layers, width),
+            (shape(1, layers), shape(1, 1)) + (shape(1, part),) * 4,
+            [at],
+            [v.sums],
+        )
+
+    def placed(streams, *sizes):
+        pieces = [piece for stream in streams for piece in stream.pieces]
+        return place(all_tokens, me, v.sums, streams, pieces, sizes)
+
+    def place_down():
+        v.d_w_down = placed([down], hidden_units)[0]
+
+    def place_up():
+        v.d_w_up = placed([up], model)[0]
+
+    def place_tail():
+        v.d_w_qkv, v.d_w_out = placed([first, second], 3 * part, part)
+
+    row_send = lambda stride: lambda value: to_row(value, stride)
+    down_1, down_2, down_3, down_4, down_5 = steps_of(down)
+    up_1, up_2, up_3, up_4, up_5 = steps_of(up)
+    first_1, first_2, first_3, first_4, first_5 = steps_of(first)
+    second_1, second_2, second_3, second_4, second_5 = steps_of(second)
+    schedule = (
+        (down_product, 10),
+        (middle_sum, 8),
+        (up_product, 10),
+        (output_product, 100),
+        (middle_gradient, 10),
+        (output_sum, 10),
+        (down_1, 10),
+        (up_1, 100),
+        (attention_gradient, 8),
+        (tail_product, 4),
+        (down_2, 100),
+        (up_2, 0.3),
+        (input_gradient, 1),
+        (mix, 8),
+        (first_1, 1),
+        (second_1, 1),
+        (up_3, 100),
+        (down_3, 1),
+        (first_2, 2),
+        (sums_1, 4),
+        (sums_2, 1),
+        (input_sum, 1),
+        (second_2, 1),
+        (sums_3, 1),
+        (up_4, 2),
+        (sums_4, 1),
+        (down_4, 4),
+        (first_3, 40),
+        (input_total, 1),
+        (second_3, 2),
+        (down_5, 1),
+        (first_4, 200),
+        (up_5, 0.3),
+        (second_4, 16),
+        (last_sums, 1),
+        (scale_input, 0.1),
+        (first_5, 40),
+        (ends, 1),
+        (history_gradient, 1),
+        (place_down, 1),
+        (second_5, 200),
+        (place_up, 4),
+        (place_tail, 1),
     )
-    out_got = to_width(out_send, 1), to_width(out_send_far, 1)
-
-    d_middle, g_own, gains_two = kernel(
-        middle_gradient_kernel,
-        (shape(model, half), shape(model, half, kind=BF16), shape(2, model)),
-        [at, self_weight, counts],
-        [chip, received, middle, stats_two, cot_half, norms],
-        [pltpu.VMEM((model, half), F32), pltpu.VMEM((model, 128), F32), pltpu.VMEM((model, 128), F32)],
-    )
-    g_other = to_width(g_own, 1)
-    out_send = add([out_keep_far, out_got[1]], (0, part, BF16))[0]
-    out_far = to_width(out_send, 2)
-    down_parts = add_stage(down, down_parts, down_got, 0)
-    down_got = start_stage(down, down_parts, 1)
-    up_parts = add_stage(up, up_parts, up_got, 0)
-    up_got = start_stage(up, up_parts, 1)
-    d_project, g_mid = kernel(
-        attention_gradient_kernel,
-        (shape(3 * part, tokens, kind=BF16), shape(model, tokens, kind=BF16)),
-        [at],
-        [g_own, g_other, w_out, qkv, probs, cosine, sine],
-        [
-            pltpu.VMEM((part, tokens), BF16),
-            pltpu.VMEM((tokens, half), BF16),
-            pltpu.VMEM((tokens, half), F32),
-            pltpu.VMEM((HEAD_DIM, tokens), F32),
-            pltpu.VMEM((HEAD_DIM, tokens), F32),
-            pltpu.VMEM((HEAD_DIM, tokens), F32),
-        ],
-    )
-    tail_rows = 4 * part
-    tail = [
-        Stream(row_devices, 0, tail_rows // 2, "halving"),
-        Stream(row_devices, tail_rows // 2, tail_rows // 2, "crossed"),
-    ]
-    first, second = tail
-    first_parts, second_parts = weight_gradient(me, tail, d_project, normed_one, heads_out, g_mid)
-    first_got = start_stage(first, first_parts, 0)
-    second_got = start_stage(second, second_parts, 0)
-
-    Order.cost = 10**8
-    down_parts = add_stage(down, down_parts, down_got, 1)
-    down_got = start_stage(down, down_parts, 2)
-    up_parts = add_stage(up, up_parts, up_got, 1)
-    up_got = start_stage(up, up_parts, 2)
-    in_send, in_send_far, in_keep, in_keep_far, sums = kernel(
-        functools.partial(input_gradient_kernel, width),
-        blocks + (shape(8, model),),
-        [at, counts],
-        [d_project, w_qkv, x_all, stats_one, d_middle, norms, gains_two],
-        [pltpu.VMEM((model, tokens), F32), pltpu.VMEM((model, 128), F32), pltpu.VMEM((model, 128), F32)],
-    )
-    in_got = to_width(in_send, 1), to_width(in_send_far, 1)
-    last = len(down.digits) - 1
-    mixed, sums = kernel(
-        mixed_kernel,
-        (shape(part, tokens, kind=BF16), shape(8, model)),
-        [self_weight, counts],
-        [out_keep, out_got[0], out_far, running, cotangent, d_mix, sums],
-        [pltpu.VMEM((128, 128), F32)],
-    )
-    sums_got = to_width(sums, 1)
-    first_parts = add_stage(first, first_parts, first_got, 0)
-    first_got = start_stage(first, first_parts, 1)
-    second_parts = add_stage(second, second_parts, second_got, 0)
-    second_got = start_stage(second, second_parts, 1)
-    down_value = sum_rest(down, add_stage(down, down_parts, down_got, 2)[0])
-    down_pieces = gather_stage(down, down_value, last)
-    up_value = sum_rest(up, add_stage(up, up_parts, up_got, 2)[0])
-    up_pieces = gather_stage(up, up_value, last)
-    first_parts = add_stage(first, first_parts, first_got, 1)
-    first_got = start_stage(first, first_parts, 2)
-    second_parts = add_stage(second, second_parts, second_got, 1)
-    second_got = start_stage(second, second_parts, 2)
-    sums = add([sums, sums_got], (0, 8, F32))[0]
-    sums_got = to_width(sums, 2)
-    row_sums = add([sums, sums_got], (0, 8, F32))[0]
-    sums_got = to_row(row_sums, strides[0])
-    down_pieces = gather_stage(down, join(down_pieces), last - 1)
-    up_pieces = gather_stage(up, join(up_pieces), last - 1)
-    in_send = add([in_keep_far, in_got[1]], (0, part, BF16))[0]
-    in_far = to_width(in_send, 2)
-    sums = row_sums
-    for stride in strides[1:-1]:
-        sums = add([sums, sums_got], (0, 8, F32))[0]
-        sums_got = to_row(sums, stride)
-    first_value = sum_rest(first, add_stage(first, first_parts, first_got, 2)[0])
-    first_pieces = gather_stage(first, first_value, last)
-    second_value = sum_rest(second, add_stage(second, second_parts, second_got, 2)[0])
-    second_pieces = gather_stage(second, second_value, last)
-    sums = add([sums, sums_got], (0, 8, F32))[0]
-    sums_got = to_row(sums, strides[-1])
-    in_total = kernel(d_input_kernel, shape(part, tokens), [], [in_keep, in_got[0], in_far, x_in, stats_one, row_sums])
-    down_pieces = gather_stage(down, join(down_pieces), 0)
-    up_pieces = gather_stage(up, join(up_pieces), 0)
-    first_pieces = gather_stage(first, join(first_pieces), last - 1)
-    second_pieces = gather_stage(second, join(second_pieces), last - 1)
-    sums = add([sums, sums_got], (0, 8, F32))[0]
-    d_input = kernel(
-        functools.partial(scale_kernel, all_tokens), shape(part, tokens), [], [in_total, sums]
-    )
-    d_history = history_call(
-        functools.partial(d_history_kernel, all_tokens, 32),
-        (shape(*history.shape, kind=BF16),),
-        (False, False),
-        (True,),
-        [mix_weights, counts],
-        [cotangent, sums],
-    )[0]
-    d_mix, d_self, *ends = kernel(
-        functools.partial(ends_kernel, all_tokens, layers, width),
-        (shape(1, layers), shape(1, 1)) + (shape(1, part),) * 4,
-        [at],
-        [sums],
-    )
-    first_pieces = gather_stage(first, join(first_pieces), 0)
-    Order.cost = 2 * 10**10
-    second_pieces = gather_stage(second, join(second_pieces), 0)
-    Order.cost = 10**8
-    d_w_down = place(all_tokens, me, sums, [down], down_pieces, (hidden_units,))[0]
-    d_w_up = place(all_tokens, me, sums, [up], up_pieces, (model,))[0]
-    d_w_qkv, d_w_out = place(all_tokens, me, sums, tail, first_pieces + second_pieces, (3 * part, part))
+    for step, weight in schedule:
+        Order.cost = weight
+        step()
+    d_mix, d_self, *vectors = v.ends
     return (
-        mixed,
-        d_input,
-        d_history,
+        v.mixed,
+        v.d_input,
+        v.d_history,
         d_mix[0],
         d_self[0],
-        ends[0][0],
-        ends[1][0],
-        d_w_qkv.reshape(3, part, model),
-        d_w_out,
-        ends[2][0],
-        ends[3][0],
-        d_w_up,
-        d_w_down,
+        vectors[0][0],
+        vectors[1][0],
+        v.d_w_qkv.reshape(3, part, model),
+        v.d_w_out,
+        vectors[2][0],
+        vectors[3][0],
+        v.d_w_up,
+        v.d_w_down,
     )
 
 

time: 150 us -> 147 us (0.980)
  waiting for transfers between devices: 52.5 us -> 50.8 us
    pallas_call x50 -> x48, Pallas kernels: 35.5 us -> 29.4 us  [kernel(): pl.pallas_call(body, out_shape=outs, in_specs=[pl.BlockSpec(memory_space=...]
    pallas_call x0 -> x3, Pallas kernels: none -> 4.88 us  [place(): pl.pallas_call(functools.partial(place_kernel, all_tokens, streams, bound...]
    ppermute x49 -> x52, waiting for transfers between devices: 52.5 us -> 50.8 us  [xor_send(): return lax.ppermute(value, axis, [(i, i ^ offset) for i in range(size)])]
    ppermute x49 -> x52, starting transfers between devices: 48.7 us -> 48 us  [xor_send(): return lax.ppermute(value, axis, [(i, i ^ offset) for i in range(size)])]
  transfers between devices with their start and end apart: 49 -> 52, of which waited for: 23 -> 20; matrix products, arithmetic and copies ran while one was open for 0% -> 0% of each run, Pallas kernels for 23% -> 26%
where the time goes in v7:
time: 147 us
  waiting for transfers between devices  50.8 us (35%)
  starting transfers between devices  48 us (33%)
  Pallas kernels  45.2 us (31%)
  between operations  2.68 us (2%)
    ppermute x52, waiting for transfers between devices, xor_send(): return lax.ppermute(value, axis, [(i, i ^ offset) for i in range(size)])  50.8 us
    ppermute x52, starting transfers between devices, xor_send(): return lax.ppermute(value, axis, [(i, i ^ offset) for i in range(size)])  48 us
    pallas_call x48, Pallas kernels, kernel(): pl.pallas_call(body, out_shape=outs, in_specs=[pl.BlockSpec(memory_space=...  29.4 us
    pallas_call x2, Pallas kernels, history_call(): pl.pallas_call(body, out_shape=outs, in_specs=[pl.BlockSpec(memory_space=...  9.77 us
    pallas_call x3, Pallas kernels, place(): pl.pallas_call(functools.partial(place_kernel, all_tokens, streams, bound...  4.88 us
  transfers between devices with their start and end apart: 52, of which 20 were waited for; matrix products, arithmetic and copies ran while one was open for 0% of the time, Pallas kernels for 26%

profile of v7, /device:TPU:0, one launch (start us, length us, event | category | flops | bytes accessed | tf_op | source)
XLA Modules:
  0.0 146.8 jit_solution(18162514757559591440)
XLA Ops:
  1.2 2.6 %collective-permute-start.3 = (bf16[192,512]{1,0:T(8,128)(2,1)}, bf16[192,512]{1,0:T(8,128)(2,1)S(1)}, u32[]{:S(2)}, u32[]{:S(2)}) collective-permute-start(bf16[192,512]{1,0:T(8,128)(2,1)} %refs_7_), channel_id=1, source_target_pairs={{0,2},{1,3},{2,0},{3,1},{4,6},{5,7},{6,4},{7,5},{8,10},{9,11},{10,... | collective-permute-start | bytes 589832 | tf_op jit(solution)/shard_map/ppermute | solution.py:128
  6.2 1.6 %collective-permute-start.2 = (f32[16,256]{1,0:T(8,128)S(1)}, f32[16,256]{1,0:T(8,128)S(1)}, u32[]{:S(2)}, u32[]{:S(2)}) collective-permute-start(f32[16,256]{1,0:T(8,128)S(1)} %shard_map.256.n01), channel_id=1, source_target_pairs={{0,2},{1,3},{2,0},{3,1},{4,6},{5,7},{6,4},{7,5},{8,10},{9,11},{10,... | collective-permute-start | bytes 49160 | tf_op jit(solution)/shard_map/ppermute | solution.py:128
  7.7 2.2 %collective-permute-done.2.n23 = f32[16,256]{1,0:T(8,128)S(1)} collective-permute-done((f32[16,256]{1,0:T(8,128)S(1)}, f32[16,256]{1,0:T(8,128)S(1)}, u32[]{:S(2)}, u32[]{:S(2)}) %collective-permute-start.2) | collective-permute-done | bytes 16416 | tf_op jit(solution)/shard_map/ppermute | solution.py:128
  10.2 1.8 %collective-permute-start.6 = (bf16[192,768]{1,0:T(8,128)(2,1)}, bf16[192,768]{1,0:T(8,128)(2,1)S(1)}, u32[]{:S(2)}, u32[]{:S(2)}) collective-permute-start(bf16[192,768]{1,0:T(8,128)(2,1)} %w_out.1), channel_id=1, source_target_pairs={{0,2},{1,3},{2,0},{3,1},{4,6},{5,7},{6,4},{7,5},{8,10},{9,11},{10,... | collective-permute-start | bytes 884744 | tf_op jit(solution)/shard_map/ppermute | solution.py:128
  12.3 2.2 %shard_map.258 = (bf16[768,512]{1,0:T(8,128)(2,1)S(1)}, bf16[768,512]{1,0:T(8,128)(2,1)S(1)}, f32[2,512]{1,0:T(2,128)S(1)}, bf16[576,512]{1,0:T(8,128)(2,1)S(1)}) custom-call(s32[1]{0:T(128)} %bitcast.at_ref, bf16[192,512]{1,0:T(8,128)(2,1)S(1)} %get-tuple-element.158.x0.x_in, bf16[192,512]{1,0:T(8,128)(2,1)S(1)} %collective-permute-done.refs_0_.x1, ...), custom_call_target="tpu_custom_call" | custom-call | flops 100000000 | bytes 1024 | tf_op jit(solution)/shard_map/pallas_call | solution.py:93
  14.5 4.3 %shard_map.259 = (bf16[192,256]{1,0:T(8,128)(2,1)S(1)}, bf16[192,256]{1,0:T(8,128)(2,1)S(1)}, bf16[768,256]{1,0:T(8,128)(2,1)S(1)}, bf16[192,512]{1,0:T(8,128)(2,1)S(1)}, bf16[3,512,512]{2,1,0:T(8,128)(2,1)S(1)}) custom-call(s32[1]{0:T(128)} %bitcast.at_ref, bf16[576,512]{1,0:T(8,128)(2,1)S(1)} %get-tuple-element.164.qkv, ...), custom_call_target="tpu_custom_call" | custom-call | flops 100000000 | bytes 1024 | tf_op jit(solution)/shard_map/pallas_call | solution.py:93
  19.4 4.6 %collective-permute-done.5.c2 = bf16[192,512]{1,0:T(8,128)(2,1)S(1)} collective-permute-done((bf16[192,512]{1,0:T(8,128)(2,1)}, bf16[192,512]{1,0:T(8,128)(2,1)S(1)}, u32[]{:S(2)}, u32[]{:S(2)}) %collective-permute-start.5) | collective-permute-done | bytes 196640 | tf_op jit(solution)/shard_map/ppermute | solution.py:128
  26.0 1.8 %collective-permute-start.12 = (bf16[384,256]{1,0:T(8,128)(2,1)S(1)}, bf16[384,256]{1,0:T(8,128)(2,1)S(1)}, u32[]{:S(2)}, u32[]{:S(2)}) collective-permute-start(bf16[384,256]{1,0:T(8,128)(2,1)S(1)} %shard_map.260.pair), channel_id=1, source_target_pairs={{0,2},{1,3},{2,0},{3,1},{4,6},{5,7},{6,4},{7,5},{8,10},{9,11},{10,... | collective-permute-start | bytes 589832 | tf_op jit(solution)/shard_map/ppermute | solution.py:128
  27.8 5.7 %shard_map.261 = (f32[192,512]{1,0:T(8,128)S(1)}, f32[30,8,128]{2,1,0:T(8,128)S(1)}) custom-call(f32[30]{0:T(128)S(1)} %copy-done.3, s32[1]{0:T(128)S(6)} %copy.29.counts_ref, bf16[192,512]{1,0:T(8,128)(2,1)S(1)} %copy-done.1, bf16[30,192,512]{2,1,0:T(8,128)(2,1)} %history_ref.1), custom_call_target="tpu_custom_call" | custom-call | flops 1000000000 | bytes 1024 | tf_op jit(solution)/shard_map/pallas_call | solution.py:376
  33.5 1.2 shard_map.262
  34.9 2.0 %shard_map.264 = (f32[768,256]{1,0:T(8,128)S(1)}, f32[2,256]{1,0:T(2,128)S(1)}, bf16[768,256]{1,0:T(8,128)(2,1)S(1)}) custom-call(s32[1]{0:T(128)} %bitcast.at_ref, bf16[384,256]{1,0:T(8,128)(2,1)S(1)} %shard_map.260.pair, bf16[384,256]{1,0:T(8,128)(2,1)S(1)} %collective-permute-done.12.pair_far, bf16[768,768]{1,0:T(8,128)(2,1)S(1)} %shard_map.263.w_all, ...), custom_call_target="tpu_custom_call" | custom-call | flops 1000000000 | bytes 1024 | tf_op jit(solution)/shard_map/pallas_call | solution.py:93
  37.1 1.6 %collective-permute-done.13.other = bf16[768,256]{1,0:T(8,128)(2,1)S(1)} collective-permute-done((bf16[768,256]{1,0:T(8,128)(2,1)S(1)}, bf16[768,256]{1,0:T(8,128)(2,1)S(1)}, u32[]{:S(2)}, u32[]{:S(2)}) %collective-permute-start.13) | collective-permute-done | bytes 393248 | tf_op jit(solution)/shard_map/ppermute | solution.py:128
  38.6 2.6 %shard_map.265 = (bf16[768,512]{1,0:T(8,128)(2,1)S(1)}, bf16[768,512]{1,0:T(8,128)(2,1)S(1)}, bf16[768,512]{1,0:T(8,128)(2,1)S(1)}, bf16[768,256]{1,0:T(8,128)(2,1)S(1)}, f32[768,256]{1,0:T(8,128)S(1)}) custom-call(bf16[768,256]{1,0:T(8,128)(2,1)S(1)} %get-tuple-element.183.own, bf16[768,256]{1,0:T(8,128)(2,1)S(1)} %collective-permute-done.13.other, ...), custom_call_target="tpu_custom_call" | custom-call | flops 1000000000 | bytes 1024 | tf_op jit(solution)/shard_map/pallas_call | solution.py:93
  42.4 1.6 %collective-permute-start.17 = (bf16[384,768]{1,0:T(8,128)(2,1)S(1)}, bf16[384,768]{1,0:T(8,128)(2,1)S(1)}, u32[]{:S(2)}, u32[]{:S(2)}) collective-permute-start(bf16[384,768]{1,0:T(8,128)(2,1)S(1)} %get-tuple-element.209), channel_id=1, source_target_pairs={{0,4},{4,0},{8,12},{12,8},{16,20},{20,16},{24,28},{28,24},{1,5},{5... | collective-permute-start | bytes 1769480 | tf_op jit(solution)/shard_map/ppermute | solution.py:128
  45.7 1.6 %collective-permute-start.18 = (bf16[384,768]{1,0:T(8,128)(2,1)S(1)}, bf16[384,768]{1,0:T(8,128)(2,1)S(1)}, u32[]{:S(2)}, u32[]{:S(2)}) collective-permute-start(bf16[384,768]{1,0:T(8,128)(2,1)S(1)} %get-tuple-element.212), channel_id=1, source_target_pairs={{0,8},{4,12},{8,0},{12,4},{16,24},{20,28},{24,16},{28,20},{1,9},{5... | collective-permute-start | bytes 1769480 | tf_op jit(solution)/shard_map/ppermute | solution.py:128
  47.3 1.2 shard_map.269
  49.1 7.3 %collective-permute-done.15.received = bf16[768,256]{1,0:T(8,128)(2,1)S(1)} collective-permute-done((bf16[768,256]{1,0:T(8,128)(2,1)S(1)}, bf16[768,256]{1,0:T(8,128)(2,1)S(1)}, u32[]{:S(2)}, u32[]{:S(2)}) %collective-permute-start.15) | collective-permute-done | bytes 393248 | tf_op jit(solution)/shard_map/ppermute | solution.py:128
  56.3 2.3 %shard_map.270 = (f32[768,256]{1,0:T(8,128)S(1)}, bf16[768,256]{1,0:T(8,128)(2,1)S(1)}, f32[2,768]{1,0:T(2,128)S(1)}) custom-call(s32[1]{0:T(128)} %bitcast.at_ref, f32[1]{0:T(128)S(6)} %copy.30.self_ref, s32[1]{0:T(128)S(6)} %copy.29.counts_ref, f32[768,256]{1,0:T(8,128)S(1)} %get-tuple-element.200.chip, ...), custom_call_target="tpu_custom_call" | custom-call | flops 1000000000 | bytes 1024 | tf_op jit(solution)/shard_map/pallas_call | solution.py:93
  59.5 1.6 %collective-permute-start.20 = (bf16[192,768]{1,0:T(8,128)(2,1)S(1)}, bf16[192,768]{1,0:T(8,128)(2,1)S(1)}, u32[]{:S(2)}, u32[]{:S(2)}) collective-permute-start(bf16[192,768]{1,0:T(8,128)(2,1)S(1)} %get-tuple-element.223), channel_id=1, source_target_pairs={{0,8},{4,12},{8,0},{12,4},{16,24},{20,28},{24,16},{28,20},{1,9},{5... | collective-permute-start | bytes 884744 | tf_op jit(solution)/shard_map/ppermute | solution.py:128
  62.1 3.6 %shard_map.274 = (bf16[576,512]{1,0:T(8,128)(2,1)S(1)}, bf16[768,512]{1,0:T(8,128)(2,1)S(1)}) custom-call(s32[1]{0:T(128)} %bitcast.at_ref, bf16[768,256]{1,0:T(8,128)(2,1)S(1)} %get-tuple-element.214.own, bf16[768,256]{1,0:T(8,128)(2,1)S(1)} %collective-permute-done.19.other, bf16[192,768]{1,0:T(8,128)(2,1)S(1)} %copy-done.2, ...), custom_call_target="tpu_custom_call" | custom-call | flops 800000000 | bytes 1024 | tf_op jit(solution)/shard_map/pallas_call | solution.py:93
  66.6 1.4 collective-permute-start.24
  69.0 1.6 %collective-permute-start.25 = (bf16[192,768]{1,0:T(8,128)(2,1)S(1)}, bf16[192,768]{1,0:T(8,128)(2,1)S(1)}, u32[]{:S(2)}, u32[]{:S(2)}) collective-permute-start(bf16[192,768]{1,0:T(8,128)(2,1)S(1)} %get-tuple-element.243), channel_id=1, source_target_pairs={{0,8},{4,12},{8,0},{12,4},{16,24},{20,28},{24,16},{28,20},{1,9},{5... | collective-permute-start | bytes 884744 | tf_op jit(solution)/shard_map/ppermute | solution.py:128
  71.3 2.7 %collective-permute-start.26 = (bf16[96,768]{1,0:T(8,128)(2,1)S(1)}, bf16[96,768]{1,0:T(8,128)(2,1)S(1)}, u32[]{:S(2)}, u32[]{:S(2)}) collective-permute-start(bf16[96,768]{1,0:T(8,128)(2,1)S(1)} %get-tuple-element.246), channel_id=1, source_target_pairs={{0,16},{4,20},{8,24},{12,28},{16,0},{20,4},{24,8},{28,12},{1,17},{... | collective-permute-start | bytes 442376 | tf_op jit(solution)/shard_map/ppermute | solution.py:128
  74.0 2.8 %shard_map.278 = (bf16[192,512]{1,0:T(8,128)(2,1)S(1)}, bf16[192,512]{1,0:T(8,128)(2,1)S(1)}, f32[192,512]{1,0:T(8,128)S(1)}, f32[192,512]{1,0:T(8,128)S(1)}, f32[8,768]{1,0:T(8,128)S(1)}) custom-call(s32[1]{0:T(128)} %bitcast.at_ref, s32[1]{0:T(128)S(6)} %copy.29.counts_ref, bf16[576,512]{1,0:T(8,128)(2,1)S(1)} %get-tuple-element.228.refs_0_.d_project, ...), custom_call_target="tpu_custom_call" | custom-call | flops 100000000 | bytes 1024 | tf_op jit(solution)/shard_map/pallas_call | solution.py:93
  78.1 3.7 %collective-permute-done.25.refs_1_ = bf16[192,768]{1,0:T(8,128)(2,1)S(1)} collective-permute-done((bf16[192,768]{1,0:T(8,128)(2,1)S(1)}, bf16[192,768]{1,0:T(8,128)(2,1)S(1)}, u32[]{:S(2)}, u32[]{:S(2)}) %collective-permute-start.25) | collective-permute-done | bytes 294944 | tf_op jit(solution)/shard_map/ppermute | solution.py:128
  82.7 4.5 %collective-permute-start.34 = (bf16[96,768]{1,0:T(8,128)(2,1)S(1)}, bf16[96,768]{1,0:T(8,128)(2,1)S(1)}, u32[]{:S(2)}, u32[]{:S(2)}) collective-permute-start(bf16[96,768]{1,0:T(8,128)(2,1)S(1)} %shard_map.282.refs_0_), channel_id=1, source_target_pairs={{0,16},{4,20},{8,24},{12,28},{16,0},{20,4},{24,8},{28,12},{1,17},{... | collective-permute-start | bytes 442376 | tf_op jit(solution)/shard_map/ppermute | solution.py:128
  87.2 5.2 %collective-permute-done.27.refs_1_ = bf16[96,768]{1,0:T(8,128)(2,1)S(1)} collective-permute-done((bf16[96,768]{1,0:T(8,128)(2,1)S(1)}, bf16[96,768]{1,0:T(8,128)(2,1)S(1)}, u32[]{:S(2)}, u32[]{:S(2)}) %collective-permute-start.27) | collective-permute-done | bytes 147488 | tf_op jit(solution)/shard_map/ppermute | solution.py:128
  93.6 1.5 %collective-permute-start.30 = (f32[8,768]{1,0:T(8,128)S(1)}, f32[8,768]{1,0:T(8,128)S(1)}, u32[]{:S(2)}, u32[]{:S(2)}) collective-permute-start(f32[8,768]{1,0:T(8,128)S(1)} %shard_map.285.refs_0_), channel_id=1, source_target_pairs={{0,2},{1,3},{2,0},{3,1},{4,6},{5,7},{6,4},{7,5},{8,10},{9,11},{10,... | collective-permute-start | bytes 73736 | tf_op jit(solution)/shard_map/ppermute | solution.py:128
  95.1 2.3 %collective-permute-done.30.refs_1_ = f32[8,768]{1,0:T(8,128)S(1)} collective-permute-done((f32[8,768]{1,0:T(8,128)S(1)}, f32[8,768]{1,0:T(8,128)S(1)}, u32[]{:S(2)}, u32[]{:S(2)}) %collective-permute-start.30) | collective-permute-done | bytes 24608 | tf_op jit(solution)/shard_map/ppermute | solution.py:128
  97.5 2.1 %collective-permute-start.37 = (bf16[48,768]{1,0:T(8,128)(2,1)S(1)}, bf16[48,768]{1,0:T(8,128)(2,1)S(1)}, u32[]{:S(2)}, u32[]{:S(2)}) collective-permute-start(bf16[48,768]{1,0:T(8,128)(2,1)S(1)} %get-tuple-element.266), channel_id=1, source_target_pairs={{0,16},{4,20},{8,24},{12,28},{16,0},{20,4},{24,8},{28,12},{1,17},{... | collective-permute-start | bytes 221192 | tf_op jit(solution)/shard_map/ppermute | solution.py:128
  99.7 1.6 %collective-permute-done.33.refs_1_ = f32[8,768]{1,0:T(8,128)S(1)} collective-permute-done((f32[8,768]{1,0:T(8,128)S(1)}, f32[8,768]{1,0:T(8,128)S(1)}, u32[]{:S(2)}, u32[]{:S(2)}) %collective-permute-start.33) | collective-permute-done | bytes 24608 | tf_op jit(solution)/shard_map/ppermute | solution.py:128
  102.0 1.5 %collective-permute-start.39 = (bf16[192,512]{1,0:T(8,128)(2,1)S(1)}, bf16[192,512]{1,0:T(8,128)(2,1)S(1)}, u32[]{:S(2)}, u32[]{:S(2)}) collective-permute-start(bf16[192,512]{1,0:T(8,128)(2,1)S(1)} %shard_map.287), channel_id=1, source_target_pairs={{0,2},{1,3},{2,0},{3,1},{4,6},{5,7},{6,4},{7,5},{8,10},{9,11},{10,... | collective-permute-start | bytes 589832 | tf_op jit(solution)/shard_map/ppermute | solution.py:128
  103.6 1.5 %collective-permute-done.35.refs_1_ = f32[8,768]{1,0:T(8,128)S(1)} collective-permute-done((f32[8,768]{1,0:T(8,128)S(1)}, f32[8,768]{1,0:T(8,128)S(1)}, u32[]{:S(2)}, u32[]{:S(2)}) %collective-permute-start.35) | collective-permute-done | bytes 24608 | tf_op jit(solution)/shard_map/ppermute | solution.py:128
  105.1 2.0 %collective-permute-start.40 = (bf16[48,768]{1,0:T(8,128)(2,1)S(1)}, bf16[48,768]{1,0:T(8,128)(2,1)S(1)}, u32[]{:S(2)}, u32[]{:S(2)}) collective-permute-start(bf16[48,768]{1,0:T(8,128)(2,1)S(1)} %get-tuple-element.269), channel_id=1, source_target_pairs={{0,16},{4,20},{8,24},{12,28},{16,0},{20,4},{24,8},{28,12},{1,17},{... | collective-permute-start | bytes 221192 | tf_op jit(solution)/shard_map/ppermute | solution.py:128
  107.3 1.7 %collective-permute-start.42 = (bf16[48,768]{1,0:T(8,128)(2,1)S(1)}, bf16[48,768]{1,0:T(8,128)(2,1)S(1)}, u32[]{:S(2)}, u32[]{:S(2)}) collective-permute-start(bf16[48,768]{1,0:T(8,128)(2,1)S(1)} %shard_map.293.refs_0_), channel_id=1, source_target_pairs={{0,16},{4,20},{8,24},{12,28},{16,0},{20,4},{24,8},{28,12},{1,17},{... | collective-permute-start | bytes 221192 | tf_op jit(solution)/shard_map/ppermute | solution.py:128
  111.6 1.8 %collective-permute-start.44 = (bf16[48,768]{1,0:T(8,128)(2,1)S(1)}, bf16[48,768]{1,0:T(8,128)(2,1)S(1)}, u32[]{:S(2)}, u32[]{:S(2)}) collective-permute-start(bf16[48,768]{1,0:T(8,128)(2,1)S(1)} %shard_map.295.refs_0_), channel_id=1, source_target_pairs={{0,16},{4,20},{8,24},{12,28},{16,0},{20,4},{24,8},{28,12},{1,17},{... | collective-permute-start | bytes 221192 | tf_op jit(solution)/shard_map/ppermute | solution.py:128
  113.3 5.6 %collective-permute-done.41.refs_1_ = bf16[192,768]{1,0:T(8,128)(2,1)S(1)} collective-permute-done((bf16[192,768]{1,0:T(8,128)(2,1)S(1)}, bf16[192,768]{1,0:T(8,128)(2,1)S(1)}, u32[]{:S(2)}, u32[]{:S(2)}) %collective-permute-start.41) | collective-permute-done | bytes 294944 | tf_op jit(solution)/shard_map/ppermute | solution.py:128
  119.7 1.6 %collective-permute-start.48 = (bf16[96,768]{1,0:T(8,128)(2,1)S(1)}, bf16[96,768]{1,0:T(8,128)(2,1)S(1)}, u32[]{:S(2)}, u32[]{:S(2)}) collective-permute-start(bf16[96,768]{1,0:T(8,128)(2,1)S(1)} %shard_map.299.refs_0_), channel_id=1, source_target_pairs={{0,4},{4,0},{8,12},{12,8},{16,20},{20,16},{24,28},{28,24},{1,5},{5... | collective-permute-start | bytes 442376 | tf_op jit(solution)/shard_map/ppermute | solution.py:128
  121.3 2.0 %collective-permute-start.49 = (bf16[384,768]{1,0:T(8,128)(2,1)S(1)}, bf16[384,768]{1,0:T(8,128)(2,1)S(1)}, u32[]{:S(2)}, u32[]{:S(2)}) collective-permute-start(bf16[384,768]{1,0:T(8,128)(2,1)S(1)} %shard_map.298.refs_0_), channel_id=1, source_target_pairs={{0,8},{4,12},{8,0},{12,4},{16,24},{20,28},{24,16},{28,20},{1,9},{5... | collective-permute-start | bytes 1769480 | tf_op jit(solution)/shard_map/ppermute | solution.py:128
  124.2 2.2 %collective-permute-done.46.refs_1_ = bf16[96,768]{1,0:T(8,128)(2,1)S(1)} collective-permute-done((bf16[96,768]{1,0:T(8,128)(2,1)S(1)}, bf16[96,768]{1,0:T(8,128)(2,1)S(1)}, u32[]{:S(2)}, u32[]{:S(2)}) %collective-permute-start.46) | collective-permute-done | bytes 147488 | tf_op jit(solution)/shard_map/ppermute | solution.py:128
  126.5 1.6 %collective-permute-start.50 = (bf16[192,768]{1,0:T(8,128)(2,1)S(1)}, bf16[192,768]{1,0:T(8,128)(2,1)S(1)}, u32[]{:S(2)}, u32[]{:S(2)}) collective-permute-start(bf16[192,768]{1,0:T(8,128)(2,1)S(1)} %shard_map.302.refs_0_), channel_id=1, source_target_pairs={{0,4},{4,0},{8,12},{12,8},{16,20},{20,16},{24,28},{28,24},{1,5},{5... | collective-permute-start | bytes 884744 | tf_op jit(solution)/shard_map/ppermute | solution.py:128
  128.8 4.1 %shard_map.304 = bf16[30,192,512]{2,1,0:T(8,128)(2,1)} custom-call(f32[30]{0:T(128)S(1)} %copy-done.3, s32[1]{0:T(128)S(6)} %copy.29.counts_ref, bf16[192,512]{1,0:T(8,128)(2,1)S(1)} %copy-done.1, f32[8,768]{1,0:T(8,128)S(1)} %shard_map.300.sums), custom_call_target="tpu_custom_call" | custom-call | flops 100000000 | bytes 1024 | tf_op jit(solution)/shard_map/pallas_call | solution.py:376
  132.8 2.5 %collective-permute-done.47.refs_1_ = bf16[384,768]{1,0:T(8,128)(2,1)S(1)} collective-permute-done((bf16[384,768]{1,0:T(8,128)(2,1)S(1)}, bf16[384,768]{1,0:T(8,128)(2,1)S(1)}, u32[]{:S(2)}, u32[]{:S(2)}) %collective-permute-start.47) | collective-permute-done | bytes 589856 | tf_op jit(solution)/shard_map/ppermute | solution.py:128
  135.3 1.6 %shard_map.305 = f32[768,768]{1,0:T(8,128)} custom-call(s32[1]{0:T(128)} %bitcast.1.me_ref, f32[8,768]{1,0:T(8,128)S(1)} %shard_map.300.sums, bf16[384,768]{1,0:T(8,128)(2,1)S(1)} %shard_map.296.refs_0_, bf16[384,768]{1,0:T(8,128)(2,1)S(1)} %collective-permute-done.47.refs_1_), custom_call_target="tpu_custom_call" | custom-call | flops 100000000 | bytes 1024 | tf_op jit(solution)/shard_map/pallas_call | solution.py:312
  138.2 1.6 %shard_map.307 = f32[768,768]{1,0:T(8,128)} custom-call(s32[1]{0:T(128)} %bitcast.1.me_ref, f32[8,768]{1,0:T(8,128)S(1)} %shard_map.300.sums, bf16[384,768]{1,0:T(8,128)(2,1)S(1)} %shard_map.298.refs_0_, bf16[384,768]{1,0:T(8,128)(2,1)S(1)} %collective-permute-done.49.refs_1_), custom_call_target="tpu_custom_call" | custom-call | flops 400000000 | bytes 1024 | tf_op jit(solution)/shard_map/pallas_call | solution.py:312
  139.7 1.5 %collective-permute-done.50.refs_1_ = bf16[192,768]{1,0:T(8,128)(2,1)S(1)} collective-permute-done((bf16[192,768]{1,0:T(8,128)(2,1)S(1)}, bf16[192,768]{1,0:T(8,128)(2,1)S(1)}, u32[]{:S(2)}, u32[]{:S(2)}) %collective-permute-start.50) | collective-permute-done | bytes 294944 | tf_op jit(solution)/shard_map/ppermute | solution.py:128
  141.2 3.7 %collective-permute-done.51.refs_3_ = bf16[192,768]{1,0:T(8,128)(2,1)S(1)} collective-permute-done((bf16[192,768]{1,0:T(8,128)(2,1)S(1)}, bf16[192,768]{1,0:T(8,128)(2,1)S(1)}, u32[]{:S(2)}, u32[]{:S(2)}) %collective-permute-start.51) | collective-permute-done | bytes 294944 | tf_op jit(solution)/shard_map/ppermute | solution.py:128
  144.9 1.8 %shard_map.308 = (f32[576,768]{1,0:T(8,128)}, f32[192,768]{1,0:T(8,128)}) custom-call(s32[1]{0:T(128)} %bitcast.1.me_ref, f32[8,768]{1,0:T(8,128)S(1)} %shard_map.300.sums, bf16[192,768]{1,0:T(8,128)(2,1)S(1)} %shard_map.302.refs_0_, bf16[192,768]{1,0:T(8,128)(2,1)S(1)} %collective-permute-done.50.refs_1_, bf16[192,768]{1,0:T(8,128)(2,1)S(1)} %shard_map.306.refs_2_, ...), custom_call_target="tpu_custom_call" | custom-call | flops 100000000 | bytes 1024 | tf_op jit(solution)/shard_map/pallas_call | solution.py:312
  (122 shorter events, 23.5 us)
Async XLA Ops:
  0.7 3.1 %collective-permute-start = (bf16[192,512]{1,0:T(8,128)(2,1)}, bf16[192,512]{1,0:T(8,128)(2,1)S(1)}, u32[]{:S(2)}, u32[]{:S(2)}) collective-permute-start(bf16[192,512]{1,0:T(8,128)(2,1)} %refs_7_), channel_id=1, source_target_pairs={{0,1},{1,0},{2,3},{3,2},{4,5},{5,4},{6,7},{7,6},{8,9},{9,8},{10,11... | collective-permute-start | bytes 589832 | tf_op jit(solution)/shard_map/ppermute | solution.py:128
  1.2 8.9 %collective-permute-start.3 = (bf16[192,512]{1,0:T(8,128)(2,1)}, bf16[192,512]{1,0:T(8,128)(2,1)S(1)}, u32[]{:S(2)}, u32[]{:S(2)}) collective-permute-start(bf16[192,512]{1,0:T(8,128)(2,1)} %refs_7_), channel_id=1, source_target_pairs={{0,2},{1,3},{2,0},{3,1},{4,6},{5,7},{6,4},{7,5},{8,10},{9,11},{10,... | collective-permute-start | bytes 589832 | tf_op jit(solution)/shard_map/ppermute | solution.py:128
  6.2 3.7 %collective-permute-start.2 = (f32[16,256]{1,0:T(8,128)S(1)}, f32[16,256]{1,0:T(8,128)S(1)}, u32[]{:S(2)}, u32[]{:S(2)}) collective-permute-start(f32[16,256]{1,0:T(8,128)S(1)} %shard_map.256.n01), channel_id=1, source_target_pairs={{0,2},{1,3},{2,0},{3,1},{4,6},{5,7},{6,4},{7,5},{8,10},{9,11},{10,... | collective-permute-start | bytes 49160 | tf_op jit(solution)/shard_map/ppermute | solution.py:128
  10.2 13.9 %collective-permute-start.6 = (bf16[192,768]{1,0:T(8,128)(2,1)}, bf16[192,768]{1,0:T(8,128)(2,1)S(1)}, u32[]{:S(2)}, u32[]{:S(2)}) collective-permute-start(bf16[192,768]{1,0:T(8,128)(2,1)} %w_out.1), channel_id=1, source_target_pairs={{0,2},{1,3},{2,0},{3,1},{4,6},{5,7},{6,4},{7,5},{8,10},{9,11},{10,... | collective-permute-start | bytes 884744 | tf_op jit(solution)/shard_map/ppermute | solution.py:128
  11.9 12.1 %collective-permute-start.5 = (bf16[192,512]{1,0:T(8,128)(2,1)}, bf16[192,512]{1,0:T(8,128)(2,1)S(1)}, u32[]{:S(2)}, u32[]{:S(2)}) collective-permute-start(bf16[192,512]{1,0:T(8,128)(2,1)} %cot_ref.1), channel_id=1, source_target_pairs={{0,2},{1,3},{2,0},{3,1},{4,6},{5,7},{6,4},{7,5},{8,10},{9,11},{10,... | collective-permute-start | bytes 589832 | tf_op jit(solution)/shard_map/ppermute | solution.py:128
  18.9 5.2 %collective-permute-start.7 = (bf16[192,256]{1,0:T(8,128)(2,1)S(1)}, bf16[192,256]{1,0:T(8,128)(2,1)S(1)}, u32[]{:S(2)}, u32[]{:S(2)}) collective-permute-start(bf16[192,256]{1,0:T(8,128)(2,1)S(1)} %get-tuple-element.170), channel_id=1, source_target_pairs={{0,1},{1,0},{2,3},{3,2},{4,5},{5,4},{6,7},{7,6},{8,9},{9,8},{10,11... | collective-permute-start | bytes 294920 | tf_op jit(solution)/shard_map/ppermute | solution.py:128
  19.0 15.8 %collective-permute-start.10 = (bf16[192,768]{1,0:T(8,128)(2,1)S(1)}, bf16[192,768]{1,0:T(8,128)(2,1)S(1)}, u32[]{:S(2)}, u32[]{:S(2)}) collective-permute-start(bf16[192,768]{1,0:T(8,128)(2,1)S(1)} %copy-done.2), channel_id=1, source_target_pairs={{0,1},{1,0},{2,3},{3,2},{4,5},{5,4},{6,7},{7,6},{8,9},{9,8},{10,11... | collective-permute-start | bytes 884744 | tf_op jit(solution)/shard_map/ppermute | solution.py:128
  24.1 10.7 %collective-permute-start.11 = (bf16[192,768]{1,0:T(8,128)(2,1)S(1)}, bf16[192,768]{1,0:T(8,128)(2,1)S(1)}, u32[]{:S(2)}, u32[]{:S(2)}) collective-permute-start(bf16[192,768]{1,0:T(8,128)(2,1)S(1)} %collective-permute-done.6.refs_2_), channel_id=1, source_target_pairs={{0,1},{1,0},{2,3},{3,2},{4,5},{5,4},{6,7},{7,6},{8,9},{9,8},{10,11... | collective-permute-start | bytes 884744 | tf_op jit(solution)/shard_map/ppermute | solution.py:128
  24.2 9.4 %collective-permute-start.8 = (bf16[192,512]{1,0:T(8,128)(2,1)S(1)}, bf16[192,512]{1,0:T(8,128)(2,1)S(1)}, u32[]{:S(2)}, u32[]{:S(2)}) collective-permute-start(bf16[192,512]{1,0:T(8,128)(2,1)S(1)} %copy-done.1), channel_id=1, source_target_pairs={{0,1},{1,0},{2,3},{3,2},{4,5},{5,4},{6,7},{7,6},{8,9},{9,8},{10,11... | collective-permute-start | bytes 589832 | tf_op jit(solution)/shard_map/ppermute | solution.py:128
  24.6 8.9 %collective-permute-start.9 = (bf16[192,512]{1,0:T(8,128)(2,1)S(1)}, bf16[192,512]{1,0:T(8,128)(2,1)S(1)}, u32[]{:S(2)}, u32[]{:S(2)}) collective-permute-start(bf16[192,512]{1,0:T(8,128)(2,1)S(1)} %collective-permute-done.5.c2), channel_id=1, source_target_pairs={{0,1},{1,0},{2,3},{3,2},{4,5},{5,4},{6,7},{7,6},{8,9},{9,8},{10,11... | collective-permute-start | bytes 589832 | tf_op jit(solution)/shard_map/ppermute | solution.py:128
  26.0 8.8 %collective-permute-start.12 = (bf16[384,256]{1,0:T(8,128)(2,1)S(1)}, bf16[384,256]{1,0:T(8,128)(2,1)S(1)}, u32[]{:S(2)}, u32[]{:S(2)}) collective-permute-start(bf16[384,256]{1,0:T(8,128)(2,1)S(1)} %shard_map.260.pair), channel_id=1, source_target_pairs={{0,2},{1,3},{2,0},{3,1},{4,6},{5,7},{6,4},{7,5},{8,10},{9,11},{10,... | collective-permute-start | bytes 589832 | tf_op jit(solution)/shard_map/ppermute | solution.py:128
  41.3 2.7 %collective-permute-start.14 = (bf16[768,256]{1,0:T(8,128)(2,1)S(1)}, bf16[768,256]{1,0:T(8,128)(2,1)S(1)}, u32[]{:S(2)}, u32[]{:S(2)}) collective-permute-start(bf16[768,256]{1,0:T(8,128)(2,1)S(1)} %get-tuple-element.191), channel_id=1, source_target_pairs={{0,1},{1,0},{2,3},{3,2},{4,5},{5,4},{6,7},{7,6},{8,9},{9,8},{10,11... | collective-permute-start | bytes 1179656 | tf_op jit(solution)/shard_map/ppermute | solution.py:128
  42.4 16.9 %collective-permute-start.17 = (bf16[384,768]{1,0:T(8,128)(2,1)S(1)}, bf16[384,768]{1,0:T(8,128)(2,1)S(1)}, u32[]{:S(2)}, u32[]{:S(2)}) collective-permute-start(bf16[384,768]{1,0:T(8,128)(2,1)S(1)} %get-tuple-element.209), channel_id=1, source_target_pairs={{0,4},{4,0},{8,12},{12,8},{16,20},{20,16},{24,28},{28,24},{1,5},{5... | collective-permute-start | bytes 1769480 | tf_op jit(solution)/shard_map/ppermute | solution.py:128
  45.2 11.2 %collective-permute-start.15 = (bf16[768,256]{1,0:T(8,128)(2,1)S(1)}, bf16[768,256]{1,0:T(8,128)(2,1)S(1)}, u32[]{:S(2)}, u32[]{:S(2)}) collective-permute-start(bf16[768,256]{1,0:T(8,128)(2,1)S(1)} %get-tuple-element.201), channel_id=1, source_target_pairs={{0,2},{1,3},{2,0},{3,1},{4,6},{5,7},{6,4},{7,5},{8,10},{9,11},{10,... | collective-permute-start | bytes 1179656 | tf_op jit(solution)/shard_map/ppermute | solution.py:128
  45.7 15.4 %collective-permute-start.18 = (bf16[384,768]{1,0:T(8,128)(2,1)S(1)}, bf16[384,768]{1,0:T(8,128)(2,1)S(1)}, u32[]{:S(2)}, u32[]{:S(2)}) collective-permute-start(bf16[384,768]{1,0:T(8,128)(2,1)S(1)} %get-tuple-element.212), channel_id=1, source_target_pairs={{0,8},{4,12},{8,0},{12,4},{16,24},{20,28},{24,16},{28,20},{1,9},{5... | collective-permute-start | bytes 1769480 | tf_op jit(solution)/shard_map/ppermute | solution.py:128
  48.5 10.1 %collective-permute-start.16 = (bf16[192,512]{1,0:T(8,128)(2,1)S(1)}, bf16[192,512]{1,0:T(8,128)(2,1)S(1)}, u32[]{:S(2)}, u32[]{:S(2)}) collective-permute-start(bf16[192,512]{1,0:T(8,128)(2,1)S(1)} %get-tuple-element.207), channel_id=1, source_target_pairs={{0,1},{1,0},{2,3},{3,2},{4,5},{5,4},{6,7},{7,6},{8,9},{9,8},{10,11... | collective-permute-start | bytes 589832 | tf_op jit(solution)/shard_map/ppermute | solution.py:128
  48.6 28.2 %collective-permute-start.22 = (bf16[192,512]{1,0:T(8,128)(2,1)S(1)}, bf16[192,512]{1,0:T(8,128)(2,1)S(1)}, u32[]{:S(2)}, u32[]{:S(2)}) collective-permute-start(bf16[192,512]{1,0:T(8,128)(2,1)S(1)} %get-tuple-element.199), channel_id=1, source_target_pairs={{0,1},{1,0},{2,3},{3,2},{4,5},{5,4},{6,7},{7,6},{8,9},{9,8},{10,11... | collective-permute-start | bytes 589832 | tf_op jit(solution)/shard_map/ppermute | solution.py:128
  58.7 18.5 %collective-permute-start.23 = (bf16[192,512]{1,0:T(8,128)(2,1)S(1)}, bf16[192,512]{1,0:T(8,128)(2,1)S(1)}, u32[]{:S(2)}, u32[]{:S(2)}) collective-permute-start(bf16[192,512]{1,0:T(8,128)(2,1)S(1)} %shard_map.271), channel_id=1, source_target_pairs={{0,2},{1,3},{2,0},{3,1},{4,6},{5,7},{6,4},{7,5},{8,10},{9,11},{10,... | collective-permute-start | bytes 589832 | tf_op jit(solution)/shard_map/ppermute | solution.py:128
  59.3 2.8 %collective-permute-start.19 = (bf16[768,256]{1,0:T(8,128)(2,1)S(1)}, bf16[768,256]{1,0:T(8,128)(2,1)S(1)}, u32[]{:S(2)}, u32[]{:S(2)}) collective-permute-start(bf16[768,256]{1,0:T(8,128)(2,1)S(1)} %get-tuple-element.214.own), channel_id=1, source_target_pairs={{0,1},{1,0},{2,3},{3,2},{4,5},{5,4},{6,7},{7,6},{8,9},{9,8},{10,11... | collective-permute-start | bytes 1179656 | tf_op jit(solution)/shard_map/ppermute | solution.py:128
  59.5 9.5 %collective-permute-start.20 = (bf16[192,768]{1,0:T(8,128)(2,1)S(1)}, bf16[192,768]{1,0:T(8,128)(2,1)S(1)}, u32[]{:S(2)}, u32[]{:S(2)}) collective-permute-start(bf16[192,768]{1,0:T(8,128)(2,1)S(1)} %get-tuple-element.223), channel_id=1, source_target_pairs={{0,8},{4,12},{8,0},{12,4},{16,24},{20,28},{24,16},{28,20},{1,9},{5... | collective-permute-start | bytes 884744 | tf_op jit(solution)/shard_map/ppermute | solution.py:128
  61.3 9.9 %collective-permute-start.21 = (bf16[192,768]{1,0:T(8,128)(2,1)S(1)}, bf16[192,768]{1,0:T(8,128)(2,1)S(1)}, u32[]{:S(2)}, u32[]{:S(2)}) collective-permute-start(bf16[192,768]{1,0:T(8,128)(2,1)S(1)} %get-tuple-element.226), channel_id=1, source_target_pairs={{0,4},{4,0},{8,12},{12,8},{16,20},{20,16},{24,28},{28,24},{1,5},{5... | collective-permute-start | bytes 884744 | tf_op jit(solution)/shard_map/ppermute | solution.py:128
  66.6 11.4 %collective-permute-start.24 = (bf16[192,768]{1,0:T(8,128)(2,1)S(1)}, bf16[192,768]{1,0:T(8,128)(2,1)S(1)}, u32[]{:S(2)}, u32[]{:S(2)}) collective-permute-start(bf16[192,768]{1,0:T(8,128)(2,1)S(1)} %get-tuple-element.239), channel_id=1, source_target_pairs={{0,4},{4,0},{8,12},{12,8},{16,20},{20,16},{24,28},{28,24},{1,5},{5... | collective-permute-start | bytes 884744 | tf_op jit(solution)/shard_map/ppermute | solution.py:128
  69.0 12.9 %collective-permute-start.25 = (bf16[192,768]{1,0:T(8,128)(2,1)S(1)}, bf16[192,768]{1,0:T(8,128)(2,1)S(1)}, u32[]{:S(2)}, u32[]{:S(2)}) collective-permute-start(bf16[192,768]{1,0:T(8,128)(2,1)S(1)} %get-tuple-element.243), channel_id=1, source_target_pairs={{0,8},{4,12},{8,0},{12,4},{16,24},{20,28},{24,16},{28,20},{1,9},{5... | collective-permute-start | bytes 884744 | tf_op jit(solution)/shard_map/ppermute | solution.py:128
  71.3 11.4 %collective-permute-start.26 = (bf16[96,768]{1,0:T(8,128)(2,1)S(1)}, bf16[96,768]{1,0:T(8,128)(2,1)S(1)}, u32[]{:S(2)}, u32[]{:S(2)}) collective-permute-start(bf16[96,768]{1,0:T(8,128)(2,1)S(1)} %get-tuple-element.246), channel_id=1, source_target_pairs={{0,16},{4,20},{8,24},{12,28},{16,0},{20,4},{24,8},{28,12},{1,17},{... | collective-permute-start | bytes 442376 | tf_op jit(solution)/shard_map/ppermute | solution.py:128
  76.8 15.6 %collective-permute-start.27 = (bf16[96,768]{1,0:T(8,128)(2,1)S(1)}, bf16[96,768]{1,0:T(8,128)(2,1)S(1)}, u32[]{:S(2)}, u32[]{:S(2)}) collective-permute-start(bf16[96,768]{1,0:T(8,128)(2,1)S(1)} %get-tuple-element.248), channel_id=1, source_target_pairs={{0,16},{4,20},{8,24},{12,28},{16,0},{20,4},{24,8},{28,12},{1,17},{... | collective-permute-start | bytes 442376 | tf_op jit(solution)/shard_map/ppermute | solution.py:128
  78.0 19.5 %collective-permute-start.31 = (bf16[192,512]{1,0:T(8,128)(2,1)S(1)}, bf16[192,512]{1,0:T(8,128)(2,1)S(1)}, u32[]{:S(2)}, u32[]{:S(2)}) collective-permute-start(bf16[192,512]{1,0:T(8,128)(2,1)S(1)} %get-tuple-element.257), channel_id=1, source_target_pairs={{0,1},{1,0},{2,3},{3,2},{4,5},{5,4},{6,7},{7,6},{8,9},{9,8},{10,11... | collective-permute-start | bytes 589832 | tf_op jit(solution)/shard_map/ppermute | solution.py:128
  81.9 17.7 %collective-permute-start.32 = (bf16[96,768]{1,0:T(8,128)(2,1)S(1)}, bf16[96,768]{1,0:T(8,128)(2,1)S(1)}, u32[]{:S(2)}, u32[]{:S(2)}) collective-permute-start(bf16[96,768]{1,0:T(8,128)(2,1)S(1)} %get-tuple-element.259), channel_id=1, source_target_pairs={{0,4},{4,0},{8,12},{12,8},{16,20},{20,16},{24,28},{28,24},{1,5},{5... | collective-permute-start | bytes 442376 | tf_op jit(solution)/shard_map/ppermute | solution.py:128
  82.7 9.8 %collective-permute-start.28 = (bf16[96,768]{1,0:T(8,128)(2,1)S(1)}, bf16[96,768]{1,0:T(8,128)(2,1)S(1)}, u32[]{:S(2)}, u32[]{:S(2)}) collective-permute-start(bf16[96,768]{1,0:T(8,128)(2,1)S(1)} %get-tuple-element.250), channel_id=1, source_target_pairs={{0,8},{4,12},{8,0},{12,4},{16,24},{20,28},{24,16},{28,20},{1,9},{5... | collective-permute-start | bytes 442376 | tf_op jit(solution)/shard_map/ppermute | solution.py:128
  82.7 19.3 %collective-permute-start.34 = (bf16[96,768]{1,0:T(8,128)(2,1)S(1)}, bf16[96,768]{1,0:T(8,128)(2,1)S(1)}, u32[]{:S(2)}, u32[]{:S(2)}) collective-permute-start(bf16[96,768]{1,0:T(8,128)(2,1)S(1)} %shard_map.282.refs_0_), channel_id=1, source_target_pairs={{0,16},{4,20},{8,24},{12,28},{16,0},{20,4},{24,8},{28,12},{1,17},{... | collective-permute-start | bytes 442376 | tf_op jit(solution)/shard_map/ppermute | solution.py:128
  92.5 14.7 %collective-permute-start.36 = (bf16[96,768]{1,0:T(8,128)(2,1)S(1)}, bf16[96,768]{1,0:T(8,128)(2,1)S(1)}, u32[]{:S(2)}, u32[]{:S(2)}) collective-permute-start(bf16[96,768]{1,0:T(8,128)(2,1)S(1)} %shard_map.283.refs_0_), channel_id=1, source_target_pairs={{0,16},{4,20},{8,24},{12,28},{16,0},{20,4},{24,8},{28,12},{1,17},{... | collective-permute-start | bytes 442376 | tf_op jit(solution)/shard_map/ppermute | solution.py:128
  93.6 3.8 %collective-permute-start.30 = (f32[8,768]{1,0:T(8,128)S(1)}, f32[8,768]{1,0:T(8,128)S(1)}, u32[]{:S(2)}, u32[]{:S(2)}) collective-permute-start(f32[8,768]{1,0:T(8,128)S(1)} %shard_map.285.refs_0_), channel_id=1, source_target_pairs={{0,2},{1,3},{2,0},{3,1},{4,6},{5,7},{6,4},{7,5},{8,10},{9,11},{10,... | collective-permute-start | bytes 73736 | tf_op jit(solution)/shard_map/ppermute | solution.py:128
  97.5 3.8 %collective-permute-start.33 = (f32[8,768]{1,0:T(8,128)S(1)}, f32[8,768]{1,0:T(8,128)S(1)}, u32[]{:S(2)}, u32[]{:S(2)}) collective-permute-start(f32[8,768]{1,0:T(8,128)S(1)} %shard_map.286.refs_0_.row_sums), channel_id=1, source_target_pairs={{0,4},{4,0},{8,12},{12,8},{16,20},{20,16},{24,28},{28,24},{1,5},{5... | collective-permute-start | bytes 73736 | tf_op jit(solution)/shard_map/ppermute | solution.py:128
  97.5 9.8 %collective-permute-start.37 = (bf16[48,768]{1,0:T(8,128)(2,1)S(1)}, bf16[48,768]{1,0:T(8,128)(2,1)S(1)}, u32[]{:S(2)}, u32[]{:S(2)}) collective-permute-start(bf16[48,768]{1,0:T(8,128)(2,1)S(1)} %get-tuple-element.266), channel_id=1, source_target_pairs={{0,16},{4,20},{8,24},{12,28},{16,0},{20,4},{24,8},{28,12},{1,17},{... | collective-permute-start | bytes 221192 | tf_op jit(solution)/shard_map/ppermute | solution.py:128
  101.3 3.8 %collective-permute-start.35 = (f32[8,768]{1,0:T(8,128)S(1)}, f32[8,768]{1,0:T(8,128)S(1)}, u32[]{:S(2)}, u32[]{:S(2)}) collective-permute-start(f32[8,768]{1,0:T(8,128)S(1)} %shard_map.289.refs_0_), channel_id=1, source_target_pairs={{0,8},{4,12},{8,0},{12,4},{16,24},{20,28},{24,16},{28,20},{1,9},{5... | collective-permute-start | bytes 73736 | tf_op jit(solution)/shard_map/ppermute | solution.py:128
  102.0 7.0 %collective-permute-start.38 = (bf16[192,512]{1,0:T(8,128)(2,1)S(1)}, bf16[192,512]{1,0:T(8,128)(2,1)S(1)}, u32[]{:S(2)}, u32[]{:S(2)}) collective-permute-start(bf16[192,512]{1,0:T(8,128)(2,1)S(1)} %get-tuple-element.231), channel_id=1, source_target_pairs={{0,1},{1,0},{2,3},{3,2},{4,5},{5,4},{6,7},{7,6},{8,9},{9,8},{10,11... | collective-permute-start | bytes 589832 | tf_op jit(solution)/shard_map/ppermute | solution.py:128
  102.0 8.1 %collective-permute-start.39 = (bf16[192,512]{1,0:T(8,128)(2,1)S(1)}, bf16[192,512]{1,0:T(8,128)(2,1)S(1)}, u32[]{:S(2)}, u32[]{:S(2)}) collective-permute-start(bf16[192,512]{1,0:T(8,128)(2,1)S(1)} %shard_map.287), channel_id=1, source_target_pairs={{0,2},{1,3},{2,0},{3,1},{4,6},{5,7},{6,4},{7,5},{8,10},{9,11},{10,... | collective-permute-start | bytes 589832 | tf_op jit(solution)/shard_map/ppermute | solution.py:128
  105.1 6.4 %collective-permute-start.40 = (bf16[48,768]{1,0:T(8,128)(2,1)S(1)}, bf16[48,768]{1,0:T(8,128)(2,1)S(1)}, u32[]{:S(2)}, u32[]{:S(2)}) collective-permute-start(bf16[48,768]{1,0:T(8,128)(2,1)S(1)} %get-tuple-element.269), channel_id=1, source_target_pairs={{0,16},{4,20},{8,24},{12,28},{16,0},{20,4},{24,8},{28,12},{1,17},{... | collective-permute-start | bytes 221192 | tf_op jit(solution)/shard_map/ppermute | solution.py:128
  107.2 11.8 %collective-permute-start.41 = (bf16[192,768]{1,0:T(8,128)(2,1)S(1)}, bf16[192,768]{1,0:T(8,128)(2,1)S(1)}, u32[]{:S(2)}, u32[]{:S(2)}) collective-permute-start(bf16[192,768]{1,0:T(8,128)(2,1)S(1)} %shard_map.292.refs_0_), channel_id=1, source_target_pairs={{0,8},{4,12},{8,0},{12,4},{16,24},{20,28},{24,16},{28,20},{1,9},{5... | collective-permute-start | bytes 884744 | tf_op jit(solution)/shard_map/ppermute | solution.py:128
  107.3 12.3 %collective-permute-start.42 = (bf16[48,768]{1,0:T(8,128)(2,1)S(1)}, bf16[48,768]{1,0:T(8,128)(2,1)S(1)}, u32[]{:S(2)}, u32[]{:S(2)}) collective-permute-start(bf16[48,768]{1,0:T(8,128)(2,1)S(1)} %shard_map.293.refs_0_), channel_id=1, source_target_pairs={{0,16},{4,20},{8,24},{12,28},{16,0},{20,4},{24,8},{28,12},{1,17},{... | collective-permute-start | bytes 221192 | tf_op jit(solution)/shard_map/ppermute | solution.py:128
  109.0 10.7 %collective-permute-start.43 = (bf16[192,768]{1,0:T(8,128)(2,1)S(1)}, bf16[192,768]{1,0:T(8,128)(2,1)S(1)}, u32[]{:S(2)}, u32[]{:S(2)}) collective-permute-start(bf16[192,768]{1,0:T(8,128)(2,1)S(1)} %shard_map.290.refs_0_), channel_id=1, source_target_pairs={{0,4},{4,0},{8,12},{12,8},{16,20},{20,16},{24,28},{28,24},{1,5},{5... | collective-permute-start | bytes 884744 | tf_op jit(solution)/shard_map/ppermute | solution.py:128
  110.1 13.3 %collective-permute-start.45 = (f32[8,768]{1,0:T(8,128)S(1)}, f32[8,768]{1,0:T(8,128)S(1)}, u32[]{:S(2)}, u32[]{:S(2)}) collective-permute-start(f32[8,768]{1,0:T(8,128)S(1)} %shard_map.291.refs_0_), channel_id=1, source_target_pairs={{0,16},{4,20},{8,24},{12,28},{16,0},{20,4},{24,8},{28,12},{1,17},{... | collective-permute-start | bytes 73736 | tf_op jit(solution)/shard_map/ppermute | solution.py:128
  111.6 8.2 %collective-permute-start.44 = (bf16[48,768]{1,0:T(8,128)(2,1)S(1)}, bf16[48,768]{1,0:T(8,128)(2,1)S(1)}, u32[]{:S(2)}, u32[]{:S(2)}) collective-permute-start(bf16[48,768]{1,0:T(8,128)(2,1)S(1)} %shard_map.295.refs_0_), channel_id=1, source_target_pairs={{0,16},{4,20},{8,24},{12,28},{16,0},{20,4},{24,8},{28,12},{1,17},{... | collective-permute-start | bytes 221192 | tf_op jit(solution)/shard_map/ppermute | solution.py:128
  119.0 16.3 %collective-permute-start.47 = (bf16[384,768]{1,0:T(8,128)(2,1)S(1)}, bf16[384,768]{1,0:T(8,128)(2,1)S(1)}, u32[]{:S(2)}, u32[]{:S(2)}) collective-permute-start(bf16[384,768]{1,0:T(8,128)(2,1)S(1)} %shard_map.296.refs_0_), channel_id=1, source_target_pairs={{0,4},{4,0},{8,12},{12,8},{16,20},{20,16},{24,28},{28,24},{1,5},{5... | collective-permute-start | bytes 1769480 | tf_op jit(solution)/shard_map/ppermute | solution.py:128
  119.6 6.8 %collective-permute-start.46 = (bf16[96,768]{1,0:T(8,128)(2,1)S(1)}, bf16[96,768]{1,0:T(8,128)(2,1)S(1)}, u32[]{:S(2)}, u32[]{:S(2)}) collective-permute-start(bf16[96,768]{1,0:T(8,128)(2,1)S(1)} %shard_map.297.refs_0_), channel_id=1, source_target_pairs={{0,8},{4,12},{8,0},{12,4},{16,24},{20,28},{24,16},{28,20},{1,9},{5... | collective-permute-start | bytes 442376 | tf_op jit(solution)/shard_map/ppermute | solution.py:128
  119.7 18.3 %collective-permute-start.48 = (bf16[96,768]{1,0:T(8,128)(2,1)S(1)}, bf16[96,768]{1,0:T(8,128)(2,1)S(1)}, u32[]{:S(2)}, u32[]{:S(2)}) collective-permute-start(bf16[96,768]{1,0:T(8,128)(2,1)S(1)} %shard_map.299.refs_0_), channel_id=1, source_target_pairs={{0,4},{4,0},{8,12},{12,8},{16,20},{20,16},{24,28},{28,24},{1,5},{5... | collective-permute-start | bytes 442376 | tf_op jit(solution)/shard_map/ppermute | solution.py:128
  121.3 16.8 %collective-permute-start.49 = (bf16[384,768]{1,0:T(8,128)(2,1)S(1)}, bf16[384,768]{1,0:T(8,128)(2,1)S(1)}, u32[]{:S(2)}, u32[]{:S(2)}) collective-permute-start(bf16[384,768]{1,0:T(8,128)(2,1)S(1)} %shard_map.298.refs_0_), channel_id=1, source_target_pairs={{0,8},{4,12},{8,0},{12,4},{16,24},{20,28},{24,16},{28,20},{1,9},{5... | collective-permute-start | bytes 1769480 | tf_op jit(solution)/shard_map/ppermute | solution.py:128
  126.5 14.7 %collective-permute-start.50 = (bf16[192,768]{1,0:T(8,128)(2,1)S(1)}, bf16[192,768]{1,0:T(8,128)(2,1)S(1)}, u32[]{:S(2)}, u32[]{:S(2)}) collective-permute-start(bf16[192,768]{1,0:T(8,128)(2,1)S(1)} %shard_map.302.refs_0_), channel_id=1, source_target_pairs={{0,4},{4,0},{8,12},{12,8},{16,20},{20,16},{24,28},{28,24},{1,5},{5... | collective-permute-start | bytes 884744 | tf_op jit(solution)/shard_map/ppermute | solution.py:128
  138.1 6.8 %collective-permute-start.51 = (bf16[192,768]{1,0:T(8,128)(2,1)S(1)}, bf16[192,768]{1,0:T(8,128)(2,1)S(1)}, u32[]{:S(2)}, u32[]{:S(2)}) collective-permute-start(bf16[192,768]{1,0:T(8,128)(2,1)S(1)} %shard_map.306.refs_2_), channel_id=1, source_target_pairs={{0,8},{4,12},{8,0},{12,4},{16,24},{20,28},{24,16},{28,20},{1,9},{5... | collective-permute-start | bytes 884744 | tf_op jit(solution)/shard_map/ppermute | solution.py:128
  (10 other events, 63.4 us)

commit v8 on v7

--- a/solution.py
+++ b/solution.py
@@ -61,7 +61,7 @@
     ("place_tail", 1),
 )
 
-FRONT = (1, 1, 1, 1, 1, 1, 10, 10, 10, 10, 10)
+FRONT = (1, 1, 1, 1, 1, 1, 10, 10, 10, 10)
 
 
 def shape(*dims, kind=F32):
@@ -857,8 +857,7 @@
     norms_far = to_width(norms_near, 2)
     norms = kernel(norms_kernel, shape(model, 8), [at], [norms_near, norms_far])
     x_both = to_width(after(x_far, norms), 1)
-    cot_now, w_now = after((cotangent, w_out), norms_near)
-    cot_far, cot_near = to_width(cot_now, 2), to_width(cot_now, 1)
+    w_now = after(w_out, norms_near)
     w_far, w_near = to_width(w_now, 2), to_width(w_now, 1)
 
     x_all, normed_one, stats_one, qkv = kernel(
@@ -886,25 +885,11 @@
         [qkv, x_all],
         [pltpu.VMEM((tokens, half), F32)],
     )
-    pair = join([after(heads_own, cot_far, w_far), to_width(heads_send, 1)])
+    pair = join([after(heads_own, w_far), to_width(heads_send, 1)])
     pair_far = to_width(pair, 2)
-    cot_both = to_width(after(cot_far, pair), 1)
+    cot_now = after(cotangent, pair)
+    cot_far, cot_near = to_width(cot_now, 2), to_width(cot_now, 1)
     w_both = to_width(after(w_far, pair), 1)
-
-    running, d_mix = history_call(
-        functools.partial(history_kernel, 32),
-        (shape(part, tokens), shape(layers, STEP // 2, 128)),
-        (False, True),
-        (False, False),
-        [mix_weights, counts],
-        [cotangent, pltpu.with_memory_space_constraint(history, pltpu.HBM)],
-    )
-    g_out, d_active, cot_all = kernel(
-        output_gradient_kernel,
-        (shape(model, tokens, kind=BF16), shape(hidden_units, tokens), shape(model, tokens, kind=BF16)),
-        [at, self_weight, counts],
-        [cotangent, cot_near, cot_far, cot_both, w_down],
-    )
 
     w_all = kernel(rows_kernel, shape(model, model, kind=BF16), [at], [w_out, w_near, w_far, w_both])
     middle, stats_two, normed_own = kernel(
@@ -914,6 +899,15 @@
         [pair, pair_far, w_all, x_half, norms],
         [pltpu.VMEM((model, half), BF16)],
     )
+    normed_near = to_width(normed_own, 1)
+    cot_both = to_width(after(cot_far, middle), 1)
+    g_out, d_active, cot_all = kernel(
+        output_gradient_kernel,
+        (shape(model, tokens, kind=BF16), shape(hidden_units, tokens), shape(model, tokens, kind=BF16)),
+        [at, self_weight, counts],
+        [cotangent, cot_near, cot_far, cot_both, w_down],
+    )
+
     normed_two, active, d_hidden, send, keep = kernel(
         feed_forward_kernel,
         (
@@ -924,7 +918,7 @@
             shape(model, half),
         ),
         [],
-        [normed_own, to_width(normed_own, 1), w_up, d_active],
+        [normed_own, normed_near, w_up, d_active],
         [pltpu.VMEM((hidden_units, tokens), F32)],
     )
 
@@ -983,6 +977,16 @@
             [pltpu.VMEM((model, tokens), F32)],
         )
         v.out_got = to_width(near, 1), to_width(far, 1)
+
+    def history_sums():
+        v.running, v.d_mix = history_call(
+            functools.partial(history_kernel, 32),
+            (shape(part, tokens), shape(layers, STEP // 2, 128)),
+            (False, True),
+            (False, False),
+            [mix_weights, counts],
+            [cotangent, pltpu.with_memory_space_constraint(history, pltpu.HBM)],
+        )
 
     def output_sum():
         v.out_last = to_width(add([v.out_far, v.out_got[1]], (0, part, BF16))[0], 2)
@@ -1043,8 +1047,8 @@
                 v.out,
                 v.out_got[0],
                 v.out_last,
-                running,
-                d_mix,
+                v.running,
+                v.d_mix,
                 v.product,
                 v.sums,
             ],
@@ -1119,6 +1123,7 @@
         (middle_sum, 8),
         (up_product, 10),
         (output_product, 100),
+        (history_sums, 10),
         (middle_gradient, 10),
         (output_sum, 10),
         (down_1, 10),

time: 147 us -> 141 us (0.959)
  waiting for transfers between devices: 50.8 us -> 42.1 us
  starting transfers between devices: 48 us -> 50.2 us
    ppermute x52, waiting for transfers between devices: 50.8 us -> 42.1 us  [xor_send(): return lax.ppermute(value, axis, [(i, i ^ offset) for i in range(size)])]
    ppermute x52, starting transfers between devices: 48 us -> 50.2 us  [xor_send(): return lax.ppermute(value, axis, [(i, i ^ offset) for i in range(size)])]
  transfers between devices with their start and end apart: 52 -> 52, of which waited for: 20 -> 23; matrix products, arithmetic and copies ran while one was open for 0% -> 0% of each run, Pallas kernels for 26% -> 29%
where the time goes in v8:
time: 141 us; the launch traced here: 140 us
  starting transfers between devices  50.2 us (36%)
  Pallas kernels  45.1 us (32%)
  waiting for transfers between devices  42.1 us (30%)
  between operations  2.57 us (2%)
    ppermute x52, starting transfers between devices, xor_send(): return lax.ppermute(value, axis, [(i, i ^ offset) for i in range(size)])  50.2 us
    ppermute x52, waiting for transfers between devices, xor_send(): return lax.ppermute(value, axis, [(i, i ^ offset) for i in range(size)])  42.1 us
    pallas_call x48, Pallas kernels, kernel(): pl.pallas_call(body, out_shape=outs, in_specs=[pl.BlockSpec(memory_space=...  29.4 us
    pallas_call x2, Pallas kernels, history_call(): pl.pallas_call(body, out_shape=outs, in_specs=[pl.BlockSpec(memory_space=...  9.77 us
    pallas_call x3, Pallas kernels, place(): pl.pallas_call(functools.partial(place_kernel, all_tokens, streams, bound...  4.87 us
  transfers between devices with their start and end apart: 52, of which 23 were waited for; matrix products, arithmetic and copies ran while one was open for 0% of the time, Pallas kernels for 29%

profile of v8, /device:TPU:0, one launch (start us, length us, event | category | flops | bytes accessed | tf_op | source)
XLA Modules:
  0.0 140.0 jit_solution(12370906140764816083)
XLA Ops:
  1.2 2.6 %collective-permute-start.3 = (bf16[192,512]{1,0:T(8,128)(2,1)}, bf16[192,512]{1,0:T(8,128)(2,1)S(1)}, u32[]{:S(2)}, u32[]{:S(2)}) collective-permute-start(bf16[192,512]{1,0:T(8,128)(2,1)} %refs_7_), channel_id=1, source_target_pairs={{0,2},{1,3},{2,0},{3,1},{4,6},{5,7},{6,4},{7,5},{8,10},{9,11},{10,... | collective-permute-start | bytes 589832 | tf_op jit(solution)/shard_map/ppermute | solution.py:128
  3.8 1.1 shard_map.255
  6.2 1.6 %collective-permute-start.2 = (f32[16,256]{1,0:T(8,128)S(1)}, f32[16,256]{1,0:T(8,128)S(1)}, u32[]{:S(2)}, u32[]{:S(2)}) collective-permute-start(f32[16,256]{1,0:T(8,128)S(1)} %shard_map.256.n01), channel_id=1, source_target_pairs={{0,2},{1,3},{2,0},{3,1},{4,6},{5,7},{6,4},{7,5},{8,10},{9,11},{10,... | collective-permute-start | bytes 49160 | tf_op jit(solution)/shard_map/ppermute | solution.py:128
  7.7 2.2 %collective-permute-done.2.n23 = f32[16,256]{1,0:T(8,128)S(1)} collective-permute-done((f32[16,256]{1,0:T(8,128)S(1)}, f32[16,256]{1,0:T(8,128)S(1)}, u32[]{:S(2)}, u32[]{:S(2)}) %collective-permute-start.2) | collective-permute-done | bytes 16416 | tf_op jit(solution)/shard_map/ppermute | solution.py:128
  10.2 1.8 %collective-permute-start.5 = (bf16[192,768]{1,0:T(8,128)(2,1)}, bf16[192,768]{1,0:T(8,128)(2,1)S(1)}, u32[]{:S(2)}, u32[]{:S(2)}) collective-permute-start(bf16[192,768]{1,0:T(8,128)(2,1)} %w_out.1), channel_id=1, source_target_pairs={{0,2},{1,3},{2,0},{3,1},{4,6},{5,7},{6,4},{7,5},{8,10},{9,11},{10,... | collective-permute-start | bytes 884744 | tf_op jit(solution)/shard_map/ppermute | solution.py:128
  12.0 2.2 %shard_map.258 = (bf16[768,512]{1,0:T(8,128)(2,1)S(1)}, bf16[768,512]{1,0:T(8,128)(2,1)S(1)}, f32[2,512]{1,0:T(2,128)S(1)}, bf16[576,512]{1,0:T(8,128)(2,1)S(1)}) custom-call(s32[1]{0:T(128)} %bitcast.at_ref, bf16[192,512]{1,0:T(8,128)(2,1)S(1)} %get-tuple-element.158.x0.x_in, bf16[192,512]{1,0:T(8,128)(2,1)S(1)} %collective-permute-done.refs_0_.x1, ...), custom_call_target="tpu_custom_call" | custom-call | flops 100000000 | bytes 1024 | tf_op jit(solution)/shard_map/pallas_call | solution.py:93
  14.2 4.3 %shard_map.259 = (bf16[192,256]{1,0:T(8,128)(2,1)S(1)}, bf16[192,256]{1,0:T(8,128)(2,1)S(1)}, bf16[768,256]{1,0:T(8,128)(2,1)S(1)}, bf16[192,512]{1,0:T(8,128)(2,1)S(1)}, bf16[3,512,512]{2,1,0:T(8,128)(2,1)S(1)}) custom-call(s32[1]{0:T(128)} %bitcast.at_ref, bf16[576,512]{1,0:T(8,128)(2,1)S(1)} %get-tuple-element.164.qkv, ...), custom_call_target="tpu_custom_call" | custom-call | flops 100000000 | bytes 1024 | tf_op jit(solution)/shard_map/pallas_call | solution.py:93
  20.1 1.5 %collective-permute-start.9 = (bf16[384,256]{1,0:T(8,128)(2,1)S(1)}, bf16[384,256]{1,0:T(8,128)(2,1)S(1)}, u32[]{:S(2)}, u32[]{:S(2)}) collective-permute-start(bf16[384,256]{1,0:T(8,128)(2,1)S(1)} %shard_map.260.pair), channel_id=1, source_target_pairs={{0,2},{1,3},{2,0},{3,1},{4,6},{5,7},{6,4},{7,5},{8,10},{9,11},{10,... | collective-permute-start | bytes 589832 | tf_op jit(solution)/shard_map/ppermute | solution.py:128
  22.3 5.6 %collective-permute-done.9.pair_far = bf16[384,256]{1,0:T(8,128)(2,1)S(1)} collective-permute-done((bf16[384,256]{1,0:T(8,128)(2,1)S(1)}, bf16[384,256]{1,0:T(8,128)(2,1)S(1)}, u32[]{:S(2)}, u32[]{:S(2)}) %collective-permute-start.9) | collective-permute-done | bytes 196640 | tf_op jit(solution)/shard_map/ppermute | solution.py:128
  27.9 2.0 %shard_map.262 = (f32[768,256]{1,0:T(8,128)S(1)}, f32[2,256]{1,0:T(2,128)S(1)}, bf16[768,256]{1,0:T(8,128)(2,1)S(1)}) custom-call(s32[1]{0:T(128)} %bitcast.at_ref, bf16[384,256]{1,0:T(8,128)(2,1)S(1)} %shard_map.260.pair, bf16[384,256]{1,0:T(8,128)(2,1)S(1)} %collective-permute-done.9.pair_far, bf16[768,768]{1,0:T(8,128)(2,1)S(1)} %shard_map.261.w_all, ...), custom_call_target="tpu_custom_call" | custom-call | flops 1000000000 | bytes 1024 | tf_op jit(solution)/shard_map/pallas_call | solution.py:93
  30.4 1.1 collective-permute-done.11.c2
  33.0 1.2 shard_map.263
  34.2 2.6 %shard_map.264 = (bf16[768,512]{1,0:T(8,128)(2,1)S(1)}, bf16[768,512]{1,0:T(8,128)(2,1)S(1)}, bf16[768,512]{1,0:T(8,128)(2,1)S(1)}, bf16[768,256]{1,0:T(8,128)(2,1)S(1)}, f32[768,256]{1,0:T(8,128)S(1)}) custom-call(bf16[768,256]{1,0:T(8,128)(2,1)S(1)} %get-tuple-element.181.own, bf16[768,256]{1,0:T(8,128)(2,1)S(1)} %collective-permute-done.13.other, ...), custom_call_target="tpu_custom_call" | custom-call | flops 1000000000 | bytes 1024 | tf_op jit(solution)/shard_map/pallas_call | solution.py:93
  38.2 1.7 %collective-permute-start.17 = (bf16[384,768]{1,0:T(8,128)(2,1)S(1)}, bf16[384,768]{1,0:T(8,128)(2,1)S(1)}, u32[]{:S(2)}, u32[]{:S(2)}) collective-permute-start(bf16[384,768]{1,0:T(8,128)(2,1)S(1)} %get-tuple-element.209), channel_id=1, source_target_pairs={{0,4},{4,0},{8,12},{12,8},{16,20},{20,16},{24,28},{28,24},{1,5},{5... | collective-permute-start | bytes 1769480 | tf_op jit(solution)/shard_map/ppermute | solution.py:128
  41.1 1.6 %collective-permute-start.15 = (bf16[768,256]{1,0:T(8,128)(2,1)S(1)}, bf16[768,256]{1,0:T(8,128)(2,1)S(1)}, u32[]{:S(2)}, u32[]{:S(2)}) collective-permute-start(bf16[768,256]{1,0:T(8,128)(2,1)S(1)} %get-tuple-element.201), channel_id=1, source_target_pairs={{0,2},{1,3},{2,0},{3,1},{4,6},{5,7},{6,4},{7,5},{8,10},{9,11},{10,... | collective-permute-start | bytes 1179656 | tf_op jit(solution)/shard_map/ppermute | solution.py:128
  42.7 1.6 %collective-permute-start.18 = (bf16[384,768]{1,0:T(8,128)(2,1)S(1)}, bf16[384,768]{1,0:T(8,128)(2,1)S(1)}, u32[]{:S(2)}, u32[]{:S(2)}) collective-permute-start(bf16[384,768]{1,0:T(8,128)(2,1)S(1)} %get-tuple-element.212), channel_id=1, source_target_pairs={{0,8},{4,12},{8,0},{12,4},{16,24},{20,28},{24,16},{28,20},{1,9},{5... | collective-permute-start | bytes 1769480 | tf_op jit(solution)/shard_map/ppermute | solution.py:128
  44.2 1.2 shard_map.268
  46.0 5.7 %shard_map.269 = (f32[192,512]{1,0:T(8,128)S(1)}, f32[30,8,128]{2,1,0:T(8,128)S(1)}) custom-call(f32[30]{0:T(128)S(1)} %copy-done.3, s32[1]{0:T(128)S(6)} %copy.29.counts_ref, bf16[192,512]{1,0:T(8,128)(2,1)S(1)} %copy-done.1, bf16[30,192,512]{2,1,0:T(8,128)(2,1)} %history_ref.1), custom_call_target="tpu_custom_call" | custom-call | flops 1000000000 | bytes 1024 | tf_op jit(solution)/shard_map/pallas_call | solution.py:376
  52.0 2.3 %shard_map.270 = (f32[768,256]{1,0:T(8,128)S(1)}, bf16[768,256]{1,0:T(8,128)(2,1)S(1)}, f32[2,768]{1,0:T(2,128)S(1)}) custom-call(s32[1]{0:T(128)} %bitcast.at_ref, f32[1]{0:T(128)S(6)} %copy.30.self_ref, s32[1]{0:T(128)S(6)} %copy.29.counts_ref, f32[768,256]{1,0:T(8,128)S(1)} %get-tuple-element.200.chip, ...), custom_call_target="tpu_custom_call" | custom-call | flops 1000000000 | bytes 1024 | tf_op jit(solution)/shard_map/pallas_call | solution.py:93
  54.3 1.6 %collective-permute-start.23 = (bf16[192,512]{1,0:T(8,128)(2,1)S(1)}, bf16[192,512]{1,0:T(8,128)(2,1)S(1)}, u32[]{:S(2)}, u32[]{:S(2)}) collective-permute-start(bf16[192,512]{1,0:T(8,128)(2,1)S(1)} %shard_map.271), channel_id=1, source_target_pairs={{0,2},{1,3},{2,0},{3,1},{4,6},{5,7},{6,4},{7,5},{8,10},{9,11},{10,... | collective-permute-start | bytes 589832 | tf_op jit(solution)/shard_map/ppermute | solution.py:128
  56.1 1.6 %collective-permute-start.20 = (bf16[192,768]{1,0:T(8,128)(2,1)S(1)}, bf16[192,768]{1,0:T(8,128)(2,1)S(1)}, u32[]{:S(2)}, u32[]{:S(2)}) collective-permute-start(bf16[192,768]{1,0:T(8,128)(2,1)S(1)} %get-tuple-element.223), channel_id=1, source_target_pairs={{0,8},{4,12},{8,0},{12,4},{16,24},{20,28},{24,16},{28,20},{1,9},{5... | collective-permute-start | bytes 884744 | tf_op jit(solution)/shard_map/ppermute | solution.py:128
  58.9 3.6 %shard_map.274 = (bf16[576,512]{1,0:T(8,128)(2,1)S(1)}, bf16[768,512]{1,0:T(8,128)(2,1)S(1)}) custom-call(s32[1]{0:T(128)} %bitcast.at_ref, bf16[768,256]{1,0:T(8,128)(2,1)S(1)} %get-tuple-element.214.own, bf16[768,256]{1,0:T(8,128)(2,1)S(1)} %collective-permute-done.19.other, bf16[192,768]{1,0:T(8,128)(2,1)S(1)} %copy-done.2, ...), custom_call_target="tpu_custom_call" | custom-call | flops 800000000 | bytes 1024 | tf_op jit(solution)/shard_map/pallas_call | solution.py:93
  63.5 1.1 collective-permute-start.24
  65.6 1.6 %collective-permute-start.25 = (bf16[192,768]{1,0:T(8,128)(2,1)S(1)}, bf16[192,768]{1,0:T(8,128)(2,1)S(1)}, u32[]{:S(2)}, u32[]{:S(2)}) collective-permute-start(bf16[192,768]{1,0:T(8,128)(2,1)S(1)} %get-tuple-element.243), channel_id=1, source_target_pairs={{0,8},{4,12},{8,0},{12,4},{16,24},{20,28},{24,16},{28,20},{1,9},{5... | collective-permute-start | bytes 884744 | tf_op jit(solution)/shard_map/ppermute | solution.py:128
  67.9 2.7 %collective-permute-start.26 = (bf16[96,768]{1,0:T(8,128)(2,1)S(1)}, bf16[96,768]{1,0:T(8,128)(2,1)S(1)}, u32[]{:S(2)}, u32[]{:S(2)}) collective-permute-start(bf16[96,768]{1,0:T(8,128)(2,1)S(1)} %get-tuple-element.246), channel_id=1, source_target_pairs={{0,16},{4,20},{8,24},{12,28},{16,0},{20,4},{24,8},{28,12},{1,17},{... | collective-permute-start | bytes 442376 | tf_op jit(solution)/shard_map/ppermute | solution.py:128
  70.6 2.8 %shard_map.278 = (bf16[192,512]{1,0:T(8,128)(2,1)S(1)}, bf16[192,512]{1,0:T(8,128)(2,1)S(1)}, f32[192,512]{1,0:T(8,128)S(1)}, f32[192,512]{1,0:T(8,128)S(1)}, f32[8,768]{1,0:T(8,128)S(1)}) custom-call(s32[1]{0:T(128)} %bitcast.at_ref, s32[1]{0:T(128)S(6)} %copy.29.counts_ref, bf16[576,512]{1,0:T(8,128)(2,1)S(1)} %get-tuple-element.228.refs_0_.d_project, ...), custom_call_target="tpu_custom_call" | custom-call | flops 100000000 | bytes 1024 | tf_op jit(solution)/shard_map/pallas_call | solution.py:93
  74.7 3.8 %collective-permute-done.25.refs_1_ = bf16[192,768]{1,0:T(8,128)(2,1)S(1)} collective-permute-done((bf16[192,768]{1,0:T(8,128)(2,1)S(1)}, bf16[192,768]{1,0:T(8,128)(2,1)S(1)}, u32[]{:S(2)}, u32[]{:S(2)}) %collective-permute-start.25) | collective-permute-done | bytes 294944 | tf_op jit(solution)/shard_map/ppermute | solution.py:128
  79.6 4.2 %collective-permute-start.34 = (bf16[96,768]{1,0:T(8,128)(2,1)S(1)}, bf16[96,768]{1,0:T(8,128)(2,1)S(1)}, u32[]{:S(2)}, u32[]{:S(2)}) collective-permute-start(bf16[96,768]{1,0:T(8,128)(2,1)S(1)} %shard_map.282.refs_0_), channel_id=1, source_target_pairs={{0,16},{4,20},{8,24},{12,28},{16,0},{20,4},{24,8},{28,12},{1,17},{... | collective-permute-start | bytes 442376 | tf_op jit(solution)/shard_map/ppermute | solution.py:128
  83.8 5.3 %collective-permute-done.27.refs_1_ = bf16[96,768]{1,0:T(8,128)(2,1)S(1)} collective-permute-done((bf16[96,768]{1,0:T(8,128)(2,1)S(1)}, bf16[96,768]{1,0:T(8,128)(2,1)S(1)}, u32[]{:S(2)}, u32[]{:S(2)}) %collective-permute-start.27) | collective-permute-done | bytes 147488 | tf_op jit(solution)/shard_map/ppermute | solution.py:128
  90.8 3.3 %collective-permute-done.30.refs_1_ = f32[8,768]{1,0:T(8,128)S(1)} collective-permute-done((f32[8,768]{1,0:T(8,128)S(1)}, f32[8,768]{1,0:T(8,128)S(1)}, u32[]{:S(2)}, u32[]{:S(2)}) %collective-permute-start.30) | collective-permute-done | bytes 24608 | tf_op jit(solution)/shard_map/ppermute | solution.py:128
  95.0 2.0 %collective-permute-start.37 = (bf16[48,768]{1,0:T(8,128)(2,1)S(1)}, bf16[48,768]{1,0:T(8,128)(2,1)S(1)}, u32[]{:S(2)}, u32[]{:S(2)}) collective-permute-start(bf16[48,768]{1,0:T(8,128)(2,1)S(1)} %get-tuple-element.266), channel_id=1, source_target_pairs={{0,16},{4,20},{8,24},{12,28},{16,0},{20,4},{24,8},{28,12},{1,17},{... | collective-permute-start | bytes 221192 | tf_op jit(solution)/shard_map/ppermute | solution.py:128
  99.1 2.6 %collective-permute-done.35.refs_1_ = f32[8,768]{1,0:T(8,128)S(1)} collective-permute-done((f32[8,768]{1,0:T(8,128)S(1)}, f32[8,768]{1,0:T(8,128)S(1)}, u32[]{:S(2)}, u32[]{:S(2)}) %collective-permute-start.35) | collective-permute-done | bytes 24608 | tf_op jit(solution)/shard_map/ppermute | solution.py:128
  101.7 2.0 %collective-permute-start.40 = (bf16[48,768]{1,0:T(8,128)(2,1)S(1)}, bf16[48,768]{1,0:T(8,128)(2,1)S(1)}, u32[]{:S(2)}, u32[]{:S(2)}) collective-permute-start(bf16[48,768]{1,0:T(8,128)(2,1)S(1)} %get-tuple-element.269), channel_id=1, source_target_pairs={{0,16},{4,20},{8,24},{12,28},{16,0},{20,4},{24,8},{28,12},{1,17},{... | collective-permute-start | bytes 221192 | tf_op jit(solution)/shard_map/ppermute | solution.py:128
  103.9 1.6 %collective-permute-start.42 = (bf16[48,768]{1,0:T(8,128)(2,1)S(1)}, bf16[48,768]{1,0:T(8,128)(2,1)S(1)}, u32[]{:S(2)}, u32[]{:S(2)}) collective-permute-start(bf16[48,768]{1,0:T(8,128)(2,1)S(1)} %shard_map.293.refs_0_), channel_id=1, source_target_pairs={{0,16},{4,20},{8,24},{12,28},{16,0},{20,4},{24,8},{28,12},{1,17},{... | collective-permute-start | bytes 221192 | tf_op jit(solution)/shard_map/ppermute | solution.py:128
  106.5 1.4 collective-permute-start.45
  108.4 1.6 %collective-permute-start.44 = (bf16[48,768]{1,0:T(8,128)(2,1)S(1)}, bf16[48,768]{1,0:T(8,128)(2,1)S(1)}, u32[]{:S(2)}, u32[]{:S(2)}) collective-permute-start(bf16[48,768]{1,0:T(8,128)(2,1)S(1)} %shard_map.295.refs_0_), channel_id=1, source_target_pairs={{0,16},{4,20},{8,24},{12,28},{16,0},{20,4},{24,8},{28,12},{1,17},{... | collective-permute-start | bytes 221192 | tf_op jit(solution)/shard_map/ppermute | solution.py:128
  110.0 4.6 %collective-permute-done.41.refs_1_ = bf16[192,768]{1,0:T(8,128)(2,1)S(1)} collective-permute-done((bf16[192,768]{1,0:T(8,128)(2,1)S(1)}, bf16[192,768]{1,0:T(8,128)(2,1)S(1)}, u32[]{:S(2)}, u32[]{:S(2)}) %collective-permute-start.41) | collective-permute-done | bytes 294944 | tf_op jit(solution)/shard_map/ppermute | solution.py:128
  114.6 1.0 collective-permute-start.47
  117.0 1.9 %collective-permute-start.49 = (bf16[384,768]{1,0:T(8,128)(2,1)S(1)}, bf16[384,768]{1,0:T(8,128)(2,1)S(1)}, u32[]{:S(2)}, u32[]{:S(2)}) collective-permute-start(bf16[384,768]{1,0:T(8,128)(2,1)S(1)} %shard_map.298.refs_0_), channel_id=1, source_target_pairs={{0,8},{4,12},{8,0},{12,4},{16,24},{20,28},{24,16},{28,20},{1,9},{5... | collective-permute-start | bytes 1769480 | tf_op jit(solution)/shard_map/ppermute | solution.py:128
  119.8 2.7 %collective-permute-done.46.refs_1_ = bf16[96,768]{1,0:T(8,128)(2,1)S(1)} collective-permute-done((bf16[96,768]{1,0:T(8,128)(2,1)S(1)}, bf16[96,768]{1,0:T(8,128)(2,1)S(1)}, u32[]{:S(2)}, u32[]{:S(2)}) %collective-permute-start.46) | collective-permute-done | bytes 147488 | tf_op jit(solution)/shard_map/ppermute | solution.py:128
  122.5 1.1 collective-permute-start.50
  124.4 4.1 %shard_map.304 = bf16[30,192,512]{2,1,0:T(8,128)(2,1)} custom-call(f32[30]{0:T(128)S(1)} %copy-done.3, s32[1]{0:T(128)S(6)} %copy.29.counts_ref, bf16[192,512]{1,0:T(8,128)(2,1)S(1)} %copy-done.1, f32[8,768]{1,0:T(8,128)S(1)} %shard_map.300.sums), custom_call_target="tpu_custom_call" | custom-call | flops 100000000 | bytes 1024 | tf_op jit(solution)/shard_map/pallas_call | solution.py:376
  128.5 1.2 collective-permute-done.47.refs_1_
  129.7 1.6 %shard_map.305 = f32[768,768]{1,0:T(8,128)} custom-call(s32[1]{0:T(128)} %bitcast.1.me_ref, f32[8,768]{1,0:T(8,128)S(1)} %shard_map.300.sums, bf16[384,768]{1,0:T(8,128)(2,1)S(1)} %shard_map.296.refs_0_, bf16[384,768]{1,0:T(8,128)(2,1)S(1)} %collective-permute-done.47.refs_1_), custom_call_target="tpu_custom_call" | custom-call | flops 100000000 | bytes 1024 | tf_op jit(solution)/shard_map/pallas_call | solution.py:312
  131.3 1.4 collective-permute-start.51
  133.4 1.6 %shard_map.307 = f32[768,768]{1,0:T(8,128)} custom-call(s32[1]{0:T(128)} %bitcast.1.me_ref, f32[8,768]{1,0:T(8,128)S(1)} %shard_map.300.sums, bf16[384,768]{1,0:T(8,128)(2,1)S(1)} %shard_map.298.refs_0_, bf16[384,768]{1,0:T(8,128)(2,1)S(1)} %collective-permute-done.49.refs_1_), custom_call_target="tpu_custom_call" | custom-call | flops 400000000 | bytes 1024 | tf_op jit(solution)/shard_map/pallas_call | solution.py:312
  135.0 3.1 %collective-permute-done.51.refs_3_ = bf16[192,768]{1,0:T(8,128)(2,1)S(1)} collective-permute-done((bf16[192,768]{1,0:T(8,128)(2,1)S(1)}, bf16[192,768]{1,0:T(8,128)(2,1)S(1)}, u32[]{:S(2)}, u32[]{:S(2)}) %collective-permute-start.51) | collective-permute-done | bytes 294944 | tf_op jit(solution)/shard_map/ppermute | solution.py:128
  138.1 1.8 %shard_map.308 = (f32[576,768]{1,0:T(8,128)}, f32[192,768]{1,0:T(8,128)}) custom-call(s32[1]{0:T(128)} %bitcast.1.me_ref, f32[8,768]{1,0:T(8,128)S(1)} %shard_map.300.sums, bf16[192,768]{1,0:T(8,128)(2,1)S(1)} %shard_map.302.refs_0_, bf16[192,768]{1,0:T(8,128)(2,1)S(1)} %collective-permute-done.50.refs_1_, bf16[192,768]{1,0:T(8,128)(2,1)S(1)} %shard_map.306.refs_2_, ...), custom_call_target="tpu_custom_call" | custom-call | flops 100000000 | bytes 1024 | tf_op jit(solution)/shard_map/pallas_call | solution.py:312
  (122 shorter events, 24.9 us)
Async XLA Ops:
  0.7 3.1 %collective-permute-start = (bf16[192,512]{1,0:T(8,128)(2,1)}, bf16[192,512]{1,0:T(8,128)(2,1)S(1)}, u32[]{:S(2)}, u32[]{:S(2)}) collective-permute-start(bf16[192,512]{1,0:T(8,128)(2,1)} %refs_7_), channel_id=1, source_target_pairs={{0,1},{1,0},{2,3},{3,2},{4,5},{5,4},{6,7},{7,6},{8,9},{9,8},{10,11... | collective-permute-start | bytes 589832 | tf_op jit(solution)/shard_map/ppermute | solution.py:128
  1.2 8.9 %collective-permute-start.3 = (bf16[192,512]{1,0:T(8,128)(2,1)}, bf16[192,512]{1,0:T(8,128)(2,1)S(1)}, u32[]{:S(2)}, u32[]{:S(2)}) collective-permute-start(bf16[192,512]{1,0:T(8,128)(2,1)} %refs_7_), channel_id=1, source_target_pairs={{0,2},{1,3},{2,0},{3,1},{4,6},{5,7},{6,4},{7,5},{8,10},{9,11},{10,... | collective-permute-start | bytes 589832 | tf_op jit(solution)/shard_map/ppermute | solution.py:128
  6.2 3.7 %collective-permute-start.2 = (f32[16,256]{1,0:T(8,128)S(1)}, f32[16,256]{1,0:T(8,128)S(1)}, u32[]{:S(2)}, u32[]{:S(2)}) collective-permute-start(f32[16,256]{1,0:T(8,128)S(1)} %shard_map.256.n01), channel_id=1, source_target_pairs={{0,2},{1,3},{2,0},{3,1},{4,6},{5,7},{6,4},{7,5},{8,10},{9,11},{10,... | collective-permute-start | bytes 49160 | tf_op jit(solution)/shard_map/ppermute | solution.py:128
  10.1 1.8 %collective-permute-start.4 = (bf16[192,512]{1,0:T(8,128)(2,1)S(1)}, bf16[192,512]{1,0:T(8,128)(2,1)S(1)}, u32[]{:S(2)}, u32[]{:S(2)}) collective-permute-start(bf16[192,512]{1,0:T(8,128)(2,1)S(1)} %collective-permute-done.3.x2), channel_id=1, source_target_pairs={{0,1},{1,0},{2,3},{3,2},{4,5},{5,4},{6,7},{7,6},{8,9},{9,8},{10,11... | collective-permute-start | bytes 589832 | tf_op jit(solution)/shard_map/ppermute | solution.py:128
  10.2 9.6 %collective-permute-start.5 = (bf16[192,768]{1,0:T(8,128)(2,1)}, bf16[192,768]{1,0:T(8,128)(2,1)S(1)}, u32[]{:S(2)}, u32[]{:S(2)}) collective-permute-start(bf16[192,768]{1,0:T(8,128)(2,1)} %w_out.1), channel_id=1, source_target_pairs={{0,2},{1,3},{2,0},{3,1},{4,6},{5,7},{6,4},{7,5},{8,10},{9,11},{10,... | collective-permute-start | bytes 884744 | tf_op jit(solution)/shard_map/ppermute | solution.py:128
  18.8 3.4 %collective-permute-start.7 = (bf16[192,768]{1,0:T(8,128)(2,1)S(1)}, bf16[192,768]{1,0:T(8,128)(2,1)S(1)}, u32[]{:S(2)}, u32[]{:S(2)}) collective-permute-start(bf16[192,768]{1,0:T(8,128)(2,1)S(1)} %copy-done.2), channel_id=1, source_target_pairs={{0,1},{1,0},{2,3},{3,2},{4,5},{5,4},{6,7},{7,6},{8,9},{9,8},{10,11... | collective-permute-start | bytes 884744 | tf_op jit(solution)/shard_map/ppermute | solution.py:128
  19.9 2.3 %collective-permute-start.8 = (bf16[192,768]{1,0:T(8,128)(2,1)S(1)}, bf16[192,768]{1,0:T(8,128)(2,1)S(1)}, u32[]{:S(2)}, u32[]{:S(2)}) collective-permute-start(bf16[192,768]{1,0:T(8,128)(2,1)S(1)} %collective-permute-done.5.refs_2_), channel_id=1, source_target_pairs={{0,1},{1,0},{2,3},{3,2},{4,5},{5,4},{6,7},{7,6},{8,9},{9,8},{10,11... | collective-permute-start | bytes 884744 | tf_op jit(solution)/shard_map/ppermute | solution.py:128
  20.1 7.7 %collective-permute-start.9 = (bf16[384,256]{1,0:T(8,128)(2,1)S(1)}, bf16[384,256]{1,0:T(8,128)(2,1)S(1)}, u32[]{:S(2)}, u32[]{:S(2)}) collective-permute-start(bf16[384,256]{1,0:T(8,128)(2,1)S(1)} %shard_map.260.pair), channel_id=1, source_target_pairs={{0,2},{1,3},{2,0},{3,1},{4,6},{5,7},{6,4},{7,5},{8,10},{9,11},{10,... | collective-permute-start | bytes 589832 | tf_op jit(solution)/shard_map/ppermute | solution.py:128
  21.7 9.8 %collective-permute-start.11 = (bf16[192,512]{1,0:T(8,128)(2,1)S(1)}, bf16[192,512]{1,0:T(8,128)(2,1)S(1)}, u32[]{:S(2)}, u32[]{:S(2)}) collective-permute-start(bf16[192,512]{1,0:T(8,128)(2,1)S(1)} %copy-done.1), channel_id=1, source_target_pairs={{0,2},{1,3},{2,0},{3,1},{4,6},{5,7},{6,4},{7,5},{8,10},{9,11},{10,... | collective-permute-start | bytes 589832 | tf_op jit(solution)/shard_map/ppermute | solution.py:128
  29.9 4.3 %collective-permute-start.13 = (bf16[768,256]{1,0:T(8,128)(2,1)S(1)}, bf16[768,256]{1,0:T(8,128)(2,1)S(1)}, u32[]{:S(2)}, u32[]{:S(2)}) collective-permute-start(bf16[768,256]{1,0:T(8,128)(2,1)S(1)} %get-tuple-element.181.own), channel_id=1, source_target_pairs={{0,1},{1,0},{2,3},{3,2},{4,5},{5,4},{6,7},{7,6},{8,9},{9,8},{10,11... | collective-permute-start | bytes 1179656 | tf_op jit(solution)/shard_map/ppermute | solution.py:128
  29.9 2.9 %collective-permute-start.10 = (bf16[192,512]{1,0:T(8,128)(2,1)S(1)}, bf16[192,512]{1,0:T(8,128)(2,1)S(1)}, u32[]{:S(2)}, u32[]{:S(2)}) collective-permute-start(bf16[192,512]{1,0:T(8,128)(2,1)S(1)} %copy-done.1), channel_id=1, source_target_pairs={{0,1},{1,0},{2,3},{3,2},{4,5},{5,4},{6,7},{7,6},{8,9},{9,8},{10,11... | collective-permute-start | bytes 589832 | tf_op jit(solution)/shard_map/ppermute | solution.py:128
  36.8 3.1 %collective-permute-start.14 = (bf16[768,256]{1,0:T(8,128)(2,1)S(1)}, bf16[768,256]{1,0:T(8,128)(2,1)S(1)}, u32[]{:S(2)}, u32[]{:S(2)}) collective-permute-start(bf16[768,256]{1,0:T(8,128)(2,1)S(1)} %get-tuple-element.189), channel_id=1, source_target_pairs={{0,1},{1,0},{2,3},{3,2},{4,5},{5,4},{6,7},{7,6},{8,9},{9,8},{10,11... | collective-permute-start | bytes 1179656 | tf_op jit(solution)/shard_map/ppermute | solution.py:128
  38.2 17.7 %collective-permute-start.17 = (bf16[384,768]{1,0:T(8,128)(2,1)S(1)}, bf16[384,768]{1,0:T(8,128)(2,1)S(1)}, u32[]{:S(2)}, u32[]{:S(2)}) collective-permute-start(bf16[384,768]{1,0:T(8,128)(2,1)S(1)} %get-tuple-element.209), channel_id=1, source_target_pairs={{0,4},{4,0},{8,12},{12,8},{16,20},{20,16},{24,28},{28,24},{1,5},{5... | collective-permute-start | bytes 1769480 | tf_op jit(solution)/shard_map/ppermute | solution.py:128
  41.1 10.9 %collective-permute-start.15 = (bf16[768,256]{1,0:T(8,128)(2,1)S(1)}, bf16[768,256]{1,0:T(8,128)(2,1)S(1)}, u32[]{:S(2)}, u32[]{:S(2)}) collective-permute-start(bf16[768,256]{1,0:T(8,128)(2,1)S(1)} %get-tuple-element.201), channel_id=1, source_target_pairs={{0,2},{1,3},{2,0},{3,1},{4,6},{5,7},{6,4},{7,5},{8,10},{9,11},{10,... | collective-permute-start | bytes 1179656 | tf_op jit(solution)/shard_map/ppermute | solution.py:128
  42.7 15.1 %collective-permute-start.18 = (bf16[384,768]{1,0:T(8,128)(2,1)S(1)}, bf16[384,768]{1,0:T(8,128)(2,1)S(1)}, u32[]{:S(2)}, u32[]{:S(2)}) collective-permute-start(bf16[384,768]{1,0:T(8,128)(2,1)S(1)} %get-tuple-element.212), channel_id=1, source_target_pairs={{0,8},{4,12},{8,0},{12,4},{16,24},{20,28},{24,16},{28,20},{1,9},{5... | collective-permute-start | bytes 1769480 | tf_op jit(solution)/shard_map/ppermute | solution.py:128
  45.4 8.8 %collective-permute-start.16 = (bf16[192,512]{1,0:T(8,128)(2,1)S(1)}, bf16[192,512]{1,0:T(8,128)(2,1)S(1)}, u32[]{:S(2)}, u32[]{:S(2)}) collective-permute-start(bf16[192,512]{1,0:T(8,128)(2,1)S(1)} %get-tuple-element.207), channel_id=1, source_target_pairs={{0,1},{1,0},{2,3},{3,2},{4,5},{5,4},{6,7},{7,6},{8,9},{9,8},{10,11... | collective-permute-start | bytes 589832 | tf_op jit(solution)/shard_map/ppermute | solution.py:128
  45.5 27.9 %collective-permute-start.22 = (bf16[192,512]{1,0:T(8,128)(2,1)S(1)}, bf16[192,512]{1,0:T(8,128)(2,1)S(1)}, u32[]{:S(2)}, u32[]{:S(2)}) collective-permute-start(bf16[192,512]{1,0:T(8,128)(2,1)S(1)} %get-tuple-element.197), channel_id=1, source_target_pairs={{0,1},{1,0},{2,3},{3,2},{4,5},{5,4},{6,7},{7,6},{8,9},{9,8},{10,11... | collective-permute-start | bytes 589832 | tf_op jit(solution)/shard_map/ppermute | solution.py:128
  54.3 19.5 %collective-permute-start.23 = (bf16[192,512]{1,0:T(8,128)(2,1)S(1)}, bf16[192,512]{1,0:T(8,128)(2,1)S(1)}, u32[]{:S(2)}, u32[]{:S(2)}) collective-permute-start(bf16[192,512]{1,0:T(8,128)(2,1)S(1)} %shard_map.271), channel_id=1, source_target_pairs={{0,2},{1,3},{2,0},{3,1},{4,6},{5,7},{6,4},{7,5},{8,10},{9,11},{10,... | collective-permute-start | bytes 589832 | tf_op jit(solution)/shard_map/ppermute | solution.py:128
  55.9 3.0 %collective-permute-start.19 = (bf16[768,256]{1,0:T(8,128)(2,1)S(1)}, bf16[768,256]{1,0:T(8,128)(2,1)S(1)}, u32[]{:S(2)}, u32[]{:S(2)}) collective-permute-start(bf16[768,256]{1,0:T(8,128)(2,1)S(1)} %get-tuple-element.214.own), channel_id=1, source_target_pairs={{0,1},{1,0},{2,3},{3,2},{4,5},{5,4},{6,7},{7,6},{8,9},{9,8},{10,11... | collective-permute-start | bytes 1179656 | tf_op jit(solution)/shard_map/ppermute | solution.py:128
  56.1 9.5 %collective-permute-start.20 = (bf16[192,768]{1,0:T(8,128)(2,1)S(1)}, bf16[192,768]{1,0:T(8,128)(2,1)S(1)}, u32[]{:S(2)}, u32[]{:S(2)}) collective-permute-start(bf16[192,768]{1,0:T(8,128)(2,1)S(1)} %get-tuple-element.223), channel_id=1, source_target_pairs={{0,8},{4,12},{8,0},{12,4},{16,24},{20,28},{24,16},{28,20},{1,9},{5... | collective-permute-start | bytes 884744 | tf_op jit(solution)/shard_map/ppermute | solution.py:128
  57.9 9.9 %collective-permute-start.21 = (bf16[192,768]{1,0:T(8,128)(2,1)S(1)}, bf16[192,768]{1,0:T(8,128)(2,1)S(1)}, u32[]{:S(2)}, u32[]{:S(2)}) collective-permute-start(bf16[192,768]{1,0:T(8,128)(2,1)S(1)} %get-tuple-element.226), channel_id=1, source_target_pairs={{0,4},{4,0},{8,12},{12,8},{16,20},{20,16},{24,28},{28,24},{1,5},{5... | collective-permute-start | bytes 884744 | tf_op jit(solution)/shard_map/ppermute | solution.py:128
  63.5 11.1 %collective-permute-start.24 = (bf16[192,768]{1,0:T(8,128)(2,1)S(1)}, bf16[192,768]{1,0:T(8,128)(2,1)S(1)}, u32[]{:S(2)}, u32[]{:S(2)}) collective-permute-start(bf16[192,768]{1,0:T(8,128)(2,1)S(1)} %get-tuple-element.239), channel_id=1, source_target_pairs={{0,4},{4,0},{8,12},{12,8},{16,20},{20,16},{24,28},{28,24},{1,5},{5... | collective-permute-start | bytes 884744 | tf_op jit(solution)/shard_map/ppermute | solution.py:128
  65.6 12.9 %collective-permute-start.25 = (bf16[192,768]{1,0:T(8,128)(2,1)S(1)}, bf16[192,768]{1,0:T(8,128)(2,1)S(1)}, u32[]{:S(2)}, u32[]{:S(2)}) collective-permute-start(bf16[192,768]{1,0:T(8,128)(2,1)S(1)} %get-tuple-element.243), channel_id=1, source_target_pairs={{0,8},{4,12},{8,0},{12,4},{16,24},{20,28},{24,16},{28,20},{1,9},{5... | collective-permute-start | bytes 884744 | tf_op jit(solution)/shard_map/ppermute | solution.py:128
  67.9 11.6 %collective-permute-start.26 = (bf16[96,768]{1,0:T(8,128)(2,1)S(1)}, bf16[96,768]{1,0:T(8,128)(2,1)S(1)}, u32[]{:S(2)}, u32[]{:S(2)}) collective-permute-start(bf16[96,768]{1,0:T(8,128)(2,1)S(1)} %get-tuple-element.246), channel_id=1, source_target_pairs={{0,16},{4,20},{8,24},{12,28},{16,0},{20,4},{24,8},{28,12},{1,17},{... | collective-permute-start | bytes 442376 | tf_op jit(solution)/shard_map/ppermute | solution.py:128
  73.4 15.7 %collective-permute-start.27 = (bf16[96,768]{1,0:T(8,128)(2,1)S(1)}, bf16[96,768]{1,0:T(8,128)(2,1)S(1)}, u32[]{:S(2)}, u32[]{:S(2)}) collective-permute-start(bf16[96,768]{1,0:T(8,128)(2,1)S(1)} %get-tuple-element.248), channel_id=1, source_target_pairs={{0,16},{4,20},{8,24},{12,28},{16,0},{20,4},{24,8},{28,12},{1,17},{... | collective-permute-start | bytes 442376 | tf_op jit(solution)/shard_map/ppermute | solution.py:128
  74.6 20.5 %collective-permute-start.31 = (bf16[192,512]{1,0:T(8,128)(2,1)S(1)}, bf16[192,512]{1,0:T(8,128)(2,1)S(1)}, u32[]{:S(2)}, u32[]{:S(2)}) collective-permute-start(bf16[192,512]{1,0:T(8,128)(2,1)S(1)} %get-tuple-element.257), channel_id=1, source_target_pairs={{0,1},{1,0},{2,3},{3,2},{4,5},{5,4},{6,7},{7,6},{8,9},{9,8},{10,11... | collective-permute-start | bytes 589832 | tf_op jit(solution)/shard_map/ppermute | solution.py:128
  78.5 18.6 %collective-permute-start.32 = (bf16[96,768]{1,0:T(8,128)(2,1)S(1)}, bf16[96,768]{1,0:T(8,128)(2,1)S(1)}, u32[]{:S(2)}, u32[]{:S(2)}) collective-permute-start(bf16[96,768]{1,0:T(8,128)(2,1)S(1)} %get-tuple-element.259), channel_id=1, source_target_pairs={{0,4},{4,0},{8,12},{12,8},{16,20},{20,16},{24,28},{28,24},{1,5},{5... | collective-permute-start | bytes 442376 | tf_op jit(solution)/shard_map/ppermute | solution.py:128
  79.6 9.5 %collective-permute-start.28 = (bf16[96,768]{1,0:T(8,128)(2,1)S(1)}, bf16[96,768]{1,0:T(8,128)(2,1)S(1)}, u32[]{:S(2)}, u32[]{:S(2)}) collective-permute-start(bf16[96,768]{1,0:T(8,128)(2,1)S(1)} %get-tuple-element.250), channel_id=1, source_target_pairs={{0,8},{4,12},{8,0},{12,4},{16,24},{20,28},{24,16},{28,20},{1,9},{5... | collective-permute-start | bytes 442376 | tf_op jit(solution)/shard_map/ppermute | solution.py:128
  79.6 19.0 %collective-permute-start.34 = (bf16[96,768]{1,0:T(8,128)(2,1)S(1)}, bf16[96,768]{1,0:T(8,128)(2,1)S(1)}, u32[]{:S(2)}, u32[]{:S(2)}) collective-permute-start(bf16[96,768]{1,0:T(8,128)(2,1)S(1)} %shard_map.282.refs_0_), channel_id=1, source_target_pairs={{0,16},{4,20},{8,24},{12,28},{16,0},{20,4},{24,8},{28,12},{1,17},{... | collective-permute-start | bytes 442376 | tf_op jit(solution)/shard_map/ppermute | solution.py:128
  89.1 14.7 %collective-permute-start.36 = (bf16[96,768]{1,0:T(8,128)(2,1)S(1)}, bf16[96,768]{1,0:T(8,128)(2,1)S(1)}, u32[]{:S(2)}, u32[]{:S(2)}) collective-permute-start(bf16[96,768]{1,0:T(8,128)(2,1)S(1)} %shard_map.283.refs_0_), channel_id=1, source_target_pairs={{0,16},{4,20},{8,24},{12,28},{16,0},{20,4},{24,8},{28,12},{1,17},{... | collective-permute-start | bytes 442376 | tf_op jit(solution)/shard_map/ppermute | solution.py:128
  90.2 3.8 %collective-permute-start.30 = (f32[8,768]{1,0:T(8,128)S(1)}, f32[8,768]{1,0:T(8,128)S(1)}, u32[]{:S(2)}, u32[]{:S(2)}) collective-permute-start(f32[8,768]{1,0:T(8,128)S(1)} %shard_map.285.refs_0_), channel_id=1, source_target_pairs={{0,2},{1,3},{2,0},{3,1},{4,6},{5,7},{6,4},{7,5},{8,10},{9,11},{10,... | collective-permute-start | bytes 73736 | tf_op jit(solution)/shard_map/ppermute | solution.py:128
  94.1 3.8 %collective-permute-start.33 = (f32[8,768]{1,0:T(8,128)S(1)}, f32[8,768]{1,0:T(8,128)S(1)}, u32[]{:S(2)}, u32[]{:S(2)}) collective-permute-start(f32[8,768]{1,0:T(8,128)S(1)} %shard_map.286.refs_0_.row_sums), channel_id=1, source_target_pairs={{0,4},{4,0},{8,12},{12,8},{16,20},{20,16},{24,28},{28,24},{1,5},{5... | collective-permute-start | bytes 73736 | tf_op jit(solution)/shard_map/ppermute | solution.py:128
  95.0 8.8 %collective-permute-start.37 = (bf16[48,768]{1,0:T(8,128)(2,1)S(1)}, bf16[48,768]{1,0:T(8,128)(2,1)S(1)}, u32[]{:S(2)}, u32[]{:S(2)}) collective-permute-start(bf16[48,768]{1,0:T(8,128)(2,1)S(1)} %get-tuple-element.266), channel_id=1, source_target_pairs={{0,16},{4,20},{8,24},{12,28},{16,0},{20,4},{24,8},{28,12},{1,17},{... | collective-permute-start | bytes 221192 | tf_op jit(solution)/shard_map/ppermute | solution.py:128
  97.9 3.8 %collective-permute-start.35 = (f32[8,768]{1,0:T(8,128)S(1)}, f32[8,768]{1,0:T(8,128)S(1)}, u32[]{:S(2)}, u32[]{:S(2)}) collective-permute-start(f32[8,768]{1,0:T(8,128)S(1)} %shard_map.289.refs_0_), channel_id=1, source_target_pairs={{0,8},{4,12},{8,0},{12,4},{16,24},{20,28},{24,16},{28,20},{1,9},{5... | collective-permute-start | bytes 73736 | tf_op jit(solution)/shard_map/ppermute | solution.py:128
  98.6 7.0 %collective-permute-start.38 = (bf16[192,512]{1,0:T(8,128)(2,1)S(1)}, bf16[192,512]{1,0:T(8,128)(2,1)S(1)}, u32[]{:S(2)}, u32[]{:S(2)}) collective-permute-start(bf16[192,512]{1,0:T(8,128)(2,1)S(1)} %get-tuple-element.231), channel_id=1, source_target_pairs={{0,1},{1,0},{2,3},{3,2},{4,5},{5,4},{6,7},{7,6},{8,9},{9,8},{10,11... | collective-permute-start | bytes 589832 | tf_op jit(solution)/shard_map/ppermute | solution.py:128
  98.6 7.9 %collective-permute-start.39 = (bf16[192,512]{1,0:T(8,128)(2,1)S(1)}, bf16[192,512]{1,0:T(8,128)(2,1)S(1)}, u32[]{:S(2)}, u32[]{:S(2)}) collective-permute-start(bf16[192,512]{1,0:T(8,128)(2,1)S(1)} %shard_map.287), channel_id=1, source_target_pairs={{0,2},{1,3},{2,0},{3,1},{4,6},{5,7},{6,4},{7,5},{8,10},{9,11},{10,... | collective-permute-start | bytes 589832 | tf_op jit(solution)/shard_map/ppermute | solution.py:128
  101.7 6.6 %collective-permute-start.40 = (bf16[48,768]{1,0:T(8,128)(2,1)S(1)}, bf16[48,768]{1,0:T(8,128)(2,1)S(1)}, u32[]{:S(2)}, u32[]{:S(2)}) collective-permute-start(bf16[48,768]{1,0:T(8,128)(2,1)S(1)} %get-tuple-element.269), channel_id=1, source_target_pairs={{0,16},{4,20},{8,24},{12,28},{16,0},{20,4},{24,8},{28,12},{1,17},{... | collective-permute-start | bytes 221192 | tf_op jit(solution)/shard_map/ppermute | solution.py:128
  103.8 10.8 %collective-permute-start.41 = (bf16[192,768]{1,0:T(8,128)(2,1)S(1)}, bf16[192,768]{1,0:T(8,128)(2,1)S(1)}, u32[]{:S(2)}, u32[]{:S(2)}) collective-permute-start(bf16[192,768]{1,0:T(8,128)(2,1)S(1)} %shard_map.292.refs_0_), channel_id=1, source_target_pairs={{0,8},{4,12},{8,0},{12,4},{16,24},{20,28},{24,16},{28,20},{1,9},{5... | collective-permute-start | bytes 884744 | tf_op jit(solution)/shard_map/ppermute | solution.py:128
  103.9 11.7 %collective-permute-start.42 = (bf16[48,768]{1,0:T(8,128)(2,1)S(1)}, bf16[48,768]{1,0:T(8,128)(2,1)S(1)}, u32[]{:S(2)}, u32[]{:S(2)}) collective-permute-start(bf16[48,768]{1,0:T(8,128)(2,1)S(1)} %shard_map.293.refs_0_), channel_id=1, source_target_pairs={{0,16},{4,20},{8,24},{12,28},{16,0},{20,4},{24,8},{28,12},{1,17},{... | collective-permute-start | bytes 221192 | tf_op jit(solution)/shard_map/ppermute | solution.py:128
  105.5 10.3 %collective-permute-start.43 = (bf16[192,768]{1,0:T(8,128)(2,1)S(1)}, bf16[192,768]{1,0:T(8,128)(2,1)S(1)}, u32[]{:S(2)}, u32[]{:S(2)}) collective-permute-start(bf16[192,768]{1,0:T(8,128)(2,1)S(1)} %shard_map.290.refs_0_), channel_id=1, source_target_pairs={{0,4},{4,0},{8,12},{12,8},{16,20},{20,16},{24,28},{28,24},{1,5},{5... | collective-permute-start | bytes 884744 | tf_op jit(solution)/shard_map/ppermute | solution.py:128
  106.5 12.5 %collective-permute-start.45 = (f32[8,768]{1,0:T(8,128)S(1)}, f32[8,768]{1,0:T(8,128)S(1)}, u32[]{:S(2)}, u32[]{:S(2)}) collective-permute-start(f32[8,768]{1,0:T(8,128)S(1)} %shard_map.291.refs_0_), channel_id=1, source_target_pairs={{0,16},{4,20},{8,24},{12,28},{16,0},{20,4},{24,8},{28,12},{1,17},{... | collective-permute-start | bytes 73736 | tf_op jit(solution)/shard_map/ppermute | solution.py:128
  108.4 7.6 %collective-permute-start.44 = (bf16[48,768]{1,0:T(8,128)(2,1)S(1)}, bf16[48,768]{1,0:T(8,128)(2,1)S(1)}, u32[]{:S(2)}, u32[]{:S(2)}) collective-permute-start(bf16[48,768]{1,0:T(8,128)(2,1)S(1)} %shard_map.295.refs_0_), channel_id=1, source_target_pairs={{0,16},{4,20},{8,24},{12,28},{16,0},{20,4},{24,8},{28,12},{1,17},{... | collective-permute-start | bytes 221192 | tf_op jit(solution)/shard_map/ppermute | solution.py:128
  114.6 15.1 %collective-permute-start.47 = (bf16[384,768]{1,0:T(8,128)(2,1)S(1)}, bf16[384,768]{1,0:T(8,128)(2,1)S(1)}, u32[]{:S(2)}, u32[]{:S(2)}) collective-permute-start(bf16[384,768]{1,0:T(8,128)(2,1)S(1)} %shard_map.296.refs_0_), channel_id=1, source_target_pairs={{0,4},{4,0},{8,12},{12,8},{16,20},{20,16},{24,28},{28,24},{1,5},{5... | collective-permute-start | bytes 1769480 | tf_op jit(solution)/shard_map/ppermute | solution.py:128
  115.7 6.9 %collective-permute-start.46 = (bf16[96,768]{1,0:T(8,128)(2,1)S(1)}, bf16[96,768]{1,0:T(8,128)(2,1)S(1)}, u32[]{:S(2)}, u32[]{:S(2)}) collective-permute-start(bf16[96,768]{1,0:T(8,128)(2,1)S(1)} %shard_map.297.refs_0_), channel_id=1, source_target_pairs={{0,8},{4,12},{8,0},{12,4},{16,24},{20,28},{24,16},{28,20},{1,9},{5... | collective-permute-start | bytes 442376 | tf_op jit(solution)/shard_map/ppermute | solution.py:128
  116.0 15.3 %collective-permute-start.48 = (bf16[96,768]{1,0:T(8,128)(2,1)S(1)}, bf16[96,768]{1,0:T(8,128)(2,1)S(1)}, u32[]{:S(2)}, u32[]{:S(2)}) collective-permute-start(bf16[96,768]{1,0:T(8,128)(2,1)S(1)} %shard_map.299.refs_0_), channel_id=1, source_target_pairs={{0,4},{4,0},{8,12},{12,8},{16,20},{20,16},{24,28},{28,24},{1,5},{5... | collective-permute-start | bytes 442376 | tf_op jit(solution)/shard_map/ppermute | solution.py:128
  117.0 16.4 %collective-permute-start.49 = (bf16[384,768]{1,0:T(8,128)(2,1)S(1)}, bf16[384,768]{1,0:T(8,128)(2,1)S(1)}, u32[]{:S(2)}, u32[]{:S(2)}) collective-permute-start(bf16[384,768]{1,0:T(8,128)(2,1)S(1)} %shard_map.298.refs_0_), channel_id=1, source_target_pairs={{0,8},{4,12},{8,0},{12,4},{16,24},{20,28},{24,16},{28,20},{1,9},{5... | collective-permute-start | bytes 1769480 | tf_op jit(solution)/shard_map/ppermute | solution.py:128
  122.5 12.5 %collective-permute-start.50 = (bf16[192,768]{1,0:T(8,128)(2,1)S(1)}, bf16[192,768]{1,0:T(8,128)(2,1)S(1)}, u32[]{:S(2)}, u32[]{:S(2)}) collective-permute-start(bf16[192,768]{1,0:T(8,128)(2,1)S(1)} %shard_map.302.refs_0_), channel_id=1, source_target_pairs={{0,4},{4,0},{8,12},{12,8},{16,20},{20,16},{24,28},{28,24},{1,5},{5... | collective-permute-start | bytes 884744 | tf_op jit(solution)/shard_map/ppermute | solution.py:128
  131.3 6.8 %collective-permute-start.51 = (bf16[192,768]{1,0:T(8,128)(2,1)S(1)}, bf16[192,768]{1,0:T(8,128)(2,1)S(1)}, u32[]{:S(2)}, u32[]{:S(2)}) collective-permute-start(bf16[192,768]{1,0:T(8,128)(2,1)S(1)} %shard_map.306.refs_2_), channel_id=1, source_target_pairs={{0,8},{4,12},{8,0},{12,4},{16,24},{20,28},{24,16},{28,20},{1,9},{5... | collective-permute-start | bytes 884744 | tf_op jit(solution)/shard_map/ppermute | solution.py:128
  (10 other events, 41.3 us)

commit v9 on v8

--- a/solution.py
+++ b/solution.py
@@ -61,7 +61,7 @@
     ("place_tail", 1),
 )
 
-FRONT = (1, 1, 1, 1, 1, 1, 10, 10, 10, 10)
+FRONT = (0.3, 0.1, 0.3, 4, 2, 4, 0.1, 0.3, 100, 10)
 
 
 def shape(*dims, kind=F32):
@@ -1119,50 +1119,50 @@
     first_1, first_2, first_3, first_4, first_5 = steps_of(first)
     second_1, second_2, second_3, second_4, second_5 = steps_of(second)
     schedule = (
-        (down_product, 10),
-        (middle_sum, 8),
+        (down_product, 2),
+        (middle_sum, 200),
         (up_product, 10),
-        (output_product, 100),
         (history_sums, 10),
-        (middle_gradient, 10),
-        (output_sum, 10),
+        (output_product, 0.3),
+        (middle_gradient, 8),
+        (output_sum, 1),
         (down_1, 10),
-        (up_1, 100),
-        (attention_gradient, 8),
+        (up_1, 200),
+        (attention_gradient, 200),
         (tail_product, 4),
-        (down_2, 100),
-        (up_2, 0.3),
+        (down_2, 4),
+        (up_2, 0.1),
         (input_gradient, 1),
-        (mix, 8),
+        (mix, 4),
         (first_1, 1),
         (second_1, 1),
         (up_3, 100),
-        (down_3, 1),
-        (first_2, 2),
-        (sums_1, 4),
+        (down_3, 0.1),
+        (second_2, 1),
+        (first_2, 0.1),
+        (sums_1, 1),
         (sums_2, 1),
         (input_sum, 1),
-        (second_2, 1),
         (sums_3, 1),
-        (up_4, 2),
+        (up_4, 0.1),
+        (down_4, 200),
+        (up_5, 1),
         (sums_4, 1),
-        (down_4, 4),
-        (first_3, 40),
+        (first_3, 1),
+        (second_3, 2),
+        (down_5, 200),
         (input_total, 1),
-        (second_3, 2),
-        (down_5, 1),
-        (first_4, 200),
-        (up_5, 0.3),
-        (second_4, 16),
-        (last_sums, 1),
+        (first_4, 1),
+        (second_4, 40),
+        (last_sums, 0.1),
         (scale_input, 0.1),
-        (first_5, 40),
-        (ends, 1),
-        (history_gradient, 1),
-        (place_down, 1),
-        (second_5, 200),
-        (place_up, 4),
-        (place_tail, 1),
+        (first_5, 8),
+        (ends, 0.3),
+        (second_5, 0.3),
+        (place_up, 40),
+        (place_down, 2),
+        (history_gradient, 4),
+        (place_tail, 0.1),
     )
     for step, weight in schedule:
         Order.cost = weight

time: 141 us -> 149 us (1.057)
  starting transfers between devices: 50.2 us -> 61 us
  waiting for transfers between devices: 42.1 us -> 38.4 us
    ppermute x52, starting transfers between devices: 50.2 us -> 61 us  [xor_send(): return lax.ppermute(value, axis, [(i, i ^ offset) for i in range(size)])]
    ppermute x52, waiting for transfers between devices: 42.1 us -> 38.4 us  [xor_send(): return lax.ppermute(value, axis, [(i, i ^ offset) for i in range(size)])]
  transfers between devices with their start and end apart: 52 -> 52, of which waited for: 23 -> 17; matrix products, arithmetic and copies ran while one was open for 0% -> 0% of each run, Pallas kernels for 29% -> 27%
where the time goes in v9:
time: 149 us; the launch traced here: 148 us
  starting transfers between devices  61 us (41%)
  Pallas kernels  45.2 us (30%)
  waiting for transfers between devices  38.4 us (26%)
  between operations  2.59 us (2%)
    ppermute x52, starting transfers between devices, xor_send(): return lax.ppermute(value, axis, [(i, i ^ offset) for i in range(size)])  61 us
    ppermute x52, waiting for transfers between devices, xor_send(): return lax.ppermute(value, axis, [(i, i ^ offset) for i in range(size)])  38.4 us
    pallas_call x48, Pallas kernels, kernel(): pl.pallas_call(body, out_shape=outs, in_specs=[pl.BlockSpec(memory_space=...  29.4 us
    pallas_call x2, Pallas kernels, history_call(): pl.pallas_call(body, out_shape=outs, in_specs=[pl.BlockSpec(memory_space=...  9.78 us
    pallas_call x3, Pallas kernels, place(): pl.pallas_call(functools.partial(place_kernel, all_tokens, streams, bound...  4.88 us
  transfers between devices with their start and end apart: 52, of which 17 were waited for; matrix products, arithmetic and copies ran while one was open for 0% of the time, Pallas kernels for 27%

profile of v9, /device:TPU:0, one launch (start us, length us, event | category | flops | bytes accessed | tf_op | source)
XLA Modules:
  0.0 148.4 jit_solution(9624739891344361032)
XLA Ops:
  1.2 2.6 %collective-permute-start.3 = (bf16[192,512]{1,0:T(8,128)(2,1)}, bf16[192,512]{1,0:T(8,128)(2,1)S(1)}, u32[]{:S(2)}, u32[]{:S(2)}) collective-permute-start(bf16[192,512]{1,0:T(8,128)(2,1)} %refs_7_), channel_id=1, source_target_pairs={{0,2},{1,3},{2,0},{3,1},{4,6},{5,7},{6,4},{7,5},{8,10},{9,11},{10,... | collective-permute-start | bytes 589832 | tf_op jit(solution)/shard_map/ppermute | solution.py:128
  6.1 1.6 %collective-permute-start.2 = (f32[16,256]{1,0:T(8,128)S(1)}, f32[16,256]{1,0:T(8,128)S(1)}, u32[]{:S(2)}, u32[]{:S(2)}) collective-permute-start(f32[16,256]{1,0:T(8,128)S(1)} %shard_map.256.n01), channel_id=1, source_target_pairs={{0,2},{1,3},{2,0},{3,1},{4,6},{5,7},{6,4},{7,5},{8,10},{9,11},{10,... | collective-permute-start | bytes 49160 | tf_op jit(solution)/shard_map/ppermute | solution.py:128
  7.7 2.2 %collective-permute-done.2.n23 = f32[16,256]{1,0:T(8,128)S(1)} collective-permute-done((f32[16,256]{1,0:T(8,128)S(1)}, f32[16,256]{1,0:T(8,128)S(1)}, u32[]{:S(2)}, u32[]{:S(2)}) %collective-permute-start.2) | collective-permute-done | bytes 16416 | tf_op jit(solution)/shard_map/ppermute | solution.py:128
  10.2 1.8 %collective-permute-start.5 = (bf16[192,768]{1,0:T(8,128)(2,1)}, bf16[192,768]{1,0:T(8,128)(2,1)S(1)}, u32[]{:S(2)}, u32[]{:S(2)}) collective-permute-start(bf16[192,768]{1,0:T(8,128)(2,1)} %w_out.1), channel_id=1, source_target_pairs={{0,2},{1,3},{2,0},{3,1},{4,6},{5,7},{6,4},{7,5},{8,10},{9,11},{10,... | collective-permute-start | bytes 884744 | tf_op jit(solution)/shard_map/ppermute | solution.py:128
  13.1 2.2 %shard_map.258 = (bf16[768,512]{1,0:T(8,128)(2,1)S(1)}, bf16[768,512]{1,0:T(8,128)(2,1)S(1)}, f32[2,512]{1,0:T(2,128)S(1)}, bf16[576,512]{1,0:T(8,128)(2,1)S(1)}) custom-call(s32[1]{0:T(128)} %bitcast.at_ref, bf16[192,512]{1,0:T(8,128)(2,1)S(1)} %get-tuple-element.158.x0.x_in, bf16[192,512]{1,0:T(8,128)(2,1)S(1)} %collective-permute-done.refs_0_.x1, ...), custom_call_target="tpu_custom_call" | custom-call | flops 400000000 | bytes 1024 | tf_op jit(solution)/shard_map/pallas_call | solution.py:93
  15.3 4.3 %shard_map.259 = (bf16[192,256]{1,0:T(8,128)(2,1)S(1)}, bf16[192,256]{1,0:T(8,128)(2,1)S(1)}, bf16[768,256]{1,0:T(8,128)(2,1)S(1)}, bf16[192,512]{1,0:T(8,128)(2,1)S(1)}, bf16[3,512,512]{2,1,0:T(8,128)(2,1)S(1)}) custom-call(s32[1]{0:T(128)} %bitcast.at_ref, bf16[576,512]{1,0:T(8,128)(2,1)S(1)} %get-tuple-element.164.qkv, ...), custom_call_target="tpu_custom_call" | custom-call | flops 200000000 | bytes 1024 | tf_op jit(solution)/shard_map/pallas_call | solution.py:93
  21.3 1.4 collective-permute-start.9
  23.4 5.6 %collective-permute-done.9.pair_far = bf16[384,256]{1,0:T(8,128)(2,1)S(1)} collective-permute-done((bf16[384,256]{1,0:T(8,128)(2,1)S(1)}, bf16[384,256]{1,0:T(8,128)(2,1)S(1)}, u32[]{:S(2)}, u32[]{:S(2)}) %collective-permute-start.9) | collective-permute-done | bytes 196640 | tf_op jit(solution)/shard_map/ppermute | solution.py:128
  29.0 2.0 %shard_map.262 = (f32[768,256]{1,0:T(8,128)S(1)}, f32[2,256]{1,0:T(2,128)S(1)}, bf16[768,256]{1,0:T(8,128)(2,1)S(1)}) custom-call(s32[1]{0:T(128)} %bitcast.at_ref, bf16[384,256]{1,0:T(8,128)(2,1)S(1)} %shard_map.260.pair, bf16[384,256]{1,0:T(8,128)(2,1)S(1)} %collective-permute-done.9.pair_far, bf16[768,768]{1,0:T(8,128)(2,1)S(1)} %shard_map.261.w_all, ...), custom_call_target="tpu_custom_call" | custom-call | flops 30000000 | bytes 1024 | tf_op jit(solution)/shard_map/pallas_call | solution.py:93
  31.0 1.7 %collective-permute-done.11.c2 = bf16[192,512]{1,0:T(8,128)(2,1)S(1)} collective-permute-done((bf16[192,512]{1,0:T(8,128)(2,1)S(1)}, bf16[192,512]{1,0:T(8,128)(2,1)S(1)}, u32[]{:S(2)}, u32[]{:S(2)}) %collective-permute-start.11) | collective-permute-done | bytes 196640 | tf_op jit(solution)/shard_map/ppermute | solution.py:128
  34.6 1.2 shard_map.263
  35.9 2.7 %shard_map.264 = (bf16[768,512]{1,0:T(8,128)(2,1)S(1)}, bf16[768,512]{1,0:T(8,128)(2,1)S(1)}, bf16[768,512]{1,0:T(8,128)(2,1)S(1)}, bf16[768,256]{1,0:T(8,128)(2,1)S(1)}, f32[768,256]{1,0:T(8,128)S(1)}) custom-call(bf16[768,256]{1,0:T(8,128)(2,1)S(1)} %get-tuple-element.181.own, bf16[768,256]{1,0:T(8,128)(2,1)S(1)} %collective-permute-done.13.other, ...), custom_call_target="tpu_custom_call" | custom-call | flops 1000000000 | bytes 1024 | tf_op jit(solution)/shard_map/pallas_call | solution.py:93
  39.9 1.6 %collective-permute-start.17 = (bf16[384,768]{1,0:T(8,128)(2,1)S(1)}, bf16[384,768]{1,0:T(8,128)(2,1)S(1)}, u32[]{:S(2)}, u32[]{:S(2)}) collective-permute-start(bf16[384,768]{1,0:T(8,128)(2,1)S(1)} %get-tuple-element.209), channel_id=1, source_target_pairs={{0,4},{4,0},{8,12},{12,8},{16,20},{20,16},{24,28},{28,24},{1,5},{5... | collective-permute-start | bytes 1769480 | tf_op jit(solution)/shard_map/ppermute | solution.py:128
  42.7 1.6 %collective-permute-start.18 = (bf16[384,768]{1,0:T(8,128)(2,1)S(1)}, bf16[384,768]{1,0:T(8,128)(2,1)S(1)}, u32[]{:S(2)}, u32[]{:S(2)}) collective-permute-start(bf16[384,768]{1,0:T(8,128)(2,1)S(1)} %get-tuple-element.212), channel_id=1, source_target_pairs={{0,8},{4,12},{8,0},{12,4},{16,24},{20,28},{24,16},{28,20},{1,9},{5... | collective-permute-start | bytes 1769480 | tf_op jit(solution)/shard_map/ppermute | solution.py:128
  44.3 1.4 collective-permute-start.15
  45.7 5.7 %shard_map.268 = (f32[192,512]{1,0:T(8,128)S(1)}, f32[30,8,128]{2,1,0:T(8,128)S(1)}) custom-call(f32[30]{0:T(128)S(1)} %copy-done.5, s32[1]{0:T(128)S(6)} %copy.29.counts_ref, bf16[192,512]{1,0:T(8,128)(2,1)S(1)} %copy-done.3, bf16[30,192,512]{2,1,0:T(8,128)(2,1)} %history_ref.1), custom_call_target="tpu_custom_call" | custom-call | flops 1000000000 | bytes 1024 | tf_op jit(solution)/shard_map/pallas_call | solution.py:376
  51.4 1.2 shard_map.269
  52.6 2.3 %collective-permute-done.15.received = bf16[768,256]{1,0:T(8,128)(2,1)S(1)} collective-permute-done((bf16[768,256]{1,0:T(8,128)(2,1)S(1)}, bf16[768,256]{1,0:T(8,128)(2,1)S(1)}, u32[]{:S(2)}, u32[]{:S(2)}) %collective-permute-start.15) | collective-permute-done | bytes 393248 | tf_op jit(solution)/shard_map/ppermute | solution.py:128
  54.9 2.3 %shard_map.270 = (f32[768,256]{1,0:T(8,128)S(1)}, bf16[768,256]{1,0:T(8,128)(2,1)S(1)}, f32[2,768]{1,0:T(2,128)S(1)}) custom-call(s32[1]{0:T(128)} %bitcast.at_ref, f32[1]{0:T(128)S(6)} %copy.30.self_ref, s32[1]{0:T(128)S(6)} %copy.29.counts_ref, f32[768,256]{1,0:T(8,128)S(1)} %get-tuple-element.200.chip, ...), custom_call_target="tpu_custom_call" | custom-call | flops 800000000 | bytes 1024 | tf_op jit(solution)/shard_map/pallas_call | solution.py:93
  59.2 3.6 %shard_map.274 = (bf16[576,512]{1,0:T(8,128)(2,1)S(1)}, bf16[768,512]{1,0:T(8,128)(2,1)S(1)}) custom-call(s32[1]{0:T(128)} %bitcast.at_ref, bf16[768,256]{1,0:T(8,128)(2,1)S(1)} %get-tuple-element.214.own, bf16[768,256]{1,0:T(8,128)(2,1)S(1)} %collective-permute-done.19.other, bf16[192,768]{1,0:T(8,128)(2,1)S(1)} %copy-done.4, ...), custom_call_target="tpu_custom_call" | custom-call | flops 20000000000 | bytes 1024 | tf_op jit(solution)/shard_map/pallas_call | solution.py:93
  63.8 1.2 collective-permute-start.24
  65.0 1.6 %collective-permute-start.25 = (bf16[192,768]{1,0:T(8,128)(2,1)S(1)}, bf16[192,768]{1,0:T(8,128)(2,1)S(1)}, u32[]{:S(2)}, u32[]{:S(2)}) collective-permute-start(bf16[192,768]{1,0:T(8,128)(2,1)S(1)} %get-tuple-element.243), channel_id=1, source_target_pairs={{0,8},{4,12},{8,0},{12,4},{16,24},{20,28},{24,16},{28,20},{1,9},{5... | collective-permute-start | bytes 884744 | tf_op jit(solution)/shard_map/ppermute | solution.py:128
  67.0 1.4 collective-permute-start.23
  68.6 2.7 %collective-permute-start.26 = (bf16[96,768]{1,0:T(8,128)(2,1)S(1)}, bf16[96,768]{1,0:T(8,128)(2,1)S(1)}, u32[]{:S(2)}, u32[]{:S(2)}) collective-permute-start(bf16[96,768]{1,0:T(8,128)(2,1)S(1)} %get-tuple-element.246), channel_id=1, source_target_pairs={{0,16},{4,20},{8,24},{12,28},{16,0},{20,4},{24,8},{28,12},{1,17},{... | collective-permute-start | bytes 442376 | tf_op jit(solution)/shard_map/ppermute | solution.py:128
  71.2 2.8 %shard_map.278 = (bf16[192,512]{1,0:T(8,128)(2,1)S(1)}, bf16[192,512]{1,0:T(8,128)(2,1)S(1)}, f32[192,512]{1,0:T(8,128)S(1)}, f32[192,512]{1,0:T(8,128)S(1)}, f32[8,768]{1,0:T(8,128)S(1)}) custom-call(s32[1]{0:T(128)} %bitcast.at_ref, s32[1]{0:T(128)S(6)} %copy.29.counts_ref, bf16[576,512]{1,0:T(8,128)(2,1)S(1)} %get-tuple-element.228.refs_0_.d_project, ...), custom_call_target="tpu_custom_call" | custom-call | flops 100000000 | bytes 1024 | tf_op jit(solution)/shard_map/pallas_call | solution.py:93
  75.3 1.4 collective-permute-done.25.refs_1_
  77.9 3.6 %collective-permute-start.34 = (bf16[96,768]{1,0:T(8,128)(2,1)S(1)}, bf16[96,768]{1,0:T(8,128)(2,1)S(1)}, u32[]{:S(2)}, u32[]{:S(2)}) collective-permute-start(bf16[96,768]{1,0:T(8,128)(2,1)S(1)} %shard_map.282.refs_0_), channel_id=1, source_target_pairs={{0,16},{4,20},{8,24},{12,28},{16,0},{20,4},{24,8},{28,12},{1,17},{... | collective-permute-start | bytes 442376 | tf_op jit(solution)/shard_map/ppermute | solution.py:128
  81.5 4.3 %collective-permute-done.27.refs_1_ = bf16[96,768]{1,0:T(8,128)(2,1)S(1)} collective-permute-done((bf16[96,768]{1,0:T(8,128)(2,1)S(1)}, bf16[96,768]{1,0:T(8,128)(2,1)S(1)}, u32[]{:S(2)}, u32[]{:S(2)}) %collective-permute-start.27) | collective-permute-done | bytes 147488 | tf_op jit(solution)/shard_map/ppermute | solution.py:128
  87.2 1.7 %collective-permute-start.31 = (f32[8,768]{1,0:T(8,128)S(1)}, f32[8,768]{1,0:T(8,128)S(1)}, u32[]{:S(2)}, u32[]{:S(2)}) collective-permute-start(f32[8,768]{1,0:T(8,128)S(1)} %shard_map.286.refs_0_), channel_id=1, source_target_pairs={{0,2},{1,3},{2,0},{3,1},{4,6},{5,7},{6,4},{7,5},{8,10},{9,11},{10,... | collective-permute-start | bytes 73736 | tf_op jit(solution)/shard_map/ppermute | solution.py:128
  88.9 2.2 %collective-permute-done.31.refs_1_ = f32[8,768]{1,0:T(8,128)S(1)} collective-permute-done((f32[8,768]{1,0:T(8,128)S(1)}, f32[8,768]{1,0:T(8,128)S(1)}, u32[]{:S(2)}, u32[]{:S(2)}) %collective-permute-start.31) | collective-permute-done | bytes 24608 | tf_op jit(solution)/shard_map/ppermute | solution.py:128
  92.0 2.8 %collective-permute-done.33.refs_1_ = f32[8,768]{1,0:T(8,128)S(1)} collective-permute-done((f32[8,768]{1,0:T(8,128)S(1)}, f32[8,768]{1,0:T(8,128)S(1)}, u32[]{:S(2)}, u32[]{:S(2)}) %collective-permute-start.33) | collective-permute-done | bytes 24608 | tf_op jit(solution)/shard_map/ppermute | solution.py:128
  96.2 9.1 %collective-permute-start.40 = (bf16[192,768]{1,0:T(8,128)(2,1)S(1)}, bf16[192,768]{1,0:T(8,128)(2,1)S(1)}, u32[]{:S(2)}, u32[]{:S(2)}) collective-permute-start(bf16[192,768]{1,0:T(8,128)(2,1)S(1)} %shard_map.291.refs_0_), channel_id=1, source_target_pairs={{0,8},{4,12},{8,0},{12,4},{16,24},{20,28},{24,16},{28,20},{1,9},{5... | collective-permute-start | bytes 884744 | tf_op jit(solution)/shard_map/ppermute | solution.py:128
  105.3 2.8 %collective-permute-start.39 = (bf16[48,768]{1,0:T(8,128)(2,1)S(1)}, bf16[48,768]{1,0:T(8,128)(2,1)S(1)}, u32[]{:S(2)}, u32[]{:S(2)}) collective-permute-start(bf16[48,768]{1,0:T(8,128)(2,1)S(1)} %get-tuple-element.269), channel_id=1, source_target_pairs={{0,16},{4,20},{8,24},{12,28},{16,0},{20,4},{24,8},{28,12},{1,17},{... | collective-permute-start | bytes 221192 | tf_op jit(solution)/shard_map/ppermute | solution.py:128
  108.3 5.4 %collective-permute-done.37.refs_1_ = f32[8,768]{1,0:T(8,128)S(1)} collective-permute-done((f32[8,768]{1,0:T(8,128)S(1)}, f32[8,768]{1,0:T(8,128)S(1)}, u32[]{:S(2)}, u32[]{:S(2)}) %collective-permute-start.37) | collective-permute-done | bytes 24608 | tf_op jit(solution)/shard_map/ppermute | solution.py:128
  113.7 1.4 collective-permute-start.42
  115.2 1.2 collective-permute-start.44
  116.5 1.8 %collective-permute-start.43 = (bf16[48,768]{1,0:T(8,128)(2,1)S(1)}, bf16[48,768]{1,0:T(8,128)(2,1)S(1)}, u32[]{:S(2)}, u32[]{:S(2)}) collective-permute-start(bf16[48,768]{1,0:T(8,128)(2,1)S(1)} %shard_map.294.refs_0_), channel_id=1, source_target_pairs={{0,16},{4,20},{8,24},{12,28},{16,0},{20,4},{24,8},{28,12},{1,17},{... | collective-permute-start | bytes 221192 | tf_op jit(solution)/shard_map/ppermute | solution.py:128
  118.2 2.2 %collective-permute-start.48 = (bf16[384,768]{1,0:T(8,128)(2,1)S(1)}, bf16[384,768]{1,0:T(8,128)(2,1)S(1)}, u32[]{:S(2)}, u32[]{:S(2)}) collective-permute-start(bf16[384,768]{1,0:T(8,128)(2,1)S(1)} %shard_map.292.refs_0_), channel_id=1, source_target_pairs={{0,8},{4,12},{8,0},{12,4},{16,24},{20,28},{24,16},{28,20},{1,9},{5... | collective-permute-start | bytes 1769480 | tf_op jit(solution)/shard_map/ppermute | solution.py:128
  120.5 1.2 collective-permute-start.49
  122.0 3.3 %collective-permute-start.46 = (bf16[96,768]{1,0:T(8,128)(2,1)S(1)}, bf16[96,768]{1,0:T(8,128)(2,1)S(1)}, u32[]{:S(2)}, u32[]{:S(2)}) collective-permute-start(bf16[96,768]{1,0:T(8,128)(2,1)S(1)} %shard_map.298.refs_0_), channel_id=1, source_target_pairs={{0,8},{4,12},{8,0},{12,4},{16,24},{20,28},{24,16},{28,20},{1,9},{5... | collective-permute-start | bytes 442376 | tf_op jit(solution)/shard_map/ppermute | solution.py:128
  125.3 1.2 collective-permute-start.47
  126.5 1.3 collective-permute-start.45
  127.8 6.8 %collective-permute-done.45.refs_1_ = f32[8,768]{1,0:T(8,128)S(1)} collective-permute-done((f32[8,768]{1,0:T(8,128)S(1)}, f32[8,768]{1,0:T(8,128)S(1)}, u32[]{:S(2)}, u32[]{:S(2)}) %collective-permute-start.45) | collective-permute-done | bytes 24608 | tf_op jit(solution)/shard_map/ppermute | solution.py:128
  136.3 1.8 %collective-permute-start.51 = (bf16[192,768]{1,0:T(8,128)(2,1)S(1)}, bf16[192,768]{1,0:T(8,128)(2,1)S(1)}, u32[]{:S(2)}, u32[]{:S(2)}) collective-permute-start(bf16[192,768]{1,0:T(8,128)(2,1)S(1)} %shard_map.304.refs_2_), channel_id=1, source_target_pairs={{0,8},{4,12},{8,0},{12,4},{16,24},{20,28},{24,16},{28,20},{1,9},{5... | collective-permute-start | bytes 884744 | tf_op jit(solution)/shard_map/ppermute | solution.py:128
  139.2 1.6 %shard_map.305 = f32[768,768]{1,0:T(8,128)} custom-call(s32[1]{0:T(128)} %bitcast.1.me_ref, f32[8,768]{1,0:T(8,128)S(1)} %shard_map.300.sums, bf16[384,768]{1,0:T(8,128)(2,1)S(1)} %shard_map.292.refs_0_, bf16[384,768]{1,0:T(8,128)(2,1)S(1)} %collective-permute-done.48.refs_1_), custom_call_target="tpu_custom_call" | custom-call | flops 4000000000 | bytes 1024 | tf_op jit(solution)/shard_map/pallas_call | solution.py:312
  140.8 1.6 %shard_map.306 = f32[768,768]{1,0:T(8,128)} custom-call(s32[1]{0:T(128)} %bitcast.1.me_ref, f32[8,768]{1,0:T(8,128)S(1)} %shard_map.300.sums, bf16[384,768]{1,0:T(8,128)(2,1)S(1)} %shard_map.296.refs_0_, bf16[384,768]{1,0:T(8,128)(2,1)S(1)} %collective-permute-done.49.refs_1_), custom_call_target="tpu_custom_call" | custom-call | flops 200000000 | bytes 1024 | tf_op jit(solution)/shard_map/pallas_call | solution.py:312
  142.4 4.1 %shard_map.307 = bf16[30,192,512]{2,1,0:T(8,128)(2,1)} custom-call(f32[30]{0:T(128)S(1)} %copy-done.5, s32[1]{0:T(128)S(6)} %copy.29.counts_ref, bf16[192,512]{1,0:T(8,128)(2,1)S(1)} %copy-done.3, f32[8,768]{1,0:T(8,128)S(1)} %shard_map.300.sums), custom_call_target="tpu_custom_call" | custom-call | flops 400000000 | bytes 1024 | tf_op jit(solution)/shard_map/pallas_call | solution.py:376
  146.5 1.8 %shard_map.308 = (f32[576,768]{1,0:T(8,128)}, f32[192,768]{1,0:T(8,128)}) custom-call(s32[1]{0:T(128)} %bitcast.1.me_ref, f32[8,768]{1,0:T(8,128)S(1)} %shard_map.300.sums, bf16[192,768]{1,0:T(8,128)(2,1)S(1)} %shard_map.302.refs_0_, bf16[192,768]{1,0:T(8,128)(2,1)S(1)} %collective-permute-done.50.refs_1_, bf16[192,768]{1,0:T(8,128)(2,1)S(1)} %shard_map.304.refs_2_, ...), custom_call_target="tpu_custom_call" | custom-call | flops 10000000 | bytes 1024 | tf_op jit(solution)/shard_map/pallas_call | solution.py:312
  (124 shorter events, 23.1 us)
Async XLA Ops:
  0.7 3.1 %collective-permute-start = (bf16[192,512]{1,0:T(8,128)(2,1)}, bf16[192,512]{1,0:T(8,128)(2,1)S(1)}, u32[]{:S(2)}, u32[]{:S(2)}) collective-permute-start(bf16[192,512]{1,0:T(8,128)(2,1)} %refs_7_), channel_id=1, source_target_pairs={{0,1},{1,0},{2,3},{3,2},{4,5},{5,4},{6,7},{7,6},{8,9},{9,8},{10,11... | collective-permute-start | bytes 589832 | tf_op jit(solution)/shard_map/ppermute | solution.py:128
  1.2 8.9 %collective-permute-start.3 = (bf16[192,512]{1,0:T(8,128)(2,1)}, bf16[192,512]{1,0:T(8,128)(2,1)S(1)}, u32[]{:S(2)}, u32[]{:S(2)}) collective-permute-start(bf16[192,512]{1,0:T(8,128)(2,1)} %refs_7_), channel_id=1, source_target_pairs={{0,2},{1,3},{2,0},{3,1},{4,6},{5,7},{6,4},{7,5},{8,10},{9,11},{10,... | collective-permute-start | bytes 589832 | tf_op jit(solution)/shard_map/ppermute | solution.py:128
  6.1 3.7 %collective-permute-start.2 = (f32[16,256]{1,0:T(8,128)S(1)}, f32[16,256]{1,0:T(8,128)S(1)}, u32[]{:S(2)}, u32[]{:S(2)}) collective-permute-start(f32[16,256]{1,0:T(8,128)S(1)} %shard_map.256.n01), channel_id=1, source_target_pairs={{0,2},{1,3},{2,0},{3,1},{4,6},{5,7},{6,4},{7,5},{8,10},{9,11},{10,... | collective-permute-start | bytes 49160 | tf_op jit(solution)/shard_map/ppermute | solution.py:128
  10.2 10.1 %collective-permute-start.5 = (bf16[192,768]{1,0:T(8,128)(2,1)}, bf16[192,768]{1,0:T(8,128)(2,1)S(1)}, u32[]{:S(2)}, u32[]{:S(2)}) collective-permute-start(bf16[192,768]{1,0:T(8,128)(2,1)} %w_out.1), channel_id=1, source_target_pairs={{0,2},{1,3},{2,0},{3,1},{4,6},{5,7},{6,4},{7,5},{8,10},{9,11},{10,... | collective-permute-start | bytes 884744 | tf_op jit(solution)/shard_map/ppermute | solution.py:128
  19.9 3.4 %collective-permute-start.7 = (bf16[192,768]{1,0:T(8,128)(2,1)S(1)}, bf16[192,768]{1,0:T(8,128)(2,1)S(1)}, u32[]{:S(2)}, u32[]{:S(2)}) collective-permute-start(bf16[192,768]{1,0:T(8,128)(2,1)S(1)} %copy-done.4), channel_id=1, source_target_pairs={{0,1},{1,0},{2,3},{3,2},{4,5},{5,4},{6,7},{7,6},{8,9},{9,8},{10,11... | collective-permute-start | bytes 884744 | tf_op jit(solution)/shard_map/ppermute | solution.py:128
  21.1 2.3 %collective-permute-start.8 = (bf16[192,768]{1,0:T(8,128)(2,1)S(1)}, bf16[192,768]{1,0:T(8,128)(2,1)S(1)}, u32[]{:S(2)}, u32[]{:S(2)}) collective-permute-start(bf16[192,768]{1,0:T(8,128)(2,1)S(1)} %collective-permute-done.5.refs_2_), channel_id=1, source_target_pairs={{0,1},{1,0},{2,3},{3,2},{4,5},{5,4},{6,7},{7,6},{8,9},{9,8},{10,11... | collective-permute-start | bytes 884744 | tf_op jit(solution)/shard_map/ppermute | solution.py:128
  21.3 7.7 %collective-permute-start.9 = (bf16[384,256]{1,0:T(8,128)(2,1)S(1)}, bf16[384,256]{1,0:T(8,128)(2,1)S(1)}, u32[]{:S(2)}, u32[]{:S(2)}) collective-permute-start(bf16[384,256]{1,0:T(8,128)(2,1)S(1)} %shard_map.260.pair), channel_id=1, source_target_pairs={{0,2},{1,3},{2,0},{3,1},{4,6},{5,7},{6,4},{7,5},{8,10},{9,11},{10,... | collective-permute-start | bytes 589832 | tf_op jit(solution)/shard_map/ppermute | solution.py:128
  22.7 10.0 %collective-permute-start.11 = (bf16[192,512]{1,0:T(8,128)(2,1)S(1)}, bf16[192,512]{1,0:T(8,128)(2,1)S(1)}, u32[]{:S(2)}, u32[]{:S(2)}) collective-permute-start(bf16[192,512]{1,0:T(8,128)(2,1)S(1)} %copy-done.3), channel_id=1, source_target_pairs={{0,2},{1,3},{2,0},{3,1},{4,6},{5,7},{6,4},{7,5},{8,10},{9,11},{10,... | collective-permute-start | bytes 589832 | tf_op jit(solution)/shard_map/ppermute | solution.py:128
  23.3 11.2 %collective-permute-start.10 = (bf16[192,512]{1,0:T(8,128)(2,1)S(1)}, bf16[192,512]{1,0:T(8,128)(2,1)S(1)}, u32[]{:S(2)}, u32[]{:S(2)}) collective-permute-start(bf16[192,512]{1,0:T(8,128)(2,1)S(1)} %copy-done.3), channel_id=1, source_target_pairs={{0,1},{1,0},{2,3},{3,2},{4,5},{5,4},{6,7},{7,6},{8,9},{9,8},{10,11... | collective-permute-start | bytes 589832 | tf_op jit(solution)/shard_map/ppermute | solution.py:128
  32.7 1.9 %collective-permute-start.12 = (bf16[192,512]{1,0:T(8,128)(2,1)S(1)}, bf16[192,512]{1,0:T(8,128)(2,1)S(1)}, u32[]{:S(2)}, u32[]{:S(2)}) collective-permute-start(bf16[192,512]{1,0:T(8,128)(2,1)S(1)} %collective-permute-done.11.c2), channel_id=1, source_target_pairs={{0,1},{1,0},{2,3},{3,2},{4,5},{5,4},{6,7},{7,6},{8,9},{9,8},{10,11... | collective-permute-start | bytes 589832 | tf_op jit(solution)/shard_map/ppermute | solution.py:128
  34.0 1.9 %collective-permute-start.13 = (bf16[768,256]{1,0:T(8,128)(2,1)S(1)}, bf16[768,256]{1,0:T(8,128)(2,1)S(1)}, u32[]{:S(2)}, u32[]{:S(2)}) collective-permute-start(bf16[768,256]{1,0:T(8,128)(2,1)S(1)} %get-tuple-element.181.own), channel_id=1, source_target_pairs={{0,1},{1,0},{2,3},{3,2},{4,5},{5,4},{6,7},{7,6},{8,9},{9,8},{10,11... | collective-permute-start | bytes 1179656 | tf_op jit(solution)/shard_map/ppermute | solution.py:128
  38.6 2.9 %collective-permute-start.14 = (bf16[768,256]{1,0:T(8,128)(2,1)S(1)}, bf16[768,256]{1,0:T(8,128)(2,1)S(1)}, u32[]{:S(2)}, u32[]{:S(2)}) collective-permute-start(bf16[768,256]{1,0:T(8,128)(2,1)S(1)} %get-tuple-element.189), channel_id=1, source_target_pairs={{0,1},{1,0},{2,3},{3,2},{4,5},{5,4},{6,7},{7,6},{8,9},{9,8},{10,11... | collective-permute-start | bytes 1179656 | tf_op jit(solution)/shard_map/ppermute | solution.py:128
  39.9 17.5 %collective-permute-start.17 = (bf16[384,768]{1,0:T(8,128)(2,1)S(1)}, bf16[384,768]{1,0:T(8,128)(2,1)S(1)}, u32[]{:S(2)}, u32[]{:S(2)}) collective-permute-start(bf16[384,768]{1,0:T(8,128)(2,1)S(1)} %get-tuple-element.209), channel_id=1, source_target_pairs={{0,4},{4,0},{8,12},{12,8},{16,20},{20,16},{24,28},{28,24},{1,5},{5... | collective-permute-start | bytes 1769480 | tf_op jit(solution)/shard_map/ppermute | solution.py:128
  42.7 15.4 %collective-permute-start.18 = (bf16[384,768]{1,0:T(8,128)(2,1)S(1)}, bf16[384,768]{1,0:T(8,128)(2,1)S(1)}, u32[]{:S(2)}, u32[]{:S(2)}) collective-permute-start(bf16[384,768]{1,0:T(8,128)(2,1)S(1)} %get-tuple-element.212), channel_id=1, source_target_pairs={{0,8},{4,12},{8,0},{12,4},{16,24},{20,28},{24,16},{28,20},{1,9},{5... | collective-permute-start | bytes 1769480 | tf_op jit(solution)/shard_map/ppermute | solution.py:128
  44.3 10.6 %collective-permute-start.15 = (bf16[768,256]{1,0:T(8,128)(2,1)S(1)}, bf16[768,256]{1,0:T(8,128)(2,1)S(1)}, u32[]{:S(2)}, u32[]{:S(2)}) collective-permute-start(bf16[768,256]{1,0:T(8,128)(2,1)S(1)} %get-tuple-element.201), channel_id=1, source_target_pairs={{0,2},{1,3},{2,0},{3,1},{4,6},{5,7},{6,4},{7,5},{8,10},{9,11},{10,... | collective-permute-start | bytes 1179656 | tf_op jit(solution)/shard_map/ppermute | solution.py:128
  52.6 4.6 %collective-permute-start.16 = (bf16[192,512]{1,0:T(8,128)(2,1)S(1)}, bf16[192,512]{1,0:T(8,128)(2,1)S(1)}, u32[]{:S(2)}, u32[]{:S(2)}) collective-permute-start(bf16[192,512]{1,0:T(8,128)(2,1)S(1)} %get-tuple-element.207), channel_id=1, source_target_pairs={{0,1},{1,0},{2,3},{3,2},{4,5},{5,4},{6,7},{7,6},{8,9},{9,8},{10,11... | collective-permute-start | bytes 589832 | tf_op jit(solution)/shard_map/ppermute | solution.py:128
  57.3 2.0 %collective-permute-start.19 = (bf16[768,256]{1,0:T(8,128)(2,1)S(1)}, bf16[768,256]{1,0:T(8,128)(2,1)S(1)}, u32[]{:S(2)}, u32[]{:S(2)}) collective-permute-start(bf16[768,256]{1,0:T(8,128)(2,1)S(1)} %get-tuple-element.214.own), channel_id=1, source_target_pairs={{0,1},{1,0},{2,3},{3,2},{4,5},{5,4},{6,7},{7,6},{8,9},{9,8},{10,11... | collective-permute-start | bytes 1179656 | tf_op jit(solution)/shard_map/ppermute | solution.py:128
  57.6 9.5 %collective-permute-start.20 = (bf16[192,768]{1,0:T(8,128)(2,1)S(1)}, bf16[192,768]{1,0:T(8,128)(2,1)S(1)}, u32[]{:S(2)}, u32[]{:S(2)}) collective-permute-start(bf16[192,768]{1,0:T(8,128)(2,1)S(1)} %get-tuple-element.223), channel_id=1, source_target_pairs={{0,8},{4,12},{8,0},{12,4},{16,24},{20,28},{24,16},{28,20},{1,9},{5... | collective-permute-start | bytes 884744 | tf_op jit(solution)/shard_map/ppermute | solution.py:128
  58.3 10.2 %collective-permute-start.21 = (bf16[192,768]{1,0:T(8,128)(2,1)S(1)}, bf16[192,768]{1,0:T(8,128)(2,1)S(1)}, u32[]{:S(2)}, u32[]{:S(2)}) collective-permute-start(bf16[192,768]{1,0:T(8,128)(2,1)S(1)} %get-tuple-element.226), channel_id=1, source_target_pairs={{0,4},{4,0},{8,12},{12,8},{16,20},{20,16},{24,28},{28,24},{1,5},{5... | collective-permute-start | bytes 884744 | tf_op jit(solution)/shard_map/ppermute | solution.py:128
  63.8 11.4 %collective-permute-start.24 = (bf16[192,768]{1,0:T(8,128)(2,1)S(1)}, bf16[192,768]{1,0:T(8,128)(2,1)S(1)}, u32[]{:S(2)}, u32[]{:S(2)}) collective-permute-start(bf16[192,768]{1,0:T(8,128)(2,1)S(1)} %get-tuple-element.240), channel_id=1, source_target_pairs={{0,4},{4,0},{8,12},{12,8},{16,20},{20,16},{24,28},{28,24},{1,5},{5... | collective-permute-start | bytes 884744 | tf_op jit(solution)/shard_map/ppermute | solution.py:128
  65.0 11.7 %collective-permute-start.25 = (bf16[192,768]{1,0:T(8,128)(2,1)S(1)}, bf16[192,768]{1,0:T(8,128)(2,1)S(1)}, u32[]{:S(2)}, u32[]{:S(2)}) collective-permute-start(bf16[192,768]{1,0:T(8,128)(2,1)S(1)} %get-tuple-element.243), channel_id=1, source_target_pairs={{0,8},{4,12},{8,0},{12,4},{16,24},{20,28},{24,16},{28,20},{1,9},{5... | collective-permute-start | bytes 884744 | tf_op jit(solution)/shard_map/ppermute | solution.py:128
  66.6 7.5 %collective-permute-start.22 = (bf16[192,512]{1,0:T(8,128)(2,1)S(1)}, bf16[192,512]{1,0:T(8,128)(2,1)S(1)}, u32[]{:S(2)}, u32[]{:S(2)}) collective-permute-start(bf16[192,512]{1,0:T(8,128)(2,1)S(1)} %get-tuple-element.199), channel_id=1, source_target_pairs={{0,1},{1,0},{2,3},{3,2},{4,5},{5,4},{6,7},{7,6},{8,9},{9,8},{10,11... | collective-permute-start | bytes 589832 | tf_op jit(solution)/shard_map/ppermute | solution.py:128
  67.0 7.4 %collective-permute-start.23 = (bf16[192,512]{1,0:T(8,128)(2,1)S(1)}, bf16[192,512]{1,0:T(8,128)(2,1)S(1)}, u32[]{:S(2)}, u32[]{:S(2)}) collective-permute-start(bf16[192,512]{1,0:T(8,128)(2,1)S(1)} %shard_map.271), channel_id=1, source_target_pairs={{0,2},{1,3},{2,0},{3,1},{4,6},{5,7},{6,4},{7,5},{8,10},{9,11},{10,... | collective-permute-start | bytes 589832 | tf_op jit(solution)/shard_map/ppermute | solution.py:128
  68.6 9.2 %collective-permute-start.26 = (bf16[96,768]{1,0:T(8,128)(2,1)S(1)}, bf16[96,768]{1,0:T(8,128)(2,1)S(1)}, u32[]{:S(2)}, u32[]{:S(2)}) collective-permute-start(bf16[96,768]{1,0:T(8,128)(2,1)S(1)} %get-tuple-element.246), channel_id=1, source_target_pairs={{0,16},{4,20},{8,24},{12,28},{16,0},{20,4},{24,8},{28,12},{1,17},{... | collective-permute-start | bytes 442376 | tf_op jit(solution)/shard_map/ppermute | solution.py:128
  74.1 11.8 %collective-permute-start.27 = (bf16[96,768]{1,0:T(8,128)(2,1)S(1)}, bf16[96,768]{1,0:T(8,128)(2,1)S(1)}, u32[]{:S(2)}, u32[]{:S(2)}) collective-permute-start(bf16[96,768]{1,0:T(8,128)(2,1)S(1)} %get-tuple-element.248), channel_id=1, source_target_pairs={{0,16},{4,20},{8,24},{12,28},{16,0},{20,4},{24,8},{28,12},{1,17},{... | collective-permute-start | bytes 442376 | tf_op jit(solution)/shard_map/ppermute | solution.py:128
  75.2 16.7 %collective-permute-start.32 = (bf16[192,512]{1,0:T(8,128)(2,1)S(1)}, bf16[192,512]{1,0:T(8,128)(2,1)S(1)}, u32[]{:S(2)}, u32[]{:S(2)}) collective-permute-start(bf16[192,512]{1,0:T(8,128)(2,1)S(1)} %get-tuple-element.260), channel_id=1, source_target_pairs={{0,1},{1,0},{2,3},{3,2},{4,5},{5,4},{6,7},{7,6},{8,9},{9,8},{10,11... | collective-permute-start | bytes 589832 | tf_op jit(solution)/shard_map/ppermute | solution.py:128
  76.8 9.1 %collective-permute-start.28 = (bf16[96,768]{1,0:T(8,128)(2,1)S(1)}, bf16[96,768]{1,0:T(8,128)(2,1)S(1)}, u32[]{:S(2)}, u32[]{:S(2)}) collective-permute-start(bf16[96,768]{1,0:T(8,128)(2,1)S(1)} %get-tuple-element.251), channel_id=1, source_target_pairs={{0,4},{4,0},{8,12},{12,8},{16,20},{20,16},{24,28},{28,24},{1,5},{5... | collective-permute-start | bytes 442376 | tf_op jit(solution)/shard_map/ppermute | solution.py:128
  77.8 8.3 %collective-permute-start.29 = (bf16[96,768]{1,0:T(8,128)(2,1)S(1)}, bf16[96,768]{1,0:T(8,128)(2,1)S(1)}, u32[]{:S(2)}, u32[]{:S(2)}) collective-permute-start(bf16[96,768]{1,0:T(8,128)(2,1)S(1)} %get-tuple-element.254), channel_id=1, source_target_pairs={{0,8},{4,12},{8,0},{12,4},{16,24},{20,28},{24,16},{28,20},{1,9},{5... | collective-permute-start | bytes 442376 | tf_op jit(solution)/shard_map/ppermute | solution.py:128
  77.9 17.0 %collective-permute-start.34 = (bf16[96,768]{1,0:T(8,128)(2,1)S(1)}, bf16[96,768]{1,0:T(8,128)(2,1)S(1)}, u32[]{:S(2)}, u32[]{:S(2)}) collective-permute-start(bf16[96,768]{1,0:T(8,128)(2,1)S(1)} %shard_map.282.refs_0_), channel_id=1, source_target_pairs={{0,16},{4,20},{8,24},{12,28},{16,0},{20,4},{24,8},{28,12},{1,17},{... | collective-permute-start | bytes 442376 | tf_op jit(solution)/shard_map/ppermute | solution.py:128
  85.9 10.3 %collective-permute-start.35 = (bf16[96,768]{1,0:T(8,128)(2,1)S(1)}, bf16[96,768]{1,0:T(8,128)(2,1)S(1)}, u32[]{:S(2)}, u32[]{:S(2)}) collective-permute-start(bf16[96,768]{1,0:T(8,128)(2,1)S(1)} %shard_map.283.refs_0_), channel_id=1, source_target_pairs={{0,16},{4,20},{8,24},{12,28},{16,0},{20,4},{24,8},{28,12},{1,17},{... | collective-permute-start | bytes 442376 | tf_op jit(solution)/shard_map/ppermute | solution.py:128
  87.2 3.8 %collective-permute-start.31 = (f32[8,768]{1,0:T(8,128)S(1)}, f32[8,768]{1,0:T(8,128)S(1)}, u32[]{:S(2)}, u32[]{:S(2)}) collective-permute-start(f32[8,768]{1,0:T(8,128)S(1)} %shard_map.286.refs_0_), channel_id=1, source_target_pairs={{0,2},{1,3},{2,0},{3,1},{4,6},{5,7},{6,4},{7,5},{8,10},{9,11},{10,... | collective-permute-start | bytes 73736 | tf_op jit(solution)/shard_map/ppermute | solution.py:128
  91.0 3.8 %collective-permute-start.33 = (f32[8,768]{1,0:T(8,128)S(1)}, f32[8,768]{1,0:T(8,128)S(1)}, u32[]{:S(2)}, u32[]{:S(2)}) collective-permute-start(f32[8,768]{1,0:T(8,128)S(1)} %shard_map.287.refs_0_.row_sums), channel_id=1, source_target_pairs={{0,4},{4,0},{8,12},{12,8},{16,20},{20,16},{24,28},{28,24},{1,5},{5... | collective-permute-start | bytes 73736 | tf_op jit(solution)/shard_map/ppermute | solution.py:128
  94.9 13.4 %collective-permute-start.36 = (bf16[192,768]{1,0:T(8,128)(2,1)S(1)}, bf16[192,768]{1,0:T(8,128)(2,1)S(1)}, u32[]{:S(2)}, u32[]{:S(2)}) collective-permute-start(bf16[192,768]{1,0:T(8,128)(2,1)S(1)} %shard_map.290.refs_0_), channel_id=1, source_target_pairs={{0,4},{4,0},{8,12},{12,8},{16,20},{20,16},{24,28},{28,24},{1,5},{5... | collective-permute-start | bytes 884744 | tf_op jit(solution)/shard_map/ppermute | solution.py:128
  96.2 22.0 %collective-permute-start.40 = (bf16[192,768]{1,0:T(8,128)(2,1)S(1)}, bf16[192,768]{1,0:T(8,128)(2,1)S(1)}, u32[]{:S(2)}, u32[]{:S(2)}) collective-permute-start(bf16[192,768]{1,0:T(8,128)(2,1)S(1)} %shard_map.291.refs_0_), channel_id=1, source_target_pairs={{0,8},{4,12},{8,0},{12,4},{16,24},{20,28},{24,16},{28,20},{1,9},{5... | collective-permute-start | bytes 884744 | tf_op jit(solution)/shard_map/ppermute | solution.py:128
  105.3 9.9 %collective-permute-start.38 = (bf16[48,768]{1,0:T(8,128)(2,1)S(1)}, bf16[48,768]{1,0:T(8,128)(2,1)S(1)}, u32[]{:S(2)}, u32[]{:S(2)}) collective-permute-start(bf16[48,768]{1,0:T(8,128)(2,1)S(1)} %get-tuple-element.267), channel_id=1, source_target_pairs={{0,16},{4,20},{8,24},{12,28},{16,0},{20,4},{24,8},{28,12},{1,17},{... | collective-permute-start | bytes 221192 | tf_op jit(solution)/shard_map/ppermute | solution.py:128
  105.3 9.8 %collective-permute-start.39 = (bf16[48,768]{1,0:T(8,128)(2,1)S(1)}, bf16[48,768]{1,0:T(8,128)(2,1)S(1)}, u32[]{:S(2)}, u32[]{:S(2)}) collective-permute-start(bf16[48,768]{1,0:T(8,128)(2,1)S(1)} %get-tuple-element.269), channel_id=1, source_target_pairs={{0,16},{4,20},{8,24},{12,28},{16,0},{20,4},{24,8},{28,12},{1,17},{... | collective-permute-start | bytes 221192 | tf_op jit(solution)/shard_map/ppermute | solution.py:128
  108.2 5.5 %collective-permute-start.37 = (f32[8,768]{1,0:T(8,128)S(1)}, f32[8,768]{1,0:T(8,128)S(1)}, u32[]{:S(2)}, u32[]{:S(2)}) collective-permute-start(f32[8,768]{1,0:T(8,128)S(1)} %shard_map.289.refs_0_), channel_id=1, source_target_pairs={{0,8},{4,12},{8,0},{12,4},{16,24},{20,28},{24,16},{28,20},{1,9},{5... | collective-permute-start | bytes 73736 | tf_op jit(solution)/shard_map/ppermute | solution.py:128
  108.3 12.2 %collective-permute-start.41 = (bf16[192,512]{1,0:T(8,128)(2,1)S(1)}, bf16[192,512]{1,0:T(8,128)(2,1)S(1)}, u32[]{:S(2)}, u32[]{:S(2)}) collective-permute-start(bf16[192,512]{1,0:T(8,128)(2,1)S(1)} %get-tuple-element.231), channel_id=1, source_target_pairs={{0,1},{1,0},{2,3},{3,2},{4,5},{5,4},{6,7},{7,6},{8,9},{9,8},{10,11... | collective-permute-start | bytes 589832 | tf_op jit(solution)/shard_map/ppermute | solution.py:128
  113.7 8.0 %collective-permute-start.42 = (bf16[192,512]{1,0:T(8,128)(2,1)S(1)}, bf16[192,512]{1,0:T(8,128)(2,1)S(1)}, u32[]{:S(2)}, u32[]{:S(2)}) collective-permute-start(bf16[192,512]{1,0:T(8,128)(2,1)S(1)} %shard_map.288), channel_id=1, source_target_pairs={{0,2},{1,3},{2,0},{3,1},{4,6},{5,7},{6,4},{7,5},{8,10},{9,11},{10,... | collective-permute-start | bytes 589832 | tf_op jit(solution)/shard_map/ppermute | solution.py:128
  115.2 10.0 %collective-permute-start.44 = (bf16[48,768]{1,0:T(8,128)(2,1)S(1)}, bf16[48,768]{1,0:T(8,128)(2,1)S(1)}, u32[]{:S(2)}, u32[]{:S(2)}) collective-permute-start(bf16[48,768]{1,0:T(8,128)(2,1)S(1)} %shard_map.295.refs_0_), channel_id=1, source_target_pairs={{0,16},{4,20},{8,24},{12,28},{16,0},{20,4},{24,8},{28,12},{1,17},{... | collective-permute-start | bytes 221192 | tf_op jit(solution)/shard_map/ppermute | solution.py:128
  116.5 5.5 %collective-permute-start.43 = (bf16[48,768]{1,0:T(8,128)(2,1)S(1)}, bf16[48,768]{1,0:T(8,128)(2,1)S(1)}, u32[]{:S(2)}, u32[]{:S(2)}) collective-permute-start(bf16[48,768]{1,0:T(8,128)(2,1)S(1)} %shard_map.294.refs_0_), channel_id=1, source_target_pairs={{0,16},{4,20},{8,24},{12,28},{16,0},{20,4},{24,8},{28,12},{1,17},{... | collective-permute-start | bytes 221192 | tf_op jit(solution)/shard_map/ppermute | solution.py:128
  118.2 21.0 %collective-permute-start.48 = (bf16[384,768]{1,0:T(8,128)(2,1)S(1)}, bf16[384,768]{1,0:T(8,128)(2,1)S(1)}, u32[]{:S(2)}, u32[]{:S(2)}) collective-permute-start(bf16[384,768]{1,0:T(8,128)(2,1)S(1)} %shard_map.292.refs_0_), channel_id=1, source_target_pairs={{0,8},{4,12},{8,0},{12,4},{16,24},{20,28},{24,16},{28,20},{1,9},{5... | collective-permute-start | bytes 1769480 | tf_op jit(solution)/shard_map/ppermute | solution.py:128
  120.5 20.3 %collective-permute-start.49 = (bf16[384,768]{1,0:T(8,128)(2,1)S(1)}, bf16[384,768]{1,0:T(8,128)(2,1)S(1)}, u32[]{:S(2)}, u32[]{:S(2)}) collective-permute-start(bf16[384,768]{1,0:T(8,128)(2,1)S(1)} %shard_map.296.refs_0_), channel_id=1, source_target_pairs={{0,4},{4,0},{8,12},{12,8},{16,20},{20,16},{24,28},{28,24},{1,5},{5... | collective-permute-start | bytes 1769480 | tf_op jit(solution)/shard_map/ppermute | solution.py:128
  122.0 13.5 %collective-permute-start.46 = (bf16[96,768]{1,0:T(8,128)(2,1)S(1)}, bf16[96,768]{1,0:T(8,128)(2,1)S(1)}, u32[]{:S(2)}, u32[]{:S(2)}) collective-permute-start(bf16[96,768]{1,0:T(8,128)(2,1)S(1)} %shard_map.298.refs_0_), channel_id=1, source_target_pairs={{0,8},{4,12},{8,0},{12,4},{16,24},{20,28},{24,16},{28,20},{1,9},{5... | collective-permute-start | bytes 442376 | tf_op jit(solution)/shard_map/ppermute | solution.py:128
  125.3 11.0 %collective-permute-start.47 = (bf16[96,768]{1,0:T(8,128)(2,1)S(1)}, bf16[96,768]{1,0:T(8,128)(2,1)S(1)}, u32[]{:S(2)}, u32[]{:S(2)}) collective-permute-start(bf16[96,768]{1,0:T(8,128)(2,1)S(1)} %shard_map.299.refs_0_), channel_id=1, source_target_pairs={{0,4},{4,0},{8,12},{12,8},{16,20},{20,16},{24,28},{28,24},{1,5},{5... | collective-permute-start | bytes 442376 | tf_op jit(solution)/shard_map/ppermute | solution.py:128
  126.5 8.2 %collective-permute-start.45 = (f32[8,768]{1,0:T(8,128)S(1)}, f32[8,768]{1,0:T(8,128)S(1)}, u32[]{:S(2)}, u32[]{:S(2)}) collective-permute-start(f32[8,768]{1,0:T(8,128)S(1)} %shard_map.293.refs_0_), channel_id=1, source_target_pairs={{0,16},{4,20},{8,24},{12,28},{16,0},{20,4},{24,8},{28,12},{1,17},{... | collective-permute-start | bytes 73736 | tf_op jit(solution)/shard_map/ppermute | solution.py:128
  136.3 10.2 %collective-permute-start.51 = (bf16[192,768]{1,0:T(8,128)(2,1)S(1)}, bf16[192,768]{1,0:T(8,128)(2,1)S(1)}, u32[]{:S(2)}, u32[]{:S(2)}) collective-permute-start(bf16[192,768]{1,0:T(8,128)(2,1)S(1)} %shard_map.304.refs_2_), channel_id=1, source_target_pairs={{0,8},{4,12},{8,0},{12,4},{16,24},{20,28},{24,16},{28,20},{1,9},{5... | collective-permute-start | bytes 884744 | tf_op jit(solution)/shard_map/ppermute | solution.py:128
  138.1 8.3 %collective-permute-start.50 = (bf16[192,768]{1,0:T(8,128)(2,1)S(1)}, bf16[192,768]{1,0:T(8,128)(2,1)S(1)}, u32[]{:S(2)}, u32[]{:S(2)}) collective-permute-start(bf16[192,768]{1,0:T(8,128)(2,1)S(1)} %shard_map.302.refs_0_), channel_id=1, source_target_pairs={{0,4},{4,0},{8,12},{12,8},{16,20},{20,16},{24,28},{28,24},{1,5},{5... | collective-permute-start | bytes 884744 | tf_op jit(solution)/shard_map/ppermute | solution.py:128
  (11 other events, 46.4 us)

commit v10 on v8

--- a/solution.py
+++ b/solution.py
@@ -117,7 +117,7 @@
 
 
 def each_rows(count, body, start=None, first=0):
-    return lax.fori_loop(first // STEP, count // STEP, body, start, unroll=4)
+    return lax.fori_loop(first // STEP, count // STEP, body, start, unroll=8)
 
 
 def column_sum(value):
@@ -1128,39 +1128,39 @@
         (output_sum, 10),
         (down_1, 10),
         (up_1, 100),
-        (attention_gradient, 8),
+        (attention_gradient, 10),
         (tail_product, 4),
         (down_2, 100),
         (up_2, 0.3),
+        (up_3, 100),
         (input_gradient, 1),
         (mix, 8),
         (first_1, 1),
         (second_1, 1),
-        (up_3, 100),
         (down_3, 1),
         (first_2, 2),
         (sums_1, 4),
         (sums_2, 1),
         (input_sum, 1),
+        (sums_3, 1),
         (second_2, 1),
-        (sums_3, 1),
         (up_4, 2),
         (sums_4, 1),
         (down_4, 4),
         (first_3, 40),
+        (second_3, 2),
         (input_total, 1),
-        (second_3, 2),
         (down_5, 1),
         (first_4, 200),
-        (up_5, 0.3),
         (second_4, 16),
         (last_sums, 1),
+        (up_5, 0.3),
+        (first_5, 40),
+        (second_5, 200),
+        (ends, 200),
+        (history_gradient, 1),
         (scale_input, 0.1),
-        (first_5, 40),
-        (ends, 1),
-        (history_gradient, 1),
         (place_down, 1),
-        (second_5, 200),
         (place_up, 4),
         (place_tail, 1),
     )

time: 141 us -> 138 us (0.979)
  starting transfers between devices: 50.2 us -> 55.3 us
  waiting for transfers between devices: 42.1 us -> 37.3 us
  Pallas kernels: 45.1 us -> 42.8 us
    ppermute x52, starting transfers between devices: 50.2 us -> 55.3 us  [xor_send(): return lax.ppermute(value, axis, [(i, i ^ offset) for i in range(size)])]
    ppermute x52, waiting for transfers between devices: 42.1 us -> 37.3 us  [xor_send(): return lax.ppermute(value, axis, [(i, i ^ offset) for i in range(size)])]
    pallas_call x48, Pallas kernels: 29.4 us -> 27 us  [kernel(): pl.pallas_call(body, out_shape=outs, in_specs=[pl.BlockSpec(memory_space=...]
  transfers between devices with their start and end apart: 52 -> 52, of which waited for: 23 -> 22; matrix products, arithmetic and copies ran while one was open for 0% -> 0% of each run, Pallas kernels for 29% -> 28%
where the time goes in v10:
time: 138 us
  starting transfers between devices  55.3 us (40%)
  Pallas kernels  42.8 us (31%)
  waiting for transfers between devices  37.3 us (27%)
  between operations  2.63 us (2%)
    ppermute x52, starting transfers between devices, xor_send(): return lax.ppermute(value, axis, [(i, i ^ offset) for i in range(size)])  55.3 us
    ppermute x52, waiting for transfers between devices, xor_send(): return lax.ppermute(value, axis, [(i, i ^ offset) for i in range(size)])  37.3 us
    pallas_call x48, Pallas kernels, kernel(): pl.pallas_call(body, out_shape=outs, in_specs=[pl.BlockSpec(memory_space=...  27 us
    pallas_call x2, Pallas kernels, history_call(): pl.pallas_call(body, out_shape=outs, in_specs=[pl.BlockSpec(memory_space=...  9.78 us
    pallas_call x3, Pallas kernels, place(): pl.pallas_call(functools.partial(place_kernel, all_tokens, streams, bound...  4.88 us
  transfers between devices with their start and end apart: 52, of which 22 were waited for; matrix products, arithmetic and copies ran while one was open for 0% of the time, Pallas kernels for 28%

profile of v10, /device:TPU:0, one launch (start us, length us, event | category | flops | bytes accessed | tf_op | source)
XLA Modules:
  0.0 138.0 jit_solution(12301130205581889895)
XLA Ops:
  1.2 2.6 %collective-permute-start.3 = (bf16[192,512]{1,0:T(8,128)(2,1)}, bf16[192,512]{1,0:T(8,128)(2,1)S(1)}, u32[]{:S(2)}, u32[]{:S(2)}) collective-permute-start(bf16[192,512]{1,0:T(8,128)(2,1)} %refs_7_), channel_id=1, source_target_pairs={{0,2},{1,3},{2,0},{3,1},{4,6},{5,7},{6,4},{7,5},{8,10},{9,11},{10,... | collective-permute-start | bytes 589832 | tf_op jit(solution)/shard_map/ppermute | solution.py:128
  6.2 1.6 %collective-permute-start.2 = (f32[16,256]{1,0:T(8,128)S(1)}, f32[16,256]{1,0:T(8,128)S(1)}, u32[]{:S(2)}, u32[]{:S(2)}) collective-permute-start(f32[16,256]{1,0:T(8,128)S(1)} %shard_map.256.n01), channel_id=1, source_target_pairs={{0,2},{1,3},{2,0},{3,1},{4,6},{5,7},{6,4},{7,5},{8,10},{9,11},{10,... | collective-permute-start | bytes 49160 | tf_op jit(solution)/shard_map/ppermute | solution.py:128
  7.7 2.2 %collective-permute-done.2.n23 = f32[16,256]{1,0:T(8,128)S(1)} collective-permute-done((f32[16,256]{1,0:T(8,128)S(1)}, f32[16,256]{1,0:T(8,128)S(1)}, u32[]{:S(2)}, u32[]{:S(2)}) %collective-permute-start.2) | collective-permute-done | bytes 16416 | tf_op jit(solution)/shard_map/ppermute | solution.py:128
  10.2 1.8 %collective-permute-start.5 = (bf16[192,768]{1,0:T(8,128)(2,1)}, bf16[192,768]{1,0:T(8,128)(2,1)S(1)}, u32[]{:S(2)}, u32[]{:S(2)}) collective-permute-start(bf16[192,768]{1,0:T(8,128)(2,1)} %w_out.1), channel_id=1, source_target_pairs={{0,2},{1,3},{2,0},{3,1},{4,6},{5,7},{6,4},{7,5},{8,10},{9,11},{10,... | collective-permute-start | bytes 884744 | tf_op jit(solution)/shard_map/ppermute | solution.py:128
  12.0 1.8 %shard_map.258 = (bf16[768,512]{1,0:T(8,128)(2,1)S(1)}, bf16[768,512]{1,0:T(8,128)(2,1)S(1)}, f32[2,512]{1,0:T(2,128)S(1)}, bf16[576,512]{1,0:T(8,128)(2,1)S(1)}) custom-call(s32[1]{0:T(128)} %bitcast.at_ref, bf16[192,512]{1,0:T(8,128)(2,1)S(1)} %get-tuple-element.157.x0.x_in, bf16[192,512]{1,0:T(8,128)(2,1)S(1)} %collective-permute-done.refs_0_.x1, ...), custom_call_target="tpu_custom_call" | custom-call | flops 100000000 | bytes 1024 | tf_op jit(solution)/shard_map/pallas_call | solution.py:93
  13.7 4.2 %shard_map.259 = (bf16[192,256]{1,0:T(8,128)(2,1)S(1)}, bf16[192,256]{1,0:T(8,128)(2,1)S(1)}, bf16[768,256]{1,0:T(8,128)(2,1)S(1)}, bf16[192,512]{1,0:T(8,128)(2,1)S(1)}, bf16[3,512,512]{2,1,0:T(8,128)(2,1)S(1)}) custom-call(s32[1]{0:T(128)} %bitcast.at_ref, bf16[576,512]{1,0:T(8,128)(2,1)S(1)} %get-tuple-element.163.qkv, ...), custom_call_target="tpu_custom_call" | custom-call | flops 100000000 | bytes 1024 | tf_op jit(solution)/shard_map/pallas_call | solution.py:93
  18.5 1.4 collective-permute-done.5.refs_2_
  19.9 1.8 %collective-permute-start.9 = (bf16[384,256]{1,0:T(8,128)(2,1)S(1)}, bf16[384,256]{1,0:T(8,128)(2,1)S(1)}, u32[]{:S(2)}, u32[]{:S(2)}) collective-permute-start(bf16[384,256]{1,0:T(8,128)(2,1)S(1)} %shard_map.260.pair), channel_id=1, source_target_pairs={{0,2},{1,3},{2,0},{3,1},{4,6},{5,7},{6,4},{7,5},{8,10},{9,11},{10,... | collective-permute-start | bytes 589832 | tf_op jit(solution)/shard_map/ppermute | solution.py:128
  22.1 5.6 %collective-permute-done.9.pair_far = bf16[384,256]{1,0:T(8,128)(2,1)S(1)} collective-permute-done((bf16[384,256]{1,0:T(8,128)(2,1)S(1)}, bf16[384,256]{1,0:T(8,128)(2,1)S(1)}, u32[]{:S(2)}, u32[]{:S(2)}) %collective-permute-start.9) | collective-permute-done | bytes 196640 | tf_op jit(solution)/shard_map/ppermute | solution.py:128
  27.7 1.5 %shard_map.262 = (f32[768,256]{1,0:T(8,128)S(1)}, f32[2,256]{1,0:T(2,128)S(1)}, bf16[768,256]{1,0:T(8,128)(2,1)S(1)}) custom-call(s32[1]{0:T(128)} %bitcast.at_ref, bf16[384,256]{1,0:T(8,128)(2,1)S(1)} %shard_map.260.pair, bf16[384,256]{1,0:T(8,128)(2,1)S(1)} %collective-permute-done.9.pair_far, bf16[768,768]{1,0:T(8,128)(2,1)S(1)} %shard_map.261.w_all, ...), custom_call_target="tpu_custom_call" | custom-call | flops 1000000000 | bytes 1024 | tf_op jit(solution)/shard_map/pallas_call | solution.py:93
  29.8 1.6 %collective-permute-done.11.c2 = bf16[192,512]{1,0:T(8,128)(2,1)S(1)} collective-permute-done((bf16[192,512]{1,0:T(8,128)(2,1)S(1)}, bf16[192,512]{1,0:T(8,128)(2,1)S(1)}, u32[]{:S(2)}, u32[]{:S(2)}) %collective-permute-start.11) | collective-permute-done | bytes 196640 | tf_op jit(solution)/shard_map/ppermute | solution.py:128
  34.0 2.6 %shard_map.264 = (bf16[768,512]{1,0:T(8,128)(2,1)S(1)}, bf16[768,512]{1,0:T(8,128)(2,1)S(1)}, bf16[768,512]{1,0:T(8,128)(2,1)S(1)}, bf16[768,256]{1,0:T(8,128)(2,1)S(1)}, f32[768,256]{1,0:T(8,128)S(1)}) custom-call(bf16[768,256]{1,0:T(8,128)(2,1)S(1)} %get-tuple-element.180.own, bf16[768,256]{1,0:T(8,128)(2,1)S(1)} %collective-permute-done.13.other, ...), custom_call_target="tpu_custom_call" | custom-call | flops 1000000000 | bytes 1024 | tf_op jit(solution)/shard_map/pallas_call | solution.py:93
  38.1 1.7 %collective-permute-start.17 = (bf16[384,768]{1,0:T(8,128)(2,1)S(1)}, bf16[384,768]{1,0:T(8,128)(2,1)S(1)}, u32[]{:S(2)}, u32[]{:S(2)}) collective-permute-start(bf16[384,768]{1,0:T(8,128)(2,1)S(1)} %get-tuple-element.208), channel_id=1, source_target_pairs={{0,4},{4,0},{8,12},{12,8},{16,20},{20,16},{24,28},{28,24},{1,5},{5... | collective-permute-start | bytes 1769480 | tf_op jit(solution)/shard_map/ppermute | solution.py:128
  41.0 1.6 %collective-permute-start.15 = (bf16[768,256]{1,0:T(8,128)(2,1)S(1)}, bf16[768,256]{1,0:T(8,128)(2,1)S(1)}, u32[]{:S(2)}, u32[]{:S(2)}) collective-permute-start(bf16[768,256]{1,0:T(8,128)(2,1)S(1)} %get-tuple-element.200), channel_id=1, source_target_pairs={{0,2},{1,3},{2,0},{3,1},{4,6},{5,7},{6,4},{7,5},{8,10},{9,11},{10,... | collective-permute-start | bytes 1179656 | tf_op jit(solution)/shard_map/ppermute | solution.py:128
  42.6 1.6 %collective-permute-start.18 = (bf16[384,768]{1,0:T(8,128)(2,1)S(1)}, bf16[384,768]{1,0:T(8,128)(2,1)S(1)}, u32[]{:S(2)}, u32[]{:S(2)}) collective-permute-start(bf16[384,768]{1,0:T(8,128)(2,1)S(1)} %get-tuple-element.211), channel_id=1, source_target_pairs={{0,8},{4,12},{8,0},{12,4},{16,24},{20,28},{24,16},{28,20},{1,9},{5... | collective-permute-start | bytes 1769480 | tf_op jit(solution)/shard_map/ppermute | solution.py:128
  45.4 5.7 %shard_map.269 = (f32[192,512]{1,0:T(8,128)S(1)}, f32[30,8,128]{2,1,0:T(8,128)S(1)}) custom-call(f32[30]{0:T(128)S(1)} %copy-done.2, s32[1]{0:T(128)S(6)} %copy.29.counts_ref, bf16[192,512]{1,0:T(8,128)(2,1)S(1)} %copy-done.1, bf16[30,192,512]{2,1,0:T(8,128)(2,1)} %history_ref.1), custom_call_target="tpu_custom_call" | custom-call | flops 1000000000 | bytes 1024 | tf_op jit(solution)/shard_map/pallas_call | solution.py:376
  51.9 1.4 %shard_map.270 = (f32[768,256]{1,0:T(8,128)S(1)}, bf16[768,256]{1,0:T(8,128)(2,1)S(1)}, f32[2,768]{1,0:T(2,128)S(1)}) custom-call(s32[1]{0:T(128)} %bitcast.at_ref, f32[1]{0:T(128)S(6)} %copy.30.self_ref, s32[1]{0:T(128)S(6)} %copy.29.counts_ref, f32[768,256]{1,0:T(8,128)S(1)} %get-tuple-element.199.chip, ...), custom_call_target="tpu_custom_call" | custom-call | flops 1000000000 | bytes 1024 | tf_op jit(solution)/shard_map/pallas_call | solution.py:93
  53.7 1.8 %collective-permute-start.20 = (bf16[192,768]{1,0:T(8,128)(2,1)S(1)}, bf16[192,768]{1,0:T(8,128)(2,1)S(1)}, u32[]{:S(2)}, u32[]{:S(2)}) collective-permute-start(bf16[192,768]{1,0:T(8,128)(2,1)S(1)} %get-tuple-element.222), channel_id=1, source_target_pairs={{0,8},{4,12},{8,0},{12,4},{16,24},{20,28},{24,16},{28,20},{1,9},{5... | collective-permute-start | bytes 884744 | tf_op jit(solution)/shard_map/ppermute | solution.py:128
  55.5 2.3 %collective-permute-done.18.refs_1_ = bf16[384,768]{1,0:T(8,128)(2,1)S(1)} collective-permute-done((bf16[384,768]{1,0:T(8,128)(2,1)S(1)}, bf16[384,768]{1,0:T(8,128)(2,1)S(1)}, u32[]{:S(2)}, u32[]{:S(2)}) %collective-permute-start.18) | collective-permute-done | bytes 589856 | tf_op jit(solution)/shard_map/ppermute | solution.py:128
  59.0 3.6 %shard_map.274 = (bf16[576,512]{1,0:T(8,128)(2,1)S(1)}, bf16[768,512]{1,0:T(8,128)(2,1)S(1)}) custom-call(s32[1]{0:T(128)} %bitcast.at_ref, bf16[768,256]{1,0:T(8,128)(2,1)S(1)} %get-tuple-element.213.own, bf16[768,256]{1,0:T(8,128)(2,1)S(1)} %collective-permute-done.19.other, bf16[192,768]{1,0:T(8,128)(2,1)S(1)} %copy-done.5, ...), custom_call_target="tpu_custom_call" | custom-call | flops 1000000000 | bytes 1024 | tf_op jit(solution)/shard_map/pallas_call | solution.py:93
  65.1 2.7 %collective-permute-start.22 = (bf16[96,768]{1,0:T(8,128)(2,1)S(1)}, bf16[96,768]{1,0:T(8,128)(2,1)S(1)}, u32[]{:S(2)}, u32[]{:S(2)}) collective-permute-start(bf16[96,768]{1,0:T(8,128)(2,1)S(1)} %get-tuple-element.227), channel_id=1, source_target_pairs={{0,16},{4,20},{8,24},{12,28},{16,0},{20,4},{24,8},{28,12},{1,17},{... | collective-permute-start | bytes 442376 | tf_op jit(solution)/shard_map/ppermute | solution.py:128
  70.0 1.4 %collective-permute-start.26 = (bf16[192,768]{1,0:T(8,128)(2,1)S(1)}, bf16[192,768]{1,0:T(8,128)(2,1)S(1)}, u32[]{:S(2)}, u32[]{:S(2)}) collective-permute-start(bf16[192,768]{1,0:T(8,128)(2,1)S(1)} %get-tuple-element.243), channel_id=1, source_target_pairs={{0,8},{4,12},{8,0},{12,4},{16,24},{20,28},{24,16},{28,20},{1,9},{5... | collective-permute-start | bytes 884744 | tf_op jit(solution)/shard_map/ppermute | solution.py:128
  71.5 2.1 %collective-permute-done.22.refs_1_ = bf16[96,768]{1,0:T(8,128)(2,1)S(1)} collective-permute-done((bf16[96,768]{1,0:T(8,128)(2,1)S(1)}, bf16[96,768]{1,0:T(8,128)(2,1)S(1)}, u32[]{:S(2)}, u32[]{:S(2)}) %collective-permute-start.22) | collective-permute-done | bytes 147488 | tf_op jit(solution)/shard_map/ppermute | solution.py:128
  74.0 2.3 %shard_map.279 = (bf16[192,512]{1,0:T(8,128)(2,1)S(1)}, bf16[192,512]{1,0:T(8,128)(2,1)S(1)}, f32[192,512]{1,0:T(8,128)S(1)}, f32[192,512]{1,0:T(8,128)S(1)}, f32[8,768]{1,0:T(8,128)S(1)}) custom-call(s32[1]{0:T(128)} %bitcast.at_ref, s32[1]{0:T(128)S(6)} %copy.29.counts_ref, bf16[576,512]{1,0:T(8,128)(2,1)S(1)} %get-tuple-element.228.refs_0_.d_project, ...), custom_call_target="tpu_custom_call" | custom-call | flops 100000000 | bytes 1024 | tf_op jit(solution)/shard_map/pallas_call | solution.py:93
  78.3 2.7 %collective-permute-start.28 = (bf16[96,768]{1,0:T(8,128)(2,1)S(1)}, bf16[96,768]{1,0:T(8,128)(2,1)S(1)}, u32[]{:S(2)}, u32[]{:S(2)}) collective-permute-start(bf16[96,768]{1,0:T(8,128)(2,1)S(1)} %get-tuple-element.249), channel_id=1, source_target_pairs={{0,8},{4,12},{8,0},{12,4},{16,24},{20,28},{24,16},{28,20},{1,9},{5... | collective-permute-start | bytes 442376 | tf_op jit(solution)/shard_map/ppermute | solution.py:128
  81.0 2.1 %collective-permute-done.26.refs_1_ = bf16[192,768]{1,0:T(8,128)(2,1)S(1)} collective-permute-done((bf16[192,768]{1,0:T(8,128)(2,1)S(1)}, bf16[192,768]{1,0:T(8,128)(2,1)S(1)}, u32[]{:S(2)}, u32[]{:S(2)}) %collective-permute-start.26) | collective-permute-done | bytes 294944 | tf_op jit(solution)/shard_map/ppermute | solution.py:128
  84.7 1.4 %collective-permute-done.28.refs_1_ = bf16[96,768]{1,0:T(8,128)(2,1)S(1)} collective-permute-done((bf16[96,768]{1,0:T(8,128)(2,1)S(1)}, bf16[96,768]{1,0:T(8,128)(2,1)S(1)}, u32[]{:S(2)}, u32[]{:S(2)}) %collective-permute-start.28) | collective-permute-done | bytes 147488 | tf_op jit(solution)/shard_map/ppermute | solution.py:128
  86.1 1.3 collective-permute-start.36
  88.7 2.8 %collective-permute-done.30.refs_1_ = f32[8,768]{1,0:T(8,128)S(1)} collective-permute-done((f32[8,768]{1,0:T(8,128)S(1)}, f32[8,768]{1,0:T(8,128)S(1)}, u32[]{:S(2)}, u32[]{:S(2)}) %collective-permute-start.30) | collective-permute-done | bytes 24608 | tf_op jit(solution)/shard_map/ppermute | solution.py:128
  92.4 2.8 %collective-permute-done.32.refs_1_ = f32[8,768]{1,0:T(8,128)S(1)} collective-permute-done((f32[8,768]{1,0:T(8,128)S(1)}, f32[8,768]{1,0:T(8,128)S(1)}, u32[]{:S(2)}, u32[]{:S(2)}) %collective-permute-start.32) | collective-permute-done | bytes 24608 | tf_op jit(solution)/shard_map/ppermute | solution.py:128
  95.3 1.6 %collective-permute-start.37 = (bf16[48,768]{1,0:T(8,128)(2,1)S(1)}, bf16[48,768]{1,0:T(8,128)(2,1)S(1)}, u32[]{:S(2)}, u32[]{:S(2)}) collective-permute-start(bf16[48,768]{1,0:T(8,128)(2,1)S(1)} %get-tuple-element.264), channel_id=1, source_target_pairs={{0,16},{4,20},{8,24},{12,28},{16,0},{20,4},{24,8},{28,12},{1,17},{... | collective-permute-start | bytes 221192 | tf_op jit(solution)/shard_map/ppermute | solution.py:128
  96.9 1.4 collective-permute-start.35
  98.3 1.6 %collective-permute-start.40 = (bf16[192,512]{1,0:T(8,128)(2,1)S(1)}, bf16[192,512]{1,0:T(8,128)(2,1)S(1)}, u32[]{:S(2)}, u32[]{:S(2)}) collective-permute-start(bf16[192,512]{1,0:T(8,128)(2,1)S(1)} %shard_map.287), channel_id=1, source_target_pairs={{0,2},{1,3},{2,0},{3,1},{4,6},{5,7},{6,4},{7,5},{8,10},{9,11},{10,... | collective-permute-start | bytes 589832 | tf_op jit(solution)/shard_map/ppermute | solution.py:128
  100.9 2.8 %collective-permute-start.38 = (bf16[48,768]{1,0:T(8,128)(2,1)S(1)}, bf16[48,768]{1,0:T(8,128)(2,1)S(1)}, u32[]{:S(2)}, u32[]{:S(2)}) collective-permute-start(bf16[48,768]{1,0:T(8,128)(2,1)S(1)} %get-tuple-element.266), channel_id=1, source_target_pairs={{0,16},{4,20},{8,24},{12,28},{16,0},{20,4},{24,8},{28,12},{1,17},{... | collective-permute-start | bytes 221192 | tf_op jit(solution)/shard_map/ppermute | solution.py:128
  106.2 2.1 %collective-permute-start.45 = (bf16[192,768]{1,0:T(8,128)(2,1)S(1)}, bf16[192,768]{1,0:T(8,128)(2,1)S(1)}, u32[]{:S(2)}, u32[]{:S(2)}) collective-permute-start(bf16[192,768]{1,0:T(8,128)(2,1)S(1)} %shard_map.290.refs_0_), channel_id=1, source_target_pairs={{0,4},{4,0},{8,12},{12,8},{16,20},{20,16},{24,28},{28,24},{1,5},{5... | collective-permute-start | bytes 884744 | tf_op jit(solution)/shard_map/ppermute | solution.py:128
  108.3 1.4 %collective-permute-start.44 = (f32[8,768]{1,0:T(8,128)S(1)}, f32[8,768]{1,0:T(8,128)S(1)}, u32[]{:S(2)}, u32[]{:S(2)}) collective-permute-start(f32[8,768]{1,0:T(8,128)S(1)} %shard_map.291.refs_0_), channel_id=1, source_target_pairs={{0,16},{4,20},{8,24},{12,28},{16,0},{20,4},{24,8},{28,12},{1,17},{... | collective-permute-start | bytes 73736 | tf_op jit(solution)/shard_map/ppermute | solution.py:128
  109.7 1.6 %collective-permute-start.43 = (bf16[48,768]{1,0:T(8,128)(2,1)S(1)}, bf16[48,768]{1,0:T(8,128)(2,1)S(1)}, u32[]{:S(2)}, u32[]{:S(2)}) collective-permute-start(bf16[48,768]{1,0:T(8,128)(2,1)S(1)} %shard_map.294.refs_0_), channel_id=1, source_target_pairs={{0,16},{4,20},{8,24},{12,28},{16,0},{20,4},{24,8},{28,12},{1,17},{... | collective-permute-start | bytes 221192 | tf_op jit(solution)/shard_map/ppermute | solution.py:128
  111.5 2.4 %collective-permute-done.41.refs_1_ = bf16[192,768]{1,0:T(8,128)(2,1)S(1)} collective-permute-done((bf16[192,768]{1,0:T(8,128)(2,1)S(1)}, bf16[192,768]{1,0:T(8,128)(2,1)S(1)}, u32[]{:S(2)}, u32[]{:S(2)}) %collective-permute-start.41) | collective-permute-done | bytes 294944 | tf_op jit(solution)/shard_map/ppermute | solution.py:128
  115.3 1.9 %collective-permute-start.47 = (bf16[96,768]{1,0:T(8,128)(2,1)S(1)}, bf16[96,768]{1,0:T(8,128)(2,1)S(1)}, u32[]{:S(2)}, u32[]{:S(2)}) collective-permute-start(bf16[96,768]{1,0:T(8,128)(2,1)S(1)} %shard_map.298.refs_0_), channel_id=1, source_target_pairs={{0,4},{4,0},{8,12},{12,8},{16,20},{20,16},{24,28},{28,24},{1,5},{5... | collective-permute-start | bytes 442376 | tf_op jit(solution)/shard_map/ppermute | solution.py:128
  117.3 1.8 %collective-permute-start.49 = (bf16[384,768]{1,0:T(8,128)(2,1)S(1)}, bf16[384,768]{1,0:T(8,128)(2,1)S(1)}, u32[]{:S(2)}, u32[]{:S(2)}) collective-permute-start(bf16[384,768]{1,0:T(8,128)(2,1)S(1)} %shard_map.300.refs_0_), channel_id=1, source_target_pairs={{0,8},{4,12},{8,0},{12,4},{16,24},{20,28},{24,16},{28,20},{1,9},{5... | collective-permute-start | bytes 1769480 | tf_op jit(solution)/shard_map/ppermute | solution.py:128
  119.2 1.6 %collective-permute-done.46.refs_1_ = bf16[96,768]{1,0:T(8,128)(2,1)S(1)} collective-permute-done((bf16[96,768]{1,0:T(8,128)(2,1)S(1)}, bf16[96,768]{1,0:T(8,128)(2,1)S(1)}, u32[]{:S(2)}, u32[]{:S(2)}) %collective-permute-start.46) | collective-permute-done | bytes 147488 | tf_op jit(solution)/shard_map/ppermute | solution.py:128
  122.1 1.8 %collective-permute-start.51 = (bf16[192,768]{1,0:T(8,128)(2,1)S(1)}, bf16[192,768]{1,0:T(8,128)(2,1)S(1)}, u32[]{:S(2)}, u32[]{:S(2)}) collective-permute-start(bf16[192,768]{1,0:T(8,128)(2,1)S(1)} %shard_map.302.refs_2_), channel_id=1, source_target_pairs={{0,8},{4,12},{8,0},{12,4},{16,24},{20,28},{24,16},{28,20},{1,9},{5... | collective-permute-start | bytes 884744 | tf_op jit(solution)/shard_map/ppermute | solution.py:128
  123.9 1.9 %collective-permute-start.50 = (bf16[192,768]{1,0:T(8,128)(2,1)S(1)}, bf16[192,768]{1,0:T(8,128)(2,1)S(1)}, u32[]{:S(2)}, u32[]{:S(2)}) collective-permute-start(bf16[192,768]{1,0:T(8,128)(2,1)S(1)} %shard_map.301.refs_0_), channel_id=1, source_target_pairs={{0,4},{4,0},{8,12},{12,8},{16,20},{20,16},{24,28},{28,24},{1,5},{5... | collective-permute-start | bytes 884744 | tf_op jit(solution)/shard_map/ppermute | solution.py:128
  126.5 4.1 %shard_map.304 = bf16[30,192,512]{2,1,0:T(8,128)(2,1)} custom-call(f32[30]{0:T(128)S(1)} %copy-done.2, s32[1]{0:T(128)S(6)} %copy.29.counts_ref, bf16[192,512]{1,0:T(8,128)(2,1)S(1)} %copy-done.1, f32[8,768]{1,0:T(8,128)S(1)} %shard_map.299.sums), custom_call_target="tpu_custom_call" | custom-call | flops 100000000 | bytes 1024 | tf_op jit(solution)/shard_map/pallas_call | solution.py:376
  131.5 1.5 %collective-permute-done.48.refs_1_ = bf16[384,768]{1,0:T(8,128)(2,1)S(1)} collective-permute-done((bf16[384,768]{1,0:T(8,128)(2,1)S(1)}, bf16[384,768]{1,0:T(8,128)(2,1)S(1)}, u32[]{:S(2)}, u32[]{:S(2)}) %collective-permute-start.48) | collective-permute-done | bytes 589856 | tf_op jit(solution)/shard_map/ppermute | solution.py:128
  132.9 1.6 %shard_map.306 = f32[768,768]{1,0:T(8,128)} custom-call(s32[1]{0:T(128)} %bitcast.1.me_ref, f32[8,768]{1,0:T(8,128)S(1)} %shard_map.299.sums, bf16[384,768]{1,0:T(8,128)(2,1)S(1)} %shard_map.296.refs_0_, bf16[384,768]{1,0:T(8,128)(2,1)S(1)} %collective-permute-done.48.refs_1_), custom_call_target="tpu_custom_call" | custom-call | flops 100000000 | bytes 1024 | tf_op jit(solution)/shard_map/pallas_call | solution.py:312
  134.5 1.6 %shard_map.307 = f32[768,768]{1,0:T(8,128)} custom-call(s32[1]{0:T(128)} %bitcast.1.me_ref, f32[8,768]{1,0:T(8,128)S(1)} %shard_map.299.sums, bf16[384,768]{1,0:T(8,128)(2,1)S(1)} %shard_map.300.refs_0_, bf16[384,768]{1,0:T(8,128)(2,1)S(1)} %collective-permute-done.49.refs_1_), custom_call_target="tpu_custom_call" | custom-call | flops 400000000 | bytes 1024 | tf_op jit(solution)/shard_map/pallas_call | solution.py:312
  136.1 1.8 %shard_map.308 = (f32[576,768]{1,0:T(8,128)}, f32[192,768]{1,0:T(8,128)}) custom-call(s32[1]{0:T(128)} %bitcast.1.me_ref, f32[8,768]{1,0:T(8,128)S(1)} %shard_map.299.sums, bf16[192,768]{1,0:T(8,128)(2,1)S(1)} %shard_map.301.refs_0_, bf16[192,768]{1,0:T(8,128)(2,1)S(1)} %collective-permute-done.50.refs_1_, bf16[192,768]{1,0:T(8,128)(2,1)S(1)} %shard_map.302.refs_2_, ...), custom_call_target="tpu_custom_call" | custom-call | flops 100000000 | bytes 1024 | tf_op jit(solution)/shard_map/pallas_call | solution.py:312
  (122 shorter events, 31.3 us)
Async XLA Ops:
  0.7 3.1 %collective-permute-start = (bf16[192,512]{1,0:T(8,128)(2,1)}, bf16[192,512]{1,0:T(8,128)(2,1)S(1)}, u32[]{:S(2)}, u32[]{:S(2)}) collective-permute-start(bf16[192,512]{1,0:T(8,128)(2,1)} %refs_7_), channel_id=1, source_target_pairs={{0,1},{1,0},{2,3},{3,2},{4,5},{5,4},{6,7},{7,6},{8,9},{9,8},{10,11... | collective-permute-start | bytes 589832 | tf_op jit(solution)/shard_map/ppermute | solution.py:128
  1.2 8.9 %collective-permute-start.3 = (bf16[192,512]{1,0:T(8,128)(2,1)}, bf16[192,512]{1,0:T(8,128)(2,1)S(1)}, u32[]{:S(2)}, u32[]{:S(2)}) collective-permute-start(bf16[192,512]{1,0:T(8,128)(2,1)} %refs_7_), channel_id=1, source_target_pairs={{0,2},{1,3},{2,0},{3,1},{4,6},{5,7},{6,4},{7,5},{8,10},{9,11},{10,... | collective-permute-start | bytes 589832 | tf_op jit(solution)/shard_map/ppermute | solution.py:128
  6.2 3.7 %collective-permute-start.2 = (f32[16,256]{1,0:T(8,128)S(1)}, f32[16,256]{1,0:T(8,128)S(1)}, u32[]{:S(2)}, u32[]{:S(2)}) collective-permute-start(f32[16,256]{1,0:T(8,128)S(1)} %shard_map.256.n01), channel_id=1, source_target_pairs={{0,2},{1,3},{2,0},{3,1},{4,6},{5,7},{6,4},{7,5},{8,10},{9,11},{10,... | collective-permute-start | bytes 49160 | tf_op jit(solution)/shard_map/ppermute | solution.py:128
  10.2 9.6 %collective-permute-start.5 = (bf16[192,768]{1,0:T(8,128)(2,1)}, bf16[192,768]{1,0:T(8,128)(2,1)S(1)}, u32[]{:S(2)}, u32[]{:S(2)}) collective-permute-start(bf16[192,768]{1,0:T(8,128)(2,1)} %w_out.1), channel_id=1, source_target_pairs={{0,2},{1,3},{2,0},{3,1},{4,6},{5,7},{6,4},{7,5},{8,10},{9,11},{10,... | collective-permute-start | bytes 884744 | tf_op jit(solution)/shard_map/ppermute | solution.py:128
  18.1 3.9 %collective-permute-start.7 = (bf16[192,768]{1,0:T(8,128)(2,1)S(1)}, bf16[192,768]{1,0:T(8,128)(2,1)S(1)}, u32[]{:S(2)}, u32[]{:S(2)}) collective-permute-start(bf16[192,768]{1,0:T(8,128)(2,1)S(1)} %copy-done.5), channel_id=1, source_target_pairs={{0,1},{1,0},{2,3},{3,2},{4,5},{5,4},{6,7},{7,6},{8,9},{9,8},{10,11... | collective-permute-start | bytes 884744 | tf_op jit(solution)/shard_map/ppermute | solution.py:128
  19.8 2.2 %collective-permute-start.8 = (bf16[192,768]{1,0:T(8,128)(2,1)S(1)}, bf16[192,768]{1,0:T(8,128)(2,1)S(1)}, u32[]{:S(2)}, u32[]{:S(2)}) collective-permute-start(bf16[192,768]{1,0:T(8,128)(2,1)S(1)} %collective-permute-done.5.refs_2_), channel_id=1, source_target_pairs={{0,1},{1,0},{2,3},{3,2},{4,5},{5,4},{6,7},{7,6},{8,9},{9,8},{10,11... | collective-permute-start | bytes 884744 | tf_op jit(solution)/shard_map/ppermute | solution.py:128
  19.9 7.8 %collective-permute-start.9 = (bf16[384,256]{1,0:T(8,128)(2,1)S(1)}, bf16[384,256]{1,0:T(8,128)(2,1)S(1)}, u32[]{:S(2)}, u32[]{:S(2)}) collective-permute-start(bf16[384,256]{1,0:T(8,128)(2,1)S(1)} %shard_map.260.pair), channel_id=1, source_target_pairs={{0,2},{1,3},{2,0},{3,1},{4,6},{5,7},{6,4},{7,5},{8,10},{9,11},{10,... | collective-permute-start | bytes 589832 | tf_op jit(solution)/shard_map/ppermute | solution.py:128
  21.7 9.8 %collective-permute-start.11 = (bf16[192,512]{1,0:T(8,128)(2,1)S(1)}, bf16[192,512]{1,0:T(8,128)(2,1)S(1)}, u32[]{:S(2)}, u32[]{:S(2)}) collective-permute-start(bf16[192,512]{1,0:T(8,128)(2,1)S(1)} %copy-done.1), channel_id=1, source_target_pairs={{0,2},{1,3},{2,0},{3,1},{4,6},{5,7},{6,4},{7,5},{8,10},{9,11},{10,... | collective-permute-start | bytes 589832 | tf_op jit(solution)/shard_map/ppermute | solution.py:128
  29.2 4.8 %collective-permute-start.13 = (bf16[768,256]{1,0:T(8,128)(2,1)S(1)}, bf16[768,256]{1,0:T(8,128)(2,1)S(1)}, u32[]{:S(2)}, u32[]{:S(2)}) collective-permute-start(bf16[768,256]{1,0:T(8,128)(2,1)S(1)} %get-tuple-element.180.own), channel_id=1, source_target_pairs={{0,1},{1,0},{2,3},{3,2},{4,5},{5,4},{6,7},{7,6},{8,9},{9,8},{10,11... | collective-permute-start | bytes 1179656 | tf_op jit(solution)/shard_map/ppermute | solution.py:128
  29.3 3.5 %collective-permute-start.10 = (bf16[192,512]{1,0:T(8,128)(2,1)S(1)}, bf16[192,512]{1,0:T(8,128)(2,1)S(1)}, u32[]{:S(2)}, u32[]{:S(2)}) collective-permute-start(bf16[192,512]{1,0:T(8,128)(2,1)S(1)} %copy-done.1), channel_id=1, source_target_pairs={{0,1},{1,0},{2,3},{3,2},{4,5},{5,4},{6,7},{7,6},{8,9},{9,8},{10,11... | collective-permute-start | bytes 589832 | tf_op jit(solution)/shard_map/ppermute | solution.py:128
  36.7 3.2 %collective-permute-start.14 = (bf16[768,256]{1,0:T(8,128)(2,1)S(1)}, bf16[768,256]{1,0:T(8,128)(2,1)S(1)}, u32[]{:S(2)}, u32[]{:S(2)}) collective-permute-start(bf16[768,256]{1,0:T(8,128)(2,1)S(1)} %get-tuple-element.188), channel_id=1, source_target_pairs={{0,1},{1,0},{2,3},{3,2},{4,5},{5,4},{6,7},{7,6},{8,9},{9,8},{10,11... | collective-permute-start | bytes 1179656 | tf_op jit(solution)/shard_map/ppermute | solution.py:128
  38.1 15.3 %collective-permute-start.17 = (bf16[384,768]{1,0:T(8,128)(2,1)S(1)}, bf16[384,768]{1,0:T(8,128)(2,1)S(1)}, u32[]{:S(2)}, u32[]{:S(2)}) collective-permute-start(bf16[384,768]{1,0:T(8,128)(2,1)S(1)} %get-tuple-element.208), channel_id=1, source_target_pairs={{0,4},{4,0},{8,12},{12,8},{16,20},{20,16},{24,28},{28,24},{1,5},{5... | collective-permute-start | bytes 1769480 | tf_op jit(solution)/shard_map/ppermute | solution.py:128
  41.0 10.8 %collective-permute-start.15 = (bf16[768,256]{1,0:T(8,128)(2,1)S(1)}, bf16[768,256]{1,0:T(8,128)(2,1)S(1)}, u32[]{:S(2)}, u32[]{:S(2)}) collective-permute-start(bf16[768,256]{1,0:T(8,128)(2,1)S(1)} %get-tuple-element.200), channel_id=1, source_target_pairs={{0,2},{1,3},{2,0},{3,1},{4,6},{5,7},{6,4},{7,5},{8,10},{9,11},{10,... | collective-permute-start | bytes 1179656 | tf_op jit(solution)/shard_map/ppermute | solution.py:128
  42.6 15.1 %collective-permute-start.18 = (bf16[384,768]{1,0:T(8,128)(2,1)S(1)}, bf16[384,768]{1,0:T(8,128)(2,1)S(1)}, u32[]{:S(2)}, u32[]{:S(2)}) collective-permute-start(bf16[384,768]{1,0:T(8,128)(2,1)S(1)} %get-tuple-element.211), channel_id=1, source_target_pairs={{0,8},{4,12},{8,0},{12,4},{16,24},{20,28},{24,16},{28,20},{1,9},{5... | collective-permute-start | bytes 1769480 | tf_op jit(solution)/shard_map/ppermute | solution.py:128
  45.3 8.0 %collective-permute-start.16 = (bf16[192,512]{1,0:T(8,128)(2,1)S(1)}, bf16[192,512]{1,0:T(8,128)(2,1)S(1)}, u32[]{:S(2)}, u32[]{:S(2)}) collective-permute-start(bf16[192,512]{1,0:T(8,128)(2,1)S(1)} %get-tuple-element.206), channel_id=1, source_target_pairs={{0,1},{1,0},{2,3},{3,2},{4,5},{5,4},{6,7},{7,6},{8,9},{9,8},{10,11... | collective-permute-start | bytes 589832 | tf_op jit(solution)/shard_map/ppermute | solution.py:128
  53.4 5.6 %collective-permute-start.19 = (bf16[768,256]{1,0:T(8,128)(2,1)S(1)}, bf16[768,256]{1,0:T(8,128)(2,1)S(1)}, u32[]{:S(2)}, u32[]{:S(2)}) collective-permute-start(bf16[768,256]{1,0:T(8,128)(2,1)S(1)} %get-tuple-element.213.own), channel_id=1, source_target_pairs={{0,1},{1,0},{2,3},{3,2},{4,5},{5,4},{6,7},{7,6},{8,9},{9,8},{10,11... | collective-permute-start | bytes 1179656 | tf_op jit(solution)/shard_map/ppermute | solution.py:128
  53.7 10.0 %collective-permute-start.20 = (bf16[192,768]{1,0:T(8,128)(2,1)S(1)}, bf16[192,768]{1,0:T(8,128)(2,1)S(1)}, u32[]{:S(2)}, u32[]{:S(2)}) collective-permute-start(bf16[192,768]{1,0:T(8,128)(2,1)S(1)} %get-tuple-element.222), channel_id=1, source_target_pairs={{0,8},{4,12},{8,0},{12,4},{16,24},{20,28},{24,16},{28,20},{1,9},{5... | collective-permute-start | bytes 884744 | tf_op jit(solution)/shard_map/ppermute | solution.py:128
  57.9 7.1 %collective-permute-start.21 = (bf16[192,768]{1,0:T(8,128)(2,1)S(1)}, bf16[192,768]{1,0:T(8,128)(2,1)S(1)}, u32[]{:S(2)}, u32[]{:S(2)}) collective-permute-start(bf16[192,768]{1,0:T(8,128)(2,1)S(1)} %get-tuple-element.225), channel_id=1, source_target_pairs={{0,4},{4,0},{8,12},{12,8},{16,20},{20,16},{24,28},{28,24},{1,5},{5... | collective-permute-start | bytes 884744 | tf_op jit(solution)/shard_map/ppermute | solution.py:128
  65.1 8.4 %collective-permute-start.22 = (bf16[96,768]{1,0:T(8,128)(2,1)S(1)}, bf16[96,768]{1,0:T(8,128)(2,1)S(1)}, u32[]{:S(2)}, u32[]{:S(2)}) collective-permute-start(bf16[96,768]{1,0:T(8,128)(2,1)S(1)} %get-tuple-element.227), channel_id=1, source_target_pairs={{0,16},{4,20},{8,24},{12,28},{16,0},{20,4},{24,8},{28,12},{1,17},{... | collective-permute-start | bytes 442376 | tf_op jit(solution)/shard_map/ppermute | solution.py:128
  67.8 8.5 %collective-permute-start.23 = (bf16[192,512]{1,0:T(8,128)(2,1)S(1)}, bf16[192,512]{1,0:T(8,128)(2,1)S(1)}, u32[]{:S(2)}, u32[]{:S(2)}) collective-permute-start(bf16[192,512]{1,0:T(8,128)(2,1)S(1)} %get-tuple-element.196), channel_id=1, source_target_pairs={{0,1},{1,0},{2,3},{3,2},{4,5},{5,4},{6,7},{7,6},{8,9},{9,8},{10,11... | collective-permute-start | bytes 589832 | tf_op jit(solution)/shard_map/ppermute | solution.py:128
  67.8 8.5 %collective-permute-start.24 = (bf16[192,512]{1,0:T(8,128)(2,1)S(1)}, bf16[192,512]{1,0:T(8,128)(2,1)S(1)}, u32[]{:S(2)}, u32[]{:S(2)}) collective-permute-start(bf16[192,512]{1,0:T(8,128)(2,1)S(1)} %shard_map.271), channel_id=1, source_target_pairs={{0,2},{1,3},{2,0},{3,1},{4,6},{5,7},{6,4},{7,5},{8,10},{9,11},{10,... | collective-permute-start | bytes 589832 | tf_op jit(solution)/shard_map/ppermute | solution.py:128
  69.0 9.1 %collective-permute-start.25 = (bf16[192,768]{1,0:T(8,128)(2,1)S(1)}, bf16[192,768]{1,0:T(8,128)(2,1)S(1)}, u32[]{:S(2)}, u32[]{:S(2)}) collective-permute-start(bf16[192,768]{1,0:T(8,128)(2,1)S(1)} %get-tuple-element.240), channel_id=1, source_target_pairs={{0,4},{4,0},{8,12},{12,8},{16,20},{20,16},{24,28},{28,24},{1,5},{5... | collective-permute-start | bytes 884744 | tf_op jit(solution)/shard_map/ppermute | solution.py:128
  70.0 13.0 %collective-permute-start.26 = (bf16[192,768]{1,0:T(8,128)(2,1)S(1)}, bf16[192,768]{1,0:T(8,128)(2,1)S(1)}, u32[]{:S(2)}, u32[]{:S(2)}) collective-permute-start(bf16[192,768]{1,0:T(8,128)(2,1)S(1)} %get-tuple-element.243), channel_id=1, source_target_pairs={{0,8},{4,12},{8,0},{12,4},{16,24},{20,28},{24,16},{28,20},{1,9},{5... | collective-permute-start | bytes 884744 | tf_op jit(solution)/shard_map/ppermute | solution.py:128
  73.6 11.1 %collective-permute-start.27 = (bf16[96,768]{1,0:T(8,128)(2,1)S(1)}, bf16[96,768]{1,0:T(8,128)(2,1)S(1)}, u32[]{:S(2)}, u32[]{:S(2)}) collective-permute-start(bf16[96,768]{1,0:T(8,128)(2,1)S(1)} %get-tuple-element.247), channel_id=1, source_target_pairs={{0,16},{4,20},{8,24},{12,28},{16,0},{20,4},{24,8},{28,12},{1,17},{... | collective-permute-start | bytes 442376 | tf_op jit(solution)/shard_map/ppermute | solution.py:128
  78.3 7.8 %collective-permute-start.28 = (bf16[96,768]{1,0:T(8,128)(2,1)S(1)}, bf16[96,768]{1,0:T(8,128)(2,1)S(1)}, u32[]{:S(2)}, u32[]{:S(2)}) collective-permute-start(bf16[96,768]{1,0:T(8,128)(2,1)S(1)} %get-tuple-element.249), channel_id=1, source_target_pairs={{0,8},{4,12},{8,0},{12,4},{16,24},{20,28},{24,16},{28,20},{1,9},{5... | collective-permute-start | bytes 442376 | tf_op jit(solution)/shard_map/ppermute | solution.py:128
  81.0 11.4 %collective-permute-start.31 = (bf16[192,512]{1,0:T(8,128)(2,1)S(1)}, bf16[192,512]{1,0:T(8,128)(2,1)S(1)}, u32[]{:S(2)}, u32[]{:S(2)}) collective-permute-start(bf16[192,512]{1,0:T(8,128)(2,1)S(1)} %get-tuple-element.255), channel_id=1, source_target_pairs={{0,1},{1,0},{2,3},{3,2},{4,5},{5,4},{6,7},{7,6},{8,9},{9,8},{10,11... | collective-permute-start | bytes 589832 | tf_op jit(solution)/shard_map/ppermute | solution.py:128
  83.2 13.7 %collective-permute-start.33 = (bf16[96,768]{1,0:T(8,128)(2,1)S(1)}, bf16[96,768]{1,0:T(8,128)(2,1)S(1)}, u32[]{:S(2)}, u32[]{:S(2)}) collective-permute-start(bf16[96,768]{1,0:T(8,128)(2,1)S(1)} %get-tuple-element.258), channel_id=1, source_target_pairs={{0,4},{4,0},{8,12},{12,8},{16,20},{20,16},{24,28},{28,24},{1,5},{5... | collective-permute-start | bytes 442376 | tf_op jit(solution)/shard_map/ppermute | solution.py:128
  84.3 14.0 %collective-permute-start.34 = (bf16[96,768]{1,0:T(8,128)(2,1)S(1)}, bf16[96,768]{1,0:T(8,128)(2,1)S(1)}, u32[]{:S(2)}, u32[]{:S(2)}) collective-permute-start(bf16[96,768]{1,0:T(8,128)(2,1)S(1)} %shard_map.278.refs_0_), channel_id=1, source_target_pairs={{0,16},{4,20},{8,24},{12,28},{16,0},{20,4},{24,8},{28,12},{1,17},{... | collective-permute-start | bytes 442376 | tf_op jit(solution)/shard_map/ppermute | solution.py:128
  84.6 2.9 %collective-permute-start.29 = (f32[8,768]{1,0:T(8,128)S(1)}, f32[8,768]{1,0:T(8,128)S(1)}, u32[]{:S(2)}, u32[]{:S(2)}) collective-permute-start(f32[8,768]{1,0:T(8,128)S(1)} %get-tuple-element.251.refs_0_), channel_id=1, source_target_pairs={{0,1},{1,0},{2,3},{3,2},{4,5},{5,4},{6,7},{7,6},{8,9},{9,8},{10,11... | collective-permute-start | bytes 73736 | tf_op jit(solution)/shard_map/ppermute | solution.py:128
  86.1 17.5 %collective-permute-start.36 = (bf16[96,768]{1,0:T(8,128)(2,1)S(1)}, bf16[96,768]{1,0:T(8,128)(2,1)S(1)}, u32[]{:S(2)}, u32[]{:S(2)}) collective-permute-start(bf16[96,768]{1,0:T(8,128)(2,1)S(1)} %shard_map.283.refs_0_), channel_id=1, source_target_pairs={{0,16},{4,20},{8,24},{12,28},{16,0},{20,4},{24,8},{28,12},{1,17},{... | collective-permute-start | bytes 442376 | tf_op jit(solution)/shard_map/ppermute | solution.py:128
  87.6 3.9 %collective-permute-start.30 = (f32[8,768]{1,0:T(8,128)S(1)}, f32[8,768]{1,0:T(8,128)S(1)}, u32[]{:S(2)}, u32[]{:S(2)}) collective-permute-start(f32[8,768]{1,0:T(8,128)S(1)} %shard_map.285.refs_0_), channel_id=1, source_target_pairs={{0,2},{1,3},{2,0},{3,1},{4,6},{5,7},{6,4},{7,5},{8,10},{9,11},{10,... | collective-permute-start | bytes 73736 | tf_op jit(solution)/shard_map/ppermute | solution.py:128
  91.5 3.8 %collective-permute-start.32 = (f32[8,768]{1,0:T(8,128)S(1)}, f32[8,768]{1,0:T(8,128)S(1)}, u32[]{:S(2)}, u32[]{:S(2)}) collective-permute-start(f32[8,768]{1,0:T(8,128)S(1)} %shard_map.286.refs_0_.row_sums), channel_id=1, source_target_pairs={{0,4},{4,0},{8,12},{12,8},{16,20},{20,16},{24,28},{28,24},{1,5},{5... | collective-permute-start | bytes 73736 | tf_op jit(solution)/shard_map/ppermute | solution.py:128
  92.4 15.9 %collective-permute-start.39 = (bf16[192,512]{1,0:T(8,128)(2,1)S(1)}, bf16[192,512]{1,0:T(8,128)(2,1)S(1)}, u32[]{:S(2)}, u32[]{:S(2)}) collective-permute-start(bf16[192,512]{1,0:T(8,128)(2,1)S(1)} %get-tuple-element.231), channel_id=1, source_target_pairs={{0,1},{1,0},{2,3},{3,2},{4,5},{5,4},{6,7},{7,6},{8,9},{9,8},{10,11... | collective-permute-start | bytes 589832 | tf_op jit(solution)/shard_map/ppermute | solution.py:128
  95.3 9.6 %collective-permute-start.37 = (bf16[48,768]{1,0:T(8,128)(2,1)S(1)}, bf16[48,768]{1,0:T(8,128)(2,1)S(1)}, u32[]{:S(2)}, u32[]{:S(2)}) collective-permute-start(bf16[48,768]{1,0:T(8,128)(2,1)S(1)} %get-tuple-element.264), channel_id=1, source_target_pairs={{0,16},{4,20},{8,24},{12,28},{16,0},{20,4},{24,8},{28,12},{1,17},{... | collective-permute-start | bytes 221192 | tf_op jit(solution)/shard_map/ppermute | solution.py:128
  96.9 4.0 %collective-permute-start.35 = (f32[8,768]{1,0:T(8,128)S(1)}, f32[8,768]{1,0:T(8,128)S(1)}, u32[]{:S(2)}, u32[]{:S(2)}) collective-permute-start(f32[8,768]{1,0:T(8,128)S(1)} %shard_map.288.refs_0_), channel_id=1, source_target_pairs={{0,8},{4,12},{8,0},{12,4},{16,24},{20,28},{24,16},{28,20},{1,9},{5... | collective-permute-start | bytes 73736 | tf_op jit(solution)/shard_map/ppermute | solution.py:128
  98.3 11.4 %collective-permute-start.40 = (bf16[192,512]{1,0:T(8,128)(2,1)S(1)}, bf16[192,512]{1,0:T(8,128)(2,1)S(1)}, u32[]{:S(2)}, u32[]{:S(2)}) collective-permute-start(bf16[192,512]{1,0:T(8,128)(2,1)S(1)} %shard_map.287), channel_id=1, source_target_pairs={{0,2},{1,3},{2,0},{3,1},{4,6},{5,7},{6,4},{7,5},{8,10},{9,11},{10,... | collective-permute-start | bytes 589832 | tf_op jit(solution)/shard_map/ppermute | solution.py:128
  100.9 5.3 %collective-permute-start.38 = (bf16[48,768]{1,0:T(8,128)(2,1)S(1)}, bf16[48,768]{1,0:T(8,128)(2,1)S(1)}, u32[]{:S(2)}, u32[]{:S(2)}) collective-permute-start(bf16[48,768]{1,0:T(8,128)(2,1)S(1)} %get-tuple-element.266), channel_id=1, source_target_pairs={{0,16},{4,20},{8,24},{12,28},{16,0},{20,4},{24,8},{28,12},{1,17},{... | collective-permute-start | bytes 221192 | tf_op jit(solution)/shard_map/ppermute | solution.py:128
  103.7 10.2 %collective-permute-start.41 = (bf16[192,768]{1,0:T(8,128)(2,1)S(1)}, bf16[192,768]{1,0:T(8,128)(2,1)S(1)}, u32[]{:S(2)}, u32[]{:S(2)}) collective-permute-start(bf16[192,768]{1,0:T(8,128)(2,1)S(1)} %shard_map.292.refs_0_), channel_id=1, source_target_pairs={{0,8},{4,12},{8,0},{12,4},{16,24},{20,28},{24,16},{28,20},{1,9},{5... | collective-permute-start | bytes 884744 | tf_op jit(solution)/shard_map/ppermute | solution.py:128
  104.9 9.1 %collective-permute-start.42 = (bf16[48,768]{1,0:T(8,128)(2,1)S(1)}, bf16[48,768]{1,0:T(8,128)(2,1)S(1)}, u32[]{:S(2)}, u32[]{:S(2)}) collective-permute-start(bf16[48,768]{1,0:T(8,128)(2,1)S(1)} %shard_map.293.refs_0_), channel_id=1, source_target_pairs={{0,16},{4,20},{8,24},{12,28},{16,0},{20,4},{24,8},{28,12},{1,17},{... | collective-permute-start | bytes 221192 | tf_op jit(solution)/shard_map/ppermute | solution.py:128
  106.2 11.0 %collective-permute-start.45 = (bf16[192,768]{1,0:T(8,128)(2,1)S(1)}, bf16[192,768]{1,0:T(8,128)(2,1)S(1)}, u32[]{:S(2)}, u32[]{:S(2)}) collective-permute-start(bf16[192,768]{1,0:T(8,128)(2,1)S(1)} %shard_map.290.refs_0_), channel_id=1, source_target_pairs={{0,4},{4,0},{8,12},{12,8},{16,20},{20,16},{24,28},{28,24},{1,5},{5... | collective-permute-start | bytes 884744 | tf_op jit(solution)/shard_map/ppermute | solution.py:128
  108.3 8.9 %collective-permute-start.44 = (f32[8,768]{1,0:T(8,128)S(1)}, f32[8,768]{1,0:T(8,128)S(1)}, u32[]{:S(2)}, u32[]{:S(2)}) collective-permute-start(f32[8,768]{1,0:T(8,128)S(1)} %shard_map.291.refs_0_), channel_id=1, source_target_pairs={{0,16},{4,20},{8,24},{12,28},{16,0},{20,4},{24,8},{28,12},{1,17},{... | collective-permute-start | bytes 73736 | tf_op jit(solution)/shard_map/ppermute | solution.py:128
  109.7 5.5 %collective-permute-start.43 = (bf16[48,768]{1,0:T(8,128)(2,1)S(1)}, bf16[48,768]{1,0:T(8,128)(2,1)S(1)}, u32[]{:S(2)}, u32[]{:S(2)}) collective-permute-start(bf16[48,768]{1,0:T(8,128)(2,1)S(1)} %shard_map.294.refs_0_), channel_id=1, source_target_pairs={{0,16},{4,20},{8,24},{12,28},{16,0},{20,4},{24,8},{28,12},{1,17},{... | collective-permute-start | bytes 221192 | tf_op jit(solution)/shard_map/ppermute | solution.py:128
  114.0 6.9 %collective-permute-start.46 = (bf16[96,768]{1,0:T(8,128)(2,1)S(1)}, bf16[96,768]{1,0:T(8,128)(2,1)S(1)}, u32[]{:S(2)}, u32[]{:S(2)}) collective-permute-start(bf16[96,768]{1,0:T(8,128)(2,1)S(1)} %shard_map.297.refs_0_), channel_id=1, source_target_pairs={{0,8},{4,12},{8,0},{12,4},{16,24},{20,28},{24,16},{28,20},{1,9},{5... | collective-permute-start | bytes 442376 | tf_op jit(solution)/shard_map/ppermute | solution.py:128
  115.3 6.9 %collective-permute-start.47 = (bf16[96,768]{1,0:T(8,128)(2,1)S(1)}, bf16[96,768]{1,0:T(8,128)(2,1)S(1)}, u32[]{:S(2)}, u32[]{:S(2)}) collective-permute-start(bf16[96,768]{1,0:T(8,128)(2,1)S(1)} %shard_map.298.refs_0_), channel_id=1, source_target_pairs={{0,4},{4,0},{8,12},{12,8},{16,20},{20,16},{24,28},{28,24},{1,5},{5... | collective-permute-start | bytes 442376 | tf_op jit(solution)/shard_map/ppermute | solution.py:128
  117.3 17.2 %collective-permute-start.49 = (bf16[384,768]{1,0:T(8,128)(2,1)S(1)}, bf16[384,768]{1,0:T(8,128)(2,1)S(1)}, u32[]{:S(2)}, u32[]{:S(2)}) collective-permute-start(bf16[384,768]{1,0:T(8,128)(2,1)S(1)} %shard_map.300.refs_0_), channel_id=1, source_target_pairs={{0,8},{4,12},{8,0},{12,4},{16,24},{20,28},{24,16},{28,20},{1,9},{5... | collective-permute-start | bytes 1769480 | tf_op jit(solution)/shard_map/ppermute | solution.py:128
  119.0 13.9 %collective-permute-start.48 = (bf16[384,768]{1,0:T(8,128)(2,1)S(1)}, bf16[384,768]{1,0:T(8,128)(2,1)S(1)}, u32[]{:S(2)}, u32[]{:S(2)}) collective-permute-start(bf16[384,768]{1,0:T(8,128)(2,1)S(1)} %shard_map.296.refs_0_), channel_id=1, source_target_pairs={{0,4},{4,0},{8,12},{12,8},{16,20},{20,16},{24,28},{28,24},{1,5},{5... | collective-permute-start | bytes 1769480 | tf_op jit(solution)/shard_map/ppermute | solution.py:128
  122.1 13.9 %collective-permute-start.51 = (bf16[192,768]{1,0:T(8,128)(2,1)S(1)}, bf16[192,768]{1,0:T(8,128)(2,1)S(1)}, u32[]{:S(2)}, u32[]{:S(2)}) collective-permute-start(bf16[192,768]{1,0:T(8,128)(2,1)S(1)} %shard_map.302.refs_2_), channel_id=1, source_target_pairs={{0,8},{4,12},{8,0},{12,4},{16,24},{20,28},{24,16},{28,20},{1,9},{5... | collective-permute-start | bytes 884744 | tf_op jit(solution)/shard_map/ppermute | solution.py:128
  123.9 12.2 %collective-permute-start.50 = (bf16[192,768]{1,0:T(8,128)(2,1)S(1)}, bf16[192,768]{1,0:T(8,128)(2,1)S(1)}, u32[]{:S(2)}, u32[]{:S(2)}) collective-permute-start(bf16[192,768]{1,0:T(8,128)(2,1)S(1)} %shard_map.301.refs_0_), channel_id=1, source_target_pairs={{0,4},{4,0},{8,12},{12,8},{16,20},{20,16},{24,28},{28,24},{1,5},{5... | collective-permute-start | bytes 884744 | tf_op jit(solution)/shard_map/ppermute | solution.py:128
  (10 other events, 41.4 us)
